TPU v7x, 32 devices: a whole 2x2x4 slice. The times are simulated.
32 devices in a mesh: ctx: 4 (over y, x), head: 4 (over z), dp: 2 (over core).
Axes of the slice: x: 2, y: 2, z: 4, core: 2. Of those that a mesh axis runs over, the one named last changes fastest.
Arguments:
- queries: bfloat16 [2, 1024, 4096], P('dp', 'ctx', 'head'), may hold values from -6 to 6
- keys: bfloat16 [2, 1024, 4096], P('dp', 'ctx', 'head'), may hold values from -6 to 6
- values: bfloat16 [2, 1024, 4096], P('dp', 'ctx', 'head'), may hold values from -6 to 6
- log_decay: float32 [2, 32, 1024], P('dp', 'head', 'ctx'), may hold values from -1.5 to 0
- w_out: bfloat16 [128, 32, 3072], P(('ctx', 'dp'), 'head'), may hold values from -0.09375 to 0.09375
- grad_out: bfloat16 [2, 1024, 3072], P('dp', 'ctx'), may hold values from -6 to 6
Outputs:
- mixed: bfloat16 [2, 1024, 3072], P('dp', 'ctx', 'head')
- query_grad: bfloat16 [2, 1024, 4096], P('dp', 'ctx', 'head')
- key_grad: bfloat16 [2, 1024, 4096], P('dp', 'ctx', 'head')
- value_grad: bfloat16 [2, 1024, 4096], P('dp', 'ctx', 'head')
- w_grad: float32 [128, 32, 3072], P(('ctx', 'dp'), 'head')
All inputs are finite; a program needn't handle non-finite values.
Results may differ from a plain program's by a relative error of at most 0.015.
Values may be sent and summed in bfloat16 or wider, within the bound.
No kernel may reach another device: no remote copies, remote signals or barrier semaphores. Data moves between devices by JAX's collectives and lax.ppermute only.
A program may use at most 128 MiB of HBM per device.

v0:
```python
import jax
import jax.numpy as jnp
from jax import lax
from jax.sharding import PartitionSpec as P

DH = 128
BLOCK = 256


def entering_2(array, axis, combine, identity, reverse):
    devices, mine = (lax.axis_size(axis), lax.axis_index(axis))
    everything = jax.tree.map(lambda part: lax.all_gather(part, axis), array)
    start = jax.tree.map(
        lambda part, zero: jnp.broadcast_to(jnp.asarray(zero, part.dtype), part.shape),
        array,
        identity,
    )

    def lap(k, before):
        at = devices - 1 - k if reverse else k
        reached = at > mine if reverse else at < mine
        new = combine(before, jax.tree.map(lambda part: part[at], everything))
        return jax.tree.map(lambda a, b: jnp.where(reached, a, b), new, before)

    return lax.fori_loop(0, devices, lap, start)


def block_weights(cumul):
    width = cumul.shape[-1]
    places = jnp.arange(width)
    lower = places[:, None] >= places[None, :]
    spread = cumul[..., :, None] - cumul[..., None, :]
    return jnp.exp(jnp.where(lower, spread, -jnp.inf))


def forward_join(earlier, later):
    return (earlier[0] * later[0], later[0][:, None, None] * earlier[1] + later[1])


def backward_combine(earlier, later):
    return (earlier[0] * later[0], later[1] + later[0][:, None, None] * earlier[1])


def shards(queries, keys, values, log_decay, w_out, grad_out):
    groups = log_decay.shape[1]
    length_here = queries.shape[1]
    tile_number = length_here // BLOCK
    scale = 1.0 / DH
    query_blocks = queries[0].reshape(tile_number, BLOCK, groups, DH)
    key_blocks = keys[0].reshape(tile_number, BLOCK, groups, DH)
    value_blocks = values[0].reshape(tile_number, BLOCK, groups, DH)
    places = jnp.arange(BLOCK)
    upper = (places[:, None] <= places[None, :]).astype(jnp.float32)
    cumul = jnp.einsum(
        "hnj,jt->hnt",
        log_decay[0].reshape(groups, tile_number, BLOCK),
        upper,
        precision=lax.Precision.HIGHEST,
    )
    weights = block_weights(cumul)
    decay_multiplier = jnp.transpose(scale * jnp.exp(cumul), (1, 2, 0))[..., None]
    tail = jnp.transpose(jnp.exp(cumul[..., -1:] - cumul), (1, 2, 0))[..., None]
    block_decay = jnp.exp(cumul[..., -1])
    ones_decay = jnp.ones((groups,), jnp.float32)
    zero_state = jnp.zeros((groups, DH, DH), jnp.float32)
    scores = jnp.einsum(
        "nthd,njhd->hntj", query_blocks, key_blocks, preferred_element_type=jnp.float32
    )
    probs = (scores * scale * weights).astype(jnp.bfloat16)
    intra = jnp.einsum("hntj,njhd->nthd", probs, value_blocks, preferred_element_type=jnp.float32)
    keys_weighted = (key_blocks * tail).astype(jnp.bfloat16)
    contrib = jnp.einsum(
        "nthd,nthe->hnde", keys_weighted, value_blocks, preferred_element_type=jnp.float32
    )
    total_decay = ones_decay
    total_state = zero_state
    index = 0
    total_state = block_decay[:, index][:, None, None] * total_state + contrib[:, index]
    total_decay = total_decay * block_decay[:, index]
    incoming = entering_2(
        (total_decay, total_state), "ctx", forward_join, (ones_decay, zero_state), False
    )[1]
    running = incoming
    index = 0
    entering = [running]
    state_low = jnp.stack(entering, axis=1).astype(jnp.bfloat16)
    inter = jnp.einsum(
        "nthd,hnde->nthe", query_blocks, state_low, preferred_element_type=jnp.float32
    )
    attended = (intra + inter * decay_multiplier).astype(jnp.bfloat16)
    attended_row_list = attended.reshape(length_here, groups, DH)
    panel = lax.all_gather(w_out, ("ctx", "dp"), axis=0, tiled=True)
    partial_out = jnp.einsum(
        "thd,dho->to", attended_row_list, panel, preferred_element_type=jnp.float32
    )
    mixed = lax.psum_scatter(
        partial_out.astype(jnp.bfloat16), "head", scatter_dimension=1, tiled=True
    )
    cotangent = grad_out[0]
    grad_heads = jnp.einsum(
        "to,dho->thd", cotangent, panel, preferred_element_type=jnp.float32
    ).astype(jnp.bfloat16)
    grad_blocks = grad_heads.reshape(tile_number, BLOCK, groups, DH)
    w_grad = lax.psum_scatter(
        jnp.einsum("thd,to->dho", attended_row_list, cotangent, preferred_element_type=jnp.float32),
        ("ctx", "dp"),
        scatter_dimension=0,
        tiled=True,
    )
    logit_gradient = jnp.einsum(
        "nthe,njhe->hntj", grad_blocks, value_blocks, preferred_element_type=jnp.float32
    )
    dprobs = (logit_gradient * scale * weights).astype(jnp.bfloat16)
    queries_weighted = (query_blocks * decay_multiplier).astype(jnp.bfloat16)
    local_grad = jnp.einsum(
        "nthd,nthe->hnde", queries_weighted, grad_blocks, preferred_element_type=jnp.float32
    )
    faded_carry = ones_decay
    after_state = zero_state
    for index in reversed(range(tile_number)):
        after_state = block_decay[:, index][:, None, None] * after_state + local_grad[:, index]
        faded_carry = faded_carry * block_decay[:, index]
    leaving = entering_2(
        (faded_carry, after_state), "ctx", backward_combine, (ones_decay, zero_state), True
    )[1]
    exiting = []
    running = leaving
    for index in reversed(range(tile_number)):
        exiting = [running] + exiting
        running = block_decay[:, index][:, None, None] * running + local_grad[:, index]
    back_low = jnp.stack(exiting, axis=1).astype(jnp.bfloat16)
    query_grad = (
        jnp.einsum("hntj,njhd->nthd", dprobs, key_blocks, preferred_element_type=jnp.float32)
        + jnp.einsum("nthe,hnde->nthd", grad_blocks, state_low, preferred_element_type=jnp.float32)
        * decay_multiplier
    )
    key_grad = jnp.einsum(
        "hntj,nthd->njhd", dprobs, query_blocks, preferred_element_type=jnp.float32
    ) + tail * jnp.einsum(
        "nthe,hnde->nthd", value_blocks, back_low, preferred_element_type=jnp.float32
    )
    value_grad = jnp.einsum(
        "hntj,nthe->njhe", probs, grad_blocks, preferred_element_type=jnp.float32
    ) + tail * jnp.einsum(
        "nthd,hnde->nthe", key_blocks, back_low, preferred_element_type=jnp.float32
    )
    flat = (1, length_here, groups * DH)
    return (
        mixed[None],
        query_grad.astype(jnp.bfloat16).reshape(flat),
        key_grad.astype(jnp.bfloat16).reshape(flat),
        value_grad.astype(jnp.bfloat16).reshape(flat),
        w_grad,
    )


def solution(mesh):
    return jax.shard_map(
        shards,
        mesh=mesh,
        in_specs=(
            P("dp", "ctx", "head"),
            P("dp", "ctx", "head"),
            P("dp", "ctx", "head"),
            P("dp", "head", "ctx"),
            P(("ctx", "dp"), "head", None),
            P("dp", "ctx", None),
        ),
        out_specs=(
            P("dp", "ctx", "head"),
            P("dp", "ctx", "head"),
            P("dp", "ctx", "head"),
            P("dp", "ctx", "head"),
            P(("ctx", "dp"), "head", None),
        ),
        check_vma=False,
    )
```

profile of v0, /device:TPU:0, one launch (start us, length us, event | category | flops | bytes accessed | tf_op | source)
XLA Modules:
  0.0 274.1 jit_solution(11742911888028347455)
XLA Ops:
  7.2 0.0 copy-start
  7.2 0.0 all-gather.7.cloned.1.call-start
  7.2 2.6 copy.67
  9.8 0.0 all-gather.7.cloned.1.call-update
  9.9 0.0 all-gather.9.cloned.1.call-start
  9.9 0.1 copy.92
  10.0 0.0 copy-start.6
  10.0 0.3 copy.62
  10.4 1.3 copy.93
  11.7 0.1 fusion.30
  11.9 0.3 multiply_reduce_fusion
  12.1 0.1 exponential_bitcast_fusion
  12.2 1.1 convolution_add_fusion.1
  13.3 0.0 all-gather.9.cloned.1.call-update
  13.4 0.0 all-gather.11.cloned.1.call-start
  13.4 1.2 copy.91
  14.7 44.1 %all-gather.7.cloned.1.call-done = bf16[128,8,3072]{2,0,1:T(8,128)(2,1)} async-done(((bf16[16,8,3072]{2,0,1:T(8,128)(2,1)}), bf16[128,8,3072]{2,0,1:T(8,128)(2,1)}) %all-gather.7.cloned.1.call-update) | async-done | bytes 6291472 | tf_op jit(solution)/shard_map/all_gather | solution.py:92
  58.8 4.6 %fusion.18 = bf16[128,8,256]{2,0,1:T(8,128)(2,1)S(1)} fusion(bf16[128,8,3072]{2,0,1:T(8,128)(2,1)} %all-gather.7.cloned.1.call-done, bf16[1,256,3072]{2,1,0:T(8,128)(2,1)S(1)} %copy-done), kind=kOutput, calls=%fused_computation.35 | convolution fusion | flops 1610874880 | bytes 8388608 | tf_op jit(solution)/shard_map/to,dho->thd/dot_general | solution.py:100
  63.4 0.0 copy-start.16
  63.4 1.1 convolution_add_fusion
  64.5 0.0 all-gather.11.cloned.1.call-update
  64.5 0.0 reduce-scatter.5.cloned.1.call-start
  64.6 0.6 dynamic-slice
  65.9 0.2 dynamic-update-slice
  66.1 9.1 %all-reduce = f32[32]{0:T(128)S(1)} all-reduce(f32[32]{0:T(128)S(1)} %dynamic-update-slice), channel_id=2, replica_groups=mesh['ctx'=4,'head'=4,'dp'=2] {'ctx'}, use_global_device_ids=true, to_apply=%add | all-reduce | flops 32 | bytes 256
  75.2 0.1 reshape.167
  75.3 1.8 multiply_convert_fusion.1
  77.2 1.0 copy-done.8
  78.2 1.4 convolution_bitcast_fusion.9
  79.6 17.0 %all-gather.9.cloned.1.call-done = f32[32,128,128]{2,1,0:T(8,128)} async-done(((f32[8,128,128]{2,1,0:T(8,128)}), f32[32,128,128]{2,1,0:T(8,128)}) %all-gather.9.cloned.1.call-update) | async-done | bytes 2097168 | tf_op jit(solution)/shard_map/all_gather | solution.py:12
  96.6 4.8 %while.30 = (s32[]{:T(128)}, f32[8,128,128]{2,1,0:T(8,128)S(1)}, s32[]{:T(128)}, f32[4,8]{1,0:T(4,128)S(1)}, f32[4,8,128,128]{3,2,1,0:T(8,128)}, /*index=5*/s32[]{:T(128)}, s32[]{:T(128)}) while((s32[]{:T(128)}, f32[8,128,128]{2,1,0:T(8,128)S(1)}, s32[]{:T(128)}, f32[4,8]{1,0:T(4,128)S(1)}, f32[4,8,128,128]{3,2,1,0:T(8,128)}, ...), condition=%wide.region_1.2_spmd.clone, body=%wide.region_0.1_spmd.clone.sunk | while | flops 524292 | bytes 1573073 | solution.py:25
  96.6 1.2 fusion.55
  97.8 1.2 fusion.55
  99.0 1.2 fusion.55
  100.2 1.2 fusion.55
  101.4 1.7 fusion.21
  103.2 0.8 copy-done.11
  103.9 6.4 %convolution_bitcast_fusion = f32[128,8,3072]{2,0,1:T(8,128)} fusion(bf16[256,8,128]{2,0,1:T(8,128)(2,1)S(1)} %fusion.21, bf16[1,256,3072]{2,1,0:T(8,128)(2,1)S(1)} %copy-done), kind=kOutput, calls=%fused_computation.6 | convolution fusion | flops 1610612736 | bytes 14680064 | tf_op jit(solution)/shard_map/thd,to->dho/dot_general | solution.py:105
  110.3 0.0 reduce-scatter.5.cloned.1.call-update
  110.3 0.2 reduce-scatter.3.cloned.1.call-start
  110.6 5.9 %fusion.2 = bf16[256,3072]{1,0:T(8,128)(2,1)} fusion(bf16[256,8,128]{2,0,1:T(8,128)(2,1)} %copy-done.11, bf16[128,8,3072]{2,0,1:T(8,128)(2,1)} %all-gather.7.cloned.1.call-done), kind=kOutput, calls=%fused_computation.8 | convolution fusion | flops 1611399168 | bytes 8388608 | tf_op jit(solution)/shard_map/thd,dho->to/dot_general | solution.py:93
  116.5 0.0 reduce-scatter.3.cloned.1.call-update
  116.6 2.0 multiply_convert_fusion
  118.6 1.0 copy-done.10
  119.6 0.4 convolution_bitcast_fusion.8
  120.0 0.8 copy-done.4
  120.8 1.3 fusion.17
  122.1 2.1 copy.73
  124.2 2.1 copy.80
  126.3 2.6 convolution_bitcast_fusion.6
  128.9 1.3 convolution_bitcast_fusion.7
  130.2 3.5 %all-gather.11.cloned.1.call-done = f32[32,128,128]{2,1,0:T(8,128)} async-done(((f32[8,128,128]{2,1,0:T(8,128)}), f32[32,128,128]{2,1,0:T(8,128)}) %all-gather.11.cloned.1.call-update) | async-done | bytes 2097168 | tf_op jit(solution)/shard_map/all_gather | solution.py:12
  133.8 4.9 %while.31 = (s32[]{:T(128)}, f32[8,128,128]{2,1,0:T(8,128)S(1)}, s32[]{:T(128)}, f32[4,8,128,128]{3,2,1,0:T(8,128)}, f32[4,8]{1,0:T(4,128)S(1)}, /*index=5*/s32[]{:T(128)}, s32[]{:T(128)}, s32[]{:T(128)}, s32[]{:T(128)}) while((s32[]{:T(128)}, f32[8,128,128]{2,1,0:T(8,128)S(1)}, s32[]{:T(128)}, f32[4,8,128,128]{3,2,1,0:T(8,128)}, ...), condition=%wide.region_4.5_spmd.clone, body=%wide.region_3.4_spmd.clone.sunk | while | flops 524296 | bytes 1573135 | solution.py:25
  133.8 1.2 fusion.56
  135.0 1.2 fusion.56
  136.3 1.2 fusion.56
  137.5 1.2 fusion.56
  138.7 2.4 fusion.16
  141.1 2.0 copy.81
  143.2 1.6 fusion.15
  144.8 1.0 copy.82
  145.8 83.8 %reduce-scatter.5.cloned.1.call-done = f32[16,8,3072]{2,0,1:T(8,128)} async-done(((f32[128,8,3072]{2,0,1:T(8,128)}), f32[16,8,3072]{2,0,1:T(8,128)}) %reduce-scatter.5.cloned.1.call-update) | async-done | bytes 1572880 | tf_op jit(solution)/shard_map/reduce_scatter | solution.py:104
  229.5 3.5 %copy.83 = f32[16,8,3072]{2,1,0:T(8,128)} copy(f32[16,8,3072]{2,0,1:T(8,128)} %reduce-scatter.5.cloned.1.call-done) | data formatting | bytes 3145728
  233.0 34.6 %reduce-scatter.3.cloned.1.call-done = bf16[256,768]{1,0:T(8,128)(2,1)} async-done(((bf16[256,3072]{1,0:T(8,128)(2,1)}), bf16[256,768]{1,0:T(8,128)(2,1)}) %reduce-scatter.3.cloned.1.call-update) | async-done | bytes 393232 | tf_op jit(solution)/shard_map/reduce_scatter | solution.py:96
  (39 shorter events, 0.2 us)
Async XLA Ops:
  7.2 51.6 %copy-start = (bf16[1,256,3072]{2,1,0:T(8,128)(2,1)S(1)}, bf16[1,256,3072]{2,1,0:T(8,128)(2,1)}, u32[]{:S(2)}) copy-start(bf16[1,256,3072]{2,1,0:T(8,128)(2,1)} %param.15) | copy-start | bytes 4718596
  7.2 2.7 copy-start.14
  7.2 51.6 %all-gather.7.cloned.1.call-start = ((), (), s32[]{:S(2)}) async-start(), calls=%async_computation.2 | async-start | bytes 7077888 | tf_op jit(solution)/shard_map/all_gather | solution.py:92
  9.8 1.9 copy-start.15
  9.9 86.7 %all-gather.9.cloned.1.call-start = ((), (), s32[]{:S(2)}) async-start(), calls=%async_computation.5 | async-start | bytes 2621440 | tf_op jit(solution)/shard_map/all_gather | solution.py:12
  10.0 3.3 %copy-start.6 = (bf16[32,8,8,128]{3,2,1,0:T(8,128)(2,1)}, bf16[32,8,8,128]{3,2,1,0:T(8,128)(2,1)S(1)}, u32[]{:S(2)}) copy-start(bf16[32,8,8,128]{3,2,1,0:T(8,128)(2,1)S(1)} %copy.92) | copy-start | bytes 1572868
  10.4 4.3 %copy-start.12 = (bf16[256,8,128]{0,2,1:T(8,128)(2,1)}, bf16[256,8,128]{0,2,1:T(8,128)(2,1)S(1)}, u32[]{:S(2)}) copy-start(bf16[256,8,128]{0,2,1:T(8,128)(2,1)S(1)} %copy.62) | copy-start | bytes 1572868
  11.7 65.4 %copy-start.1 = (bf16[32,8,8,128]{3,2,1,0:T(8,128)(2,1)}, bf16[32,8,8,128]{3,2,1,0:T(8,128)(2,1)S(1)}, u32[]{:S(2)}) copy-start(bf16[32,8,8,128]{3,2,1,0:T(8,128)(2,1)S(1)} %copy.93) | copy-start | bytes 1572868
  13.4 120.4 %all-gather.11.cloned.1.call-start = ((), (), s32[]{:S(2)}) async-start(), calls=%async_computation.6 | async-start | bytes 2621440 | tf_op jit(solution)/shard_map/all_gather | solution.py:12
  63.4 1.2 copy-start.3
  63.4 1.2 copy-start.16
  64.5 165.0 %reduce-scatter.5.cloned.1.call-start = ((), (), s32[]{:S(2)}) async-start(), calls=%async_computation.4 | async-start | bytes 14155776 | tf_op jit(solution)/shard_map/reduce_scatter | solution.py:104
  77.2 1.0 copy-start.8
  103.2 0.8 copy-start.11
  110.3 157.2 %reduce-scatter.3.cloned.1.call-start = ((), (), s32[]{:S(2)}) async-start(), calls=%async_computation.3 | async-start | bytes 1966080 | tf_op jit(solution)/shard_map/reduce_scatter | solution.py:96
  116.5 3.0 %copy-start.13 = (bf16[256,8,128]{0,2,1:T(8,128)(2,1)S(1)}, bf16[256,8,128]{0,2,1:T(8,128)(2,1)}, u32[]{:S(2)}) copy-start(bf16[256,8,128]{0,2,1:T(8,128)(2,1)} %copy-done.12) | copy-start | bytes 1572868
  118.6 1.0 copy-start.10
  119.6 1.2 copy-start.4
  124.2 4.8 %copy-start.5 = (bf16[128,8,256]{2,0,1:T(8,128)(2,1)S(1)}, bf16[128,8,256]{2,0,1:T(8,128)(2,1)}, u32[]{:S(2)}) copy-start(bf16[128,8,256]{2,0,1:T(8,128)(2,1)} %copy-done.3) | copy-start | bytes 1572868
  126.3 2.7 copy-start.9
  133.8 4.9 %copy-start.2 = (bf16[32,8,8,128]{3,2,1,0:T(8,128)(2,1)S(1)}, bf16[32,8,8,128]{3,2,1,0:T(8,128)(2,1)}, u32[]{:S(2)}) copy-start(bf16[32,8,8,128]{3,2,1,0:T(8,128)(2,1)} %copy-done.1) | copy-start | bytes 1572868
  138.7 4.5 %copy-start.7 = (bf16[32,8,8,128]{3,2,1,0:T(8,128)(2,1)S(1)}, bf16[32,8,8,128]{3,2,1,0:T(8,128)(2,1)}, u32[]{:S(2)}) copy-start(bf16[32,8,8,128]{3,2,1,0:T(8,128)(2,1)} %copy-done.6) | copy-start | bytes 1572868
Sparse Core Ops, SparseCore 0:
  10.5 48.2 all-gather.6
  61.2 35.3 all-gather.8
  98.4 35.2 all-gather.10
  137.1 92.3 reduce-scatter.4
  232.3 35.2 reduce-scatter.2
where the time goes:
time: 275 us; the launch traced here: 274 us
  waiting for transfers between devices  183 us (67%)
  matrix products  36 us (13%)
  local copies, waits for them, and re-layouts  20.9 us (8%)
  between operations  14.7 us (5%)
  other arithmetic  9.82 us (4%)
  blocking collectives  9.11 us (3%)
    reduce_scatter x1, waiting for transfers between devices, shards(): lax.psum_scatter(jnp.einsum('thd,to->dho', attended_row_list, cotangent,...  83.8 us
    all_gather x1, waiting for transfers between devices, shards(): panel = lax.all_gather(w_out, ('ctx', 'dp'), axis=0, tiled=True)  44.1 us
    reduce_scatter x1, waiting for transfers between devices, shards(): lax.psum_scatter(partial_out.astype(jnp.bfloat16), 'head', scatter_dimens...  34.6 us
    all_gather x2, waiting for transfers between devices, entering_2(): everything = jax.tree.map(lambda part: lax.all_gather(part, axis), array)  20.5 us
    unnamed x44, local copies, waits for them, and re-layouts  17.1 us
    select_n x8, other arithmetic, lap(): return jax.tree.map(lambda a, b: jnp.where(reached, a, b), new, before)  9.45 us
    unnamed x1, blocking collectives  9.11 us
    dot_general x1, matrix products, shards(): jnp.einsum('thd,to->dho', attended_row_list, cotangent, preferred_element...  6.37 us
  transfers between devices with their start and end apart: 5, of which 5 were waited for; matrix products, arithmetic and copies ran while one was open for 22% of the time, Pallas kernels for 0%

commit v1 on v0

v1 whole, which is shorter than its diff:
```python
import functools

import jax
import jax.numpy as jnp
from jax import lax
from jax.experimental import pallas as pl
from jax.experimental.pallas import tpu as pltpu
from jax.sharding import PartitionSpec as P

DH = 128
SCALE = 1.0 / DH
F32 = jnp.float32
BF16 = jnp.bfloat16
EXTRA = 16


def contract(a, b, dim_a, dim_b):
    return lax.dot_general(a, b, (((dim_a,), (dim_b,)), ((), ())), preferred_element_type=F32)


def head(ref, h):
    return ref[:, h * DH : (h + 1) * DH]


def call(kernel, out_shape, scratch=()):
    return pl.pallas_call(
        kernel,
        out_shape=out_shape,
        scratch_shapes=list(scratch),
        compiler_params=pltpu.CompilerParams(vmem_limit_bytes=48 * 1024 * 1024),
    )


def struct(shape, dtype):
    return jax.ShapeDtypeStruct(shape, dtype)


def store_decay(out_ref, row, groups):
    decay = jnp.broadcast_to(jnp.exp(row[:, -1:]), (groups, DH))
    high = decay.astype(BF16).astype(F32)
    both = jnp.concatenate([high, decay - high], axis=0)
    out_ref[groups * DH : groups * DH + EXTRA, :] = both.astype(BF16)


def load_decay(ref, groups):
    both = ref[groups * DH : groups * DH + EXTRA, :].astype(F32)
    return both[:groups] + both[groups:]


def joined(refs, decays, h):
    total = refs[-1][h * DH : (h + 1) * DH, :].astype(F32)
    for ref, decay in zip(refs[-2::-1], decays[::-1]):
        total = ref[h * DH : (h + 1) * DH, :].astype(F32) + decay[h : h + 1, :] * total
    return total


def lower_mask(size):
    return lax.broadcasted_iota(jnp.int32, (size, size), 0) >= lax.broadcasted_iota(
        jnp.int32, (size, size), 1
    )


def contrib_kernel(groups, k_ref, v_ref, ld_ref, state_ref, row_ref, col_ref):
    size = k_ref.shape[0]
    lower = lower_mask(size).astype(F32)
    ld = ld_ref[...]
    row = lax.dot_general(
        ld, lower, (((1,), (1,)), ((), ())), precision=lax.Precision.HIGHEST, preferred_element_type=F32
    )
    col = lax.dot_general(
        lower, ld, (((1,), (1,)), ((), ())), precision=lax.Precision.HIGHEST, preferred_element_type=F32
    )
    row_ref[...] = row
    col_ref[...] = col
    tail = jnp.exp(col[size - 1 :, :] - col)
    for h in range(groups):
        weighted = (head(k_ref, h).astype(F32) * tail[:, h : h + 1]).astype(BF16)
        state_ref[h * DH : (h + 1) * DH, :] = contract(weighted, head(v_ref, h), 0, 0).astype(BF16)
    store_decay(state_ref, row, groups)


def spread_weights(row_ref, col_ref, lower, h):
    spread = col_ref[:, h : h + 1] - row_ref[h : h + 1, :]
    return jnp.exp(jnp.where(lower, spread, -jnp.inf))


def intra_kernel(groups, q_ref, k_ref, v_ref, row_ref, col_ref, probs_ref, intra_ref):
    lower = lower_mask(q_ref.shape[0])
    for h in range(groups):
        weights = spread_weights(row_ref, col_ref, lower, h)
        probs = (contract(head(q_ref, h), head(k_ref, h), 1, 1) * SCALE * weights).astype(BF16)
        probs_ref[h] = probs
        intra_ref[:, h * DH : (h + 1) * DH] = contract(probs, head(v_ref, h), 1, 0)


def attended_kernel(groups, count, *refs):
    states = refs[:count]
    q_ref, intra_ref, col_ref, pick_own_ref, pick_other_ref = refs[count : count + 5]
    own_ref, other_ref, low_ref, attended_ref = refs[count + 5 :]
    decays = [load_decay(ref, groups) for ref in states[:-1]]
    factor = jnp.exp(col_ref[...]) * SCALE
    for h in range(groups):
        low = joined(states, decays, h).astype(BF16)
        low_ref[h] = low
        inter = contract(head(q_ref, h), low, 1, 0)
        attended_ref[:, h * DH : (h + 1) * DH] = (
            head(intra_ref, h) + inter * factor[:, h : h + 1]
        ).astype(BF16)
    own_ref[...] = contract(attended_ref[...], pick_own_ref[...], 1, 0).astype(BF16)
    other_ref[...] = contract(attended_ref[...], pick_other_ref[...], 1, 0).astype(BF16)


def back_contrib_kernel(
    groups, own_ref, other_ref, pick_own_ref, pick_other_ref, q_ref, row_ref, col_ref, grad_ref, state_ref
):
    grad_ref[...] = (
        contract(own_ref[...], pick_own_ref[...], 1, 1) + contract(other_ref[...], pick_other_ref[...], 1, 1)
    ).astype(BF16)
    factor = jnp.exp(col_ref[...]) * SCALE
    for h in range(groups):
        weighted = (head(q_ref, h).astype(F32) * factor[:, h : h + 1]).astype(BF16)
        state_ref[h * DH : (h + 1) * DH, :] = contract(weighted, head(grad_ref, h), 0, 0).astype(BF16)
    store_decay(state_ref, row_ref[...], groups)


def back_intra_kernel(
    groups, grad_ref, q_ref, k_ref, v_ref, row_ref, col_ref, probs_ref, low_ref, qgrad_ref, kpart_ref, vpart_ref
):
    lower = lower_mask(q_ref.shape[0])
    factor = jnp.exp(col_ref[...]) * SCALE
    for h in range(groups):
        here = slice(h * DH, (h + 1) * DH)
        grad = head(grad_ref, h)
        weights = spread_weights(row_ref, col_ref, lower, h)
        dprobs = (contract(grad, head(v_ref, h), 1, 1) * SCALE * weights).astype(BF16)
        qgrad_ref[:, here] = (
            contract(dprobs, head(k_ref, h), 1, 0) + contract(grad, low_ref[h], 1, 1) * factor[:, h : h + 1]
        ).astype(BF16)
        kpart_ref[:, here] = contract(dprobs, head(q_ref, h), 0, 0)
        vpart_ref[:, here] = contract(probs_ref[h], grad, 0, 0)


def back_inter_kernel(groups, count, *refs):
    states = refs[:count]
    k_ref, v_ref, col_ref, kpart_ref, vpart_ref, kgrad_ref, vgrad_ref = refs[count:]
    decays = [load_decay(ref, groups) for ref in states[:-1]]
    col = col_ref[...]
    tail = jnp.exp(col[col.shape[0] - 1 :, :] - col)
    for h in range(groups):
        here = slice(h * DH, (h + 1) * DH)
        low = joined(states, decays, h).astype(BF16)
        kgrad_ref[:, here] = (
            head(kpart_ref, h) + tail[:, h : h + 1] * contract(head(v_ref, h), low, 1, 1)
        ).astype(BF16)
        vgrad_ref[:, here] = (
            head(vpart_ref, h) + tail[:, h : h + 1] * contract(head(k_ref, h), low, 1, 0)
        ).astype(BF16)


def neighbours(state, devices, forward):
    out = []
    for hop in range(1, devices):
        if forward:
            pairs = [(i, i + hop) for i in range(devices - hop)]
        else:
            pairs = [(i + hop, i) for i in range(devices - hop)]
        out.append(lax.ppermute(state, "ctx", pairs))
    return out


def swapped(array):
    return lax.ppermute(array, "dp", [(0, 1), (1, 0)])


def flipped(array, bit):
    return lax.ppermute(array, "ctx", [(i, i ^ bit) for i in range(4)])


def gather_rows(w):
    if lax.axis_size("ctx") != 4:
        return lax.all_gather(w, "ctx", axis=0, tiled=True)
    half = w.shape[1] // 2
    one, two = flipped(w, 1), flipped(w, 2)
    three = jnp.concatenate([flipped(one[:, :half], 2), flipped(two[:, half:], 1)], axis=1)
    return jnp.concatenate([w, one, two, three], axis=0)


def scatter_rows(attended, cotangent):
    devices = lax.axis_size("ctx")
    if devices != 4:
        part = contract(attended, cotangent, 0, 0).astype(BF16)
        return lax.psum_scatter(part, "ctx", scatter_dimension=0, tiled=True).astype(F32)
    rows = attended.shape[1] // devices
    half = cotangent.shape[1] // 2
    left, right = cotangent[:, :half], cotangent[:, half:]

    def part(k, columns):
        return contract(attended[:, k * rows : (k + 1) * rows], columns, 0, 0)

    far_left = flipped(part(3, left).astype(BF16), 1)
    far_right = flipped(part(3, right).astype(BF16), 2)
    near_left = flipped(part(1, left).astype(BF16), 1)
    near_right = flipped(part(2, right).astype(BF16), 2)
    on_left = flipped((part(2, left) + far_left.astype(F32)).astype(BF16), 2)
    on_right = flipped((part(1, right) + far_right.astype(F32)).astype(BF16), 1)
    return jnp.concatenate(
        [
            part(0, left) + near_left.astype(F32) + on_left.astype(F32),
            part(0, right) + near_right.astype(F32) + on_right.astype(F32),
        ],
        axis=1,
    )


def ring_scatter(own, other):
    devices, mine = lax.axis_size("head"), lax.axis_index("head")
    width = own.shape[1] // devices
    around = [(i, (i + 1) % devices) for i in range(devices)]

    def columns(array, k):
        start = lax.rem(mine - k + devices, devices) * width
        return lax.dynamic_slice_in_dim(array, start, width, axis=1)

    total = None
    for k in range(1, devices + 1):
        here = columns(own, k).astype(F32) + swapped(columns(other, k).astype(BF16)).astype(F32)
        if total is not None:
            here = here + lax.ppermute(total, "head", around).astype(F32)
        total = here.astype(BF16)
    return total


def picks(groups, rows_each):
    devices, mine, core = lax.axis_size("ctx"), lax.axis_index("ctx"), lax.axis_index("dp")
    width = devices * rows_each * groups
    feature = lax.broadcasted_iota(jnp.int32, (groups * DH, width), 0)
    place = lax.broadcasted_iota(jnp.int32, (groups * DH, width), 1)
    block = place // (rows_each * groups)
    if devices == 4:
        block = block ^ mine
    row = (place // groups) % rows_each
    group = place % groups

    def pick(p):
        return (feature == group * DH + (block * 2 + p) * rows_each + row).astype(BF16)

    return pick(core), pick(1 - core)


def shards(queries, keys, values, log_decay, w_out, grad_out):
    groups = log_decay.shape[1]
    size = queries.shape[1]
    devices = lax.axis_size("ctx")
    q, k, v, ld, g = queries[0], keys[0], values[0], log_decay[0], grad_out[0]
    rows_each, _, width = w_out.shape
    w = w_out.reshape(rows_each * groups, width)
    features = groups * DH
    state_shape = struct((features + EXTRA, DH), BF16)
    flat = lambda dtype: struct((size, features), dtype)
    half = struct((size, features // 2), BF16)

    w_all = gather_rows(w)
    g_all = jnp.concatenate([g, swapped(g)], axis=0)

    state, row, col = call(
        functools.partial(contrib_kernel, groups),
        (state_shape, struct((groups, size), F32), struct((size, groups), F32)),
    )(k, v, ld)
    before = neighbours(state, devices, True)
    pick_own, pick_other = picks(groups, rows_each)
    probs, intra = call(
        functools.partial(intra_kernel, groups), (struct((groups, size, size), BF16), flat(F32))
    )(q, k, v, row, col)
    a_own, a_other, low = call(
        functools.partial(attended_kernel, groups, len(before)),
        (half, half, struct((groups, DH, DH), BF16)),
        [pltpu.VMEM((size, features), BF16)],
    )(*before, q, intra, col, pick_own, pick_other)
    a_all = jnp.concatenate([a_own, swapped(a_other)], axis=0)

    w_grad = scatter_rows(a_all, g_all)
    grad_heads = contract(g_all, w_all, 1, 1).astype(BF16)
    grad_other = swapped(grad_heads[size:])
    grad, back = call(
        functools.partial(back_contrib_kernel, groups), (flat(BF16), state_shape)
    )(grad_heads[:size], grad_other, pick_own, pick_other, q, row, col)
    after = neighbours(back, devices, False)

    partial_out = contract(a_all, w_all, 1, 0)
    mixed = ring_scatter(partial_out[:size], partial_out[size:])

    query_grad, key_part, value_part = call(
        functools.partial(back_intra_kernel, groups), (flat(BF16), flat(F32), flat(F32))
    )(grad, q, k, v, row, col, probs, low)
    key_grad, value_grad = call(
        functools.partial(back_inter_kernel, groups, len(after)), (flat(BF16), flat(BF16))
    )(*after, k, v, col, key_part, value_part)
    return (
        mixed[None],
        query_grad[None],
        key_grad[None],
        value_grad[None],
        w_grad.reshape(rows_each, groups, width),
    )


def solution(mesh):
    return jax.shard_map(
        shards,
        mesh=mesh,
        in_specs=(
            P("dp", "ctx", "head"),
            P("dp", "ctx", "head"),
            P("dp", "ctx", "head"),
            P("dp", "head", "ctx"),
            P(("ctx", "dp"), "head", None),
            P("dp", "ctx", None),
        ),
        out_specs=(
            P("dp", "ctx", "head"),
            P("dp", "ctx", "head"),
            P("dp", "ctx", "head"),
            P("dp", "ctx", "head"),
            P(("ctx", "dp"), "head", None),
        ),
        check_vma=False,
    )
```

time: 275 us -> 113 us (0.41)
  waiting for transfers between devices: 183 us -> 38.8 us
  starting transfers between devices: 0.39 us -> 25 us
  matrix products: 36 us -> 14.9 us
  between operations: 14.7 us -> 0.96 us
  Pallas kernels: 0 us -> 11.8 us
  local copies, waits for them, and re-layouts: 20.9 us -> 11 us
  blocking collectives: 9.11 us -> 0 us
    reduce_scatter x2 -> x0, waiting for transfers between devices: 118 us -> none  [the longest x1 83.8 us: shards(): lax.psum_scatter(jnp.einsum('thd,to->dho', attended_row_list, cotangent,...]
    all_gather x3 -> x0, waiting for transfers between devices: 64.6 us -> none  [the longest x1 44.1 us: shards(): panel = lax.all_gather(w_out, ('ctx', 'dp'), axis=0, tiled=True)]
    ppermute x0 -> x26, waiting for transfers between devices: none -> 38.8 us  [the longest x10 19.9 us: flipped(): return lax.ppermute(array, 'ctx', [(i, i ^ bit) for i in range(4)])]
    ppermute x0 -> x26, starting transfers between devices: none -> 25 us  [the longest x6 11.1 us: neighbours(): out.append(lax.ppermute(state, 'ctx', pairs))]
    dot_general x16 -> x10, matrix products: 36 us -> 14.9 us  [contract(): lax.dot_general(a, b, (((dim_a,), (dim_b,)), ((), ())), preferred_element...]
    pallas_call x0 -> x6, Pallas kernels: none -> 11.8 us  [the longest x1 3.48 us: shards(): call(functools.partial(back_intra_kernel, groups), (flat(BF16), flat(F32)...]
    select_n x8 -> x0, other arithmetic: 9.45 us -> none  [lap(): return jax.tree.map(lambda a, b: jnp.where(reached, a, b), new, before)]
    unnamed x44 -> x41, local copies, waits for them, and re-layouts: 17.1 us -> 7.93 us
  transfers between devices with their start and end apart: 5 -> 26, of which waited for: 5 -> 12; matrix products, arithmetic and copies ran while one was open for 22% -> 25% of each run, Pallas kernels for 0% -> 10%
where the time goes in v1:
time: 113 us
  waiting for transfers between devices  38.8 us (34%)
  starting transfers between devices  25 us (22%)
  matrix products  14.9 us (13%)
  Pallas kernels  11.8 us (10%)
  local copies, waits for them, and re-layouts  11 us (10%)
  other arithmetic  10.1 us (9%)
    ppermute x10, waiting for transfers between devices, flipped(): return lax.ppermute(array, 'ctx', [(i, i ^ bit) for i in range(4)])  19.9 us
    ppermute x6, waiting for transfers between devices, neighbours(): out.append(lax.ppermute(state, 'ctx', pairs))  15 us
    dot_general x10, matrix products, contract(): lax.dot_general(a, b, (((dim_a,), (dim_b,)), ((), ())), preferred_element...  14.9 us
    ppermute x6, starting transfers between devices, neighbours(): out.append(lax.ppermute(state, 'ctx', pairs))  11.1 us
    ppermute x10, starting transfers between devices, flipped(): return lax.ppermute(array, 'ctx', [(i, i ^ bit) for i in range(4)])  10.1 us
    unnamed x41, local copies, waits for them, and re-layouts  7.93 us
    pallas_call x1, Pallas kernels, shards(): call(functools.partial(back_intra_kernel, groups), (flat(BF16), flat(F32)...  3.48 us
    convert_element_type x3, other arithmetic, ring_scatter(): total = here.astype(BF16)  3.26 us
  transfers between devices with their start and end apart: 26, of which 12 were waited for; matrix products, arithmetic and copies ran while one was open for 25% of the time, Pallas kernels for 10%

profile of v1, /device:TPU:0, one launch (start us, length us, event | category | flops | bytes accessed | tf_op | source)
XLA Modules:
  0.0 112.7 jit_solution(4817918420390407317)
XLA Ops:
  0.6 3.0 %collective-permute-start.5 = (bf16[128,3072]{1,0:T(8,128)(2,1)}, bf16[128,3072]{1,0:T(8,128)(2,1)S(1)}, u32[]{:S(2)}, u32[]{:S(2)}) collective-permute-start(bf16[128,3072]{1,0:T(8,128)(2,1)} %bitcast.38), channel_id=1, source_target_pairs={{0,16},{8,24},{16,0},{24,8},{1,17},{9,25},{17,1},{25,9},{2,18},{10... | collective-permute-start | bytes 2359304 | tf_op jit(solution)/shard_map/ppermute | solution.py:176
  3.7 1.5 %collective-permute-start.4 = (bf16[128,3072]{1,0:T(8,128)(2,1)}, bf16[128,3072]{1,0:T(8,128)(2,1)S(1)}, u32[]{:S(2)}, u32[]{:S(2)}) collective-permute-start(bf16[128,3072]{1,0:T(8,128)(2,1)} %bitcast.39), channel_id=1, source_target_pairs={{0,8},{8,0},{16,24},{24,16},{1,9},{9,1},{17,25},{25,17},{2,10},{10... | collective-permute-start | bytes 2359304 | tf_op jit(solution)/shard_map/ppermute | solution.py:176
  5.2 1.0 copy-done
  6.2 1.0 copy-done.2
  7.2 0.7 copy-done.12
  7.9 1.9 %shard_map.101 = (bf16[1040,128]{1,0:T(8,128)(2,1)}, f32[8,256]{1,0:T(8,128)S(1)}, f32[256,8]{1,0:T(8,128)S(1)}) custom-call(bf16[256,1024]{1,0:T(8,128)(2,1)S(1)} %bitcast.22, bf16[256,1024]{1,0:T(8,128)(2,1)S(1)} %bitcast.26, f32[8,256]{1,0:T(8,128)S(1)} %bitcast.34), custom_call_target="tpu_custom_call" | custom-call | tf_op jit(solution)/shard_map/pallas_call | solution.py:265
  9.9 2.1 %collective-permute-start.2 = (bf16[1040,128]{1,0:T(8,128)(2,1)}, bf16[1040,128]{1,0:T(8,128)(2,1)S(1)}, u32[]{:S(2)}, u32[]{:S(2)}) collective-permute-start(bf16[1040,128]{1,0:T(8,128)(2,1)} %get-tuple-element.20), channel_id=1, source_target_pairs={{0,24},{1,25},{2,26},{3,27},{4,28},{5,29},{6,30},{7,31}} | collective-permute-start | bytes 798728 | tf_op jit(solution)/shard_map/ppermute | solution.py:167
  12.0 2.0 %collective-permute-start.1 = (bf16[1040,128]{1,0:T(8,128)(2,1)}, bf16[1040,128]{1,0:T(8,128)(2,1)}, u32[]{:S(2)}, u32[]{:S(2)}) collective-permute-start(bf16[1040,128]{1,0:T(8,128)(2,1)} %get-tuple-element.20), channel_id=1, source_target_pairs={{0,16},{8,24},{1,17},{9,25},{2,18},{10,26},{3,19},{11,27},{4,20},{... | collective-permute-start | bytes 798728 | tf_op jit(solution)/shard_map/ppermute | solution.py:167
  14.0 3.1 %collective-permute-start = (bf16[1040,128]{1,0:T(8,128)(2,1)}, bf16[1040,128]{1,0:T(8,128)(2,1)}, u32[]{:S(2)}, u32[]{:S(2)}) collective-permute-start(bf16[1040,128]{1,0:T(8,128)(2,1)} %get-tuple-element.20), channel_id=1, source_target_pairs={{0,8},{8,16},{16,24},{1,9},{9,17},{17,25},{2,10},{10,18},{18,26},{... | collective-permute-start | bytes 798728 | tf_op jit(solution)/shard_map/ppermute | solution.py:167
  17.1 0.6 fusion.25
  17.7 0.6 broadcast_add_fusion
  18.3 0.5 fusion.27
  18.8 4.1 %collective-permute-done.5 = bf16[128,3072]{1,0:T(8,128)(2,1)S(1)} collective-permute-done((bf16[128,3072]{1,0:T(8,128)(2,1)}, bf16[128,3072]{1,0:T(8,128)(2,1)S(1)}, u32[]{:S(2)}, u32[]{:S(2)}) %collective-permute-start.5) | collective-permute-done | bytes 786464 | tf_op jit(solution)/shard_map/ppermute | solution.py:176
  22.9 0.8 slice.53
  23.7 0.7 collective-permute-done.4
  24.3 1.5 %collective-permute-start.7 = (bf16[128,1536]{1,0:T(8,128)(2,1)}, bf16[128,1536]{1,0:T(8,128)(2,1)}, u32[]{:S(2)}, u32[]{:S(2)}) collective-permute-start(bf16[128,1536]{1,0:T(8,128)(2,1)} %slice.53), channel_id=1, source_target_pairs={{0,8},{8,0},{16,24},{24,16},{1,9},{9,1},{17,25},{25,17},{2,10},{10... | collective-permute-start | bytes 1179656 | tf_op jit(solution)/shard_map/ppermute | solution.py:176
  25.8 0.8 slice.52
  26.6 2.6 %collective-permute-done.2.refs_2_ = bf16[1040,128]{1,0:T(8,128)(2,1)S(1)} collective-permute-done((bf16[1040,128]{1,0:T(8,128)(2,1)}, bf16[1040,128]{1,0:T(8,128)(2,1)S(1)}, u32[]{:S(2)}, u32[]{:S(2)}) %collective-permute-start.2) | collective-permute-done | bytes 266272 | tf_op jit(solution)/shard_map/ppermute | solution.py:167
  29.2 1.5 %fusion.7 = (bf16[1024,512]{1,0:T(8,128)(2,1)S(1)}, bf16[1024,512]{1,0:T(8,128)(2,1)S(1)}) fusion(s32[]{:T(128)S(6)} %sub.27, s32[512]{0:T(512)S(1)} %get-tuple-element.48, s32[512]{0:T(512)S(1)} %get-tuple-element.51, s32[]{:T(128)S(6)} %axis_index.33, s32[512]{0:T(512)S(1)} %get-tuple-element.47, s32[512]{0:T(512)} %get-tuple-element.52, ...), kind=kLoop, calls=%fused_computation.30 | loop fusion | flops 15204352 | bytes 2110988 | tf_op jit(solution)/shard_map/convert_element_type | solution.py:245
  30.8 1.0 copy-done.4
  31.8 0.9 shard_map.102
  32.7 1.0 copy-done.7
  33.7 1.2 %collective-permute-done.refs_0_ = bf16[1040,128]{1,0:T(8,128)(2,1)} collective-permute-done((bf16[1040,128]{1,0:T(8,128)(2,1)}, bf16[1040,128]{1,0:T(8,128)(2,1)}, u32[]{:S(2)}, u32[]{:S(2)}) %collective-permute-start) | collective-permute-done | bytes 266272 | tf_op jit(solution)/shard_map/ppermute | solution.py:167
  34.9 2.8 %shard_map.103 = (bf16[256,512]{1,0:T(8,128)(2,1)S(1)}, bf16[256,512]{1,0:T(8,128)(2,1)}, bf16[8,128,128]{2,1,0:T(8,128)(2,1)S(1)}) custom-call(bf16[1040,128]{1,0:T(8,128)(2,1)} %collective-permute-done.refs_0_, bf16[1040,128]{1,0:T(8,128)(2,1)} %collective-permute-done.1.refs_1_, bf16[1040,128]{1,0:T(8,128)(2,1)S(1)} %collective-permute-done.2.refs_2_, ...), custom_call_target="tpu_custom_call" | custom-call | tf_op jit(solution)/shard_map/pallas_call | solution.py:274
  37.7 0.7 copy-done.9
  38.4 0.7 copy-done.11
  39.1 1.0 constant_dynamic-update-slice_fusion.1
  40.1 0.8 collective-permute-done.3
  40.9 1.0 collective-permute-done.7
  41.9 4.1 %fusion.29 = f32[512,3072]{1,0:T(8,128)S(1)} fusion(bf16[512,512]{1,0:T(8,128)(2,1)S(1)} %constant_dynamic-update-slice_fusion, bf16[128,1536]{1,0:T(8,128)(2,1)} %collective-permute-done.7, bf16[128,1536]{1,0:T(8,128)(2,1)} %collective-permute-done.6, bf16[128,3072]{1,0:T(8,128)(2,1)} %copy-done.15, bf16[128,3072]{1,0:T(8,128)(2,1)} %copy-done.17, ...), kind=kOutput, calls=%fused_computation.70 | convolution fusion | flops 1626341376 | bytes 9961472 | tf_op jit(solution)/shard_map/dot_general | solution.py:18
  46.4 1.1 dynamic-slice_convert_fusion.3
  47.5 0.5 collective-permute-start.10
  48.7 3.4 %fusion.10 = bf16[512,512]{1,0:T(8,128)(2,1)S(1)} fusion(bf16[256,3072]{1,0:T(8,128)(2,1)} %collective-permute-done.15, bf16[256,3072]{1,0:T(8,128)(2,1)S(1)} %bitcast.36, bf16[128,1536]{1,0:T(8,128)(2,1)} %collective-permute-done.7, bf16[128,1536]{1,0:T(8,128)(2,1)} %collective-permute-done.6, bf16[128,3072]{1,0:T(8,128)(2,1)S(1)} %copy-done.16, ...), kind=kOutput, calls=%fused_computation.34 | convolution fusion | flops 1632894976 | bytes 6815744 | tf_op jit(solution)/shard_map/dot_general | solution.py:18
  52.3 1.5 %fusion.8 = (bf16[512,1536]{1,0:T(8,128)(2,1)S(1)}, bf16[512,1536]{1,0:T(8,128)(2,1)S(1)}) fusion(bf16[256,3072]{1,0:T(8,128)(2,1)S(1)} %bitcast.37, bf16[256,3072]{1,0:T(8,128)(2,1)} %collective-permute-done.15), kind=kLoop, calls=%fused_computation.31 | loop fusion | flops 6291456 | bytes 6291456 | tf_op jit(solution)/shard_map/concatenate | solution.py:263
  53.9 1.2 %convolution_convert_fusion.1 = bf16[128,1536]{1,0:T(8,128)(2,1)} fusion(bf16[512,1536]{1,0:T(8,128)(2,1)S(1)} %get-tuple-element.36, bf16[512,512]{1,0:T(8,128)(2,1)S(1)} %constant_dynamic-update-slice_fusion), kind=kOutput, calls=%fused_computation.21 | convolution fusion | flops 201523200 | bytes 2097152 | tf_op jit(solution)/shard_map/dot_general | solution.py:18
  55.0 1.2 %convolution_convert_fusion = bf16[128,1536]{1,0:T(8,128)(2,1)} fusion(bf16[512,1536]{1,0:T(8,128)(2,1)S(1)} %get-tuple-element.36, bf16[512,512]{1,0:T(8,128)(2,1)S(1)} %constant_dynamic-update-slice_fusion), kind=kOutput, calls=%fused_computation.20 | convolution fusion | flops 201523200 | bytes 2097152 | tf_op jit(solution)/shard_map/dot_general | solution.py:18
  56.2 0.8 add_convert_fusion.3
  57.0 1.6 %collective-permute-start.12 = (bf16[256,768]{1,0:T(8,128)(2,1)}, bf16[256,768]{1,0:T(8,128)(2,1)}, u32[]{:S(2)}, u32[]{:S(2)}) collective-permute-start(bf16[256,768]{1,0:T(8,128)(2,1)} %add_convert_fusion.3), channel_id=1, source_target_pairs={{0,2},{2,4},{4,6},{6,0},{1,3},{3,5},{5,7},{7,1},{8,10},{10,12},{12... | collective-permute-start | bytes 1179656 | tf_op jit(solution)/shard_map/ppermute | solution.py:228
  58.6 1.1 %convolution_convert_fusion.2 = bf16[128,1536]{1,0:T(8,128)(2,1)} fusion(bf16[512,1536]{1,0:T(8,128)(2,1)S(1)} %get-tuple-element.35, bf16[512,512]{1,0:T(8,128)(2,1)S(1)} %constant_dynamic-update-slice_fusion), kind=kOutput, calls=%fused_computation.22 | convolution fusion | flops 201523200 | bytes 2097152 | tf_op jit(solution)/shard_map/dot_general | solution.py:18
  59.8 2.5 %collective-permute-start.21 = (bf16[128,1536]{1,0:T(8,128)(2,1)}, bf16[128,1536]{1,0:T(8,128)(2,1)}, u32[]{:S(2)}, u32[]{:S(2)}) collective-permute-start(bf16[128,1536]{1,0:T(8,128)(2,1)} %convolution_convert_fusion.2), channel_id=1, source_target_pairs={{0,8},{8,0},{16,24},{24,16},{1,9},{9,1},{17,25},{25,17},{2,10},{10... | collective-permute-start | bytes 1179656 | tf_op jit(solution)/shard_map/ppermute | solution.py:176
  62.2 0.4 convolution_convert_fusion.3
  63.0 1.0 shard_map.104
  64.0 3.5 %shard_map.105 = (bf16[256,1024]{1,0:T(8,128)(2,1)}, f32[256,1024]{1,0:T(8,128)S(1)}, f32[256,1024]{1,0:T(8,128)S(1)}) custom-call(bf16[256,1024]{1,0:T(8,128)(2,1)S(1)} %get-tuple-element.26.grad_ref, bf16[256,1024]{1,0:T(8,128)(2,1)S(1)} %bitcast.33, bf16[256,1024]{1,0:T(8,128)(2,1)S(1)} %bitcast.24, bf16[256,1024]{1,0:T(8,128)(2,1)S(1)} %bitcast.28, ...), custom_call_target="tpu_custom_call" | custom-call | tf_op jit(solution)/shard_map/pallas_call | solution.py:292
  67.5 1.3 %collective-permute-start.19 = (bf16[1040,128]{1,0:T(8,128)(2,1)S(1)}, bf16[1040,128]{1,0:T(8,128)(2,1)S(1)}, u32[]{:S(2)}, u32[]{:S(2)}) collective-permute-start(bf16[1040,128]{1,0:T(8,128)(2,1)S(1)} %get-tuple-element.30), channel_id=1, source_target_pairs={{24,0},{25,1},{26,2},{27,3},{28,4},{29,5},{30,6},{31,7}} | collective-permute-start | bytes 798728 | tf_op jit(solution)/shard_map/ppermute | solution.py:167
  68.8 1.9 %collective-permute-done.12 = bf16[256,768]{1,0:T(8,128)(2,1)} collective-permute-done((bf16[256,768]{1,0:T(8,128)(2,1)}, bf16[256,768]{1,0:T(8,128)(2,1)}, u32[]{:S(2)}, u32[]{:S(2)}) %collective-permute-start.12) | collective-permute-done | bytes 393248 | tf_op jit(solution)/shard_map/ppermute | solution.py:228
  70.7 1.3 %collective-permute-start.18 = (bf16[1040,128]{1,0:T(8,128)(2,1)S(1)}, bf16[1040,128]{1,0:T(8,128)(2,1)S(1)}, u32[]{:S(2)}, u32[]{:S(2)}) collective-permute-start(bf16[1040,128]{1,0:T(8,128)(2,1)S(1)} %get-tuple-element.30), channel_id=1, source_target_pairs={{16,0},{24,8},{17,1},{25,9},{18,2},{26,10},{19,3},{27,11},{20,4},{... | collective-permute-start | bytes 798728 | tf_op jit(solution)/shard_map/ppermute | solution.py:167
  72.0 1.3 %add_convert_fusion.2 = bf16[256,768]{1,0:T(8,128)(2,1)S(1)} fusion(bf16[256,768]{1,0:T(8,128)(2,1)} %collective-permute-done.12, bf16[256,768]{1,0:T(8,128)(2,1)} %collective-permute-done.10, f32[256,3072]{1,0:T(8,128)S(1)} %slice.54, s32[]{:T(128)S(6)} %select_n.47), kind=kLoop, calls=%fused_computation.37 | loop fusion | flops 983040 | bytes 1966084 | tf_op jit(solution)/shard_map/convert_element_type | solution.py:229
  73.6 1.4 %fusion.3 = bf16[128,1536]{1,0:T(8,128)(2,1)S(1)} fusion(bf16[512,1536]{1,0:T(8,128)(2,1)S(1)} %get-tuple-element.35, bf16[128,1536]{1,0:T(8,128)(2,1)} %collective-permute-done.21, bf16[512,512]{1,0:T(8,128)(2,1)S(1)} %constant_dynamic-update-slice_fusion), kind=kOutput, calls=%fused_computation.18 | convolution fusion | flops 201916416 | bytes 2490368 | tf_op jit(solution)/shard_map/dot_general | solution.py:18
  75.0 5.8 %collective-permute-done.24 = bf16[128,1536]{1,0:T(8,128)(2,1)} collective-permute-done((bf16[128,1536]{1,0:T(8,128)(2,1)}, bf16[128,1536]{1,0:T(8,128)(2,1)}, u32[]{:S(2)}, u32[]{:S(2)}) %collective-permute-start.24) | collective-permute-done | bytes 393248 | tf_op jit(solution)/shard_map/ppermute | solution.py:176
  80.8 1.3 %collective-permute-start.17 = (bf16[1040,128]{1,0:T(8,128)(2,1)S(1)}, bf16[1040,128]{1,0:T(8,128)(2,1)S(1)}, u32[]{:S(2)}, u32[]{:S(2)}) collective-permute-start(bf16[1040,128]{1,0:T(8,128)(2,1)S(1)} %get-tuple-element.30), channel_id=1, source_target_pairs={{8,0},{16,8},{24,16},{9,1},{17,9},{25,17},{10,2},{18,10},{26,18},{... | collective-permute-start | bytes 798728 | tf_op jit(solution)/shard_map/ppermute | solution.py:167
  82.0 3.3 %collective-permute-done.18.refs_1_ = bf16[1040,128]{1,0:T(8,128)(2,1)S(1)} collective-permute-done((bf16[1040,128]{1,0:T(8,128)(2,1)S(1)}, bf16[1040,128]{1,0:T(8,128)(2,1)S(1)}, u32[]{:S(2)}, u32[]{:S(2)}) %collective-permute-start.18) | collective-permute-done | bytes 266272 | tf_op jit(solution)/shard_map/ppermute | solution.py:167
  85.3 0.9 collective-permute-start.22
  86.2 1.4 %fusion.4 = bf16[128,1536]{1,0:T(8,128)(2,1)S(1)} fusion(bf16[512,1536]{1,0:T(8,128)(2,1)S(1)} %get-tuple-element.36, bf16[128,1536]{1,0:T(8,128)(2,1)} %collective-permute-done.24, bf16[512,512]{1,0:T(8,128)(2,1)S(1)} %constant_dynamic-update-slice_fusion), kind=kOutput, calls=%fused_computation.19 | convolution fusion | flops 201916416 | bytes 2490368 | tf_op jit(solution)/shard_map/dot_general | solution.py:18
  87.6 7.9 %collective-permute-done.17.refs_0_ = bf16[1040,128]{1,0:T(8,128)(2,1)S(1)} collective-permute-done((bf16[1040,128]{1,0:T(8,128)(2,1)S(1)}, bf16[1040,128]{1,0:T(8,128)(2,1)S(1)}, u32[]{:S(2)}, u32[]{:S(2)}) %collective-permute-start.17) | collective-permute-done | bytes 266272 | tf_op jit(solution)/shard_map/ppermute | solution.py:167
  95.5 1.6 %shard_map.106 = (bf16[256,1024]{1,0:T(8,128)(2,1)}, bf16[256,1024]{1,0:T(8,128)(2,1)}) custom-call(bf16[1040,128]{1,0:T(8,128)(2,1)S(1)} %collective-permute-done.17.refs_0_, bf16[1040,128]{1,0:T(8,128)(2,1)S(1)} %collective-permute-done.18.refs_1_, bf16[1040,128]{1,0:T(8,128)(2,1)S(1)} %collective-permute-done.19.refs_2_, bf16[256,1024]{1,0:T(8,128)(2,1)S(1)} %bitcast.25, ...), custom_call_target="tpu_custom_call" | custom-call | tf_op jit(solution)/shard_map/pallas_call | solution.py:295
  97.1 0.4 collective-permute-start.25
  97.5 1.1 %add_convert_fusion.1 = bf16[256,768]{1,0:T(8,128)(2,1)S(1)} fusion(bf16[256,768]{1,0:T(8,128)(2,1)S(1)} %collective-permute-done.13, bf16[256,768]{1,0:T(8,128)(2,1)} %collective-permute-done.9, f32[256,3072]{1,0:T(8,128)S(1)} %slice.54, s32[]{:T(128)S(6)} %select_n.46), kind=kLoop, calls=%fused_computation.36 | loop fusion | flops 983040 | bytes 1966084 | tf_op jit(solution)/shard_map/convert_element_type | solution.py:229
  98.6 1.3 %collective-permute-start.14 = (bf16[256,768]{1,0:T(8,128)(2,1)S(1)}, bf16[256,768]{1,0:T(8,128)(2,1)S(1)}, u32[]{:S(2)}, u32[]{:S(2)}) collective-permute-start(bf16[256,768]{1,0:T(8,128)(2,1)S(1)} %add_convert_fusion.1), channel_id=1, source_target_pairs={{0,2},{2,4},{4,6},{6,0},{1,3},{3,5},{5,7},{7,1},{8,10},{10,12},{12... | collective-permute-start | bytes 1179656 | tf_op jit(solution)/shard_map/ppermute | solution.py:228
  100.0 0.4 fusion.1
  100.4 8.5 %collective-permute-done.23 = bf16[128,1536]{1,0:T(8,128)(2,1)S(1)} collective-permute-done((bf16[128,1536]{1,0:T(8,128)(2,1)}, bf16[128,1536]{1,0:T(8,128)(2,1)S(1)}, u32[]{:S(2)}, u32[]{:S(2)}) %collective-permute-start.23) | collective-permute-done | bytes 393248 | tf_op jit(solution)/shard_map/ppermute | solution.py:176
  108.8 0.4 fusion.2
  109.2 1.3 %maximum_bitcast_fusion = f32[16,8,3072]{2,1,0:T(8,128)} fusion(f32[128,1536]{1,0:T(8,128)S(1)} %fusion.2, f32[128,1536]{1,0:T(8,128)S(1)} %fusion.1), kind=kLoop, calls=%fused_computation.33 | loop fusion | flops 393216 | bytes 3145728 | tf_op jit(solution)/shard_map/reshape | solution.py:303
  110.5 1.3 %collective-permute-done.14 = bf16[256,768]{1,0:T(8,128)(2,1)S(1)} collective-permute-done((bf16[256,768]{1,0:T(8,128)(2,1)S(1)}, bf16[256,768]{1,0:T(8,128)(2,1)S(1)}, u32[]{:S(2)}, u32[]{:S(2)}) %collective-permute-start.14) | collective-permute-done | bytes 393248 | tf_op jit(solution)/shard_map/ppermute | solution.py:228
  111.7 0.9 fusion.11
  (64 shorter events, 2.0 us)
Async XLA Ops:
  0.6 22.2 %collective-permute-start.5 = (bf16[128,3072]{1,0:T(8,128)(2,1)}, bf16[128,3072]{1,0:T(8,128)(2,1)S(1)}, u32[]{:S(2)}, u32[]{:S(2)}) collective-permute-start(bf16[128,3072]{1,0:T(8,128)(2,1)} %bitcast.38), channel_id=1, source_target_pairs={{0,16},{8,24},{16,0},{24,8},{1,17},{9,25},{17,1},{25,9},{2,18},{10... | collective-permute-start | bytes 2359304 | tf_op jit(solution)/shard_map/ppermute | solution.py:176
  3.7 20.7 %collective-permute-start.4 = (bf16[128,3072]{1,0:T(8,128)(2,1)}, bf16[128,3072]{1,0:T(8,128)(2,1)S(1)}, u32[]{:S(2)}, u32[]{:S(2)}) collective-permute-start(bf16[128,3072]{1,0:T(8,128)(2,1)} %bitcast.39), channel_id=1, source_target_pairs={{0,8},{8,0},{16,24},{24,16},{1,9},{9,1},{17,25},{25,17},{2,10},{10... | collective-permute-start | bytes 2359304 | tf_op jit(solution)/shard_map/ppermute | solution.py:176
  5.2 1.0 copy-start
  6.2 1.0 copy-start.2
  7.2 0.7 copy-start.12
  9.8 20.9 %copy-start.1 = (bf16[1,256,1024]{2,1,0:T(8,128)(2,1)S(1)}, bf16[1,256,1024]{2,1,0:T(8,128)(2,1)}, u32[]{:S(2)}) copy-start(bf16[1,256,1024]{2,1,0:T(8,128)(2,1)} %param.7) | copy-start | bytes 1572868
  9.9 20.9 %copy-start.3 = (bf16[1,256,1024]{2,1,0:T(8,128)(2,1)S(1)}, bf16[1,256,1024]{2,1,0:T(8,128)(2,1)}, u32[]{:S(2)}) copy-start(bf16[1,256,1024]{2,1,0:T(8,128)(2,1)} %param.8) | copy-start | bytes 1572868
  9.9 19.4 %collective-permute-start.2 = (bf16[1040,128]{1,0:T(8,128)(2,1)}, bf16[1040,128]{1,0:T(8,128)(2,1)S(1)}, u32[]{:S(2)}, u32[]{:S(2)}) collective-permute-start(bf16[1040,128]{1,0:T(8,128)(2,1)} %get-tuple-element.20), channel_id=1, source_target_pairs={{0,24},{1,25},{2,26},{3,27},{4,28},{5,29},{6,30},{7,31}} | collective-permute-start | bytes 798728 | tf_op jit(solution)/shard_map/ppermute | solution.py:167
  12.0 21.8 %collective-permute-start.1 = (bf16[1040,128]{1,0:T(8,128)(2,1)}, bf16[1040,128]{1,0:T(8,128)(2,1)}, u32[]{:S(2)}, u32[]{:S(2)}) collective-permute-start(bf16[1040,128]{1,0:T(8,128)(2,1)} %get-tuple-element.20), channel_id=1, source_target_pairs={{0,16},{8,24},{1,17},{9,25},{2,18},{10,26},{3,19},{11,27},{4,20},{... | collective-permute-start | bytes 798728 | tf_op jit(solution)/shard_map/ppermute | solution.py:167
  14.0 21.0 %collective-permute-start = (bf16[1040,128]{1,0:T(8,128)(2,1)}, bf16[1040,128]{1,0:T(8,128)(2,1)}, u32[]{:S(2)}, u32[]{:S(2)}) collective-permute-start(bf16[1040,128]{1,0:T(8,128)(2,1)} %get-tuple-element.20), channel_id=1, source_target_pairs={{0,8},{8,16},{16,24},{1,9},{9,17},{17,25},{2,10},{10,18},{18,26},{... | collective-permute-start | bytes 798728 | tf_op jit(solution)/shard_map/ppermute | solution.py:167
  22.9 6.4 %copy-start.15 = (bf16[128,3072]{1,0:T(8,128)(2,1)}, bf16[128,3072]{1,0:T(8,128)(2,1)S(1)}, u32[]{:S(2)}) copy-start(bf16[128,3072]{1,0:T(8,128)(2,1)S(1)} %collective-permute-done.5) | copy-start | bytes 2359300
  22.9 25.2 %collective-permute-start.15 = (bf16[256,3072]{1,0:T(8,128)(2,1)}, bf16[256,3072]{1,0:T(8,128)(2,1)}, u32[]{:S(2)}, u32[]{:S(2)}) collective-permute-start(bf16[256,3072]{1,0:T(8,128)(2,1)} %bitcast.35), channel_id=1, source_target_pairs={{0,1},{1,0},{2,3},{3,2},{4,5},{5,4},{6,7},{7,6},{8,9},{9,8},{10,11... | collective-permute-start | bytes 4718600 | tf_op jit(solution)/shard_map/ppermute | solution.py:172
  24.3 4.9 %copy-start.17 = (bf16[128,3072]{1,0:T(8,128)(2,1)}, bf16[128,3072]{1,0:T(8,128)(2,1)S(1)}, u32[]{:S(2)}) copy-start(bf16[128,3072]{1,0:T(8,128)(2,1)S(1)} %collective-permute-done.4) | copy-start | bytes 2359300
  24.3 17.5 %collective-permute-start.7 = (bf16[128,1536]{1,0:T(8,128)(2,1)}, bf16[128,1536]{1,0:T(8,128)(2,1)}, u32[]{:S(2)}, u32[]{:S(2)}) collective-permute-start(bf16[128,1536]{1,0:T(8,128)(2,1)} %slice.53), channel_id=1, source_target_pairs={{0,8},{8,0},{16,24},{24,16},{1,9},{9,1},{17,25},{25,17},{2,10},{10... | collective-permute-start | bytes 1179656 | tf_op jit(solution)/shard_map/ppermute | solution.py:176
  26.6 8.3 %copy-start.5 = (bf16[1,256,1024]{2,1,0:T(8,128)(2,1)S(1)}, bf16[1,256,1024]{2,1,0:T(8,128)(2,1)}, u32[]{:S(2)}) copy-start(bf16[1,256,1024]{2,1,0:T(8,128)(2,1)} %param.6) | copy-start | bytes 1572868
  29.2 12.7 %collective-permute-start.6 = (bf16[128,1536]{1,0:T(8,128)(2,1)}, bf16[128,1536]{1,0:T(8,128)(2,1)}, u32[]{:S(2)}, u32[]{:S(2)}) collective-permute-start(bf16[128,1536]{1,0:T(8,128)(2,1)} %slice.52), channel_id=1, source_target_pairs={{0,16},{8,24},{16,0},{24,8},{1,17},{9,25},{17,1},{25,9},{2,18},{10... | collective-permute-start | bytes 1179656 | tf_op jit(solution)/shard_map/ppermute | solution.py:176
  30.7 1.0 copy-start.4
  32.7 1.0 copy-start.7
  37.7 0.7 copy-start.9
  38.4 0.7 copy-start.11
  39.1 1.7 %collective-permute-start.3 = (bf16[256,512]{1,0:T(8,128)(2,1)}, bf16[256,512]{1,0:T(8,128)(2,1)S(1)}, u32[]{:S(2)}, u32[]{:S(2)}) collective-permute-start(bf16[256,512]{1,0:T(8,128)(2,1)} %get-tuple-element.25), channel_id=1, source_target_pairs={{0,1},{1,0},{2,3},{3,2},{4,5},{5,4},{6,7},{7,6},{8,9},{9,8},{10,11... | collective-permute-start | bytes 786440 | tf_op jit(solution)/shard_map/ppermute | solution.py:172
  46.2 1.8 %copy-start.19 = (bf16[16,8,3072]{2,1,0:T(8,128)(2,1)S(1)}, bf16[16,8,3072]{2,1,0:T(8,128)(2,1)}, u32[]{:S(2)}) copy-start(bf16[16,8,3072]{2,1,0:T(8,128)(2,1)} %param.10) | copy-start | bytes 2359300
  46.4 1.9 %copy-start.13 = (bf16[1,256,3072]{2,1,0:T(8,128)(2,1)S(1)}, bf16[1,256,3072]{2,1,0:T(8,128)(2,1)}, u32[]{:S(2)}) copy-start(bf16[1,256,3072]{2,1,0:T(8,128)(2,1)} %param.11) | copy-start | bytes 4718596
  46.4 2.1 %copy-start.16 = (bf16[128,3072]{1,0:T(8,128)(2,1)S(1)}, bf16[128,3072]{1,0:T(8,128)(2,1)}, u32[]{:S(2)}) copy-start(bf16[128,3072]{1,0:T(8,128)(2,1)} %copy-done.15) | copy-start | bytes 2359300
  46.4 2.3 %copy-start.18 = (bf16[128,3072]{1,0:T(8,128)(2,1)S(1)}, bf16[128,3072]{1,0:T(8,128)(2,1)}, u32[]{:S(2)}) copy-start(bf16[128,3072]{1,0:T(8,128)(2,1)} %copy-done.17) | copy-start | bytes 2359300
  47.5 8.7 %collective-permute-start.11 = (bf16[256,768]{1,0:T(8,128)(2,1)S(1)}, bf16[256,768]{1,0:T(8,128)(2,1)S(1)}, u32[]{:S(2)}, u32[]{:S(2)}) collective-permute-start(bf16[256,768]{1,0:T(8,128)(2,1)S(1)} %get-tuple-element.38), channel_id=1, source_target_pairs={{0,1},{1,0},{2,3},{3,2},{4,5},{5,4},{6,7},{7,6},{8,9},{9,8},{10,11... | collective-permute-start | bytes 1179656 | tf_op jit(solution)/shard_map/ppermute | solution.py:172
  47.5 20.0 %collective-permute-start.10 = (bf16[256,768]{1,0:T(8,128)(2,1)}, bf16[256,768]{1,0:T(8,128)(2,1)}, u32[]{:S(2)}, u32[]{:S(2)}) collective-permute-start(bf16[256,768]{1,0:T(8,128)(2,1)} %get-tuple-element.39), channel_id=1, source_target_pairs={{0,1},{1,0},{2,3},{3,2},{4,5},{5,4},{6,7},{7,6},{8,9},{9,8},{10,11... | collective-permute-start | bytes 1179656 | tf_op jit(solution)/shard_map/ppermute | solution.py:172
  48.0 49.1 %collective-permute-start.9 = (bf16[256,768]{1,0:T(8,128)(2,1)}, bf16[256,768]{1,0:T(8,128)(2,1)}, u32[]{:S(2)}, u32[]{:S(2)}) collective-permute-start(bf16[256,768]{1,0:T(8,128)(2,1)} %get-tuple-element.40), channel_id=1, source_target_pairs={{0,1},{1,0},{2,3},{3,2},{4,5},{5,4},{6,7},{7,6},{8,9},{9,8},{10,11... | collective-permute-start | bytes 1179656 | tf_op jit(solution)/shard_map/ppermute | solution.py:172
  52.2 10.4 %collective-permute-start.16 = (bf16[256,512]{1,0:T(8,128)(2,1)S(1)}, bf16[256,512]{1,0:T(8,128)(2,1)S(1)}, u32[]{:S(2)}, u32[]{:S(2)}) collective-permute-start(bf16[256,512]{1,0:T(8,128)(2,1)S(1)} %get-tuple-element.41), channel_id=1, source_target_pairs={{0,1},{1,0},{2,3},{3,2},{4,5},{5,4},{6,7},{7,6},{8,9},{9,8},{10,11... | collective-permute-start | bytes 786440 | tf_op jit(solution)/shard_map/ppermute | solution.py:172
  57.0 13.7 %collective-permute-start.12 = (bf16[256,768]{1,0:T(8,128)(2,1)}, bf16[256,768]{1,0:T(8,128)(2,1)}, u32[]{:S(2)}, u32[]{:S(2)}) collective-permute-start(bf16[256,768]{1,0:T(8,128)(2,1)} %add_convert_fusion.3), channel_id=1, source_target_pairs={{0,2},{2,4},{4,6},{6,0},{1,3},{3,5},{5,7},{7,1},{8,10},{10,12},{12... | collective-permute-start | bytes 1179656 | tf_op jit(solution)/shard_map/ppermute | solution.py:228
  58.6 4.4 %copy-start.6 = (bf16[1,256,1024]{2,1,0:T(8,128)(2,1)S(1)}, bf16[1,256,1024]{2,1,0:T(8,128)(2,1)}, u32[]{:S(2)}) copy-start(bf16[1,256,1024]{2,1,0:T(8,128)(2,1)} %param.6) | copy-start | bytes 1572868
  59.8 13.6 %collective-permute-start.21 = (bf16[128,1536]{1,0:T(8,128)(2,1)}, bf16[128,1536]{1,0:T(8,128)(2,1)}, u32[]{:S(2)}, u32[]{:S(2)}) collective-permute-start(bf16[128,1536]{1,0:T(8,128)(2,1)} %convolution_convert_fusion.2), channel_id=1, source_target_pairs={{0,8},{8,0},{16,24},{24,16},{1,9},{9,1},{17,25},{25,17},{2,10},{10... | collective-permute-start | bytes 1179656 | tf_op jit(solution)/shard_map/ppermute | solution.py:176
  62.6 1.4 %copy-start.8 = (bf16[8,256,256]{2,1,0:T(8,128)(2,1)S(1)}, bf16[8,256,256]{2,1,0:T(8,128)(2,1)}, u32[]{:S(2)}) copy-start(bf16[8,256,256]{2,1,0:T(8,128)(2,1)} %copy-done.7) | copy-start | bytes 3145732
  62.7 1.4 %copy-start.10 = (bf16[8,128,128]{2,1,0:T(8,128)(2,1)S(1)}, bf16[8,128,128]{2,1,0:T(8,128)(2,1)}, u32[]{:S(2)}) copy-start(bf16[8,128,128]{2,1,0:T(8,128)(2,1)} %copy-done.9) | copy-start | bytes 786436
  62.7 18.1 %collective-permute-start.24 = (bf16[128,1536]{1,0:T(8,128)(2,1)}, bf16[128,1536]{1,0:T(8,128)(2,1)}, u32[]{:S(2)}, u32[]{:S(2)}) collective-permute-start(bf16[128,1536]{1,0:T(8,128)(2,1)} %convolution_convert_fusion), channel_id=1, source_target_pairs={{0,16},{8,24},{16,0},{24,8},{1,17},{9,25},{17,1},{25,9},{2,18},{10... | collective-permute-start | bytes 1179656 | tf_op jit(solution)/shard_map/ppermute | solution.py:176
  67.5 13.2 %collective-permute-start.19 = (bf16[1040,128]{1,0:T(8,128)(2,1)S(1)}, bf16[1040,128]{1,0:T(8,128)(2,1)S(1)}, u32[]{:S(2)}, u32[]{:S(2)}) collective-permute-start(bf16[1040,128]{1,0:T(8,128)(2,1)S(1)} %get-tuple-element.30), channel_id=1, source_target_pairs={{24,0},{25,1},{26,2},{27,3},{28,4},{29,5},{30,6},{31,7}} | collective-permute-start | bytes 798728 | tf_op jit(solution)/shard_map/ppermute | solution.py:167
  70.7 14.6 %collective-permute-start.18 = (bf16[1040,128]{1,0:T(8,128)(2,1)S(1)}, bf16[1040,128]{1,0:T(8,128)(2,1)S(1)}, u32[]{:S(2)}, u32[]{:S(2)}) collective-permute-start(bf16[1040,128]{1,0:T(8,128)(2,1)S(1)} %get-tuple-element.30), channel_id=1, source_target_pairs={{16,0},{24,8},{17,1},{25,9},{18,2},{26,10},{19,3},{27,11},{20,4},{... | collective-permute-start | bytes 798728 | tf_op jit(solution)/shard_map/ppermute | solution.py:167
  73.3 22.2 %copy-start.14 = (bf16[256,768]{1,0:T(8,128)(2,1)S(1)}, bf16[256,768]{1,0:T(8,128)(2,1)}, u32[]{:S(2)}) copy-start(bf16[256,768]{1,0:T(8,128)(2,1)} %get-tuple-element.37) | copy-start | bytes 1179652
  73.3 23.8 %collective-permute-start.13 = (bf16[256,768]{1,0:T(8,128)(2,1)S(1)}, bf16[256,768]{1,0:T(8,128)(2,1)S(1)}, u32[]{:S(2)}, u32[]{:S(2)}) collective-permute-start(bf16[256,768]{1,0:T(8,128)(2,1)S(1)} %add_convert_fusion.2), channel_id=1, source_target_pairs={{0,2},{2,4},{4,6},{6,0},{1,3},{3,5},{5,7},{7,1},{8,10},{10,12},{12... | collective-permute-start | bytes 1179656 | tf_op jit(solution)/shard_map/ppermute | solution.py:228
  80.7 17.9 %collective-permute-start.20 = (bf16[128,1536]{1,0:T(8,128)(2,1)S(1)}, bf16[128,1536]{1,0:T(8,128)(2,1)S(1)}, u32[]{:S(2)}, u32[]{:S(2)}) collective-permute-start(bf16[128,1536]{1,0:T(8,128)(2,1)S(1)} %convolution_convert_fusion.3), channel_id=1, source_target_pairs={{0,8},{8,0},{16,24},{24,16},{1,9},{9,1},{17,25},{25,17},{2,10},{10... | collective-permute-start | bytes 1179656 | tf_op jit(solution)/shard_map/ppermute | solution.py:176
  80.8 14.7 %collective-permute-start.17 = (bf16[1040,128]{1,0:T(8,128)(2,1)S(1)}, bf16[1040,128]{1,0:T(8,128)(2,1)S(1)}, u32[]{:S(2)}, u32[]{:S(2)}) collective-permute-start(bf16[1040,128]{1,0:T(8,128)(2,1)S(1)} %get-tuple-element.30), channel_id=1, source_target_pairs={{8,0},{16,8},{24,16},{9,1},{17,9},{25,17},{10,2},{18,10},{26,18},{... | collective-permute-start | bytes 798728 | tf_op jit(solution)/shard_map/ppermute | solution.py:167
  85.3 14.7 %collective-permute-start.22 = (bf16[128,1536]{1,0:T(8,128)(2,1)S(1)}, bf16[128,1536]{1,0:T(8,128)(2,1)S(1)}, u32[]{:S(2)}, u32[]{:S(2)}) collective-permute-start(bf16[128,1536]{1,0:T(8,128)(2,1)S(1)} %fusion.3), channel_id=1, source_target_pairs={{0,16},{8,24},{16,0},{24,8},{1,17},{9,25},{17,1},{25,9},{2,18},{10... | collective-permute-start | bytes 1179656 | tf_op jit(solution)/shard_map/ppermute | solution.py:176
  95.5 15.0 %collective-permute-start.8 = (bf16[256,768]{1,0:T(8,128)(2,1)S(1)}, bf16[256,768]{1,0:T(8,128)(2,1)S(1)}, u32[]{:S(2)}, u32[]{:S(2)}) collective-permute-start(bf16[256,768]{1,0:T(8,128)(2,1)S(1)} %copy-done.14), channel_id=1, source_target_pairs={{0,1},{1,0},{2,3},{3,2},{4,5},{5,4},{6,7},{7,6},{8,9},{9,8},{10,11... | collective-permute-start | bytes 1179656 | tf_op jit(solution)/shard_map/ppermute | solution.py:172
  97.1 11.7 %collective-permute-start.23 = (bf16[128,1536]{1,0:T(8,128)(2,1)}, bf16[128,1536]{1,0:T(8,128)(2,1)S(1)}, u32[]{:S(2)}, u32[]{:S(2)}) collective-permute-start(bf16[128,1536]{1,0:T(8,128)(2,1)} %convolution_convert_fusion.1), channel_id=1, source_target_pairs={{0,16},{8,24},{16,0},{24,8},{1,17},{9,25},{17,1},{25,9},{2,18},{10... | collective-permute-start | bytes 1179656 | tf_op jit(solution)/shard_map/ppermute | solution.py:176
  97.1 11.7 %collective-permute-start.25 = (bf16[128,1536]{1,0:T(8,128)(2,1)S(1)}, bf16[128,1536]{1,0:T(8,128)(2,1)S(1)}, u32[]{:S(2)}, u32[]{:S(2)}) collective-permute-start(bf16[128,1536]{1,0:T(8,128)(2,1)S(1)} %fusion.4), channel_id=1, source_target_pairs={{0,8},{8,0},{16,24},{24,16},{1,9},{9,1},{17,25},{25,17},{2,10},{10... | collective-permute-start | bytes 1179656 | tf_op jit(solution)/shard_map/ppermute | solution.py:176
  98.6 13.1 %collective-permute-start.14 = (bf16[256,768]{1,0:T(8,128)(2,1)S(1)}, bf16[256,768]{1,0:T(8,128)(2,1)S(1)}, u32[]{:S(2)}, u32[]{:S(2)}) collective-permute-start(bf16[256,768]{1,0:T(8,128)(2,1)S(1)} %add_convert_fusion.1), channel_id=1, source_target_pairs={{0,2},{2,4},{4,6},{6,0},{1,3},{3,5},{5,7},{7,1},{8,10},{10,12},{12... | collective-permute-start | bytes 1179656 | tf_op jit(solution)/shard_map/ppermute | solution.py:228

commit v2 on v1

--- a/solution.py
+++ b/solution.py
@@ -22,13 +22,36 @@
     return ref[:, h * DH : (h + 1) * DH]
 
 
-def call(kernel, out_shape, scratch=()):
+def call(kernel, out_shape, *args, staged=(), free_in=(), free_out=(), scratch=(), after=(), room=24):
+    n, waits, count = len(args), len(after), len(staged)
+
+    def body(*refs):
+        ins, rest = list(refs[:n]), refs[n + waits :]
+        rest, buffers, sem = rest[: len(rest) - count - 1], rest[len(rest) - count - 1 : -1], rest[-1]
+        copies = [pltpu.make_async_copy(ins[i], buffers[j], sem.at[j]) for j, i in enumerate(staged)]
+        for copy in copies:
+            copy.start()
+        for copy in copies:
+            copy.wait()
+        for j, i in enumerate(staged):
+            ins[i] = buffers[j]
+        kernel(*ins, *rest)
+
+    anywhere, local, far = (pl.BlockSpec(memory_space=m) for m in (pl.ANY, pltpu.VMEM, pltpu.HBM))
+    specs = [far if i in free_out else local for i in range(len(jax.tree.leaves(out_shape)))]
     return pl.pallas_call(
-        kernel,
+        body,
         out_shape=out_shape,
-        scratch_shapes=list(scratch),
-        compiler_params=pltpu.CompilerParams(vmem_limit_bytes=48 * 1024 * 1024),
-    )
+        in_specs=[far if i in staged or i in free_in else local for i in range(n)] + [anywhere] * waits,
+        out_specs=specs if isinstance(out_shape, (list, tuple)) else specs[0],
+        scratch_shapes=[
+            *scratch,
+            *[pltpu.VMEM(args[i].shape, args[i].dtype) for i in staged],
+            pltpu.SemaphoreType.DMA((max(count, 1),)),
+        ],
+        compiler_params=pltpu.CompilerParams(vmem_limit_bytes=room * 1024 * 1024),
+        cost_estimate=pl.CostEstimate(flops=0, bytes_accessed=0, transcendentals=0),
+    )(*args, *after)
 
 
 def struct(shape, dtype):
@@ -47,11 +70,44 @@
     return both[:groups] + both[groups:]
 
 
-def joined(refs, decays, h):
-    total = refs[-1][h * DH : (h + 1) * DH, :].astype(F32)
-    for ref, decay in zip(refs[-2::-1], decays[::-1]):
-        total = ref[h * DH : (h + 1) * DH, :].astype(F32) + decay[h : h + 1, :] * total
-    return total
+def entering(refs, groups, forward):
+    if lax.axis_size("ctx") == 4:
+        near, far = refs
+        bit = side(forward)
+        decay = load_decay(near, groups) * bit + (1.0 - bit)
+        return lambda h: rows_of(near, h) * bit + decay[h : h + 1, :] * rows_of(far, h)
+    decays = [load_decay(ref, groups) for ref in refs[:-1]]
+
+    def state(h):
+        total = rows_of(refs[-1], h)
+        for ref, decay in zip(refs[-2::-1], decays[::-1]):
+            total = rows_of(ref, h) + decay[h : h + 1, :] * total
+        return total
+
+    return state
+
+
+def rows_of(ref, h):
+    return ref[h * DH : (h + 1) * DH, :].astype(F32)
+
+
+def side(forward):
+    bit = lax.rem(lax.axis_index("ctx"), 2).astype(F32)
+    return bit if forward else 1.0 - bit
+
+
+def pair_kernel(groups, forward, own_ref, near_ref, *refs):
+    out_ref = refs[-1]
+    if len(refs) == 3:
+        refs[1][...] = refs[0][...]
+    bit = side(forward)
+    own_decay, near_decay = load_decay(own_ref, groups), load_decay(near_ref, groups)
+    for h in range(groups):
+        here = slice(h, h + 1)
+        own, near = rows_of(own_ref, h), rows_of(near_ref, h)
+        own_share = bit + (1.0 - bit) * near_decay[here]
+        near_share = bit * own_decay[here] + (1.0 - bit)
+        out_ref[h * DH : (h + 1) * DH, :] = (own_share * own + near_share * near).astype(BF16)
 
 
 def lower_mask(size):
@@ -60,7 +116,23 @@
     )
 
 
-def contrib_kernel(groups, k_ref, v_ref, ld_ref, state_ref, row_ref, col_ref):
+def ring_columns(w_ref, out_ref, hops, sem):
+    width = w_ref.shape[1] // lax.axis_size("head")
+    copies = []
+    for j in range(out_ref.shape[1] // width):
+        here = pl.ds(j * width, width)
+        copies.append(pltpu.make_async_copy(w_ref.at[:, columns_after(hops + j, width)], out_ref.at[:, here], sem.at[j]))
+        copies[-1].start()
+    return copies
+
+
+def first_columns_kernel(w_ref, out_ref, sem):
+    for copy in ring_columns(w_ref, out_ref, 1, sem):
+        copy.wait()
+
+
+def contrib_kernel(groups, hops, k_ref, v_ref, ld_ref, w_ref, state_ref, row_ref, col_ref, copy_ref, sem):
+    copies = ring_columns(w_ref, copy_ref, hops, sem)
     size = k_ref.shape[0]
     lower = lower_mask(size).astype(F32)
     ld = ld_ref[...]
@@ -77,6 +149,8 @@
         weighted = (head(k_ref, h).astype(F32) * tail[:, h : h + 1]).astype(BF16)
         state_ref[h * DH : (h + 1) * DH, :] = contract(weighted, head(v_ref, h), 0, 0).astype(BF16)
     store_decay(state_ref, row, groups)
+    for copy in copies:
+        copy.wait()
 
 
 def spread_weights(row_ref, col_ref, lower, h):
@@ -97,10 +171,10 @@
     states = refs[:count]
     q_ref, intra_ref, col_ref, pick_own_ref, pick_other_ref = refs[count : count + 5]
     own_ref, other_ref, low_ref, attended_ref = refs[count + 5 :]
-    decays = [load_decay(ref, groups) for ref in states[:-1]]
+    state = entering(states, groups, True)
     factor = jnp.exp(col_ref[...]) * SCALE
     for h in range(groups):
-        low = joined(states, decays, h).astype(BF16)
+        low = state(h).astype(BF16)
         low_ref[h] = low
         inter = contract(head(q_ref, h), low, 1, 0)
         attended_ref[:, h * DH : (h + 1) * DH] = (
@@ -143,12 +217,12 @@
 def back_inter_kernel(groups, count, *refs):
     states = refs[:count]
     k_ref, v_ref, col_ref, kpart_ref, vpart_ref, kgrad_ref, vgrad_ref = refs[count:]
-    decays = [load_decay(ref, groups) for ref in states[:-1]]
+    state = entering(states, groups, False)
     col = col_ref[...]
     tail = jnp.exp(col[col.shape[0] - 1 :, :] - col)
     for h in range(groups):
         here = slice(h * DH, (h + 1) * DH)
-        low = joined(states, decays, h).astype(BF16)
+        low = state(h).astype(BF16)
         kgrad_ref[:, here] = (
             head(kpart_ref, h) + tail[:, h : h + 1] * contract(head(v_ref, h), low, 1, 1)
         ).astype(BF16)
@@ -157,7 +231,8 @@
         ).astype(BF16)
 
 
-def neighbours(state, devices, forward):
+def hops_of(state, forward):
+    devices = lax.axis_size("ctx")
     out = []
     for hop in range(1, devices):
         if forward:
@@ -176,58 +251,83 @@
     return lax.ppermute(array, "ctx", [(i, i ^ bit) for i in range(4)])
 
 
-def gather_rows(w):
-    if lax.axis_size("ctx") != 4:
-        return lax.all_gather(w, "ctx", axis=0, tiled=True)
-    half = w.shape[1] // 2
-    one, two = flipped(w, 1), flipped(w, 2)
-    three = jnp.concatenate([flipped(one[:, :half], 2), flipped(two[:, half:], 1)], axis=1)
-    return jnp.concatenate([w, one, two, three], axis=0)
-
-
-def scatter_rows(attended, cotangent):
-    devices = lax.axis_size("ctx")
-    if devices != 4:
-        part = contract(attended, cotangent, 0, 0).astype(BF16)
-        return lax.psum_scatter(part, "ctx", scatter_dimension=0, tiled=True).astype(F32)
-    rows = attended.shape[1] // devices
-    half = cotangent.shape[1] // 2
-    left, right = cotangent[:, :half], cotangent[:, half:]
-
-    def part(k, columns):
-        return contract(attended[:, k * rows : (k + 1) * rows], columns, 0, 0)
-
-    far_left = flipped(part(3, left).astype(BF16), 1)
-    far_right = flipped(part(3, right).astype(BF16), 2)
-    near_left = flipped(part(1, left).astype(BF16), 1)
-    near_right = flipped(part(2, right).astype(BF16), 2)
-    on_left = flipped((part(2, left) + far_left.astype(F32)).astype(BF16), 2)
-    on_right = flipped((part(1, right) + far_right.astype(F32)).astype(BF16), 1)
-    return jnp.concatenate(
-        [
-            part(0, left) + near_left.astype(F32) + on_left.astype(F32),
-            part(0, right) + near_right.astype(F32) + on_right.astype(F32),
-        ],
-        axis=1,
-    )
-
-
-def ring_scatter(own, other):
-    devices, mine = lax.axis_size("head"), lax.axis_index("head")
-    width = own.shape[1] // devices
-    around = [(i, (i + 1) % devices) for i in range(devices)]
-
-    def columns(array, k):
-        start = lax.rem(mine - k + devices, devices) * width
-        return lax.dynamic_slice_in_dim(array, start, width, axis=1)
-
-    total = None
-    for k in range(1, devices + 1):
-        here = columns(own, k).astype(F32) + swapped(columns(other, k).astype(BF16)).astype(F32)
-        if total is not None:
-            here = here + lax.ppermute(total, "head", around).astype(F32)
-        total = here.astype(BF16)
-    return total
+def rows_kernel(count, *refs):
+    ins, outs = refs[: len(refs) // 2], refs[len(refs) // 2 :]
+    for i, (ref, out) in enumerate(zip(ins, outs)):
+        rows = out.shape[0]
+        out[...] = ref[:rows] if i < count else ref[rows:]
+
+
+def lay_out(pieces, out_ref, columns=slice(None)):
+    top = 0
+    for piece in pieces:
+        out_ref[top : top + piece.shape[0], :] = piece[:, columns]
+        top += piece.shape[0]
+
+
+def columns_after(hops, width):
+    devices = lax.axis_size("head")
+    return pl.ds(pl.multiple_of(lax.rem(lax.axis_index("head") + hops, devices) * width, width), width)
+
+
+def mix_kernel(count, place, a_own, a_other, *refs):
+    pieces, owns, other, w_ref = refs[:count], refs[count:-2], refs[-2], refs[-1]
+    width = w_ref.shape[1]
+    for j, own in enumerate(owns):
+        lay_out(pieces, w_ref, slice((place + j) * width, (place + j + 1) * width))
+        own[...] = contract(a_own[...], w_ref[...], 1, 0)
+        other[:, j * width : (j + 1) * width] = contract(a_other[...], w_ref[...], 1, 0).astype(BF16)
+
+
+def grad_kernel(count, g_own, g_other, *refs):
+    first, rest, (own, other, w_ref) = refs[:count], refs[count : 2 * count], refs[2 * count :]
+    heads = lax.axis_size("head")
+    left, width = first[0].shape[1], w_ref.shape[1] // heads
+    lay_out(first, w_ref.at[:, 0:left])
+    lay_out(rest, w_ref.at[:, left:])
+    for g_ref, out in ((g_own, own), (g_other, other)):
+        total = None
+        for j in range(heads):
+            term = contract(
+                g_ref[:, columns_after(1 + j, width)], w_ref[:, j * width : (j + 1) * width], 1, 1
+            )
+            total = term if total is None else total + term
+        out[...] = total.astype(BF16)
+
+
+def weight_kernel(blocks, a_own, a_other, g_own, g_other, *outs):
+    rows = a_own.shape[1] // 4
+    for (k, left, right), out in zip(blocks, outs):
+        here = slice(k * rows, (k + 1) * rows)
+        out[...] = (
+            contract(a_own[:, here], g_own[:, left:right], 0, 0)
+            + contract(a_other[:, here], g_other[:, left:right], 0, 0)
+        ).astype(out.dtype)
+
+
+def onward_kernel(mid_left, mid_right, far_left, far_right, left_ref, right_ref):
+    left_ref[...] = (mid_left[...] + far_left[...].astype(F32)).astype(BF16)
+    right_ref[...] = (mid_right[...] + far_right[...].astype(F32)).astype(BF16)
+
+
+def total_kernel(own_ref, left_ref, right_ref, out_ref):
+    half = own_ref.shape[1] // 2
+    left, right = slice(0, half), slice(half, 2 * half)
+    out_ref[:, left] = own_ref[:, left] + left_ref[...].astype(F32)
+    out_ref[:, right] = own_ref[:, right] + right_ref[...].astype(F32)
+
+
+def ring_kernel(j, own_ref, other_ref, *refs):
+    width = own_ref.shape[1]
+    total = own_ref[...] + other_ref[:, j * width : (j + 1) * width].astype(F32)
+    if len(refs) == 2:
+        total = total + refs[0][...].astype(F32)
+    refs[-1][...] = total.astype(BF16)
+
+
+def passed(array):
+    devices = lax.axis_size("head")
+    return lax.ppermute(array, "head", [(i, (i - 1) % devices) for i in range(devices)])
 
 
 def picks(groups, rows_each):
@@ -250,51 +350,207 @@
 def shards(queries, keys, values, log_decay, w_out, grad_out):
     groups = log_decay.shape[1]
     size = queries.shape[1]
-    devices = lax.axis_size("ctx")
+    devices, heads = lax.axis_size("ctx"), lax.axis_size("head")
+    four = devices == 4
     q, k, v, ld, g = queries[0], keys[0], values[0], log_decay[0], grad_out[0]
     rows_each, _, width = w_out.shape
-    w = w_out.reshape(rows_each * groups, width)
+    rows, part, middle = rows_each * groups, width // heads, width // 2
+    w = w_out.reshape(rows, width)
     features = groups * DH
     state_shape = struct((features + EXTRA, DH), BF16)
     flat = lambda dtype: struct((size, features), dtype)
     half = struct((size, features // 2), BF16)
-
-    w_all = gather_rows(w)
-    g_all = jnp.concatenate([g, swapped(g)], axis=0)
-
-    state, row, col = call(
-        functools.partial(contrib_kernel, groups),
-        (state_shape, struct((groups, size), F32), struct((size, groups), F32)),
-    )(k, v, ld)
-    before = neighbours(state, devices, True)
+    last = []
+
+    def step(kernel, out_shape, *args, after=(), **kwargs):
+        out = call(kernel, out_shape, *args, after=[*last, *after], **kwargs)
+        last[:] = [min(jax.tree.leaves(out), key=lambda x: x.size)]
+        return out
+
+    near_heads = heads // 2
+    w_first = step(
+        first_columns_kernel,
+        struct((rows, near_heads * part), BF16),
+        w,
+        free_in=(0,),
+        scratch=[pltpu.SemaphoreType.DMA((near_heads,))],
+        room=60,
+    )
+    if four:
+        first_two, first_one = flipped(w_first, 2), flipped(w_first, 1)
+    g_other = swapped(g)
+    rest_shape = struct((rows, width - near_heads * part), BF16)
+    state, row, col, w_rest = step(
+        functools.partial(contrib_kernel, groups, near_heads + 1),
+        (state_shape, struct((groups, size), F32), struct((size, groups), F32), rest_shape),
+        k,
+        v,
+        ld,
+        w,
+        staged=(0, 1, 2),
+        free_in=(3,),
+        scratch=[pltpu.SemaphoreType.DMA((heads - near_heads,))],
+        room=60,
+    )
+    if four:
+        near = flipped(state, 1)
+        rest_two = flipped(w_rest, 2)
+    else:
+        before = hops_of(state, True)
     pick_own, pick_other = picks(groups, rows_each)
-    probs, intra = call(
-        functools.partial(intra_kernel, groups), (struct((groups, size, size), BF16), flat(F32))
-    )(q, k, v, row, col)
-    a_own, a_other, low = call(
+    probs, intra = step(
+        functools.partial(intra_kernel, groups),
+        (struct((groups, size, size), BF16), flat(F32)),
+        q,
+        k,
+        v,
+        row,
+        col,
+        staged=(0, 1, 2),
+        after=[g_other],
+    )
+    if four:
+        lower = lambda array: struct((rows // 2, array.shape[1]), BF16)
+        on_one, on_two = step(
+            functools.partial(rows_kernel, 1), [lower(w_first)] * 2, first_one, first_two
+        )
+        first = [w_first, first_one, first_two, flipped(on_one, 2), flipped(on_two, 1)]
+        w_again, pair = step(
+            functools.partial(pair_kernel, groups, True), [rest_shape, struct((features, DH), BF16)], state, near, w_rest
+        )
+        before = [near, lax.ppermute(pair, "ctx", [(0, 2), (1, 3)])]
+        rest_one = flipped(w_again, 1)
+        (on_two,) = step(functools.partial(rows_kernel, 0), [lower(w_rest)], rest_two, after=first[3:])
+    else:
+        first = [lax.all_gather(w_first, "ctx", axis=0, tiled=True)]
+        rest = [lax.all_gather(w_rest, "ctx", axis=0, tiled=True)]
+    a_own, a_away, low = step(
         functools.partial(attended_kernel, groups, len(before)),
         (half, half, struct((groups, DH, DH), BF16)),
-        [pltpu.VMEM((size, features), BF16)],
-    )(*before, q, intra, col, pick_own, pick_other)
-    a_all = jnp.concatenate([a_own, swapped(a_other)], axis=0)
-
-    w_grad = scatter_rows(a_all, g_all)
-    grad_heads = contract(g_all, w_all, 1, 1).astype(BF16)
-    grad_other = swapped(grad_heads[size:])
-    grad, back = call(
-        functools.partial(back_contrib_kernel, groups), (flat(BF16), state_shape)
-    )(grad_heads[:size], grad_other, pick_own, pick_other, q, row, col)
-    after = neighbours(back, devices, False)
-
-    partial_out = contract(a_all, w_all, 1, 0)
-    mixed = ring_scatter(partial_out[:size], partial_out[size:])
-
-    query_grad, key_part, value_part = call(
-        functools.partial(back_intra_kernel, groups), (flat(BF16), flat(F32), flat(F32))
-    )(grad, q, k, v, row, col, probs, low)
-    key_grad, value_grad = call(
-        functools.partial(back_inter_kernel, groups, len(after)), (flat(BF16), flat(BF16))
-    )(*after, k, v, col, key_part, value_part)
+        *before,
+        q,
+        intra,
+        col,
+        pick_own,
+        pick_other,
+        staged=(len(before),),
+        scratch=[pltpu.VMEM((size, features), BF16)],
+    )
+    a_other = swapped(a_away)
+    if four:
+        (on_one,) = step(functools.partial(rows_kernel, 1), [lower(w_rest)], rest_one)
+        rest = [w_rest, rest_one, rest_two, flipped(on_one, 2), flipped(on_two, 1)]
+
+    held = pltpu.VMEM((features // 2, part), BF16)
+
+    def mix(pieces, place, count):
+        out = step(
+            functools.partial(mix_kernel, len(pieces), place),
+            [struct((size, part), F32)] * count + [struct((size, count * part), BF16)],
+            a_own,
+            a_other,
+            *pieces,
+            scratch=[held],
+        )
+        away = swapped(out[-1])
+        return [(own, away, j) for j, own in enumerate(out[:-1])]
+
+    def ring(terms, *arrived):
+        own, away, j = terms
+        return step(functools.partial(ring_kernel, j), struct((size, part), BF16), own, away, *arrived)
+
+    def weights(blocks, shapes):
+        return step(functools.partial(weight_kernel, blocks), shapes, a_own, a_other, g, g_other, staged=(2,))
+
+    def grad_of(some):
+        here = sum(piece.shape[0] for piece, _ in some)
+        return step(
+            functools.partial(grad_kernel, len(some)),
+            [struct((size, here), BF16)] * 2,
+            g,
+            g_other,
+            *[piece for piece, _ in some],
+            *[piece for _, piece in some],
+            staged=(0,),
+            scratch=[pltpu.VMEM((here, width), BF16)],
+        )
+
+    terms = mix(first, 0, near_heads)
+    if four:
+        small = lambda dtype: struct((rows, middle), dtype)
+        far = weights([(3, 0, middle), (3, middle, width)], [small(BF16)] * 2)
+        far_left, far_right = flipped(far[0], 1), flipped(far[1], 2)
+    arrived = passed(ring(terms[0]))
+    both = list(zip(first, rest))
+    if four:
+        near_grads = grad_of(both[:3])
+        parts = weights(
+            [(2, 0, middle), (1, middle, width), (1, 0, middle), (2, middle, width), (0, 0, width)],
+            [small(F32)] * 2 + [small(BF16)] * 2 + [struct((rows, width), F32)],
+        )
+        last_grads = grad_of(both[3:])
+        grad_own = jnp.concatenate([near_grads[0], last_grads[0]], axis=1)
+        grad_away = jnp.concatenate([near_grads[1], last_grads[1]], axis=1)
+    else:
+        grad_own, grad_away = grad_of(both)
+    grad_other = swapped(grad_away)
+    grad, back = step(
+        functools.partial(back_contrib_kernel, groups),
+        (flat(BF16), state_shape),
+        grad_own,
+        grad_other,
+        pick_own,
+        pick_other,
+        q,
+        row,
+        col,
+    )
+    if four:
+        near = flipped(back, 1)
+        to_left, to_right = step(onward_kernel, [small(BF16)] * 2, parts[0], parts[1], far_left, far_right)
+        on_left, on_right = flipped(to_left, 2), flipped(to_right, 1)
+    else:
+        after = hops_of(back, False)
+    for j in range(1, near_heads):
+        arrived = passed(ring(terms[j], arrived))
+    terms = mix(rest, 0, 1)
+    query_grad, key_part, value_part = step(
+        functools.partial(back_intra_kernel, groups),
+        (flat(BF16), flat(F32), flat(F32)),
+        grad,
+        q,
+        k,
+        v,
+        row,
+        col,
+        probs,
+        low,
+        staged=(1, 2, 3),
+    )
+    if four:
+        pair = step(functools.partial(pair_kernel, groups, False), struct((features, DH), BF16), back, near)
+        after = [near, lax.ppermute(pair, "ctx", [(2, 0), (3, 1)])]
+        w_sum = step(total_kernel, struct((rows, width), F32), parts[4], on_left, on_right)
+        near_left, near_right = flipped(parts[2], 1), flipped(parts[3], 2)
+    for j in range(1, heads - near_heads):
+        arrived = passed(ring(terms[0], arrived))
+        terms = mix(rest, j, 1)
+    key_grad, value_grad = step(
+        functools.partial(back_inter_kernel, groups, len(after)),
+        (flat(BF16), flat(BF16)),
+        *after,
+        k,
+        v,
+        col,
+        key_part,
+        value_part,
+    )
+    if four:
+        w_grad = step(total_kernel, struct((rows, width), F32), w_sum, near_left, near_right)
+    else:
+        w_grad = contract(a_own, g, 0, 0) + contract(a_other, g_other, 0, 0)
+        w_grad = lax.psum_scatter(w_grad.astype(BF16), "ctx", scatter_dimension=0, tiled=True).astype(F32)
+    mixed = ring(terms[0], arrived)
     return (
         mixed[None],
         query_grad[None],

time: 113 us -> 99.4 us (0.88)
  Pallas kernels: 11.8 us -> 29.6 us
  matrix products: 14.9 us -> 0 us
  waiting for transfers between devices: 38.8 us -> 27.2 us
  starting transfers between devices: 25 us -> 34.3 us
  other arithmetic: 10.1 us -> 1.4 us
  local copies, waits for them, and re-layouts: 11 us -> 5.12 us
    pallas_call x6 -> x26, Pallas kernels: 11.8 us -> 29.6 us  [call(): pl.pallas_call(body, out_shape=out_shape, in_specs=[far if i in staged or...]
    dot_general x10 -> x0, matrix products: 14.9 us -> none  [contract(): lax.dot_general(a, b, (((dim_a,), (dim_b,)), ((), ())), preferred_element...]
    ppermute x10 -> x16, starting transfers between devices: 10.1 us -> 22.2 us  [flipped(): return lax.ppermute(array, 'ctx', [(i, i ^ bit) for i in range(4)])]
    ppermute x10 -> x16, waiting for transfers between devices: 19.9 us -> 12.2 us  [flipped(): return lax.ppermute(array, 'ctx', [(i, i ^ bit) for i in range(4)])]
    ppermute x9 -> x5, waiting for transfers between devices: 18.1 us -> 13.5 us  [the longest x1 9.98 us: shards(): after = [near, lax.ppermute(pair, 'ctx', [(2, 0), (3, 1)])]]
    convert_element_type x3 -> x0, other arithmetic: 3.26 us -> none  [ring_scatter(): total = here.astype(BF16)]
    ppermute x9 -> x5, starting transfers between devices: 14.3 us -> 11.2 us  [the longest x3 7.96 us: passed(): lax.ppermute(array, 'head', [(i, (i - 1) % devices) for i in range(device...]
    unnamed x41 -> x30, local copies, waits for them, and re-layouts: 7.93 us -> 5.12 us
  transfers between devices with their start and end apart: 26 -> 27, of which waited for: 12 -> 8; matrix products, arithmetic and copies ran while one was open for 25% -> 1% of each run, Pallas kernels for 10% -> 27%
where the time goes in v2:
time: 99.4 us; the launch traced here: 98.9 us
  starting transfers between devices  34.3 us (35%)
  Pallas kernels  29.6 us (30%)
  waiting for transfers between devices  27.2 us (27%)
  local copies, waits for them, and re-layouts  5.12 us (5%)
  other arithmetic  1.4 us (1%)
  between operations  1.28 us (1%)
    pallas_call x26, Pallas kernels, call(): pl.pallas_call(body, out_shape=out_shape, in_specs=[far if i in staged or...  29.6 us
    ppermute x16, starting transfers between devices, flipped(): return lax.ppermute(array, 'ctx', [(i, i ^ bit) for i in range(4)])  22.2 us
    ppermute x16, waiting for transfers between devices, flipped(): return lax.ppermute(array, 'ctx', [(i, i ^ bit) for i in range(4)])  12.2 us
    ppermute x1, waiting for transfers between devices, shards(): after = [near, lax.ppermute(pair, 'ctx', [(2, 0), (3, 1)])]  9.98 us
    ppermute x3, starting transfers between devices, passed(): lax.ppermute(array, 'head', [(i, (i - 1) % devices) for i in range(device...  7.96 us
    unnamed x30, local copies, waits for them, and re-layouts  5.12 us
    ppermute x1, waiting for transfers between devices, shards(): before = [near, lax.ppermute(pair, 'ctx', [(0, 2), (1, 3)])]  3.52 us
  transfers between devices with their start and end apart: 27, of which 8 were waited for; matrix products, arithmetic and copies ran while one was open for 1% of the time, Pallas kernels for 27%

profile of v2, /device:TPU:0, one launch (start us, length us, event | category | flops | bytes accessed | tf_op | source)
XLA Modules:
  0.0 98.9 jit_solution(14542971340283088662)
XLA Ops:
  0.6 0.5 collective-permute-start.3
  1.2 1.9 %shard_map.101.refs_4_.refs_2_ = bf16[128,1536]{1,0:T(8,128)(2,1)} custom-call(bf16[128,3072]{1,0:T(8,128)(2,1)} %bitcast.31), custom_call_target="tpu_custom_call" | custom-call | tf_op jit(solution)/shard_map/pallas_call | solution.py:42
  3.1 2.6 %collective-permute-start.2 = (bf16[128,1536]{1,0:T(8,128)(2,1)}, bf16[128,1536]{1,0:T(8,128)(2,1)}, u32[]{:S(2)}, u32[]{:S(2)}) collective-permute-start(bf16[128,1536]{1,0:T(8,128)(2,1)} %shard_map.101.refs_4_.refs_2_), channel_id=1, source_target_pairs={{0,16},{8,24},{16,0},{24,8},{1,17},{9,25},{17,1},{25,9},{2,18},{10... | collective-permute-start | bytes 1179656 | tf_op jit(solution)/shard_map/ppermute | solution.py:251
  5.7 1.5 %collective-permute-start.1 = (bf16[128,1536]{1,0:T(8,128)(2,1)}, bf16[128,1536]{1,0:T(8,128)(2,1)}, u32[]{:S(2)}, u32[]{:S(2)}) collective-permute-start(bf16[128,1536]{1,0:T(8,128)(2,1)} %shard_map.101.refs_4_.refs_2_), channel_id=1, source_target_pairs={{0,8},{8,0},{16,24},{24,16},{1,9},{9,1},{17,25},{25,17},{2,10},{10... | collective-permute-start | bytes 1179656 | tf_op jit(solution)/shard_map/ppermute | solution.py:251
  7.2 3.3 %shard_map.102 = (bf16[1040,128]{1,0:T(8,128)(2,1)}, f32[8,256]{1,0:T(8,128)}, f32[256,8]{1,0:T(8,128)}, bf16[128,1536]{1,0:T(8,128)(2,1)}) custom-call(bf16[256,1024]{1,0:T(8,128)(2,1)} %bitcast.20, bf16[256,1024]{1,0:T(8,128)(2,1)} %bitcast.24, f32[8,256]{1,0:T(8,128)} %bitcast.34, bf16[128,3072]{1,0:T(8,128)(2,1)} %bitcast.32, ...), custom_call_target="tpu_custom_call" | custom-call | tf_op jit(solution)/shard_map/pallas_call | solution.py:42
  10.5 0.6 collective-permute-start
  11.1 0.1 collective-permute-start.5
  11.2 0.5 fusion.10
  11.8 0.9 copy-done.7
  12.7 0.7 copy-done.12
  13.4 1.1 %shard_map.103 = (bf16[8,256,256]{2,1,0:T(8,128)(2,1)S(1)}, f32[256,1024]{1,0:T(8,128)S(1)}) custom-call(bf16[256,1024]{1,0:T(8,128)(2,1)S(1)} %bitcast.16, bf16[256,1024]{1,0:T(8,128)(2,1)S(1)} %bitcast.21, bf16[256,1024]{1,0:T(8,128)(2,1)S(1)} %bitcast.25, f32[8,256]{1,0:T(8,128)S(1)} %copy-done.12, f32[256,8]{1,0:T(8,128)S(1)} %copy-done.7, ...), custom_call_target="tpu_custom_call" | custom-call | tf_op jit(solution)/shard_map/pallas_call | solution.py:42
  14.5 1.5 %collective-permute-done.2.refs_1_.refs_4_ = bf16[128,1536]{1,0:T(8,128)(2,1)} collective-permute-done((bf16[128,1536]{1,0:T(8,128)(2,1)}, bf16[128,1536]{1,0:T(8,128)(2,1)}, u32[]{:S(2)}, u32[]{:S(2)}) %collective-permute-start.2) | collective-permute-done | bytes 393248 | tf_op jit(solution)/shard_map/ppermute | solution.py:251
  16.0 2.0 %collective-permute-done.1.refs_0_.refs_3_ = bf16[128,1536]{1,0:T(8,128)(2,1)} collective-permute-done((bf16[128,1536]{1,0:T(8,128)(2,1)}, bf16[128,1536]{1,0:T(8,128)(2,1)}, u32[]{:S(2)}, u32[]{:S(2)}) %collective-permute-start.1) | collective-permute-done | bytes 393248 | tf_op jit(solution)/shard_map/ppermute | solution.py:251
  18.0 1.1 %shard_map.104 = (bf16[64,1536]{1,0:T(8,128)(2,1)S(1)}, bf16[64,1536]{1,0:T(8,128)(2,1)S(1)}) custom-call(bf16[128,1536]{1,0:T(8,128)(2,1)} %collective-permute-done.1.refs_0_.refs_3_, bf16[128,1536]{1,0:T(8,128)(2,1)} %collective-permute-done.2.refs_1_.refs_4_, f32[256,1024]{1,0:T(8,128)S(1)} %get-tuple-element.49.refs_2_.refs_3_), custom_call_target="tpu_custom_call" | custom-call | tf_op jit(solution)/shard_map/pallas_call | solution.py:42
  19.1 1.6 %collective-permute-start.7 = (bf16[64,1536]{1,0:T(8,128)(2,1)S(1)}, bf16[64,1536]{1,0:T(8,128)(2,1)S(1)}, u32[]{:S(2)}, u32[]{:S(2)}) collective-permute-start(bf16[64,1536]{1,0:T(8,128)(2,1)S(1)} %get-tuple-element.52), channel_id=1, source_target_pairs={{0,8},{8,0},{16,24},{24,16},{1,9},{9,1},{17,25},{25,17},{2,10},{10... | collective-permute-start | bytes 589832 | tf_op jit(solution)/shard_map/ppermute | solution.py:251
  20.7 0.5 collective-permute-start.6
  21.2 2.5 %collective-permute-done.refs_1_.refs_0_ = bf16[1040,128]{1,0:T(8,128)(2,1)} collective-permute-done((bf16[1040,128]{1,0:T(8,128)(2,1)}, bf16[1040,128]{1,0:T(8,128)(2,1)}, u32[]{:S(2)}, u32[]{:S(2)}) %collective-permute-start) | collective-permute-done | bytes 266272 | tf_op jit(solution)/shard_map/ppermute | solution.py:251
  23.7 1.1 %shard_map.105 = (bf16[128,1536]{1,0:T(8,128)(2,1)S(1)}, bf16[1024,128]{1,0:T(8,128)(2,1)S(1)}) custom-call(bf16[1040,128]{1,0:T(8,128)(2,1)S(1)} %copy-done.11, bf16[1040,128]{1,0:T(8,128)(2,1)} %collective-permute-done.refs_1_.refs_0_, bf16[128,1536]{1,0:T(8,128)(2,1)S(1)} %copy-done.4, bf16[64,1536]{1,0:T(8,128)(2,1)S(1)} %get-tuple-element.50.refs_3_), custom_call_target="tpu_custom_call" | custom-call | tf_op jit(solution)/shard_map/pallas_call | solution.py:42
  24.8 2.0 %collective-permute-start.4 = (bf16[1024,128]{1,0:T(8,128)(2,1)S(1)}, bf16[1024,128]{1,0:T(8,128)(2,1)S(1)}, u32[]{:S(2)}, u32[]{:S(2)}) collective-permute-start(bf16[1024,128]{1,0:T(8,128)(2,1)S(1)} %get-tuple-element.51.refs_1_), channel_id=1, source_target_pairs={{0,16},{8,24},{1,17},{9,25},{2,18},{10,26},{3,19},{11,27},{4,20},{... | collective-permute-start | bytes 786440 | tf_op jit(solution)/shard_map/ppermute | solution.py:421
  26.8 2.0 %collective-permute-start.9 = (bf16[128,1536]{1,0:T(8,128)(2,1)S(1)}, bf16[128,1536]{1,0:T(8,128)(2,1)S(1)}, u32[]{:S(2)}, u32[]{:S(2)}) collective-permute-start(bf16[128,1536]{1,0:T(8,128)(2,1)S(1)} %get-tuple-element.55), channel_id=1, source_target_pairs={{0,8},{8,0},{16,24},{24,16},{1,9},{9,1},{17,25},{25,17},{2,10},{10... | collective-permute-start | bytes 1179656 | tf_op jit(solution)/shard_map/ppermute | solution.py:251
  28.8 0.8 fusion.2
  29.6 3.5 %collective-permute-done.4.refs_1_ = bf16[1024,128]{1,0:T(8,128)(2,1)S(1)} collective-permute-done((bf16[1024,128]{1,0:T(8,128)(2,1)S(1)}, bf16[1024,128]{1,0:T(8,128)(2,1)S(1)}, u32[]{:S(2)}, u32[]{:S(2)}) %collective-permute-start.4) | collective-permute-done | bytes 262176 | tf_op jit(solution)/shard_map/ppermute | solution.py:421
  33.2 2.0 %shard_map.107 = (bf16[256,512]{1,0:T(8,128)(2,1)S(1)}, bf16[256,512]{1,0:T(8,128)(2,1)S(1)}, bf16[8,128,128]{2,1,0:T(8,128)(2,1)S(1)}) custom-call(bf16[1040,128]{1,0:T(8,128)(2,1)} %collective-permute-done.refs_1_.refs_0_, bf16[1024,128]{1,0:T(8,128)(2,1)S(1)} %collective-permute-done.4.refs_1_, bf16[256,1024]{1,0:T(8,128)(2,1)S(1)} %bitcast.17, ...), custom_call_target="tpu_custom_call" | custom-call | tf_op jit(solution)/shard_map/pallas_call | solution.py:42
  35.3 1.5 %collective-permute-done.9.refs_0_.refs_6_.refs_3_ = bf16[128,1536]{1,0:T(8,128)(2,1)S(1)} collective-permute-done((bf16[128,1536]{1,0:T(8,128)(2,1)S(1)}, bf16[128,1536]{1,0:T(8,128)(2,1)S(1)}, u32[]{:S(2)}, u32[]{:S(2)}) %collective-permute-start.9) | collective-permute-done | bytes 393248 | tf_op jit(solution)/shard_map/ppermute | solution.py:251
  36.8 2.2 %shard_map.109 = (f32[256,768]{1,0:T(8,128)S(1)}, f32[256,768]{1,0:T(8,128)S(1)}, bf16[256,1536]{1,0:T(8,128)(2,1)S(1)}) custom-call(bf16[256,512]{1,0:T(8,128)(2,1)S(1)} %get-tuple-element.53.refs_1_.refs_0_, bf16[256,512]{1,0:T(8,128)(2,1)S(1)} %collective-permute-done.8.refs_1_, bf16[128,1536]{1,0:T(8,128)(2,1)S(1)} %copy-done.6, ...), custom_call_target="tpu_custom_call" | custom-call | tf_op jit(solution)/shard_map/pallas_call | solution.py:42
  39.1 0.1 collective-permute-start.12
  39.1 1.6 %collective-permute-start.11 = (bf16[64,1536]{1,0:T(8,128)(2,1)S(1)}, bf16[64,1536]{1,0:T(8,128)(2,1)S(1)}, u32[]{:S(2)}, u32[]{:S(2)}) collective-permute-start(bf16[64,1536]{1,0:T(8,128)(2,1)S(1)} %shard_map.106.refs_7_), channel_id=1, source_target_pairs={{0,8},{8,0},{16,24},{24,16},{1,9},{9,1},{17,25},{25,17},{2,10},{10... | collective-permute-start | bytes 589832 | tf_op jit(solution)/shard_map/ppermute | solution.py:251
  40.7 2.4 %collective-permute-start.10 = (bf16[64,1536]{1,0:T(8,128)(2,1)S(1)}, bf16[64,1536]{1,0:T(8,128)(2,1)S(1)}, u32[]{:S(2)}, u32[]{:S(2)}) collective-permute-start(bf16[64,1536]{1,0:T(8,128)(2,1)S(1)} %shard_map.108.refs_7_), channel_id=1, source_target_pairs={{0,16},{8,24},{16,0},{24,8},{1,17},{9,25},{17,1},{25,9},{2,18},{10... | collective-permute-start | bytes 589832 | tf_op jit(solution)/shard_map/ppermute | solution.py:251
  43.1 0.7 shard_map.110
  44.0 0.6 collective-permute-start.14
  44.6 0.1 shard_map.111.refs_8_
  44.6 3.7 %collective-permute-start.13 = (bf16[256,768]{1,0:T(8,128)(2,1)S(1)}, bf16[256,768]{1,0:T(8,128)(2,1)S(1)}, u32[]{:S(2)}, u32[]{:S(2)}) collective-permute-start(bf16[256,768]{1,0:T(8,128)(2,1)S(1)} %shard_map.111.refs_8_), channel_id=1, source_target_pairs={{0,6},{2,0},{4,2},{6,4},{1,7},{3,1},{5,3},{7,5},{8,14},{10,8},{12,... | collective-permute-start | bytes 1179656 | tf_op jit(solution)/shard_map/ppermute | solution.py:330
  48.3 3.0 %shard_map.112 = (bf16[256,384]{1,0:T(8,128)(2,1)S(1)}, bf16[256,384]{1,0:T(8,128)(2,1)S(1)}) custom-call(bf16[256,3072]{1,0:T(8,128)(2,1)S(1)} %bitcast.13, bf16[256,3072]{1,0:T(8,128)(2,1)S(1)} %collective-permute-done.3.refs_6_.refs_3_.refs_1_, bf16[128,1536]{1,0:T(8,128)(2,1)S(1)} %copy-done.6, bf16[128,1536]{1,0:T(8,128)(2,1)} %collective-permute-done.1.refs_0_.refs_3_, ...), custom_call_target="tpu_custom_call" | custom-call | tf_op jit(solution)/shard_map/pallas_call | solution.py:42
  51.3 1.5 %shard_map.113 = (f32[128,1536]{1,0:T(8,128)S(1)}, f32[128,1536]{1,0:T(8,128)S(1)}, bf16[128,1536]{1,0:T(8,128)(2,1)S(1)}, bf16[128,1536]{1,0:T(8,128)(2,1)S(1)}, f32[128,3072]{1,0:T(8,128)S(1)}) custom-call(bf16[256,512]{1,0:T(8,128)(2,1)S(1)} %get-tuple-element.53.refs_1_.refs_0_, bf16[256,512]{1,0:T(8,128)(2,1)S(1)} %collective-permute-done.8.refs_1_, ...), custom_call_target="tpu_custom_call" | custom-call | tf_op jit(solution)/shard_map/pallas_call | solution.py:42
  52.9 1.1 %shard_map.114 = (bf16[256,128]{1,0:T(8,128)(2,1)S(1)}, bf16[256,128]{1,0:T(8,128)(2,1)S(1)}) custom-call(bf16[256,3072]{1,0:T(8,128)(2,1)S(1)} %bitcast.15, bf16[256,3072]{1,0:T(8,128)(2,1)S(1)} %collective-permute-done.3.refs_6_.refs_3_.refs_1_, bf16[64,1536]{1,0:T(8,128)(2,1)S(1)} %collective-permute-done.6.refs_2_.refs_5_, ...), custom_call_target="tpu_custom_call" | custom-call | tf_op jit(solution)/shard_map/pallas_call | solution.py:42
  54.0 0.1 collective-permute-start.16
  54.1 1.5 %collective-permute-done.16.refs_1_ = bf16[256,512]{1,0:T(8,128)(2,1)S(1)} collective-permute-done((bf16[256,512]{1,0:T(8,128)(2,1)S(1)}, bf16[256,512]{1,0:T(8,128)(2,1)S(1)}, u32[]{:S(2)}, u32[]{:S(2)}) %collective-permute-start.16) | collective-permute-done | bytes 262176 | tf_op jit(solution)/shard_map/ppermute | solution.py:247
  55.6 1.0 %shard_map.115 = (bf16[256,1024]{1,0:T(8,128)(2,1)S(1)}, bf16[1040,128]{1,0:T(8,128)(2,1)S(1)}) custom-call(bf16[256,512]{1,0:T(8,128)(2,1)S(1)} %pad_maximum_fusion.refs_0_, bf16[256,512]{1,0:T(8,128)(2,1)S(1)} %collective-permute-done.16.refs_1_, bf16[1024,512]{1,0:T(8,128)(2,1)S(1)} %get-tuple-element.86.refs_5_.refs_2_, ...), custom_call_target="tpu_custom_call" | custom-call | tf_op jit(solution)/shard_map/pallas_call | solution.py:42
  56.7 0.2 shard_map.116
  56.9 1.6 %collective-permute-start.20 = (bf16[128,1536]{1,0:T(8,128)(2,1)S(1)}, bf16[128,1536]{1,0:T(8,128)(2,1)S(1)}, u32[]{:S(2)}, u32[]{:S(2)}) collective-permute-start(bf16[128,1536]{1,0:T(8,128)(2,1)S(1)} %get-tuple-element.72), channel_id=1, source_target_pairs={{0,8},{8,0},{16,24},{24,16},{1,9},{9,1},{17,25},{25,17},{2,10},{10... | collective-permute-start | bytes 1179656 | tf_op jit(solution)/shard_map/ppermute | solution.py:251
  58.5 1.9 %collective-permute-start.19 = (bf16[128,1536]{1,0:T(8,128)(2,1)S(1)}, bf16[128,1536]{1,0:T(8,128)(2,1)S(1)}, u32[]{:S(2)}, u32[]{:S(2)}) collective-permute-start(bf16[128,1536]{1,0:T(8,128)(2,1)S(1)} %get-tuple-element.68.refs_3_), channel_id=1, source_target_pairs={{0,16},{8,24},{16,0},{24,8},{1,17},{9,25},{17,1},{25,9},{2,18},{10... | collective-permute-start | bytes 1179656 | tf_op jit(solution)/shard_map/ppermute | solution.py:251
  60.4 0.1 shard_map.117.refs_7_
  60.6 2.6 %collective-permute-start.18 = (bf16[256,768]{1,0:T(8,128)(2,1)S(1)}, bf16[256,768]{1,0:T(8,128)(2,1)S(1)}, u32[]{:S(2)}, u32[]{:S(2)}) collective-permute-start(bf16[256,768]{1,0:T(8,128)(2,1)S(1)} %shard_map.117.refs_7_), channel_id=1, source_target_pairs={{0,6},{2,0},{4,2},{6,4},{1,7},{3,1},{5,3},{7,5},{8,14},{10,8},{12,... | collective-permute-start | bytes 1179656 | tf_op jit(solution)/shard_map/ppermute | solution.py:330
  63.2 0.6 shard_map.118
  63.8 0.1 collective-permute-start.17
  63.9 1.6 %collective-permute-start.21 = (bf16[1040,128]{1,0:T(8,128)(2,1)S(1)}, bf16[1040,128]{1,0:T(8,128)(2,1)S(1)}, u32[]{:S(2)}, u32[]{:S(2)}) collective-permute-start(bf16[1040,128]{1,0:T(8,128)(2,1)S(1)} %get-tuple-element.67.refs_4_.refs_0_), channel_id=1, source_target_pairs={{0,8},{8,0},{16,24},{24,16},{1,9},{9,1},{17,25},{25,17},{2,10},{10... | collective-permute-start | bytes 798728 | tf_op jit(solution)/shard_map/ppermute | solution.py:251
  65.5 3.6 %shard_map.119 = (bf16[256,1024]{1,0:T(8,128)(2,1)}, f32[256,1024]{1,0:T(8,128)S(1)}, f32[256,1024]{1,0:T(8,128)S(1)}) custom-call(bf16[256,1024]{1,0:T(8,128)(2,1)S(1)} %get-tuple-element.73.refs_0_, bf16[256,1024]{1,0:T(8,128)(2,1)S(1)} %bitcast.19, bf16[256,1024]{1,0:T(8,128)(2,1)S(1)} %bitcast.22, bf16[256,1024]{1,0:T(8,128)(2,1)S(1)} %bitcast.26, ...), custom_call_target="tpu_custom_call" | custom-call | tf_op jit(solution)/shard_map/pallas_call | solution.py:42
  69.1 4.7 %collective-permute-done.21.refs_1_.refs_0_ = bf16[1040,128]{1,0:T(8,128)(2,1)S(1)} collective-permute-done((bf16[1040,128]{1,0:T(8,128)(2,1)S(1)}, bf16[1040,128]{1,0:T(8,128)(2,1)S(1)}, u32[]{:S(2)}, u32[]{:S(2)}) %collective-permute-start.21) | collective-permute-done | bytes 266272 | tf_op jit(solution)/shard_map/ppermute | solution.py:251
  73.8 1.5 %collective-permute-start.24 = (bf16[128,1536]{1,0:T(8,128)(2,1)S(1)}, bf16[128,1536]{1,0:T(8,128)(2,1)S(1)}, u32[]{:S(2)}, u32[]{:S(2)}) collective-permute-start(bf16[128,1536]{1,0:T(8,128)(2,1)S(1)} %get-tuple-element.79), channel_id=1, source_target_pairs={{0,8},{8,0},{16,24},{24,16},{1,9},{9,1},{17,25},{25,17},{2,10},{10... | collective-permute-start | bytes 1179656 | tf_op jit(solution)/shard_map/ppermute | solution.py:251
  75.4 1.0 %copy-done.10 = bf16[256,1024]{1,0:T(8,128)(2,1)S(1)} copy-done((bf16[256,1024]{1,0:T(8,128)(2,1)S(1)}, bf16[256,1024]{1,0:T(8,128)(2,1)}, u32[]{:S(2)}) %copy-start.10) | copy-done | bytes 524312
  76.4 0.1 shard_map.120.refs_3_
  76.5 2.0 %collective-permute-start.25 = (bf16[128,1536]{1,0:T(8,128)(2,1)S(1)}, bf16[128,1536]{1,0:T(8,128)(2,1)S(1)}, u32[]{:S(2)}, u32[]{:S(2)}) collective-permute-start(bf16[128,1536]{1,0:T(8,128)(2,1)S(1)} %get-tuple-element.80), channel_id=1, source_target_pairs={{0,16},{8,24},{16,0},{24,8},{1,17},{9,25},{17,1},{25,9},{2,18},{10... | collective-permute-start | bytes 1179656 | tf_op jit(solution)/shard_map/ppermute | solution.py:251
  78.5 0.1 shard_map.121.refs_3_.refs_0_
  78.7 0.1 shard_map.122.refs_7_
  78.9 0.6 shard_map.123
  79.5 0.1 collective-permute-start.22
  79.5 1.7 %collective-permute-start.23 = (bf16[256,768]{1,0:T(8,128)(2,1)S(1)}, bf16[256,768]{1,0:T(8,128)(2,1)S(1)}, u32[]{:S(2)}, u32[]{:S(2)}) collective-permute-start(bf16[256,768]{1,0:T(8,128)(2,1)S(1)} %shard_map.122.refs_7_), channel_id=1, source_target_pairs={{0,6},{2,0},{4,2},{6,4},{1,7},{3,1},{5,3},{7,5},{8,14},{10,8},{12,... | collective-permute-start | bytes 1179656 | tf_op jit(solution)/shard_map/ppermute | solution.py:330
  81.2 1.3 %collective-permute-start.26 = (bf16[1024,128]{1,0:T(8,128)(2,1)S(1)}, bf16[1024,128]{1,0:T(8,128)(2,1)S(1)}, u32[]{:S(2)}, u32[]{:S(2)}) collective-permute-start(bf16[1024,128]{1,0:T(8,128)(2,1)S(1)} %shard_map.120.refs_3_), channel_id=1, source_target_pairs={{16,0},{24,8},{17,1},{25,9},{18,2},{26,10},{19,3},{27,11},{20,4},{... | collective-permute-start | bytes 786440 | tf_op jit(solution)/shard_map/ppermute | solution.py:532
  82.5 10.0 %collective-permute-done.26.refs_1_ = bf16[1024,128]{1,0:T(8,128)(2,1)S(1)} collective-permute-done((bf16[1024,128]{1,0:T(8,128)(2,1)S(1)}, bf16[1024,128]{1,0:T(8,128)(2,1)S(1)}, u32[]{:S(2)}, u32[]{:S(2)}) %collective-permute-start.26) | collective-permute-done | bytes 262176 | tf_op jit(solution)/shard_map/ppermute | solution.py:532
  92.5 1.6 %shard_map.124 = (bf16[256,1024]{1,0:T(8,128)(2,1)}, bf16[256,1024]{1,0:T(8,128)(2,1)}) custom-call(bf16[1040,128]{1,0:T(8,128)(2,1)S(1)} %collective-permute-done.21.refs_1_.refs_0_, bf16[1024,128]{1,0:T(8,128)(2,1)S(1)} %collective-permute-done.26.refs_1_, bf16[256,1024]{1,0:T(8,128)(2,1)S(1)} %bitcast.23, bf16[256,1024]{1,0:T(8,128)(2,1)S(1)} %bitcast.27, ...), custom_call_target="tpu_custom_call" | custom-call | tf_op jit(solution)/shard_map/pallas_call | solution.py:42
  94.1 1.0 %copy-done.9 = bf16[256,1024]{1,0:T(8,128)(2,1)S(1)} copy-done((bf16[256,1024]{1,0:T(8,128)(2,1)S(1)}, bf16[256,1024]{1,0:T(8,128)(2,1)}, u32[]{:S(2)}) %copy-start.9) | copy-done | bytes 524312
  95.1 1.3 %shard_map.125.refs_3_ = f32[128,3072]{1,0:T(8,128)} custom-call(f32[128,3072]{1,0:T(8,128)S(1)} %shard_map.121.refs_3_.refs_0_, bf16[128,1536]{1,0:T(8,128)(2,1)S(1)} %collective-permute-done.24.refs_1_, bf16[128,1536]{1,0:T(8,128)(2,1)S(1)} %collective-permute-done.25.refs_2_, bf16[256,1024]{1,0:T(8,128)(2,1)S(1)} %copy-done.9), custom_call_target="tpu_custom_call" | custom-call | tf_op jit(solution)/shard_map/pallas_call | solution.py:42
  96.5 1.4 %copy-done.5 = f32[128,3072]{1,0:T(8,128)S(1)} copy-done((f32[128,3072]{1,0:T(8,128)S(1)}, f32[128,3072]{1,0:T(8,128)}, u32[]{:S(2)}) %copy-start.5) | copy-done | bytes 1572888
  97.9 0.9 shard_map.126
  (54 shorter events, 0.4 us)
Async XLA Ops:
  0.6 11.1 %collective-permute-start.3 = (bf16[256,3072]{1,0:T(8,128)(2,1)}, bf16[256,3072]{1,0:T(8,128)(2,1)S(1)}, u32[]{:S(2)}, u32[]{:S(2)}) collective-permute-start(bf16[256,3072]{1,0:T(8,128)(2,1)} %bitcast.11), channel_id=1, source_target_pairs={{0,1},{1,0},{2,3},{3,2},{4,5},{5,4},{6,7},{7,6},{8,9},{9,8},{10,11... | collective-permute-start | bytes 4718600 | tf_op jit(solution)/shard_map/ppermute | solution.py:247
  1.1 10.6 %copy-start.1 = (bf16[1,256,1024]{2,1,0:T(8,128)(2,1)S(1)}, bf16[1,256,1024]{2,1,0:T(8,128)(2,1)}, u32[]{:S(2)}) copy-start(bf16[1,256,1024]{2,1,0:T(8,128)(2,1)} %param.6) | copy-start | bytes 1572868
  1.2 10.6 %copy-start.2 = (bf16[1,256,1024]{2,1,0:T(8,128)(2,1)S(1)}, bf16[1,256,1024]{2,1,0:T(8,128)(2,1)}, u32[]{:S(2)}) copy-start(bf16[1,256,1024]{2,1,0:T(8,128)(2,1)} %param.7) | copy-start | bytes 1572868
  1.2 10.6 %copy-start.3 = (bf16[1,256,1024]{2,1,0:T(8,128)(2,1)S(1)}, bf16[1,256,1024]{2,1,0:T(8,128)(2,1)}, u32[]{:S(2)}) copy-start(bf16[1,256,1024]{2,1,0:T(8,128)(2,1)} %param.8) | copy-start | bytes 1572868
  3.1 12.9 %collective-permute-start.2 = (bf16[128,1536]{1,0:T(8,128)(2,1)}, bf16[128,1536]{1,0:T(8,128)(2,1)}, u32[]{:S(2)}, u32[]{:S(2)}) collective-permute-start(bf16[128,1536]{1,0:T(8,128)(2,1)} %shard_map.101.refs_4_.refs_2_), channel_id=1, source_target_pairs={{0,16},{8,24},{16,0},{24,8},{1,17},{9,25},{17,1},{25,9},{2,18},{10... | collective-permute-start | bytes 1179656 | tf_op jit(solution)/shard_map/ppermute | solution.py:251
  5.7 12.3 %collective-permute-start.1 = (bf16[128,1536]{1,0:T(8,128)(2,1)}, bf16[128,1536]{1,0:T(8,128)(2,1)}, u32[]{:S(2)}, u32[]{:S(2)}) collective-permute-start(bf16[128,1536]{1,0:T(8,128)(2,1)} %shard_map.101.refs_4_.refs_2_), channel_id=1, source_target_pairs={{0,8},{8,0},{16,24},{24,16},{1,9},{9,1},{17,25},{25,17},{2,10},{10... | collective-permute-start | bytes 1179656 | tf_op jit(solution)/shard_map/ppermute | solution.py:251
  10.5 13.2 %collective-permute-start = (bf16[1040,128]{1,0:T(8,128)(2,1)}, bf16[1040,128]{1,0:T(8,128)(2,1)}, u32[]{:S(2)}, u32[]{:S(2)}) collective-permute-start(bf16[1040,128]{1,0:T(8,128)(2,1)} %get-tuple-element.45.refs_0_), channel_id=1, source_target_pairs={{0,8},{8,0},{16,24},{24,16},{1,9},{9,1},{17,25},{25,17},{2,10},{10... | collective-permute-start | bytes 798728 | tf_op jit(solution)/shard_map/ppermute | solution.py:251
  11.1 18.5 %collective-permute-start.5 = (bf16[128,1536]{1,0:T(8,128)(2,1)}, bf16[128,1536]{1,0:T(8,128)(2,1)S(1)}, u32[]{:S(2)}, u32[]{:S(2)}) collective-permute-start(bf16[128,1536]{1,0:T(8,128)(2,1)} %get-tuple-element.46.refs_2_.refs_5_), channel_id=1, source_target_pairs={{0,16},{8,24},{16,0},{24,8},{1,17},{9,25},{17,1},{25,9},{2,18},{10... | collective-permute-start | bytes 1179656 | tf_op jit(solution)/shard_map/ppermute | solution.py:251
  11.8 0.9 copy-start.7
  12.7 0.7 copy-start.12
  14.5 9.2 %copy-start.4 = (bf16[128,1536]{1,0:T(8,128)(2,1)S(1)}, bf16[128,1536]{1,0:T(8,128)(2,1)}, u32[]{:S(2)}) copy-start(bf16[128,1536]{1,0:T(8,128)(2,1)} %get-tuple-element.46.refs_2_.refs_5_) | copy-start | bytes 1179652
  14.5 9.2 %copy-start.11 = (bf16[1040,128]{1,0:T(8,128)(2,1)S(1)}, bf16[1040,128]{1,0:T(8,128)(2,1)}, u32[]{:S(2)}) copy-start(bf16[1040,128]{1,0:T(8,128)(2,1)} %get-tuple-element.45.refs_0_) | copy-start | bytes 798724
  14.5 14.3 %copy-start.14 = (pred[512]{0:T(512)(128)(4,1)S(1)}, pred[512]{0:T(512)(128)(4,1)}, u32[]{:S(2)}) copy-start(pred[512]{0:T(512)(128)(4,1)} %fusion.10) | copy-start | bytes 1540
  19.1 10.5 %collective-permute-start.7 = (bf16[64,1536]{1,0:T(8,128)(2,1)S(1)}, bf16[64,1536]{1,0:T(8,128)(2,1)S(1)}, u32[]{:S(2)}, u32[]{:S(2)}) collective-permute-start(bf16[64,1536]{1,0:T(8,128)(2,1)S(1)} %get-tuple-element.52), channel_id=1, source_target_pairs={{0,8},{8,0},{16,24},{24,16},{1,9},{9,1},{17,25},{25,17},{2,10},{10... | collective-permute-start | bytes 589832 | tf_op jit(solution)/shard_map/ppermute | solution.py:251
  20.7 8.9 %collective-permute-start.6 = (bf16[64,1536]{1,0:T(8,128)(2,1)S(1)}, bf16[64,1536]{1,0:T(8,128)(2,1)S(1)}, u32[]{:S(2)}, u32[]{:S(2)}) collective-permute-start(bf16[64,1536]{1,0:T(8,128)(2,1)S(1)} %get-tuple-element.50.refs_3_), channel_id=1, source_target_pairs={{0,16},{8,24},{16,0},{24,8},{1,17},{9,25},{17,1},{25,9},{2,18},{10... | collective-permute-start | bytes 589832 | tf_op jit(solution)/shard_map/ppermute | solution.py:251
  24.8 8.4 %collective-permute-start.4 = (bf16[1024,128]{1,0:T(8,128)(2,1)S(1)}, bf16[1024,128]{1,0:T(8,128)(2,1)S(1)}, u32[]{:S(2)}, u32[]{:S(2)}) collective-permute-start(bf16[1024,128]{1,0:T(8,128)(2,1)S(1)} %get-tuple-element.51.refs_1_), channel_id=1, source_target_pairs={{0,16},{8,24},{1,17},{9,25},{2,18},{10,26},{3,19},{11,27},{4,20},{... | collective-permute-start | bytes 786440 | tf_op jit(solution)/shard_map/ppermute | solution.py:421
  26.8 10.0 %collective-permute-start.9 = (bf16[128,1536]{1,0:T(8,128)(2,1)S(1)}, bf16[128,1536]{1,0:T(8,128)(2,1)S(1)}, u32[]{:S(2)}, u32[]{:S(2)}) collective-permute-start(bf16[128,1536]{1,0:T(8,128)(2,1)S(1)} %get-tuple-element.55), channel_id=1, source_target_pairs={{0,8},{8,0},{16,24},{24,16},{1,9},{9,1},{17,25},{25,17},{2,10},{10... | collective-permute-start | bytes 1179656 | tf_op jit(solution)/shard_map/ppermute | solution.py:251
  28.8 4.4 %copy-start.8 = (f32[256,8]{1,0:T(8,128)S(1)}, f32[256,8]{1,0:T(8,128)}, u32[]{:S(2)}) copy-start(f32[256,8]{1,0:T(8,128)} %get-tuple-element.48.refs_4_.refs_6_.refs_5_) | copy-start | bytes 24580
  33.2 3.7 %copy-start.6 = (bf16[128,1536]{1,0:T(8,128)(2,1)S(1)}, bf16[128,1536]{1,0:T(8,128)(2,1)}, u32[]{:S(2)}) copy-start(bf16[128,1536]{1,0:T(8,128)(2,1)} %shard_map.101.refs_4_.refs_2_) | copy-start | bytes 1179652
  35.2 1.6 %collective-permute-start.8 = (bf16[256,512]{1,0:T(8,128)(2,1)S(1)}, bf16[256,512]{1,0:T(8,128)(2,1)S(1)}, u32[]{:S(2)}, u32[]{:S(2)}) collective-permute-start(bf16[256,512]{1,0:T(8,128)(2,1)S(1)} %get-tuple-element.54), channel_id=1, source_target_pairs={{0,1},{1,0},{2,3},{3,2},{4,5},{5,4},{6,7},{7,6},{8,9},{9,8},{10,11... | collective-permute-start | bytes 786440 | tf_op jit(solution)/shard_map/ppermute | solution.py:247
  36.8 6.4 %copy-start = (bf16[1,256,3072]{2,1,0:T(8,128)(2,1)S(1)}, bf16[1,256,3072]{2,1,0:T(8,128)(2,1)}, u32[]{:S(2)}) copy-start(bf16[1,256,3072]{2,1,0:T(8,128)(2,1)} %param.11) | copy-start | bytes 4718596
  39.1 5.5 %collective-permute-start.12 = (bf16[256,1536]{1,0:T(8,128)(2,1)S(1)}, bf16[256,1536]{1,0:T(8,128)(2,1)S(1)}, u32[]{:S(2)}, u32[]{:S(2)}) collective-permute-start(bf16[256,1536]{1,0:T(8,128)(2,1)S(1)} %get-tuple-element.57), channel_id=1, source_target_pairs={{0,1},{1,0},{2,3},{3,2},{4,5},{5,4},{6,7},{7,6},{8,9},{9,8},{10,11... | collective-permute-start | bytes 2359304 | tf_op jit(solution)/shard_map/ppermute | solution.py:247
  39.1 13.7 %collective-permute-start.11 = (bf16[64,1536]{1,0:T(8,128)(2,1)S(1)}, bf16[64,1536]{1,0:T(8,128)(2,1)S(1)}, u32[]{:S(2)}, u32[]{:S(2)}) collective-permute-start(bf16[64,1536]{1,0:T(8,128)(2,1)S(1)} %shard_map.106.refs_7_), channel_id=1, source_target_pairs={{0,8},{8,0},{16,24},{24,16},{1,9},{9,1},{17,25},{25,17},{2,10},{10... | collective-permute-start | bytes 589832 | tf_op jit(solution)/shard_map/ppermute | solution.py:251
  40.7 12.2 %collective-permute-start.10 = (bf16[64,1536]{1,0:T(8,128)(2,1)S(1)}, bf16[64,1536]{1,0:T(8,128)(2,1)S(1)}, u32[]{:S(2)}, u32[]{:S(2)}) collective-permute-start(bf16[64,1536]{1,0:T(8,128)(2,1)S(1)} %shard_map.108.refs_7_), channel_id=1, source_target_pairs={{0,16},{8,24},{16,0},{24,8},{1,17},{9,25},{17,1},{25,9},{2,18},{10... | collective-permute-start | bytes 589832 | tf_op jit(solution)/shard_map/ppermute | solution.py:251
  43.9 12.8 %collective-permute-start.15 = (bf16[128,1536]{1,0:T(8,128)(2,1)S(1)}, bf16[128,1536]{1,0:T(8,128)(2,1)S(1)}, u32[]{:S(2)}, u32[]{:S(2)}) collective-permute-start(bf16[128,1536]{1,0:T(8,128)(2,1)S(1)} %get-tuple-element.63), channel_id=1, source_target_pairs={{0,16},{8,24},{16,0},{24,8},{1,17},{9,25},{17,1},{25,9},{2,18},{10... | collective-permute-start | bytes 1179656 | tf_op jit(solution)/shard_map/ppermute | solution.py:251
  44.0 12.8 %collective-permute-start.14 = (bf16[128,1536]{1,0:T(8,128)(2,1)S(1)}, bf16[128,1536]{1,0:T(8,128)(2,1)S(1)}, u32[]{:S(2)}, u32[]{:S(2)}) collective-permute-start(bf16[128,1536]{1,0:T(8,128)(2,1)S(1)} %get-tuple-element.59.refs_2_), channel_id=1, source_target_pairs={{0,8},{8,0},{16,24},{24,16},{1,9},{9,1},{17,25},{25,17},{2,10},{10... | collective-permute-start | bytes 1179656 | tf_op jit(solution)/shard_map/ppermute | solution.py:251
  44.6 15.8 %collective-permute-start.13 = (bf16[256,768]{1,0:T(8,128)(2,1)S(1)}, bf16[256,768]{1,0:T(8,128)(2,1)S(1)}, u32[]{:S(2)}, u32[]{:S(2)}) collective-permute-start(bf16[256,768]{1,0:T(8,128)(2,1)S(1)} %shard_map.111.refs_8_), channel_id=1, source_target_pairs={{0,6},{2,0},{4,2},{6,4},{1,7},{3,1},{5,3},{7,5},{8,14},{10,8},{12,... | collective-permute-start | bytes 1179656 | tf_op jit(solution)/shard_map/ppermute | solution.py:330
  52.9 2.7 %copy-start.13 = (f32[8,256]{1,0:T(8,128)S(1)}, f32[8,256]{1,0:T(8,128)}, u32[]{:S(2)}) copy-start(f32[8,256]{1,0:T(8,128)} %get-tuple-element.47.refs_3_.refs_5_.refs_4_) | copy-start | bytes 24580
  54.0 1.6 %collective-permute-start.16 = (bf16[256,512]{1,0:T(8,128)(2,1)S(1)}, bf16[256,512]{1,0:T(8,128)(2,1)S(1)}, u32[]{:S(2)}, u32[]{:S(2)}) collective-permute-start(bf16[256,512]{1,0:T(8,128)(2,1)S(1)} %pad_maximum_fusion.1), channel_id=1, source_target_pairs={{0,1},{1,0},{2,3},{3,2},{4,5},{5,4},{6,7},{7,6},{8,9},{9,8},{10,11... | collective-permute-start | bytes 786440 | tf_op jit(solution)/shard_map/ppermute | solution.py:247
  56.9 19.6 %collective-permute-start.20 = (bf16[128,1536]{1,0:T(8,128)(2,1)S(1)}, bf16[128,1536]{1,0:T(8,128)(2,1)S(1)}, u32[]{:S(2)}, u32[]{:S(2)}) collective-permute-start(bf16[128,1536]{1,0:T(8,128)(2,1)S(1)} %get-tuple-element.72), channel_id=1, source_target_pairs={{0,8},{8,0},{16,24},{24,16},{1,9},{9,1},{17,25},{25,17},{2,10},{10... | collective-permute-start | bytes 1179656 | tf_op jit(solution)/shard_map/ppermute | solution.py:251
  58.5 20.0 %collective-permute-start.19 = (bf16[128,1536]{1,0:T(8,128)(2,1)S(1)}, bf16[128,1536]{1,0:T(8,128)(2,1)S(1)}, u32[]{:S(2)}, u32[]{:S(2)}) collective-permute-start(bf16[128,1536]{1,0:T(8,128)(2,1)S(1)} %get-tuple-element.68.refs_3_), channel_id=1, source_target_pairs={{0,16},{8,24},{16,0},{24,8},{1,17},{9,25},{17,1},{25,9},{2,18},{10... | collective-permute-start | bytes 1179656 | tf_op jit(solution)/shard_map/ppermute | solution.py:251
  60.6 18.1 %collective-permute-start.18 = (bf16[256,768]{1,0:T(8,128)(2,1)S(1)}, bf16[256,768]{1,0:T(8,128)(2,1)S(1)}, u32[]{:S(2)}, u32[]{:S(2)}) collective-permute-start(bf16[256,768]{1,0:T(8,128)(2,1)S(1)} %shard_map.117.refs_7_), channel_id=1, source_target_pairs={{0,6},{2,0},{4,2},{6,4},{1,7},{3,1},{5,3},{7,5},{8,14},{10,8},{12,... | collective-permute-start | bytes 1179656 | tf_op jit(solution)/shard_map/ppermute | solution.py:330
  63.8 14.9 %collective-permute-start.17 = (bf16[256,768]{1,0:T(8,128)(2,1)S(1)}, bf16[256,768]{1,0:T(8,128)(2,1)S(1)}, u32[]{:S(2)}, u32[]{:S(2)}) collective-permute-start(bf16[256,768]{1,0:T(8,128)(2,1)S(1)} %get-tuple-element.70), channel_id=1, source_target_pairs={{0,1},{1,0},{2,3},{3,2},{4,5},{5,4},{6,7},{7,6},{8,9},{9,8},{10,11... | collective-permute-start | bytes 1179656 | tf_op jit(solution)/shard_map/ppermute | solution.py:247
  63.9 9.9 %collective-permute-start.21 = (bf16[1040,128]{1,0:T(8,128)(2,1)S(1)}, bf16[1040,128]{1,0:T(8,128)(2,1)S(1)}, u32[]{:S(2)}, u32[]{:S(2)}) collective-permute-start(bf16[1040,128]{1,0:T(8,128)(2,1)S(1)} %get-tuple-element.67.refs_4_.refs_0_), channel_id=1, source_target_pairs={{0,8},{8,0},{16,24},{24,16},{1,9},{9,1},{17,25},{25,17},{2,10},{10... | collective-permute-start | bytes 798728 | tf_op jit(solution)/shard_map/ppermute | solution.py:251
  73.8 20.2 %collective-permute-start.24 = (bf16[128,1536]{1,0:T(8,128)(2,1)S(1)}, bf16[128,1536]{1,0:T(8,128)(2,1)S(1)}, u32[]{:S(2)}, u32[]{:S(2)}) collective-permute-start(bf16[128,1536]{1,0:T(8,128)(2,1)S(1)} %get-tuple-element.79), channel_id=1, source_target_pairs={{0,8},{8,0},{16,24},{24,16},{1,9},{9,1},{17,25},{25,17},{2,10},{10... | collective-permute-start | bytes 1179656 | tf_op jit(solution)/shard_map/ppermute | solution.py:251
  75.4 1.0 %copy-start.10 = (bf16[256,1024]{1,0:T(8,128)(2,1)S(1)}, bf16[256,1024]{1,0:T(8,128)(2,1)}, u32[]{:S(2)}) copy-start(bf16[256,1024]{1,0:T(8,128)(2,1)} %get-tuple-element.76.refs_2_) | copy-start | bytes 1572868
  76.5 17.5 %collective-permute-start.25 = (bf16[128,1536]{1,0:T(8,128)(2,1)S(1)}, bf16[128,1536]{1,0:T(8,128)(2,1)S(1)}, u32[]{:S(2)}, u32[]{:S(2)}) collective-permute-start(bf16[128,1536]{1,0:T(8,128)(2,1)S(1)} %get-tuple-element.80), channel_id=1, source_target_pairs={{0,16},{8,24},{16,0},{24,8},{1,17},{9,25},{17,1},{25,9},{2,18},{10... | collective-permute-start | bytes 1179656 | tf_op jit(solution)/shard_map/ppermute | solution.py:251
  79.5 17.0 %collective-permute-start.22 = (bf16[256,768]{1,0:T(8,128)(2,1)S(1)}, bf16[256,768]{1,0:T(8,128)(2,1)S(1)}, u32[]{:S(2)}, u32[]{:S(2)}) collective-permute-start(bf16[256,768]{1,0:T(8,128)(2,1)S(1)} %get-tuple-element.78), channel_id=1, source_target_pairs={{0,1},{1,0},{2,3},{3,2},{4,5},{5,4},{6,7},{7,6},{8,9},{9,8},{10,11... | collective-permute-start | bytes 1179656 | tf_op jit(solution)/shard_map/ppermute | solution.py:247
  79.5 16.9 %collective-permute-start.23 = (bf16[256,768]{1,0:T(8,128)(2,1)S(1)}, bf16[256,768]{1,0:T(8,128)(2,1)S(1)}, u32[]{:S(2)}, u32[]{:S(2)}) collective-permute-start(bf16[256,768]{1,0:T(8,128)(2,1)S(1)} %shard_map.122.refs_7_), channel_id=1, source_target_pairs={{0,6},{2,0},{4,2},{6,4},{1,7},{3,1},{5,3},{7,5},{8,14},{10,8},{12,... | collective-permute-start | bytes 1179656 | tf_op jit(solution)/shard_map/ppermute | solution.py:330
  81.2 11.3 %collective-permute-start.26 = (bf16[1024,128]{1,0:T(8,128)(2,1)S(1)}, bf16[1024,128]{1,0:T(8,128)(2,1)S(1)}, u32[]{:S(2)}, u32[]{:S(2)}) collective-permute-start(bf16[1024,128]{1,0:T(8,128)(2,1)S(1)} %shard_map.120.refs_3_), channel_id=1, source_target_pairs={{16,0},{24,8},{17,1},{25,9},{18,2},{26,10},{19,3},{27,11},{20,4},{... | collective-permute-start | bytes 786440 | tf_op jit(solution)/shard_map/ppermute | solution.py:532
  94.1 1.0 %copy-start.9 = (bf16[256,1024]{1,0:T(8,128)(2,1)S(1)}, bf16[256,1024]{1,0:T(8,128)(2,1)}, u32[]{:S(2)}) copy-start(bf16[256,1024]{1,0:T(8,128)(2,1)} %get-tuple-element.83.refs_3_) | copy-start | bytes 1572868
  96.5 1.4 %copy-start.5 = (f32[128,3072]{1,0:T(8,128)S(1)}, f32[128,3072]{1,0:T(8,128)}, u32[]{:S(2)}) copy-start(f32[128,3072]{1,0:T(8,128)} %shard_map.125.refs_3_) | copy-start | bytes 4718596

commit v3 on v2

--- a/solution.py
+++ b/solution.py
@@ -12,6 +12,7 @@
 F32 = jnp.float32
 BF16 = jnp.bfloat16
 EXTRA = 16
+C17, C20, C24 = 1284000000, 1070000000, 2140000000
 
 
 def contract(a, b, dim_a, dim_b):
@@ -22,7 +23,7 @@
     return ref[:, h * DH : (h + 1) * DH]
 
 
-def call(kernel, out_shape, *args, staged=(), free_in=(), free_out=(), scratch=(), after=(), room=24):
+def call(kernel, out_shape, *args, staged=(), free_in=(), free_out=(), scratch=(), after=(), room=24, work=0):
     n, waits, count = len(args), len(after), len(staged)
 
     def body(*refs):
@@ -41,6 +42,7 @@
     specs = [far if i in free_out else local for i in range(len(jax.tree.leaves(out_shape)))]
     return pl.pallas_call(
         body,
+        name=getattr(kernel, "func", kernel).__name__,
         out_shape=out_shape,
         in_specs=[far if i in staged or i in free_in else local for i in range(n)] + [anywhere] * waits,
         out_specs=specs if isinstance(out_shape, (list, tuple)) else specs[0],
@@ -50,7 +52,7 @@
             pltpu.SemaphoreType.DMA((max(count, 1),)),
         ],
         compiler_params=pltpu.CompilerParams(vmem_limit_bytes=room * 1024 * 1024),
-        cost_estimate=pl.CostEstimate(flops=0, bytes_accessed=0, transcendentals=0),
+        cost_estimate=pl.CostEstimate(flops=work, bytes_accessed=0, transcendentals=0),
     )(*args, *after)
 
 
@@ -126,13 +128,9 @@
     return copies
 
 
-def first_columns_kernel(w_ref, out_ref, sem):
-    for copy in ring_columns(w_ref, out_ref, 1, sem):
-        copy.wait()
-
-
-def contrib_kernel(groups, hops, k_ref, v_ref, ld_ref, w_ref, state_ref, row_ref, col_ref, copy_ref, sem):
-    copies = ring_columns(w_ref, copy_ref, hops, sem)
+def contrib_kernel(groups, k_ref, v_ref, ld_ref, w_ref, state_ref, row_ref, col_ref, first_ref, rest_ref, sem):
+    count = first_ref.shape[1] * lax.axis_size("head") // w_ref.shape[1]
+    copies = ring_columns(w_ref, first_ref, 1, sem) + ring_columns(w_ref, rest_ref, 1 + count, sem.at[pl.ds(count, sem.shape[0] - count)])
     size = k_ref.shape[0]
     lower = lower_mask(size).astype(F32)
     ld = ld_ref[...]
@@ -158,19 +156,23 @@
     return jnp.exp(jnp.where(lower, spread, -jnp.inf))
 
 
-def intra_kernel(groups, q_ref, k_ref, v_ref, row_ref, col_ref, probs_ref, intra_ref):
+def again_kernel(ref, again_ref):
+    again_ref[...] = ref[...]
+
+
+def intra_kernel(groups, q_ref, k_ref, v_ref, row_ref, col_ref, intra_ref):
     lower = lower_mask(q_ref.shape[0])
     for h in range(groups):
         weights = spread_weights(row_ref, col_ref, lower, h)
         probs = (contract(head(q_ref, h), head(k_ref, h), 1, 1) * SCALE * weights).astype(BF16)
-        probs_ref[h] = probs
         intra_ref[:, h * DH : (h + 1) * DH] = contract(probs, head(v_ref, h), 1, 0)
 
 
 def attended_kernel(groups, count, *refs):
     states = refs[:count]
-    q_ref, intra_ref, col_ref, pick_own_ref, pick_other_ref = refs[count : count + 5]
-    own_ref, other_ref, low_ref, attended_ref = refs[count + 5 :]
+    q_ref, intra_ref, col_ref, pick_own_ref, pick_other_ref, rest_ref = refs[count : count + 6]
+    own_ref, other_ref, low_ref, again_ref, attended_ref = refs[count + 6 :]
+    again_ref[...] = rest_ref[...]
     state = entering(states, groups, True)
     factor = jnp.exp(col_ref[...]) * SCALE
     for h in range(groups):
@@ -198,7 +200,7 @@
 
 
 def back_intra_kernel(
-    groups, grad_ref, q_ref, k_ref, v_ref, row_ref, col_ref, probs_ref, low_ref, qgrad_ref, kpart_ref, vpart_ref
+    groups, grad_ref, q_ref, k_ref, v_ref, row_ref, col_ref, low_ref, qgrad_ref, kpart_ref, vpart_ref
 ):
     lower = lower_mask(q_ref.shape[0])
     factor = jnp.exp(col_ref[...]) * SCALE
@@ -211,7 +213,8 @@
             contract(dprobs, head(k_ref, h), 1, 0) + contract(grad, low_ref[h], 1, 1) * factor[:, h : h + 1]
         ).astype(BF16)
         kpart_ref[:, here] = contract(dprobs, head(q_ref, h), 0, 0)
-        vpart_ref[:, here] = contract(probs_ref[h], grad, 0, 0)
+        probs = (contract(head(q_ref, h), head(k_ref, h), 1, 1) * SCALE * weights).astype(BF16)
+        vpart_ref[:, here] = contract(probs, grad, 0, 0)
 
 
 def back_inter_kernel(groups, count, *refs):
@@ -251,11 +254,10 @@
     return lax.ppermute(array, "ctx", [(i, i ^ bit) for i in range(4)])
 
 
-def rows_kernel(count, *refs):
-    ins, outs = refs[: len(refs) // 2], refs[len(refs) // 2 :]
-    for i, (ref, out) in enumerate(zip(ins, outs)):
-        rows = out.shape[0]
-        out[...] = ref[:rows] if i < count else ref[rows:]
+def rows_kernel(one, two, on_one, on_two):
+    half = on_one.shape[0]
+    on_one[...] = one[:half]
+    on_two[...] = two[half:]
 
 
 def lay_out(pieces, out_ref, columns=slice(None)):
@@ -270,29 +272,36 @@
     return pl.ds(pl.multiple_of(lax.rem(lax.axis_index("head") + hops, devices) * width, width), width)
 
 
-def mix_kernel(count, place, a_own, a_other, *refs):
-    pieces, owns, other, w_ref = refs[:count], refs[count:-2], refs[-2], refs[-1]
+def mix_kernel(count, place, splits, a_own, a_other, *refs):
+    pieces, owns, others, w_ref = refs[:count], refs[count : -1 - splits], refs[-1 - splits : -1], refs[-1]
     width = w_ref.shape[1]
+    away = []
     for j, own in enumerate(owns):
         lay_out(pieces, w_ref, slice((place + j) * width, (place + j + 1) * width))
         own[...] = contract(a_own[...], w_ref[...], 1, 0)
-        other[:, j * width : (j + 1) * width] = contract(a_other[...], w_ref[...], 1, 0).astype(BF16)
-
-
-def grad_kernel(count, g_own, g_other, *refs):
-    first, rest, (own, other, w_ref) = refs[:count], refs[count : 2 * count], refs[2 * count :]
+        away.append(contract(a_other[...], w_ref[...], 1, 0).astype(BF16))
+    away = away[0] if len(away) == 1 else jnp.concatenate(away, axis=1)
+    for i, other in enumerate(others):
+        other[...] = away[:, i * other.shape[1] : (i + 1) * other.shape[1]]
+
+
+def grad_kernel(count, earlier, g_own, g_other, *refs):
+    first, rest, (own, other, w_ref) = refs[:count], refs[count : 2 * count], refs[2 * count + earlier :]
     heads = lax.axis_size("head")
     left, width = first[0].shape[1], w_ref.shape[1] // heads
     lay_out(first, w_ref.at[:, 0:left])
     lay_out(rest, w_ref.at[:, left:])
-    for g_ref, out in ((g_own, own), (g_other, other)):
+    before = refs[2 * count : 2 * count + earlier] or (None, None)
+    for g_ref, old, out in ((g_own, before[0], own), (g_other, before[1], other)):
         total = None
         for j in range(heads):
             term = contract(
                 g_ref[:, columns_after(1 + j, width)], w_ref[:, j * width : (j + 1) * width], 1, 1
             )
             total = term if total is None else total + term
-        out[...] = total.astype(BF16)
+        if old is not None:
+            out[:, : old.shape[1]] = old[...]
+        out[:, out.shape[1] - total.shape[1] :] = total.astype(BF16)
 
 
 def weight_kernel(blocks, a_own, a_other, g_own, g_other, *outs):
@@ -317,11 +326,19 @@
     out_ref[:, right] = own_ref[:, right] + right_ref[...].astype(F32)
 
 
-def ring_kernel(j, own_ref, other_ref, *refs):
+def back_pair_kernel(groups, own_ref, near_ref, left_ref, right_ref, out_ref, left_again, right_again):
+    left_again[...] = left_ref[...]
+    right_again[...] = right_ref[...]
+    pair_kernel(groups, False, own_ref, near_ref, out_ref)
+
+
+def ring_kernel(j, count, own_ref, *refs):
     width = own_ref.shape[1]
-    total = own_ref[...] + other_ref[:, j * width : (j + 1) * width].astype(F32)
-    if len(refs) == 2:
-        total = total + refs[0][...].astype(F32)
+    other = [ref[...] for ref in refs[:count]]
+    other = other[0] if count == 1 else jnp.concatenate(other, axis=1)
+    total = own_ref[...] + other[:, j * width : (j + 1) * width].astype(F32)
+    if len(refs) == count + 2:
+        total = total + refs[count][...].astype(F32)
     refs[-1][...] = total.astype(BF16)
 
 
@@ -368,39 +385,31 @@
         return out
 
     near_heads = heads // 2
-    w_first = step(
-        first_columns_kernel,
-        struct((rows, near_heads * part), BF16),
-        w,
-        free_in=(0,),
-        scratch=[pltpu.SemaphoreType.DMA((near_heads,))],
-        room=60,
-    )
-    if four:
-        first_two, first_one = flipped(w_first, 2), flipped(w_first, 1)
-    g_other = swapped(g)
-    rest_shape = struct((rows, width - near_heads * part), BF16)
-    state, row, col, w_rest = step(
-        functools.partial(contrib_kernel, groups, near_heads + 1),
-        (state_shape, struct((groups, size), F32), struct((size, groups), F32), rest_shape),
+    first_shape, rest_shape = (struct((rows, count * part), BF16) for count in (near_heads, heads - near_heads))
+    state, row, col, w_first, w_rest = step(
+        functools.partial(contrib_kernel, groups),
+        (state_shape, struct((groups, size), F32), struct((size, groups), F32), first_shape, rest_shape),
         k,
         v,
         ld,
         w,
         staged=(0, 1, 2),
         free_in=(3,),
-        scratch=[pltpu.SemaphoreType.DMA((heads - near_heads,))],
+        scratch=[pltpu.SemaphoreType.DMA((heads,))],
         room=60,
     )
+    g_other = swapped(g)
     if four:
         near = flipped(state, 1)
-        rest_two = flipped(w_rest, 2)
+        first_two = flipped(w_first, 2)
+        w_again = step(again_kernel, first_shape, w_first)
+        first_one = flipped(w_again, 1)
     else:
         before = hops_of(state, True)
     pick_own, pick_other = picks(groups, rows_each)
-    probs, intra = step(
+    intra = step(
         functools.partial(intra_kernel, groups),
-        (struct((groups, size, size), BF16), flat(F32)),
+        flat(F32),
         q,
         k,
         v,
@@ -410,90 +419,87 @@
         after=[g_other],
     )
     if four:
+        pair = step(functools.partial(pair_kernel, groups, True), struct((features, DH), BF16), state, near)
+        before = [near, lax.ppermute(pair, "ctx", [(0, 2), (1, 3)])]
         lower = lambda array: struct((rows // 2, array.shape[1]), BF16)
-        on_one, on_two = step(
-            functools.partial(rows_kernel, 1), [lower(w_first)] * 2, first_one, first_two
-        )
+        on_one, on_two = step(rows_kernel, [lower(w_first)] * 2, first_one, first_two)
         first = [w_first, first_one, first_two, flipped(on_one, 2), flipped(on_two, 1)]
-        w_again, pair = step(
-            functools.partial(pair_kernel, groups, True), [rest_shape, struct((features, DH), BF16)], state, near, w_rest
-        )
-        before = [near, lax.ppermute(pair, "ctx", [(0, 2), (1, 3)])]
-        rest_one = flipped(w_again, 1)
-        (on_two,) = step(functools.partial(rows_kernel, 0), [lower(w_rest)], rest_two, after=first[3:])
     else:
         first = [lax.all_gather(w_first, "ctx", axis=0, tiled=True)]
         rest = [lax.all_gather(w_rest, "ctx", axis=0, tiled=True)]
-    a_own, a_away, low = step(
+    a_own, a_away, low, w_again = step(
         functools.partial(attended_kernel, groups, len(before)),
-        (half, half, struct((groups, DH, DH), BF16)),
+        (half, half, struct((groups, DH, DH), BF16), rest_shape),
         *before,
         q,
         intra,
         col,
         pick_own,
         pick_other,
-        staged=(len(before),),
+        w_rest,
         scratch=[pltpu.VMEM((size, features), BF16)],
     )
     a_other = swapped(a_away)
-    if four:
-        (on_one,) = step(functools.partial(rows_kernel, 1), [lower(w_rest)], rest_one)
-        rest = [w_rest, rest_one, rest_two, flipped(on_one, 2), flipped(on_two, 1)]
-
     held = pltpu.VMEM((features // 2, part), BF16)
 
-    def mix(pieces, place, count):
+    def mix(pieces, place, count, splits=1, work=0):
         out = step(
-            functools.partial(mix_kernel, len(pieces), place),
-            [struct((size, part), F32)] * count + [struct((size, count * part), BF16)],
+            functools.partial(mix_kernel, len(pieces), place, splits),
+            [struct((size, part), F32)] * count + [struct((size, count * part // splits), BF16)] * splits,
             a_own,
             a_other,
             *pieces,
             scratch=[held],
+            work=work,
         )
-        away = swapped(out[-1])
-        return [(own, away, j) for j, own in enumerate(out[:-1])]
-
-    def ring(terms, *arrived):
+        away = [swapped(other) for other in out[count:]]
+        return [(own, away, j) for j, own in enumerate(out[:count])]
+
+    def ring(terms, *arrived, work=0):
         own, away, j = terms
-        return step(functools.partial(ring_kernel, j), struct((size, part), BF16), own, away, *arrived)
+        return step(
+            functools.partial(ring_kernel, j, len(away)), struct((size, part), BF16), own, *away, *arrived, work=work
+        )
 
     def weights(blocks, shapes):
-        return step(functools.partial(weight_kernel, blocks), shapes, a_own, a_other, g, g_other, staged=(2,))
-
-    def grad_of(some):
+        return step(functools.partial(weight_kernel, blocks), shapes, a_own, a_other, g, g_other)
+
+    def grad_of(some, *earlier):
         here = sum(piece.shape[0] for piece, _ in some)
+        wide = here + sum(array.shape[1] for array in earlier[:1])
         return step(
-            functools.partial(grad_kernel, len(some)),
-            [struct((size, here), BF16)] * 2,
+            functools.partial(grad_kernel, len(some), len(earlier)),
+            [struct((size, wide), BF16)] * 2,
             g,
             g_other,
             *[piece for piece, _ in some],
             *[piece for _, piece in some],
-            staged=(0,),
+            *earlier,
             scratch=[pltpu.VMEM((here, width), BF16)],
         )
 
-    terms = mix(first, 0, near_heads)
     if four:
         small = lambda dtype: struct((rows, middle), dtype)
-        far = weights([(3, 0, middle), (3, middle, width)], [small(BF16)] * 2)
+        blocks = [
+            (3, 0, middle), (3, middle, width), (2, 0, middle), (1, middle, width), (1, 0, middle), (2, middle, width), (0, 0, width),
+        ]
+        *far, mid_left, mid_right, near_left, near_right, own_sum = weights(
+            blocks, [small(BF16)] * 2 + [small(F32)] * 2 + [small(BF16)] * 2 + [struct((rows, width), F32)]
+        )
+    terms = mix(first, 0, near_heads, 3 if four else 1, 0)
+    arrived = passed(ring(terms[0]))
+    if four:
+        rest_one, rest_two = flipped(w_again, 1), flipped(w_again, 2)
+        on_one, on_two = step(rows_kernel, [lower(w_rest)] * 2, rest_one, rest_two)
+        rest = [w_rest, rest_one, rest_two, flipped(on_one, 2), flipped(on_two, 1)]
         far_left, far_right = flipped(far[0], 1), flipped(far[1], 2)
-    arrived = passed(ring(terms[0]))
-    both = list(zip(first, rest))
-    if four:
-        near_grads = grad_of(both[:3])
-        parts = weights(
-            [(2, 0, middle), (1, middle, width), (1, 0, middle), (2, middle, width), (0, 0, width)],
-            [small(F32)] * 2 + [small(BF16)] * 2 + [struct((rows, width), F32)],
-        )
-        last_grads = grad_of(both[3:])
-        grad_own = jnp.concatenate([near_grads[0], last_grads[0]], axis=1)
-        grad_away = jnp.concatenate([near_grads[1], last_grads[1]], axis=1)
+        both = list(zip(first, rest))
+        grad_own, grad_away = grad_of(both[3:], *grad_of(both[:3]))
     else:
-        grad_own, grad_away = grad_of(both)
+        grad_own, grad_away = grad_of(list(zip(first, rest)))
     grad_other = swapped(grad_away)
+    for j in range(1, near_heads):
+        arrived = passed(ring(terms[j], arrived, work=C17))
     grad, back = step(
         functools.partial(back_contrib_kernel, groups),
         (flat(BF16), state_shape),
@@ -507,13 +513,24 @@
     )
     if four:
         near = flipped(back, 1)
-        to_left, to_right = step(onward_kernel, [small(BF16)] * 2, parts[0], parts[1], far_left, far_right)
-        on_left, on_right = flipped(to_left, 2), flipped(to_right, 1)
     else:
         after = hops_of(back, False)
-    for j in range(1, near_heads):
-        arrived = passed(ring(terms[j], arrived))
+    if four:
+        to_left, to_right = step(onward_kernel, [small(BF16)] * 2, mid_left, mid_right, far_left, far_right)
+        on_left, on_right = flipped(to_left, 2), flipped(to_right, 1)
     terms = mix(rest, 0, 1)
+    if four:
+        pair, near_left, near_right = step(
+            functools.partial(back_pair_kernel, groups),
+            [struct((features, DH), BF16), small(BF16), small(BF16)],
+            back,
+            near,
+            near_left,
+            near_right,
+            work=C20,
+        )
+        after = [near, lax.ppermute(pair, "ctx", [(2, 0), (3, 1)])]
+        near_left, near_right = flipped(near_left, 1), flipped(near_right, 2)
     query_grad, key_part, value_part = step(
         functools.partial(back_intra_kernel, groups),
         (flat(BF16), flat(F32), flat(F32)),
@@ -523,18 +540,14 @@
         v,
         row,
         col,
-        probs,
         low,
         staged=(1, 2, 3),
     )
-    if four:
-        pair = step(functools.partial(pair_kernel, groups, False), struct((features, DH), BF16), back, near)
-        after = [near, lax.ppermute(pair, "ctx", [(2, 0), (3, 1)])]
-        w_sum = step(total_kernel, struct((rows, width), F32), parts[4], on_left, on_right)
-        near_left, near_right = flipped(parts[2], 1), flipped(parts[3], 2)
     for j in range(1, heads - near_heads):
         arrived = passed(ring(terms[0], arrived))
         terms = mix(rest, j, 1)
+    if four:
+        own_sum = step(total_kernel, struct((rows, width), F32), own_sum, on_left, on_right)
     key_grad, value_grad = step(
         functools.partial(back_inter_kernel, groups, len(after)),
         (flat(BF16), flat(BF16)),
@@ -544,9 +557,10 @@
         col,
         key_part,
         value_part,
-    )
-    if four:
-        w_grad = step(total_kernel, struct((rows, width), F32), w_sum, near_left, near_right)
+        work=C24,
+    )
+    if four:
+        w_grad = step(total_kernel, struct((rows, width), F32), own_sum, near_left, near_right)
     else:
         w_grad = contract(a_own, g, 0, 0) + contract(a_other, g_other, 0, 0)
         w_grad = lax.psum_scatter(w_grad.astype(BF16), "ctx", scatter_dimension=0, tiled=True).astype(F32)

time: 99.4 us -> 93.9 us (0.945)
  waiting for transfers between devices: 27.2 us -> 16.7 us
  starting transfers between devices: 34.3 us -> 38.5 us
  local copies, waits for them, and re-layouts: 5.12 us -> 6.86 us
  Pallas kernels: 29.6 us -> 28.6 us
    ppermute x1, waiting for transfers between devices: 9.98 us -> 0.01 us  [shards(): after = [near, lax.ppermute(pair, 'ctx', [(2, 0), (3, 1)])]]
    ppermute x1, waiting for transfers between devices: 3.52 us -> 0.57 us  [shards(): before = [near, lax.ppermute(pair, 'ctx', [(0, 2), (1, 3)])]]
    ppermute x3, starting transfers between devices: 7.96 us -> 10.5 us  [passed(): lax.ppermute(array, 'head', [(i, (i - 1) % devices) for i in range(device...]
    unnamed x30 -> x34, local copies, waits for them, and re-layouts: 5.12 us -> 6.86 us
    ppermute x6 -> x8, waiting for transfers between devices: 1.51 us -> 3.07 us  [swapped(): return lax.ppermute(array, 'dp', [(0, 1), (1, 0)])]
    ppermute x1, starting transfers between devices: 1.96 us -> 3.51 us  [shards(): before = [near, lax.ppermute(pair, 'ctx', [(0, 2), (1, 3)])]]
    pallas_call x26 -> x24, Pallas kernels: 29.6 us -> 28.6 us  [call(): pl.pallas_call(body, name=getattr(kernel, 'func', kernel).__name__, out_s...]
  transfers between devices with their start and end apart: 27 -> 29, of which waited for: 8 -> 14; matrix products, arithmetic and copies ran while one was open for 1% -> 1% of each run, Pallas kernels for 27% -> 27%
where the time goes in v3:
time: 93.9 us; the launch traced here: 93.2 us
  starting transfers between devices  38.5 us (41%)
  Pallas kernels  28.6 us (30%)
  waiting for transfers between devices  16.7 us (18%)
  local copies, waits for them, and re-layouts  6.86 us (7%)
  other arithmetic  1.37 us (1%)
  between operations  1.23 us (1%)
    pallas_call x24, Pallas kernels, call(): pl.pallas_call(body, name=getattr(kernel, 'func', kernel).__name__, out_s...  28.6 us
    ppermute x16, starting transfers between devices, flipped(): return lax.ppermute(array, 'ctx', [(i, i ^ bit) for i in range(4)])  21.8 us
    ppermute x16, waiting for transfers between devices, flipped(): return lax.ppermute(array, 'ctx', [(i, i ^ bit) for i in range(4)])  13 us
    ppermute x3, starting transfers between devices, passed(): lax.ppermute(array, 'head', [(i, (i - 1) % devices) for i in range(device...  10.5 us
    unnamed x34, local copies, waits for them, and re-layouts  6.86 us
    ppermute x1, starting transfers between devices, shards(): before = [near, lax.ppermute(pair, 'ctx', [(0, 2), (1, 3)])]  3.51 us
    ppermute x8, waiting for transfers between devices, swapped(): return lax.ppermute(array, 'dp', [(0, 1), (1, 0)])  3.07 us
  transfers between devices with their start and end apart: 29, of which 14 were waited for; matrix products, arithmetic and copies ran while one was open for 1% of the time, Pallas kernels for 27%

profile of v3, /device:TPU:0, one launch (start us, length us, event | category | flops | bytes accessed | tf_op | source)
XLA Modules:
  0.0 93.2 jit_solution(12369630781676207099)
XLA Ops:
  0.7 0.5 collective-permute-start.1
  1.2 3.5 %contrib_kernel.1 = (bf16[1040,128]{1,0:T(8,128)(2,1)}, f32[8,256]{1,0:T(8,128)}, f32[256,8]{1,0:T(8,128)}, bf16[128,1536]{1,0:T(8,128)(2,1)}, bf16[128,1536]{1,0:T(8,128)(2,1)}) custom-call(bf16[256,1024]{1,0:T(8,128)(2,1)} %bitcast.20, bf16[256,1024]{1,0:T(8,128)(2,1)} %bitcast.24, f32[8,256]{1,0:T(8,128)} %bitcast.32, bf16[128,3072]{1,0:T(8,128)(2,1)} %bitcast.30), custom_call_target="tpu_custom_call" | custom-call | tf_op jit(solution)/shard_map/contrib_kernel/pallas_call | solution.py:43
  4.7 2.7 %collective-permute-start = (bf16[1040,128]{1,0:T(8,128)(2,1)}, bf16[1040,128]{1,0:T(8,128)(2,1)}, u32[]{:S(2)}, u32[]{:S(2)}) collective-permute-start(bf16[1040,128]{1,0:T(8,128)(2,1)} %get-tuple-element.50.refs_0_), channel_id=1, source_target_pairs={{0,8},{8,0},{16,24},{24,16},{1,9},{9,1},{17,25},{25,17},{2,10},{10... | collective-permute-start | bytes 798728 | tf_op jit(solution)/shard_map/ppermute | solution.py:254
  7.4 1.5 %collective-permute-start.4 = (bf16[128,1536]{1,0:T(8,128)(2,1)}, bf16[128,1536]{1,0:T(8,128)(2,1)S(1)}, u32[]{:S(2)}, u32[]{:S(2)}) collective-permute-start(bf16[128,1536]{1,0:T(8,128)(2,1)} %get-tuple-element.53.refs_0_.refs_2_), channel_id=1, source_target_pairs={{0,16},{8,24},{16,0},{24,8},{1,17},{9,25},{17,1},{25,9},{2,18},{10... | collective-permute-start | bytes 1179656 | tf_op jit(solution)/shard_map/ppermute | solution.py:254
  8.9 1.0 %copy-done.6 = bf16[128,1536]{1,0:T(8,128)(2,1)S(1)} copy-done((bf16[128,1536]{1,0:T(8,128)(2,1)S(1)}, bf16[128,1536]{1,0:T(8,128)(2,1)}, u32[]{:S(2)}) %copy-start.6) | copy-done | bytes 393240
  9.9 0.7 copy-done.13
  10.6 0.8 again_kernel.1.refs_5_
  11.4 0.6 collective-permute-start.3
  12.0 0.5 fusion.10
  12.6 0.9 copy-done.8
  13.5 0.7 copy-done.14
  14.2 1.1 %intra_kernel.1.refs_2_.refs_3_ = f32[256,1024]{1,0:T(8,128)S(1)} custom-call(bf16[256,1024]{1,0:T(8,128)(2,1)S(1)} %bitcast.15, bf16[256,1024]{1,0:T(8,128)(2,1)S(1)} %bitcast.21, bf16[256,1024]{1,0:T(8,128)(2,1)S(1)} %bitcast.25, f32[8,256]{1,0:T(8,128)S(1)} %copy-done.14, f32[256,8]{1,0:T(8,128)S(1)} %copy-done.8, bf16[128,1536]{1,0:T(8,128)(2,1)} %again_kernel.1.refs_5_, ...), custom_call_target="tpu_custom_call" | custom-call | tf_op jit(solution)/shard_map/intra_kernel/pallas_call | solution.py:43
  15.4 1.1 %pair_kernel.1.refs_2_ = bf16[1024,128]{1,0:T(8,128)(2,1)S(1)} custom-call(bf16[1040,128]{1,0:T(8,128)(2,1)S(1)} %copy-done.12, bf16[1040,128]{1,0:T(8,128)(2,1)} %collective-permute-done.refs_1_.refs_0_, f32[256,1024]{1,0:T(8,128)S(1)} %intra_kernel.1.refs_2_.refs_3_), custom_call_target="tpu_custom_call" | custom-call | tf_op jit(solution)/shard_map/pair_kernel/pallas_call | solution.py:43
  16.4 3.5 %collective-permute-start.2 = (bf16[1024,128]{1,0:T(8,128)(2,1)S(1)}, bf16[1024,128]{1,0:T(8,128)(2,1)S(1)}, u32[]{:S(2)}, u32[]{:S(2)}) collective-permute-start(bf16[1024,128]{1,0:T(8,128)(2,1)S(1)} %pair_kernel.1.refs_2_), channel_id=1, source_target_pairs={{0,16},{8,24},{1,17},{9,25},{2,18},{10,26},{3,19},{11,27},{4,20},{... | collective-permute-start | bytes 786440 | tf_op jit(solution)/shard_map/ppermute | solution.py:423
  20.0 0.8 fusion.2
  20.8 2.3 %collective-permute-done.3.refs_0_.refs_3_ = bf16[128,1536]{1,0:T(8,128)(2,1)} collective-permute-done((bf16[128,1536]{1,0:T(8,128)(2,1)}, bf16[128,1536]{1,0:T(8,128)(2,1)}, u32[]{:S(2)}, u32[]{:S(2)}) %collective-permute-start.3) | collective-permute-done | bytes 393248 | tf_op jit(solution)/shard_map/ppermute | solution.py:254
  23.1 1.0 %rows_kernel.2 = (bf16[64,1536]{1,0:T(8,128)(2,1)S(1)}, bf16[64,1536]{1,0:T(8,128)(2,1)S(1)}) custom-call(bf16[128,1536]{1,0:T(8,128)(2,1)} %collective-permute-done.3.refs_0_.refs_3_, bf16[128,1536]{1,0:T(8,128)(2,1)S(1)} %collective-permute-done.4.refs_1_.refs_4_, bf16[1024,128]{1,0:T(8,128)(2,1)S(1)} %pair_kernel.1.refs_2_), custom_call_target="tpu_custom_call" | custom-call | tf_op jit(solution)/shard_map/rows_kernel/pallas_call | solution.py:43
  24.1 0.6 collective-permute-done.2.refs_1_
  24.7 2.1 %attended_kernel.1 = (bf16[256,512]{1,0:T(8,128)(2,1)S(1)}, bf16[256,512]{1,0:T(8,128)(2,1)S(1)}, bf16[8,128,128]{2,1,0:T(8,128)(2,1)S(1)}, bf16[128,1536]{1,0:T(8,128)(2,1)S(1)}) custom-call(bf16[1040,128]{1,0:T(8,128)(2,1)} %collective-permute-done.refs_1_.refs_0_, bf16[1024,128]{1,0:T(8,128)(2,1)S(1)} %collective-permute-done.2.refs_1_, ...), custom_call_target="tpu_custom_call" | custom-call | tf_op jit(solution)/shard_map/attended_kernel/pallas_call | solution.py:43
  26.9 2.5 %collective-permute-start.8 = (bf16[64,1536]{1,0:T(8,128)(2,1)S(1)}, bf16[64,1536]{1,0:T(8,128)(2,1)S(1)}, u32[]{:S(2)}, u32[]{:S(2)}) collective-permute-start(bf16[64,1536]{1,0:T(8,128)(2,1)S(1)} %get-tuple-element.55.refs_8_), channel_id=1, source_target_pairs={{0,16},{8,24},{16,0},{24,8},{1,17},{9,25},{17,1},{25,9},{2,18},{10... | collective-permute-start | bytes 589832 | tf_op jit(solution)/shard_map/ppermute | solution.py:254
  29.5 1.5 %collective-permute-start.9 = (bf16[64,1536]{1,0:T(8,128)(2,1)S(1)}, bf16[64,1536]{1,0:T(8,128)(2,1)S(1)}, u32[]{:S(2)}, u32[]{:S(2)}) collective-permute-start(bf16[64,1536]{1,0:T(8,128)(2,1)S(1)} %get-tuple-element.59), channel_id=1, source_target_pairs={{0,8},{8,0},{16,24},{24,16},{1,9},{9,1},{17,25},{25,17},{2,10},{10... | collective-permute-start | bytes 589832 | tf_op jit(solution)/shard_map/ppermute | solution.py:254
  30.9 0.5 collective-permute-start.6
  31.6 1.8 %weight_kernel.1 = (bf16[128,1536]{1,0:T(8,128)(2,1)S(1)}, bf16[128,1536]{1,0:T(8,128)(2,1)S(1)}, f32[128,1536]{1,0:T(8,128)S(1)}, f32[128,1536]{1,0:T(8,128)S(1...) custom-call(bf16[256,512]{1,0:T(8,128)(2,1)S(1)} %get-tuple-element.56.refs_0_.refs_4_, ...), custom_call_target="tpu_custom_call" | custom-call | tf_op jit(solution)/shard_map/weight_kernel/pallas_call | solution.py:43
  33.4 1.8 %collective-permute-done.8.refs_5_.refs_2_ = bf16[64,1536]{1,0:T(8,128)(2,1)S(1)} collective-permute-done((bf16[64,1536]{1,0:T(8,128)(2,1)S(1)}, bf16[64,1536]{1,0:T(8,128)(2,1)S(1)}, u32[]{:S(2)}, u32[]{:S(2)}) %collective-permute-start.8) | collective-permute-done | bytes 196640 | tf_op jit(solution)/shard_map/ppermute | solution.py:254
  35.2 2.0 %collective-permute-done.9.refs_6_.refs_3_ = bf16[64,1536]{1,0:T(8,128)(2,1)S(1)} collective-permute-done((bf16[64,1536]{1,0:T(8,128)(2,1)S(1)}, bf16[64,1536]{1,0:T(8,128)(2,1)S(1)}, u32[]{:S(2)}, u32[]{:S(2)}) %collective-permute-start.9) | collective-permute-done | bytes 196640 | tf_op jit(solution)/shard_map/ppermute | solution.py:254
  37.2 2.0 %mix_kernel.3 = (f32[256,768]{1,0:T(8,128)S(1)}, f32[256,768]{1,0:T(8,128)S(1)}, bf16[256,512]{1,0:T(8,128)(2,1)S(1)}, bf16[256,512]{1,0:T(8,128)(2,1)S(1)}, bf16[256,512]{1,0:T(8,128)(2,1)S(1)}) custom-call(bf16[256,512]{1,0:T(8,128)(2,1)S(1)} %get-tuple-element.56.refs_0_.refs_4_, bf16[256,512]{1,0:T(8,128)(2,1)S(1)} %collective-permute-done.5.refs_1_, ...), custom_call_target="tpu_custom_call" | custom-call | tf_op jit(solution)/shard_map/mix_kernel/pallas_call | solution.py:43
  39.3 0.5 collective-permute-start.11
  39.9 0.9 %collective-permute-done.10.refs_1_ = bf16[256,512]{1,0:T(8,128)(2,1)S(1)} collective-permute-done((bf16[256,512]{1,0:T(8,128)(2,1)S(1)}, bf16[256,512]{1,0:T(8,128)(2,1)S(1)}, u32[]{:S(2)}, u32[]{:S(2)}) %collective-permute-start.10) | collective-permute-done | bytes 262176 | tf_op jit(solution)/shard_map/ppermute | solution.py:250
  40.8 0.4 collective-permute-done.11.refs_2_
  41.2 0.4 collective-permute-done.12.refs_3_
  41.6 3.7 %collective-permute-start.18 = (bf16[256,768]{1,0:T(8,128)(2,1)S(1)}, bf16[256,768]{1,0:T(8,128)(2,1)S(1)}, u32[]{:S(2)}, u32[]{:S(2)}) collective-permute-start(bf16[256,768]{1,0:T(8,128)(2,1)S(1)} %ring_kernel.4.refs_2_), channel_id=1, source_target_pairs={{0,6},{2,0},{4,2},{6,4},{1,7},{3,1},{5,3},{7,5},{8,14},{10,8},{12,... | collective-permute-start | bytes 1179656 | tf_op jit(solution)/shard_map/ppermute | solution.py:347
  45.5 1.5 %collective-permute-start.14 = (bf16[64,1536]{1,0:T(8,128)(2,1)S(1)}, bf16[64,1536]{1,0:T(8,128)(2,1)S(1)}, u32[]{:S(2)}, u32[]{:S(2)}) collective-permute-start(bf16[64,1536]{1,0:T(8,128)(2,1)S(1)} %get-tuple-element.66), channel_id=1, source_target_pairs={{0,8},{8,0},{16,24},{24,16},{1,9},{9,1},{17,25},{25,17},{2,10},{10... | collective-permute-start | bytes 589832 | tf_op jit(solution)/shard_map/ppermute | solution.py:254
  47.0 0.5 collective-permute-start.15
  47.5 1.9 %collective-permute-start.16 = (bf16[128,1536]{1,0:T(8,128)(2,1)S(1)}, bf16[128,1536]{1,0:T(8,128)(2,1)S(1)}, u32[]{:S(2)}, u32[]{:S(2)}) collective-permute-start(bf16[128,1536]{1,0:T(8,128)(2,1)S(1)} %get-tuple-element.69), channel_id=1, source_target_pairs={{0,16},{8,24},{16,0},{24,8},{1,17},{9,25},{17,1},{25,9},{2,18},{10... | collective-permute-start | bytes 1179656 | tf_op jit(solution)/shard_map/ppermute | solution.py:254
  49.5 2.8 %grad_kernel.2 = (bf16[256,384]{1,0:T(8,128)(2,1)S(1)}, bf16[256,384]{1,0:T(8,128)(2,1)S(1)}) custom-call(bf16[256,3072]{1,0:T(8,128)(2,1)S(1)} %bitcast.13, bf16[256,3072]{1,0:T(8,128)(2,1)S(1)} %collective-permute-done.1.refs_6_.refs_3_.refs_1_, bf16[128,1536]{1,0:T(8,128)(2,1)S(1)} %copy-done.7, bf16[128,1536]{1,0:T(8,128)(2,1)} %collective-permute-done.3.refs_0_.refs_3_, ...), custom_call_target="tpu_custom_call" | custom-call | tf_op jit(solution)/shard_map/grad_kernel/pallas_call | solution.py:43
  52.3 0.9 collective-permute-done.13.refs_4_.refs_5_
  53.3 1.0 %grad_kernel.3 = (bf16[256,512]{1,0:T(8,128)(2,1)S(1)}, bf16[256,512]{1,0:T(8,128)(2,1)S(1)}) custom-call(bf16[256,3072]{1,0:T(8,128)(2,1)S(1)} %bitcast.14, bf16[256,3072]{1,0:T(8,128)(2,1)S(1)} %collective-permute-done.1.refs_6_.refs_3_.refs_1_, bf16[64,1536]{1,0:T(8,128)(2,1)S(1)} %collective-permute-done.8.refs_5_.refs_2_, ...), custom_call_target="tpu_custom_call" | custom-call | tf_op jit(solution)/shard_map/grad_kernel/pallas_call | solution.py:43
  54.4 0.1 ring_kernel.5.refs_7_
  54.5 1.4 %collective-permute-done.17.refs_1_ = bf16[256,512]{1,0:T(8,128)(2,1)S(1)} collective-permute-done((bf16[256,512]{1,0:T(8,128)(2,1)S(1)}, bf16[256,512]{1,0:T(8,128)(2,1)S(1)}, u32[]{:S(2)}, u32[]{:S(2)}) %collective-permute-start.17) | collective-permute-done | bytes 262176 | tf_op jit(solution)/shard_map/ppermute | solution.py:250
  55.9 1.0 %back_contrib_kernel.1 = (bf16[256,1024]{1,0:T(8,128)(2,1)S(1)}, bf16[1040,128]{1,0:T(8,128)(2,1)S(1)}) custom-call(bf16[256,512]{1,0:T(8,128)(2,1)S(1)} %get-tuple-element.72.refs_5_.refs_0_, bf16[256,512]{1,0:T(8,128)(2,1)S(1)} %collective-permute-done.17.refs_1_, bf16[1024,512]{1,0:T(8,128)(2,1)S(1)} %get-tuple-element.96.refs_5_.refs_2_, ...), custom_call_target="tpu_custom_call" | custom-call | tf_op jit(solution)/shard_map/back_contrib_kernel/pallas_call | solution.py:43
  56.9 1.6 %collective-permute-start.21 = (bf16[1040,128]{1,0:T(8,128)(2,1)S(1)}, bf16[1040,128]{1,0:T(8,128)(2,1)S(1)}, u32[]{:S(2)}, u32[]{:S(2)}) collective-permute-start(bf16[1040,128]{1,0:T(8,128)(2,1)S(1)} %get-tuple-element.75.refs_4_.refs_0_), channel_id=1, source_target_pairs={{0,8},{8,0},{16,24},{24,16},{1,9},{9,1},{17,25},{25,17},{2,10},{10... | collective-permute-start | bytes 798728 | tf_op jit(solution)/shard_map/ppermute | solution.py:254
  58.5 3.4 %collective-permute-start.20 = (bf16[256,768]{1,0:T(8,128)(2,1)S(1)}, bf16[256,768]{1,0:T(8,128)(2,1)S(1)}, u32[]{:S(2)}, u32[]{:S(2)}) collective-permute-start(bf16[256,768]{1,0:T(8,128)(2,1)S(1)} %ring_kernel.5.refs_7_), channel_id=1, source_target_pairs={{0,6},{2,0},{4,2},{6,4},{1,7},{3,1},{5,3},{7,5},{8,14},{10,8},{12,... | collective-permute-start | bytes 1179656 | tf_op jit(solution)/shard_map/ppermute | solution.py:347
  61.9 0.1 onward_kernel.1
  62.1 0.6 mix_kernel.4
  62.7 1.8 %collective-permute-start.24 = (bf16[128,1536]{1,0:T(8,128)(2,1)S(1)}, bf16[128,1536]{1,0:T(8,128)(2,1)S(1)}, u32[]{:S(2)}, u32[]{:S(2)}) collective-permute-start(bf16[128,1536]{1,0:T(8,128)(2,1)S(1)} %get-tuple-element.76.refs_7_), channel_id=1, source_target_pairs={{0,16},{8,24},{16,0},{24,8},{1,17},{9,25},{17,1},{25,9},{2,18},{10... | collective-permute-start | bytes 1179656 | tf_op jit(solution)/shard_map/ppermute | solution.py:254
  64.5 0.6 collective-permute-start.25
  65.1 1.1 %collective-permute-done.21.refs_1_.refs_0_ = bf16[1040,128]{1,0:T(8,128)(2,1)S(1)} collective-permute-done((bf16[1040,128]{1,0:T(8,128)(2,1)S(1)}, bf16[1040,128]{1,0:T(8,128)(2,1)S(1)}, u32[]{:S(2)}, u32[]{:S(2)}) %collective-permute-start.21) | collective-permute-done | bytes 266272 | tf_op jit(solution)/shard_map/ppermute | solution.py:254
  66.3 0.2 back_pair_kernel.1
  66.5 1.3 %collective-permute-start.28 = (bf16[1024,128]{1,0:T(8,128)(2,1)S(1)}, bf16[1024,128]{1,0:T(8,128)(2,1)S(1)}, u32[]{:S(2)}, u32[]{:S(2)}) collective-permute-start(bf16[1024,128]{1,0:T(8,128)(2,1)S(1)} %get-tuple-element.83.refs_7_), channel_id=1, source_target_pairs={{16,0},{24,8},{17,1},{25,9},{18,2},{26,10},{19,3},{27,11},{20,4},{... | collective-permute-start | bytes 786440 | tf_op jit(solution)/shard_map/ppermute | solution.py:532
  67.8 4.5 %back_intra_kernel.1 = (bf16[256,1024]{1,0:T(8,128)(2,1)}, f32[256,1024]{1,0:T(8,128)S(1)}, f32[256,1024]{1,0:T(8,128)S(1)}) custom-call(bf16[256,1024]{1,0:T(8,128)(2,1)S(1)} %get-tuple-element.79.refs_0_, bf16[256,1024]{1,0:T(8,128)(2,1)S(1)} %bitcast.18, bf16[256,1024]{1,0:T(8,128)(2,1)S(1)} %bitcast.22, bf16[256,1024]{1,0:T(8,128)(2,1)S(1)} %bitcast.26, ...), custom_call_target="tpu_custom_call" | custom-call | tf_op jit(solution)/shard_map/back_intra_kernel/pallas_call | solution.py:43
  72.3 1.6 %collective-permute-start.26 = (bf16[128,1536]{1,0:T(8,128)(2,1)S(1)}, bf16[128,1536]{1,0:T(8,128)(2,1)S(1)}, u32[]{:S(2)}, u32[]{:S(2)}) collective-permute-start(bf16[128,1536]{1,0:T(8,128)(2,1)S(1)} %get-tuple-element.89), channel_id=1, source_target_pairs={{0,8},{8,0},{16,24},{24,16},{1,9},{9,1},{17,25},{25,17},{2,10},{10... | collective-permute-start | bytes 1179656 | tf_op jit(solution)/shard_map/ppermute | solution.py:254
  73.8 2.7 %collective-permute-start.27 = (bf16[128,1536]{1,0:T(8,128)(2,1)S(1)}, bf16[128,1536]{1,0:T(8,128)(2,1)S(1)}, u32[]{:S(2)}, u32[]{:S(2)}) collective-permute-start(bf16[128,1536]{1,0:T(8,128)(2,1)S(1)} %get-tuple-element.90), channel_id=1, source_target_pairs={{0,16},{8,24},{16,0},{24,8},{1,17},{9,25},{17,1},{25,9},{2,18},{10... | collective-permute-start | bytes 1179656 | tf_op jit(solution)/shard_map/ppermute | solution.py:254
  76.5 1.0 %copy-done.10 = bf16[256,1024]{1,0:T(8,128)(2,1)S(1)} copy-done((bf16[256,1024]{1,0:T(8,128)(2,1)S(1)}, bf16[256,1024]{1,0:T(8,128)(2,1)}, u32[]{:S(2)}) %copy-start.10) | copy-done | bytes 524312
  77.5 0.2 ring_kernel.6.refs_7_
  77.7 0.6 mix_kernel.5
  78.4 3.4 %collective-permute-start.23 = (bf16[256,768]{1,0:T(8,128)(2,1)S(1)}, bf16[256,768]{1,0:T(8,128)(2,1)S(1)}, u32[]{:S(2)}, u32[]{:S(2)}) collective-permute-start(bf16[256,768]{1,0:T(8,128)(2,1)S(1)} %ring_kernel.6.refs_7_), channel_id=1, source_target_pairs={{0,6},{2,0},{4,2},{6,4},{1,7},{3,1},{5,3},{7,5},{8,14},{10,8},{12,... | collective-permute-start | bytes 1179656 | tf_op jit(solution)/shard_map/ppermute | solution.py:347
  81.8 0.1 total_kernel.2.refs_7_.refs_0_
  82.0 1.6 %back_inter_kernel.1 = (bf16[256,1024]{1,0:T(8,128)(2,1)}, bf16[256,1024]{1,0:T(8,128)(2,1)}) custom-call(bf16[1040,128]{1,0:T(8,128)(2,1)S(1)} %collective-permute-done.21.refs_1_.refs_0_, bf16[1024,128]{1,0:T(8,128)(2,1)S(1)} %collective-permute-done.28.refs_1_, bf16[256,1024]{1,0:T(8,128)(2,1)S(1)} %bitcast.23, bf16[256,1024]{1,0:T(8,128)(2,1)S(1)} %bitcast.27, ...), custom_call_target="tpu_custom_call" | custom-call | flops 2140000000 | tf_op jit(solution)/shard_map/back_inter_kernel/pallas_call | solution.py:43
  83.5 0.6 collective-permute-done.26.refs_1_
  84.2 4.1 %collective-permute-done.27.refs_2_ = bf16[128,1536]{1,0:T(8,128)(2,1)S(1)} collective-permute-done((bf16[128,1536]{1,0:T(8,128)(2,1)S(1)}, bf16[128,1536]{1,0:T(8,128)(2,1)S(1)}, u32[]{:S(2)}, u32[]{:S(2)}) %collective-permute-start.27) | collective-permute-done | bytes 393248 | tf_op jit(solution)/shard_map/ppermute | solution.py:254
  88.3 1.0 %copy-done.11 = bf16[256,1024]{1,0:T(8,128)(2,1)S(1)} copy-done((bf16[256,1024]{1,0:T(8,128)(2,1)S(1)}, bf16[256,1024]{1,0:T(8,128)(2,1)}, u32[]{:S(2)}) %copy-start.11) | copy-done | bytes 524312
  89.3 1.3 %total_kernel.3.refs_3_ = f32[128,3072]{1,0:T(8,128)} custom-call(f32[128,3072]{1,0:T(8,128)S(1)} %total_kernel.2.refs_7_.refs_0_, bf16[128,1536]{1,0:T(8,128)(2,1)S(1)} %collective-permute-done.26.refs_1_, bf16[128,1536]{1,0:T(8,128)(2,1)S(1)} %collective-permute-done.27.refs_2_, bf16[256,1024]{1,0:T(8,128)(2,1)S(1)} %copy-done.11), custom_call_target="tpu_custom_call" | custom-call | tf_op jit(solution)/shard_map/total_kernel/pallas_call | solution.py:43
  90.8 1.4 %copy-done.2 = f32[128,3072]{1,0:T(8,128)S(1)} copy-done((f32[128,3072]{1,0:T(8,128)S(1)}, f32[128,3072]{1,0:T(8,128)}, u32[]{:S(2)}) %copy-start.2) | copy-done | bytes 1572888
  92.2 0.9 ring_kernel.7
  (58 shorter events, 1.0 us)
Async XLA Ops:
  0.6 12.0 %copy-start.4 = (bf16[1,256,1024]{2,1,0:T(8,128)(2,1)S(1)}, bf16[1,256,1024]{2,1,0:T(8,128)(2,1)}, u32[]{:S(2)}) copy-start(bf16[1,256,1024]{2,1,0:T(8,128)(2,1)} %param.7) | copy-start | bytes 1572868
  0.6 12.0 %copy-start.5 = (bf16[1,256,1024]{2,1,0:T(8,128)(2,1)S(1)}, bf16[1,256,1024]{2,1,0:T(8,128)(2,1)}, u32[]{:S(2)}) copy-start(bf16[1,256,1024]{2,1,0:T(8,128)(2,1)} %param.8) | copy-start | bytes 1572868
  0.7 12.0 %copy-start.1 = (bf16[1,256,1024]{2,1,0:T(8,128)(2,1)S(1)}, bf16[1,256,1024]{2,1,0:T(8,128)(2,1)}, u32[]{:S(2)}) copy-start(bf16[1,256,1024]{2,1,0:T(8,128)(2,1)} %param.6) | copy-start | bytes 1572868
  0.7 11.9 %collective-permute-start.1 = (bf16[256,3072]{1,0:T(8,128)(2,1)}, bf16[256,3072]{1,0:T(8,128)(2,1)S(1)}, u32[]{:S(2)}, u32[]{:S(2)}) collective-permute-start(bf16[256,3072]{1,0:T(8,128)(2,1)} %bitcast.11), channel_id=1, source_target_pairs={{0,1},{1,0},{2,3},{3,2},{4,5},{5,4},{6,7},{7,6},{8,9},{9,8},{10,11... | collective-permute-start | bytes 4718600 | tf_op jit(solution)/shard_map/ppermute | solution.py:250
  4.7 10.6 %collective-permute-start = (bf16[1040,128]{1,0:T(8,128)(2,1)}, bf16[1040,128]{1,0:T(8,128)(2,1)}, u32[]{:S(2)}, u32[]{:S(2)}) collective-permute-start(bf16[1040,128]{1,0:T(8,128)(2,1)} %get-tuple-element.50.refs_0_), channel_id=1, source_target_pairs={{0,8},{8,0},{16,24},{24,16},{1,9},{9,1},{17,25},{25,17},{2,10},{10... | collective-permute-start | bytes 798728 | tf_op jit(solution)/shard_map/ppermute | solution.py:254
  7.4 15.7 %collective-permute-start.4 = (bf16[128,1536]{1,0:T(8,128)(2,1)}, bf16[128,1536]{1,0:T(8,128)(2,1)S(1)}, u32[]{:S(2)}, u32[]{:S(2)}) collective-permute-start(bf16[128,1536]{1,0:T(8,128)(2,1)} %get-tuple-element.53.refs_0_.refs_2_), channel_id=1, source_target_pairs={{0,16},{8,24},{16,0},{24,8},{1,17},{9,25},{17,1},{25,9},{2,18},{10... | collective-permute-start | bytes 1179656 | tf_op jit(solution)/shard_map/ppermute | solution.py:254
  8.9 1.0 %copy-start.6 = (bf16[128,1536]{1,0:T(8,128)(2,1)S(1)}, bf16[128,1536]{1,0:T(8,128)(2,1)}, u32[]{:S(2)}) copy-start(bf16[128,1536]{1,0:T(8,128)(2,1)} %get-tuple-element.53.refs_0_.refs_2_) | copy-start | bytes 1179652
  9.9 0.7 copy-start.13
  11.4 11.6 %collective-permute-start.3 = (bf16[128,1536]{1,0:T(8,128)(2,1)}, bf16[128,1536]{1,0:T(8,128)(2,1)}, u32[]{:S(2)}, u32[]{:S(2)}) collective-permute-start(bf16[128,1536]{1,0:T(8,128)(2,1)} %again_kernel.1.refs_5_), channel_id=1, source_target_pairs={{0,8},{8,0},{16,24},{24,16},{1,9},{9,1},{17,25},{25,17},{2,10},{10... | collective-permute-start | bytes 1179656 | tf_op jit(solution)/shard_map/ppermute | solution.py:254
  12.6 0.9 copy-start.8
  13.5 0.7 copy-start.14
  14.2 1.1 %copy-start.12 = (bf16[1040,128]{1,0:T(8,128)(2,1)S(1)}, bf16[1040,128]{1,0:T(8,128)(2,1)}, u32[]{:S(2)}) copy-start(bf16[1040,128]{1,0:T(8,128)(2,1)} %get-tuple-element.50.refs_0_) | copy-start | bytes 798724
  15.3 4.6 %copy-start.16 = (pred[512]{0:T(512)(128)(4,1)S(1)}, pred[512]{0:T(512)(128)(4,1)}, u32[]{:S(2)}) copy-start(pred[512]{0:T(512)(128)(4,1)} %fusion.10) | copy-start | bytes 1540
  16.4 8.2 %collective-permute-start.2 = (bf16[1024,128]{1,0:T(8,128)(2,1)S(1)}, bf16[1024,128]{1,0:T(8,128)(2,1)S(1)}, u32[]{:S(2)}, u32[]{:S(2)}) collective-permute-start(bf16[1024,128]{1,0:T(8,128)(2,1)S(1)} %pair_kernel.1.refs_2_), channel_id=1, source_target_pairs={{0,16},{8,24},{1,17},{9,25},{2,18},{10,26},{3,19},{11,27},{4,20},{... | collective-permute-start | bytes 786440 | tf_op jit(solution)/shard_map/ppermute | solution.py:423
  20.0 4.7 %copy-start.3 = (bf16[128,1536]{1,0:T(8,128)(2,1)S(1)}, bf16[128,1536]{1,0:T(8,128)(2,1)}, u32[]{:S(2)}) copy-start(bf16[128,1536]{1,0:T(8,128)(2,1)} %get-tuple-element.54.refs_7_.refs_5_.refs_2_) | copy-start | bytes 1179652
  20.0 4.7 %copy-start.9 = (f32[256,8]{1,0:T(8,128)S(1)}, f32[256,8]{1,0:T(8,128)}, u32[]{:S(2)}) copy-start(f32[256,8]{1,0:T(8,128)} %get-tuple-element.52.refs_4_.refs_6_.refs_5_) | copy-start | bytes 24580
  24.7 6.9 %copy-start = (bf16[1,256,3072]{2,1,0:T(8,128)(2,1)S(1)}, bf16[1,256,3072]{2,1,0:T(8,128)(2,1)}, u32[]{:S(2)}) copy-start(bf16[1,256,3072]{2,1,0:T(8,128)(2,1)} %param.11) | copy-start | bytes 4718596
  26.8 4.7 %collective-permute-start.5 = (bf16[256,512]{1,0:T(8,128)(2,1)S(1)}, bf16[256,512]{1,0:T(8,128)(2,1)S(1)}, u32[]{:S(2)}, u32[]{:S(2)}) collective-permute-start(bf16[256,512]{1,0:T(8,128)(2,1)S(1)} %get-tuple-element.57), channel_id=1, source_target_pairs={{0,1},{1,0},{2,3},{3,2},{4,5},{5,4},{6,7},{7,6},{8,9},{9,8},{10,11... | collective-permute-start | bytes 786440 | tf_op jit(solution)/shard_map/ppermute | solution.py:250
  26.9 8.3 %collective-permute-start.8 = (bf16[64,1536]{1,0:T(8,128)(2,1)S(1)}, bf16[64,1536]{1,0:T(8,128)(2,1)S(1)}, u32[]{:S(2)}, u32[]{:S(2)}) collective-permute-start(bf16[64,1536]{1,0:T(8,128)(2,1)S(1)} %get-tuple-element.55.refs_8_), channel_id=1, source_target_pairs={{0,16},{8,24},{16,0},{24,8},{1,17},{9,25},{17,1},{25,9},{2,18},{10... | collective-permute-start | bytes 589832 | tf_op jit(solution)/shard_map/ppermute | solution.py:254
  29.5 7.7 %collective-permute-start.9 = (bf16[64,1536]{1,0:T(8,128)(2,1)S(1)}, bf16[64,1536]{1,0:T(8,128)(2,1)S(1)}, u32[]{:S(2)}, u32[]{:S(2)}) collective-permute-start(bf16[64,1536]{1,0:T(8,128)(2,1)S(1)} %get-tuple-element.59), channel_id=1, source_target_pairs={{0,8},{8,0},{16,24},{24,16},{1,9},{9,1},{17,25},{25,17},{2,10},{10... | collective-permute-start | bytes 589832 | tf_op jit(solution)/shard_map/ppermute | solution.py:254
  30.9 14.4 %collective-permute-start.6 = (bf16[128,1536]{1,0:T(8,128)(2,1)S(1)}, bf16[128,1536]{1,0:T(8,128)(2,1)S(1)}, u32[]{:S(2)}, u32[]{:S(2)}) collective-permute-start(bf16[128,1536]{1,0:T(8,128)(2,1)S(1)} %get-tuple-element.58), channel_id=1, source_target_pairs={{0,8},{8,0},{16,24},{24,16},{1,9},{9,1},{17,25},{25,17},{2,10},{10... | collective-permute-start | bytes 1179656 | tf_op jit(solution)/shard_map/ppermute | solution.py:254
  31.5 13.8 %collective-permute-start.7 = (bf16[128,1536]{1,0:T(8,128)(2,1)S(1)}, bf16[128,1536]{1,0:T(8,128)(2,1)S(1)}, u32[]{:S(2)}, u32[]{:S(2)}) collective-permute-start(bf16[128,1536]{1,0:T(8,128)(2,1)S(1)} %get-tuple-element.58), channel_id=1, source_target_pairs={{0,16},{8,24},{16,0},{24,8},{1,17},{9,25},{17,1},{25,9},{2,18},{10... | collective-permute-start | bytes 1179656 | tf_op jit(solution)/shard_map/ppermute | solution.py:254
  31.6 5.6 %copy-start.7 = (bf16[128,1536]{1,0:T(8,128)(2,1)S(1)}, bf16[128,1536]{1,0:T(8,128)(2,1)}, u32[]{:S(2)}) copy-start(bf16[128,1536]{1,0:T(8,128)(2,1)} %get-tuple-element.53.refs_0_.refs_2_) | copy-start | bytes 1179652
  39.2 1.6 %collective-permute-start.10 = (bf16[256,512]{1,0:T(8,128)(2,1)S(1)}, bf16[256,512]{1,0:T(8,128)(2,1)S(1)}, u32[]{:S(2)}, u32[]{:S(2)}) collective-permute-start(bf16[256,512]{1,0:T(8,128)(2,1)S(1)} %get-tuple-element.62.refs_4_), channel_id=1, source_target_pairs={{0,1},{1,0},{2,3},{3,2},{4,5},{5,4},{6,7},{7,6},{8,9},{9,8},{10,11... | collective-permute-start | bytes 786440 | tf_op jit(solution)/shard_map/ppermute | solution.py:250
  39.3 1.9 %collective-permute-start.11 = (bf16[256,512]{1,0:T(8,128)(2,1)S(1)}, bf16[256,512]{1,0:T(8,128)(2,1)S(1)}, u32[]{:S(2)}, u32[]{:S(2)}) collective-permute-start(bf16[256,512]{1,0:T(8,128)(2,1)S(1)} %get-tuple-element.63), channel_id=1, source_target_pairs={{0,1},{1,0},{2,3},{3,2},{4,5},{5,4},{6,7},{7,6},{8,9},{9,8},{10,11... | collective-permute-start | bytes 786440 | tf_op jit(solution)/shard_map/ppermute | solution.py:250
  39.8 1.8 %collective-permute-start.12 = (bf16[256,512]{1,0:T(8,128)(2,1)S(1)}, bf16[256,512]{1,0:T(8,128)(2,1)S(1)}, u32[]{:S(2)}, u32[]{:S(2)}) collective-permute-start(bf16[256,512]{1,0:T(8,128)(2,1)S(1)} %get-tuple-element.64), channel_id=1, source_target_pairs={{0,1},{1,0},{2,3},{3,2},{4,5},{5,4},{6,7},{7,6},{8,9},{9,8},{10,11... | collective-permute-start | bytes 786440 | tf_op jit(solution)/shard_map/ppermute | solution.py:250
  41.6 12.7 %collective-permute-start.18 = (bf16[256,768]{1,0:T(8,128)(2,1)S(1)}, bf16[256,768]{1,0:T(8,128)(2,1)S(1)}, u32[]{:S(2)}, u32[]{:S(2)}) collective-permute-start(bf16[256,768]{1,0:T(8,128)(2,1)S(1)} %ring_kernel.4.refs_2_), channel_id=1, source_target_pairs={{0,6},{2,0},{4,2},{6,4},{1,7},{3,1},{5,3},{7,5},{8,14},{10,8},{12,... | collective-permute-start | bytes 1179656 | tf_op jit(solution)/shard_map/ppermute | solution.py:347
  45.3 7.9 %collective-permute-start.13 = (bf16[64,1536]{1,0:T(8,128)(2,1)S(1)}, bf16[64,1536]{1,0:T(8,128)(2,1)S(1)}, u32[]{:S(2)}, u32[]{:S(2)}) collective-permute-start(bf16[64,1536]{1,0:T(8,128)(2,1)S(1)} %get-tuple-element.65.refs_8_), channel_id=1, source_target_pairs={{0,16},{8,24},{16,0},{24,8},{1,17},{9,25},{17,1},{25,9},{2,18},{10... | collective-permute-start | bytes 589832 | tf_op jit(solution)/shard_map/ppermute | solution.py:254
  45.5 7.8 %collective-permute-start.14 = (bf16[64,1536]{1,0:T(8,128)(2,1)S(1)}, bf16[64,1536]{1,0:T(8,128)(2,1)S(1)}, u32[]{:S(2)}, u32[]{:S(2)}) collective-permute-start(bf16[64,1536]{1,0:T(8,128)(2,1)S(1)} %get-tuple-element.66), channel_id=1, source_target_pairs={{0,8},{8,0},{16,24},{24,16},{1,9},{9,1},{17,25},{25,17},{2,10},{10... | collective-permute-start | bytes 589832 | tf_op jit(solution)/shard_map/ppermute | solution.py:254
  47.0 14.9 %collective-permute-start.15 = (bf16[128,1536]{1,0:T(8,128)(2,1)S(1)}, bf16[128,1536]{1,0:T(8,128)(2,1)S(1)}, u32[]{:S(2)}, u32[]{:S(2)}) collective-permute-start(bf16[128,1536]{1,0:T(8,128)(2,1)S(1)} %get-tuple-element.60.refs_7_), channel_id=1, source_target_pairs={{0,8},{8,0},{16,24},{24,16},{1,9},{9,1},{17,25},{25,17},{2,10},{10... | collective-permute-start | bytes 1179656 | tf_op jit(solution)/shard_map/ppermute | solution.py:254
  47.5 14.4 %collective-permute-start.16 = (bf16[128,1536]{1,0:T(8,128)(2,1)S(1)}, bf16[128,1536]{1,0:T(8,128)(2,1)S(1)}, u32[]{:S(2)}, u32[]{:S(2)}) collective-permute-start(bf16[128,1536]{1,0:T(8,128)(2,1)S(1)} %get-tuple-element.69), channel_id=1, source_target_pairs={{0,16},{8,24},{16,0},{24,8},{1,17},{9,25},{17,1},{25,9},{2,18},{10... | collective-permute-start | bytes 1179656 | tf_op jit(solution)/shard_map/ppermute | solution.py:254
  54.3 1.6 %collective-permute-start.17 = (bf16[256,512]{1,0:T(8,128)(2,1)S(1)}, bf16[256,512]{1,0:T(8,128)(2,1)S(1)}, u32[]{:S(2)}, u32[]{:S(2)}) collective-permute-start(bf16[256,512]{1,0:T(8,128)(2,1)S(1)} %get-tuple-element.73), channel_id=1, source_target_pairs={{0,1},{1,0},{2,3},{3,2},{4,5},{5,4},{6,7},{7,6},{8,9},{9,8},{10,11... | collective-permute-start | bytes 786440 | tf_op jit(solution)/shard_map/ppermute | solution.py:250
  54.4 1.5 %copy-start.15 = (f32[8,256]{1,0:T(8,128)S(1)}, f32[8,256]{1,0:T(8,128)}, u32[]{:S(2)}) copy-start(f32[8,256]{1,0:T(8,128)} %get-tuple-element.51.refs_1_.refs_3_.refs_5_.refs_4_) | copy-start | bytes 24580
  56.9 9.4 %collective-permute-start.21 = (bf16[1040,128]{1,0:T(8,128)(2,1)S(1)}, bf16[1040,128]{1,0:T(8,128)(2,1)S(1)}, u32[]{:S(2)}, u32[]{:S(2)}) collective-permute-start(bf16[1040,128]{1,0:T(8,128)(2,1)S(1)} %get-tuple-element.75.refs_4_.refs_0_), channel_id=1, source_target_pairs={{0,8},{8,0},{16,24},{24,16},{1,9},{9,1},{17,25},{25,17},{2,10},{10... | collective-permute-start | bytes 798728 | tf_op jit(solution)/shard_map/ppermute | solution.py:254
  58.5 13.8 %collective-permute-start.20 = (bf16[256,768]{1,0:T(8,128)(2,1)S(1)}, bf16[256,768]{1,0:T(8,128)(2,1)S(1)}, u32[]{:S(2)}, u32[]{:S(2)}) collective-permute-start(bf16[256,768]{1,0:T(8,128)(2,1)S(1)} %ring_kernel.5.refs_7_), channel_id=1, source_target_pairs={{0,6},{2,0},{4,2},{6,4},{1,7},{3,1},{5,3},{7,5},{8,14},{10,8},{12,... | collective-permute-start | bytes 1179656 | tf_op jit(solution)/shard_map/ppermute | solution.py:347
  62.6 11.2 %collective-permute-start.19 = (bf16[256,768]{1,0:T(8,128)(2,1)S(1)}, bf16[256,768]{1,0:T(8,128)(2,1)S(1)}, u32[]{:S(2)}, u32[]{:S(2)}) collective-permute-start(bf16[256,768]{1,0:T(8,128)(2,1)S(1)} %get-tuple-element.78), channel_id=1, source_target_pairs={{0,1},{1,0},{2,3},{3,2},{4,5},{5,4},{6,7},{7,6},{8,9},{9,8},{10,11... | collective-permute-start | bytes 1179656 | tf_op jit(solution)/shard_map/ppermute | solution.py:250
  62.7 15.6 %collective-permute-start.24 = (bf16[128,1536]{1,0:T(8,128)(2,1)S(1)}, bf16[128,1536]{1,0:T(8,128)(2,1)S(1)}, u32[]{:S(2)}, u32[]{:S(2)}) collective-permute-start(bf16[128,1536]{1,0:T(8,128)(2,1)S(1)} %get-tuple-element.76.refs_7_), channel_id=1, source_target_pairs={{0,16},{8,24},{16,0},{24,8},{1,17},{9,25},{17,1},{25,9},{2,18},{10... | collective-permute-start | bytes 1179656 | tf_op jit(solution)/shard_map/ppermute | solution.py:254
  64.5 13.8 %collective-permute-start.25 = (bf16[128,1536]{1,0:T(8,128)(2,1)S(1)}, bf16[128,1536]{1,0:T(8,128)(2,1)S(1)}, u32[]{:S(2)}, u32[]{:S(2)}) collective-permute-start(bf16[128,1536]{1,0:T(8,128)(2,1)S(1)} %get-tuple-element.88), channel_id=1, source_target_pairs={{0,8},{8,0},{16,24},{24,16},{1,9},{9,1},{17,25},{25,17},{2,10},{10... | collective-permute-start | bytes 1179656 | tf_op jit(solution)/shard_map/ppermute | solution.py:254
  66.5 15.5 %collective-permute-start.28 = (bf16[1024,128]{1,0:T(8,128)(2,1)S(1)}, bf16[1024,128]{1,0:T(8,128)(2,1)S(1)}, u32[]{:S(2)}, u32[]{:S(2)}) collective-permute-start(bf16[1024,128]{1,0:T(8,128)(2,1)S(1)} %get-tuple-element.83.refs_7_), channel_id=1, source_target_pairs={{16,0},{24,8},{17,1},{25,9},{18,2},{26,10},{19,3},{27,11},{20,4},{... | collective-permute-start | bytes 786440 | tf_op jit(solution)/shard_map/ppermute | solution.py:532
  72.3 11.9 %collective-permute-start.26 = (bf16[128,1536]{1,0:T(8,128)(2,1)S(1)}, bf16[128,1536]{1,0:T(8,128)(2,1)S(1)}, u32[]{:S(2)}, u32[]{:S(2)}) collective-permute-start(bf16[128,1536]{1,0:T(8,128)(2,1)S(1)} %get-tuple-element.89), channel_id=1, source_target_pairs={{0,8},{8,0},{16,24},{24,16},{1,9},{9,1},{17,25},{25,17},{2,10},{10... | collective-permute-start | bytes 1179656 | tf_op jit(solution)/shard_map/ppermute | solution.py:254
  73.8 14.5 %collective-permute-start.27 = (bf16[128,1536]{1,0:T(8,128)(2,1)S(1)}, bf16[128,1536]{1,0:T(8,128)(2,1)S(1)}, u32[]{:S(2)}, u32[]{:S(2)}) collective-permute-start(bf16[128,1536]{1,0:T(8,128)(2,1)S(1)} %get-tuple-element.90), channel_id=1, source_target_pairs={{0,16},{8,24},{16,0},{24,8},{1,17},{9,25},{17,1},{25,9},{2,18},{10... | collective-permute-start | bytes 1179656 | tf_op jit(solution)/shard_map/ppermute | solution.py:254
  76.5 1.0 %copy-start.10 = (bf16[256,1024]{1,0:T(8,128)(2,1)S(1)}, bf16[256,1024]{1,0:T(8,128)(2,1)}, u32[]{:S(2)}) copy-start(bf16[256,1024]{1,0:T(8,128)(2,1)} %get-tuple-element.84.refs_3_) | copy-start | bytes 1572868
  78.3 12.4 %collective-permute-start.22 = (bf16[256,768]{1,0:T(8,128)(2,1)S(1)}, bf16[256,768]{1,0:T(8,128)(2,1)S(1)}, u32[]{:S(2)}, u32[]{:S(2)}) collective-permute-start(bf16[256,768]{1,0:T(8,128)(2,1)S(1)} %get-tuple-element.86), channel_id=1, source_target_pairs={{0,1},{1,0},{2,3},{3,2},{4,5},{5,4},{6,7},{7,6},{8,9},{9,8},{10,11... | collective-permute-start | bytes 1179656 | tf_op jit(solution)/shard_map/ppermute | solution.py:250
  78.4 12.4 %collective-permute-start.23 = (bf16[256,768]{1,0:T(8,128)(2,1)S(1)}, bf16[256,768]{1,0:T(8,128)(2,1)S(1)}, u32[]{:S(2)}, u32[]{:S(2)}) collective-permute-start(bf16[256,768]{1,0:T(8,128)(2,1)S(1)} %ring_kernel.6.refs_7_), channel_id=1, source_target_pairs={{0,6},{2,0},{4,2},{6,4},{1,7},{3,1},{5,3},{7,5},{8,14},{10,8},{12,... | collective-permute-start | bytes 1179656 | tf_op jit(solution)/shard_map/ppermute | solution.py:347
  88.3 1.0 %copy-start.11 = (bf16[256,1024]{1,0:T(8,128)(2,1)S(1)}, bf16[256,1024]{1,0:T(8,128)(2,1)}, u32[]{:S(2)}) copy-start(bf16[256,1024]{1,0:T(8,128)(2,1)} %get-tuple-element.93.refs_3_) | copy-start | bytes 1572868
  90.8 1.4 %copy-start.2 = (f32[128,3072]{1,0:T(8,128)S(1)}, f32[128,3072]{1,0:T(8,128)}, u32[]{:S(2)}) copy-start(f32[128,3072]{1,0:T(8,128)} %total_kernel.3.refs_3_) | copy-start | bytes 4718596

commit v4 on v3

--- a/solution.py
+++ b/solution.py
@@ -12,7 +12,7 @@
 F32 = jnp.float32
 BF16 = jnp.bfloat16
 EXTRA = 16
-C17, C20, C24 = 1284000000, 1070000000, 2140000000
+C_JOIN, C26, C17, C20, C24 = 1070000000, 642000000, 1284000000, 1070000000, 2140000000
 
 
 def contract(a, b, dim_a, dim_b):
@@ -23,29 +23,31 @@
     return ref[:, h * DH : (h + 1) * DH]
 
 
-def call(kernel, out_shape, *args, staged=(), free_in=(), free_out=(), scratch=(), after=(), room=24, work=0):
-    n, waits, count = len(args), len(after), len(staged)
+def call(kernel, out_shape, *args, staged=(), free_in=(), scratch=(), after=(), room=24, work=0):
+    outs = list(out_shape) if isinstance(out_shape, (list, tuple)) else [out_shape]
+    n, waits, count, made = len(args), len(after), len(staged), len(outs)
 
     def body(*refs):
         ins, rest = list(refs[:n]), refs[n + waits :]
+        results, rest = rest[: made + 1], rest[made + 1 :]
         rest, buffers, sem = rest[: len(rest) - count - 1], rest[len(rest) - count - 1 : -1], rest[-1]
         copies = [pltpu.make_async_copy(ins[i], buffers[j], sem.at[j]) for j, i in enumerate(staged)]
         for copy in copies:
             copy.start()
+        results[-1][...] = jnp.zeros_like(results[-1])
         for copy in copies:
             copy.wait()
         for j, i in enumerate(staged):
             ins[i] = buffers[j]
-        kernel(*ins, *rest)
+        kernel(*ins, *results[:-1], *rest)
 
     anywhere, local, far = (pl.BlockSpec(memory_space=m) for m in (pl.ANY, pltpu.VMEM, pltpu.HBM))
-    specs = [far if i in free_out else local for i in range(len(jax.tree.leaves(out_shape)))]
-    return pl.pallas_call(
+    results = pl.pallas_call(
         body,
         name=getattr(kernel, "func", kernel).__name__,
-        out_shape=out_shape,
+        out_shape=[*outs, struct((8, 128), F32)],
         in_specs=[far if i in staged or i in free_in else local for i in range(n)] + [anywhere] * waits,
-        out_specs=specs if isinstance(out_shape, (list, tuple)) else specs[0],
+        out_specs=[local] * (made + 1),
         scratch_shapes=[
             *scratch,
             *[pltpu.VMEM(args[i].shape, args[i].dtype) for i in staged],
@@ -54,6 +56,7 @@
         compiler_params=pltpu.CompilerParams(vmem_limit_bytes=room * 1024 * 1024),
         cost_estimate=pl.CostEstimate(flops=work, bytes_accessed=0, transcendentals=0),
     )(*args, *after)
+    return (results[:-1] if isinstance(out_shape, (list, tuple)) else results[0]), results[-1]
 
 
 def struct(shape, dtype):
@@ -128,27 +131,44 @@
     return copies
 
 
-def contrib_kernel(groups, k_ref, v_ref, ld_ref, w_ref, state_ref, row_ref, col_ref, first_ref, rest_ref, sem):
+def columns_kernel(w_ref, first_ref, rest_ref, sem):
     count = first_ref.shape[1] * lax.axis_size("head") // w_ref.shape[1]
-    copies = ring_columns(w_ref, first_ref, 1, sem) + ring_columns(w_ref, rest_ref, 1 + count, sem.at[pl.ds(count, sem.shape[0] - count)])
+    copies = ring_columns(w_ref, first_ref, 1, sem)
+    copies += ring_columns(w_ref, rest_ref, 1 + count, sem.at[pl.ds(count, sem.shape[0] - count)])
+    for copy in copies:
+        copy.wait()
+
+
+def sums(ld_ref, mask, rows):
+    lower = mask.astype(F32)
+    a, b = (lower, ld_ref[...]) if rows else (ld_ref[...], lower)
+    return lax.dot_general(
+        a, b, (((1,), (1,)), ((), ())), precision=lax.Precision.HIGHEST, preferred_element_type=F32
+    )
+
+
+def contrib_kernel(groups, k_ref, v_ref, ld_ref, state_ref):
     size = k_ref.shape[0]
-    lower = lower_mask(size).astype(F32)
-    ld = ld_ref[...]
-    row = lax.dot_general(
-        ld, lower, (((1,), (1,)), ((), ())), precision=lax.Precision.HIGHEST, preferred_element_type=F32
-    )
-    col = lax.dot_general(
-        lower, ld, (((1,), (1,)), ((), ())), precision=lax.Precision.HIGHEST, preferred_element_type=F32
-    )
-    row_ref[...] = row
-    col_ref[...] = col
+    mask = lower_mask(size)
+    col = sums(ld_ref, mask, True)
     tail = jnp.exp(col[size - 1 :, :] - col)
     for h in range(groups):
         weighted = (head(k_ref, h).astype(F32) * tail[:, h : h + 1]).astype(BF16)
         state_ref[h * DH : (h + 1) * DH, :] = contract(weighted, head(v_ref, h), 0, 0).astype(BF16)
-    store_decay(state_ref, row, groups)
-    for copy in copies:
-        copy.wait()
+    store_decay(state_ref, sums(ld_ref, mask, False), groups)
+
+
+def intra_kernel(groups, q_ref, k_ref, v_ref, ld_ref, row_ref, col_ref, intra_ref):
+    mask = lower_mask(q_ref.shape[0])
+    row_ref[...] = sums(ld_ref, mask, False)
+    col_ref[...] = sums(ld_ref, mask, True)
+    for h in range(groups):
+        probs = probs_of(q_ref, k_ref, spread_weights(row_ref, col_ref, mask, h), h)
+        intra_ref[:, h * DH : (h + 1) * DH] = contract(probs, head(v_ref, h), 1, 0)
+
+
+def probs_of(q_ref, k_ref, weights, h):
+    return (contract(head(q_ref, h), head(k_ref, h), 1, 1) * SCALE * weights).astype(BF16)
 
 
 def spread_weights(row_ref, col_ref, lower, h):
@@ -156,23 +176,12 @@
     return jnp.exp(jnp.where(lower, spread, -jnp.inf))
 
 
-def again_kernel(ref, again_ref):
-    again_ref[...] = ref[...]
-
-
-def intra_kernel(groups, q_ref, k_ref, v_ref, row_ref, col_ref, intra_ref):
-    lower = lower_mask(q_ref.shape[0])
-    for h in range(groups):
-        weights = spread_weights(row_ref, col_ref, lower, h)
-        probs = (contract(head(q_ref, h), head(k_ref, h), 1, 1) * SCALE * weights).astype(BF16)
-        intra_ref[:, h * DH : (h + 1) * DH] = contract(probs, head(v_ref, h), 1, 0)
-
-
 def attended_kernel(groups, count, *refs):
     states = refs[:count]
-    q_ref, intra_ref, col_ref, pick_own_ref, pick_other_ref, rest_ref = refs[count : count + 6]
-    own_ref, other_ref, low_ref, again_ref, attended_ref = refs[count + 6 :]
-    again_ref[...] = rest_ref[...]
+    q_ref, intra_ref, col_ref, pick_own_ref, pick_other_ref, g_ref = refs[count : count + 6]
+    own_ref, other_ref, low_ref, held_ref, attended_ref, sem = refs[count + 6 :]
+    copy = pltpu.make_async_copy(g_ref, held_ref, sem.at[0])
+    copy.start()
     state = entering(states, groups, True)
     factor = jnp.exp(col_ref[...]) * SCALE
     for h in range(groups):
@@ -184,6 +193,7 @@
         ).astype(BF16)
     own_ref[...] = contract(attended_ref[...], pick_own_ref[...], 1, 0).astype(BF16)
     other_ref[...] = contract(attended_ref[...], pick_other_ref[...], 1, 0).astype(BF16)
+    copy.wait()
 
 
 def back_contrib_kernel(
@@ -213,7 +223,7 @@
             contract(dprobs, head(k_ref, h), 1, 0) + contract(grad, low_ref[h], 1, 1) * factor[:, h : h + 1]
         ).astype(BF16)
         kpart_ref[:, here] = contract(dprobs, head(q_ref, h), 0, 0)
-        probs = (contract(head(q_ref, h), head(k_ref, h), 1, 1) * SCALE * weights).astype(BF16)
+        probs = probs_of(q_ref, k_ref, weights, h)
         vpart_ref[:, here] = contract(probs, grad, 0, 0)
 
 
@@ -254,10 +264,19 @@
     return lax.ppermute(array, "ctx", [(i, i ^ bit) for i in range(4)])
 
 
+def pass_kernel(one, two, whole, on_one, on_two, again):
+    again[...] = whole[...]
+    rows_kernel(one, two, on_one, on_two)
+
+
 def rows_kernel(one, two, on_one, on_two):
     half = on_one.shape[0]
     on_one[...] = one[:half]
     on_two[...] = two[half:]
+
+
+def join_kernel(*refs):
+    lay_out(refs[:-1], refs[-1])
 
 
 def lay_out(pieces, out_ref, columns=slice(None)):
@@ -267,9 +286,14 @@
         top += piece.shape[0]
 
 
+def along(place):
+    return place ^ (place >> 1) if lax.axis_size("head") == 4 else place
+
+
 def columns_after(hops, width):
     devices = lax.axis_size("head")
-    return pl.ds(pl.multiple_of(lax.rem(lax.axis_index("head") + hops, devices) * width, width), width)
+    device = along(lax.rem(along(lax.axis_index("head")) + hops, devices))
+    return pl.ds(pl.multiple_of(device * width, width), width)
 
 
 def mix_kernel(count, place, splits, a_own, a_other, *refs):
@@ -285,23 +309,23 @@
         other[...] = away[:, i * other.shape[1] : (i + 1) * other.shape[1]]
 
 
-def grad_kernel(count, earlier, g_own, g_other, *refs):
-    first, rest, (own, other, w_ref) = refs[:count], refs[count : 2 * count], refs[2 * count + earlier :]
+def grad_kernel(top, count, earlier, g_own, g_other, first_ref, *refs):
+    pieces, before, (own, other, w_ref) = refs[:count], refs[count : count + earlier], refs[count + earlier :]
     heads = lax.axis_size("head")
-    left, width = first[0].shape[1], w_ref.shape[1] // heads
-    lay_out(first, w_ref.at[:, 0:left])
-    lay_out(rest, w_ref.at[:, left:])
-    before = refs[2 * count : 2 * count + earlier] or (None, None)
-    for g_ref, old, out in ((g_own, before[0], own), (g_other, before[1], other)):
+    rows, left, width = w_ref.shape[0], first_ref.shape[1], w_ref.shape[1] // heads
+    w_ref[:, :left] = first_ref[top : top + rows]
+    lay_out(pieces, w_ref.at[:, left:])
+    for g_ref, old, out in ((g_own, before[:1], own), (g_other, before[1:], other)):
         total = None
         for j in range(heads):
             term = contract(
                 g_ref[:, columns_after(1 + j, width)], w_ref[:, j * width : (j + 1) * width], 1, 1
             )
             total = term if total is None else total + term
-        if old is not None:
-            out[:, : old.shape[1]] = old[...]
-        out[:, out.shape[1] - total.shape[1] :] = total.astype(BF16)
+        start = out.shape[1] - rows
+        if old:
+            out[:, :start] = old[0][...]
+        out[:, start:] = total.astype(BF16)
 
 
 def weight_kernel(blocks, a_own, a_other, g_own, g_other, *outs):
@@ -319,11 +343,13 @@
     right_ref[...] = (mid_right[...] + far_right[...].astype(F32)).astype(BF16)
 
 
-def total_kernel(own_ref, left_ref, right_ref, out_ref):
+def total_kernel(parts, own_ref, *refs):
     half = own_ref.shape[1] // 2
-    left, right = slice(0, half), slice(half, 2 * half)
-    out_ref[:, left] = own_ref[:, left] + left_ref[...].astype(F32)
-    out_ref[:, right] = own_ref[:, right] + right_ref[...].astype(F32)
+    out_ref = refs[-1]
+    sides = [own_ref[:, :half], own_ref[:, half:]]
+    for left, ref in zip(parts, refs[:-1]):
+        sides[left] = sides[left] + ref[...].astype(F32)
+    out_ref[:, :half], out_ref[:, half:] = sides
 
 
 def back_pair_kernel(groups, own_ref, near_ref, left_ref, right_ref, out_ref, left_again, right_again):
@@ -344,24 +370,23 @@
 
 def passed(array):
     devices = lax.axis_size("head")
-    return lax.ppermute(array, "head", [(i, (i - 1) % devices) for i in range(devices)])
-
-
-def picks(groups, rows_each):
+    pairs = [(along(i), along((i - 1) % devices)) for i in range(devices)]
+    return lax.ppermute(array, "head", pairs)
+
+
+def picks_kernel(groups, rows_each, own_ref, other_ref):
     devices, mine, core = lax.axis_size("ctx"), lax.axis_index("ctx"), lax.axis_index("dp")
-    width = devices * rows_each * groups
-    feature = lax.broadcasted_iota(jnp.int32, (groups * DH, width), 0)
-    place = lax.broadcasted_iota(jnp.int32, (groups * DH, width), 1)
+    width = own_ref.shape[1]
+    shape = (DH, width)
+    feature, place = lax.broadcasted_iota(jnp.int32, shape, 0), lax.broadcasted_iota(jnp.int32, shape, 1)
     block = place // (rows_each * groups)
     if devices == 4:
         block = block ^ mine
     row = (place // groups) % rows_each
-    group = place % groups
-
-    def pick(p):
-        return (feature == group * DH + (block * 2 + p) * rows_each + row).astype(BF16)
-
-    return pick(core), pick(1 - core)
+    for p, ref in ((core, own_ref), (1 - core, other_ref)):
+        match = feature == (block * 2 + p) * rows_each + row
+        for h in range(groups):
+            ref[h * DH : (h + 1) * DH, :] = (match & (place % groups == h)).astype(F32).astype(BF16)
 
 
 def shards(queries, keys, values, log_decay, w_out, grad_out):
@@ -380,66 +405,68 @@
     last = []
 
     def step(kernel, out_shape, *args, after=(), **kwargs):
-        out = call(kernel, out_shape, *args, after=[*last, *after], **kwargs)
-        last[:] = [min(jax.tree.leaves(out), key=lambda x: x.size)]
+        out, done = call(kernel, out_shape, *args, after=[*last, *after], **kwargs)
+        last[:] = [done]
         return out
 
     near_heads = heads // 2
     first_shape, rest_shape = (struct((rows, count * part), BF16) for count in (near_heads, heads - near_heads))
-    state, row, col, w_first, w_rest = step(
-        functools.partial(contrib_kernel, groups),
-        (state_shape, struct((groups, size), F32), struct((size, groups), F32), first_shape, rest_shape),
+    state = step(
+        functools.partial(contrib_kernel, groups), state_shape, k, v, ld, staged=(0, 1, 2), room=60
+    )
+    w_first, w_rest = step(
+        columns_kernel,
+        [first_shape, rest_shape],
+        w,
+        free_in=(0,),
+        scratch=[pltpu.SemaphoreType.DMA((heads,))],
+        room=60,
+    )
+    g_other = swapped(g)
+    if four:
+        near = flipped(state, 1)
+        first_two, first_one = flipped(w_first, 2), flipped(w_first, 1)
+        pair = step(functools.partial(pair_kernel, groups, True), struct((features, DH), BF16), state, near)
+        before = [near, lax.ppermute(pair, "ctx", [(0, 2), (1, 3)])]
+        lower = lambda array: struct((rows // 2, array.shape[1]), BF16)
+    pick_own, pick_other = step(
+        functools.partial(picks_kernel, groups, rows_each),
+        [struct((features, features // 2), BF16)] * 2,
+        after=[g_other],
+    )
+    row, col, intra = step(
+        functools.partial(intra_kernel, groups),
+        (struct((groups, size), F32), struct((size, groups), F32), flat(F32)),
+        q,
         k,
         v,
         ld,
-        w,
-        staged=(0, 1, 2),
-        free_in=(3,),
-        scratch=[pltpu.SemaphoreType.DMA((heads,))],
-        room=60,
-    )
-    g_other = swapped(g)
-    if four:
-        near = flipped(state, 1)
-        first_two = flipped(w_first, 2)
-        w_again = step(again_kernel, first_shape, w_first)
-        first_one = flipped(w_again, 1)
+    )
+    if four:
+        on_one, on_two, w_again = step(
+            pass_kernel, [lower(w_first)] * 2 + [rest_shape], first_one, first_two, w_rest
+        )
+        first = [w_first, first_one, first_two, flipped(on_one, 2), flipped(on_two, 1)]
     else:
         before = hops_of(state, True)
-    pick_own, pick_other = picks(groups, rows_each)
-    intra = step(
-        functools.partial(intra_kernel, groups),
-        flat(F32),
-        q,
-        k,
-        v,
-        row,
-        col,
-        staged=(0, 1, 2),
-        after=[g_other],
-    )
-    if four:
-        pair = step(functools.partial(pair_kernel, groups, True), struct((features, DH), BF16), state, near)
-        before = [near, lax.ppermute(pair, "ctx", [(0, 2), (1, 3)])]
-        lower = lambda array: struct((rows // 2, array.shape[1]), BF16)
-        on_one, on_two = step(rows_kernel, [lower(w_first)] * 2, first_one, first_two)
-        first = [w_first, first_one, first_two, flipped(on_one, 2), flipped(on_two, 1)]
-    else:
-        first = [lax.all_gather(w_first, "ctx", axis=0, tiled=True)]
+        first = lax.all_gather(w_first, "ctx", axis=0, tiled=True)
         rest = [lax.all_gather(w_rest, "ctx", axis=0, tiled=True)]
-    a_own, a_away, low, w_again = step(
+    a_own, a_away, low, g_own = step(
         functools.partial(attended_kernel, groups, len(before)),
-        (half, half, struct((groups, DH, DH), BF16), rest_shape),
+        (half, half, struct((groups, DH, DH), BF16), struct(g.shape, BF16)),
         *before,
         q,
         intra,
         col,
         pick_own,
         pick_other,
-        w_rest,
-        scratch=[pltpu.VMEM((size, features), BF16)],
+        g,
+        free_in=(len(before) + 5,),
+        scratch=[pltpu.VMEM((size, features), BF16), pltpu.SemaphoreType.DMA((1,))],
     )
     a_other = swapped(a_away)
+    if four:
+        first = step(join_kernel, struct((devices * rows, first_shape.shape[1]), BF16), *first, work=C_JOIN)
     held = pltpu.VMEM((features // 2, part), BF16)
 
     def mix(pieces, place, count, splits=1, work=0):
@@ -462,18 +489,18 @@
         )
 
     def weights(blocks, shapes):
-        return step(functools.partial(weight_kernel, blocks), shapes, a_own, a_other, g, g_other)
-
-    def grad_of(some, *earlier):
-        here = sum(piece.shape[0] for piece, _ in some)
+        return step(functools.partial(weight_kernel, blocks), shapes, a_own, a_other, g_own, g_other)
+
+    def grad_of(pieces, top, *earlier):
+        here = sum(piece.shape[0] for piece in pieces)
         wide = here + sum(array.shape[1] for array in earlier[:1])
         return step(
-            functools.partial(grad_kernel, len(some), len(earlier)),
+            functools.partial(grad_kernel, top, len(pieces), len(earlier)),
             [struct((size, wide), BF16)] * 2,
-            g,
+            g_own,
             g_other,
-            *[piece for piece, _ in some],
-            *[piece for _, piece in some],
+            first,
+            *pieces,
             *earlier,
             scratch=[pltpu.VMEM((here, width), BF16)],
         )
@@ -486,17 +513,16 @@
         *far, mid_left, mid_right, near_left, near_right, own_sum = weights(
             blocks, [small(BF16)] * 2 + [small(F32)] * 2 + [small(BF16)] * 2 + [struct((rows, width), F32)]
         )
-    terms = mix(first, 0, near_heads, 3 if four else 1, 0)
+    terms = mix([first], 0, near_heads, 3 if four else 1)
     arrived = passed(ring(terms[0]))
     if four:
         rest_one, rest_two = flipped(w_again, 1), flipped(w_again, 2)
         on_one, on_two = step(rows_kernel, [lower(w_rest)] * 2, rest_one, rest_two)
         rest = [w_rest, rest_one, rest_two, flipped(on_one, 2), flipped(on_two, 1)]
         far_left, far_right = flipped(far[0], 1), flipped(far[1], 2)
-        both = list(zip(first, rest))
-        grad_own, grad_away = grad_of(both[3:], *grad_of(both[:3]))
+        grad_own, grad_away = grad_of(rest[3:], 3 * rows, *grad_of(rest[:3], 0))
     else:
-        grad_own, grad_away = grad_of(list(zip(first, rest)))
+        grad_own, grad_away = grad_of(rest, 0)
     grad_other = swapped(grad_away)
     for j in range(1, near_heads):
         arrived = passed(ring(terms[j], arrived, work=C17))
@@ -517,20 +543,21 @@
         after = hops_of(back, False)
     if four:
         to_left, to_right = step(onward_kernel, [small(BF16)] * 2, mid_left, mid_right, far_left, far_right)
-        on_left, on_right = flipped(to_left, 2), flipped(to_right, 1)
+        on_right = flipped(to_right, 1)
+        near_right = flipped(near_right, 2)
     terms = mix(rest, 0, 1)
     if four:
-        pair, near_left, near_right = step(
+        pair, near_left, to_left = step(
             functools.partial(back_pair_kernel, groups),
             [struct((features, DH), BF16), small(BF16), small(BF16)],
             back,
             near,
             near_left,
-            near_right,
+            to_left,
             work=C20,
         )
         after = [near, lax.ppermute(pair, "ctx", [(2, 0), (3, 1)])]
-        near_left, near_right = flipped(near_left, 1), flipped(near_right, 2)
+        near_left, on_left = flipped(near_left, 1), flipped(to_left, 2)
     query_grad, key_part, value_part = step(
         functools.partial(back_intra_kernel, groups),
         (flat(BF16), flat(F32), flat(F32)),
@@ -541,13 +568,12 @@
         row,
         col,
         low,
-        staged=(1, 2, 3),
     )
     for j in range(1, heads - near_heads):
         arrived = passed(ring(terms[0], arrived))
         terms = mix(rest, j, 1)
     if four:
-        own_sum = step(total_kernel, struct((rows, width), F32), own_sum, on_left, on_right)
+        own_sum = step(functools.partial(total_kernel, (1, 1)), struct((rows, width), F32), own_sum, near_right, on_right)
     key_grad, value_grad = step(
         functools.partial(back_inter_kernel, groups, len(after)),
         (flat(BF16), flat(BF16)),
@@ -559,12 +585,12 @@
         value_part,
         work=C24,
     )
-    if four:
-        w_grad = step(total_kernel, struct((rows, width), F32), own_sum, near_left, near_right)
+    mixed = ring(terms[0], arrived, work=C26)
+    if four:
+        w_grad = step(functools.partial(total_kernel, (0, 0)), struct((rows, width), F32), own_sum, near_left, on_left)
     else:
         w_grad = contract(a_own, g, 0, 0) + contract(a_other, g_other, 0, 0)
         w_grad = lax.psum_scatter(w_grad.astype(BF16), "ctx", scatter_dimension=0, tiled=True).astype(F32)
-    mixed = ring(terms[0], arrived)
     return (
         mixed[None],
         query_grad[None],

time: 93.9 us -> 86.8 us (0.924)
  local copies, waits for them, and re-layouts: 6.86 us -> 1.68 us
  Pallas kernels: 28.6 us -> 25.7 us
  waiting for transfers between devices: 16.7 us -> 19.3 us
  other arithmetic: 1.37 us -> 0 us
    unnamed x34 -> x18, local copies, waits for them, and re-layouts: 6.86 us -> 1.68 us
    ppermute x3, waiting for transfers between devices: 0.08 us -> 3.37 us  [passed(): return lax.ppermute(array, 'head', pairs)]
    pallas_call x24 -> x26, Pallas kernels: 28.6 us -> 25.7 us  [call(): pl.pallas_call(body, name=getattr(kernel, 'func', kernel).__name__, out_s...]
    ppermute x3, starting transfers between devices: 10.5 us -> 8.34 us  [passed(): return lax.ppermute(array, 'head', pairs)]
    ppermute x16, starting transfers between devices: 21.8 us -> 23.5 us  [flipped(): return lax.ppermute(array, 'ctx', [(i, i ^ bit) for i in range(4)])]
  transfers between devices with their start and end apart: 29 -> 29, of which waited for: 14 -> 14; matrix products, arithmetic and copies ran while one was open for 1% -> 0% of each run, Pallas kernels for 27% -> 28%
where the time goes in v4:
time: 86.8 us; the launch traced here: 86.5 us
  starting transfers between devices  38.6 us (44%)
  Pallas kernels  25.7 us (30%)
  waiting for transfers between devices  19.3 us (22%)
  local copies, waits for them, and re-layouts  1.68 us (2%)
  between operations  1.21 us (1%)
    pallas_call x26, Pallas kernels, call(): pl.pallas_call(body, name=getattr(kernel, 'func', kernel).__name__, out_s...  25.7 us
    ppermute x16, starting transfers between devices, flipped(): return lax.ppermute(array, 'ctx', [(i, i ^ bit) for i in range(4)])  23.5 us
    ppermute x16, waiting for transfers between devices, flipped(): return lax.ppermute(array, 'ctx', [(i, i ^ bit) for i in range(4)])  12.8 us
    ppermute x3, starting transfers between devices, passed(): return lax.ppermute(array, 'head', pairs)  8.34 us
    ppermute x1, starting transfers between devices, shards(): before = [near, lax.ppermute(pair, 'ctx', [(0, 2), (1, 3)])]  3.89 us
    ppermute x3, waiting for transfers between devices, passed(): return lax.ppermute(array, 'head', pairs)  3.37 us
    ppermute x8, waiting for transfers between devices, swapped(): return lax.ppermute(array, 'dp', [(0, 1), (1, 0)])  3.06 us
  transfers between devices with their start and end apart: 29, of which 14 were waited for; matrix products, arithmetic and copies ran while one was open for 0% of the time, Pallas kernels for 28%

profile of v4, /device:TPU:0, one launch (start us, length us, event | category | flops | bytes accessed | tf_op | source)
XLA Modules:
  0.0 86.5 jit_solution(15232076434459240136)
XLA Ops:
  0.6 0.5 collective-permute-start.2
  1.2 3.5 %contrib_kernel.1 = (bf16[1040,128]{1,0:T(8,128)(2,1)}, f32[8,128]{1,0:T(8,128)}) custom-call(bf16[256,1024]{1,0:T(8,128)(2,1)} %bitcast.15, bf16[256,1024]{1,0:T(8,128)(2,1)} %bitcast.19, f32[8,256]{1,0:T(8,128)} %bitcast.25), custom_call_target="tpu_custom_call" | custom-call | tf_op jit(solution)/shard_map/contrib_kernel/pallas_call | solution.py:45
  4.7 2.6 %collective-permute-start = (bf16[1040,128]{1,0:T(8,128)(2,1)}, bf16[1040,128]{1,0:T(8,128)(2,1)S(1)}, u32[]{:S(2)}, u32[]{:S(2)}) collective-permute-start(bf16[1040,128]{1,0:T(8,128)(2,1)} %get-tuple-element.87.refs_0_), channel_id=1, source_target_pairs={{0,8},{8,0},{16,24},{24,16},{1,9},{9,1},{17,25},{25,17},{2,10},{10... | collective-permute-start | bytes 798728 | tf_op jit(solution)/shard_map/ppermute | solution.py:264
  7.3 2.1 %columns_kernel.1 = (bf16[128,1536]{1,0:T(8,128)(2,1)}, bf16[128,1536]{1,0:T(8,128)(2,1)}, f32[8,128]{1,0:T(8,128)}) custom-call(bf16[128,3072]{1,0:T(8,128)(2,1)} %bitcast.27, f32[8,128]{1,0:T(8,128)} %get-tuple-element.88.refs_1_), custom_call_target="tpu_custom_call" | custom-call | tf_op jit(solution)/shard_map/columns_kernel/pallas_call | solution.py:45
  9.4 1.6 %collective-permute-start.4 = (bf16[128,1536]{1,0:T(8,128)(2,1)}, bf16[128,1536]{1,0:T(8,128)(2,1)S(1)}, u32[]{:S(2)}, u32[]{:S(2)}) collective-permute-start(bf16[128,1536]{1,0:T(8,128)(2,1)} %get-tuple-element.97.refs_0_), channel_id=1, source_target_pairs={{0,16},{8,24},{16,0},{24,8},{1,17},{9,25},{17,1},{25,9},{2,18},{10... | collective-permute-start | bytes 1179656 | tf_op jit(solution)/shard_map/ppermute | solution.py:264
  11.0 0.5 collective-permute-start.3
  11.6 3.2 %collective-permute-done.refs_1_.refs_0_ = bf16[1040,128]{1,0:T(8,128)(2,1)S(1)} collective-permute-done((bf16[1040,128]{1,0:T(8,128)(2,1)}, bf16[1040,128]{1,0:T(8,128)(2,1)S(1)}, u32[]{:S(2)}, u32[]{:S(2)}) %collective-permute-start) | collective-permute-done | bytes 266272 | tf_op jit(solution)/shard_map/ppermute | solution.py:264
  14.8 0.9 %copy-done.5 = bf16[1040,128]{1,0:T(8,128)(2,1)S(1)} copy-done((bf16[1040,128]{1,0:T(8,128)(2,1)S(1)}, bf16[1040,128]{1,0:T(8,128)(2,1)}, u32[]{:S(2)}) %copy-start.5) | copy-done | bytes 266264
  15.7 0.7 copy-done.7
  16.4 0.1 pair_kernel.1
  16.5 3.9 %collective-permute-start.1 = (bf16[1024,128]{1,0:T(8,128)(2,1)S(1)}, bf16[1024,128]{1,0:T(8,128)(2,1)S(1)}, u32[]{:S(2)}, u32[]{:S(2)}) collective-permute-start(bf16[1024,128]{1,0:T(8,128)(2,1)S(1)} %get-tuple-element.90), channel_id=1, source_target_pairs={{0,16},{8,24},{1,17},{9,25},{2,18},{10,26},{3,19},{11,27},{4,20},{... | collective-permute-start | bytes 786440 | tf_op jit(solution)/shard_map/ppermute | solution.py:430
  20.4 0.4 picks_kernel.1
  20.9 1.3 %intra_kernel.1 = (f32[8,256]{1,0:T(8,128)S(1)}, f32[256,8]{1,0:T(8,128)S(1)}, f32[256,1024]{1,0:T(8,128)S(1)}, f32[8,128]{1,0:T(8,128)S(1)}) custom-call(bf16[256,1024]{1,0:T(8,128)(2,1)S(1)} %bitcast.11, bf16[256,1024]{1,0:T(8,128)(2,1)S(1)} %bitcast.16, bf16[256,1024]{1,0:T(8,128)(2,1)S(1)} %bitcast.20, f32[8,256]{1,0:T(8,128)S(1)} %bitcast.26, ...), custom_call_target="tpu_custom_call" | custom-call | tf_op jit(solution)/shard_map/intra_kernel/pallas_call | solution.py:45
  22.2 0.8 collective-permute-done.3.refs_0_.refs_1_
  23.1 1.8 %collective-permute-start.8 = (bf16[64,1536]{1,0:T(8,128)(2,1)S(1)}, bf16[64,1536]{1,0:T(8,128)(2,1)S(1)}, u32[]{:S(2)}, u32[]{:S(2)}) collective-permute-start(bf16[64,1536]{1,0:T(8,128)(2,1)S(1)} %get-tuple-element.104), channel_id=1, source_target_pairs={{0,16},{8,24},{16,0},{24,8},{1,17},{9,25},{17,1},{25,9},{2,18},{10... | collective-permute-start | bytes 589832 | tf_op jit(solution)/shard_map/ppermute | solution.py:264
  24.9 1.5 %collective-permute-start.9 = (bf16[64,1536]{1,0:T(8,128)(2,1)S(1)}, bf16[64,1536]{1,0:T(8,128)(2,1)S(1)}, u32[]{:S(2)}, u32[]{:S(2)}) collective-permute-start(bf16[64,1536]{1,0:T(8,128)(2,1)S(1)} %get-tuple-element.105), channel_id=1, source_target_pairs={{0,8},{8,0},{16,24},{24,16},{1,9},{9,1},{17,25},{25,17},{2,10},{10... | collective-permute-start | bytes 589832 | tf_op jit(solution)/shard_map/ppermute | solution.py:264
  26.4 1.2 %attended_kernel.1 = (bf16[256,512]{1,0:T(8,128)(2,1)S(1)}, bf16[256,512]{1,0:T(8,128)(2,1)S(1)}, bf16[8,128,128]{2,1,0:T(8,128)(2,1)S(1)}, bf16[256,3072]{1,0:T(8,128)(2,1)S(1)}, f32[8,128]{1,0:T(8,128)S(1)}) custom-call(bf16[1040,128]{1,0:T(8,128)(2,1)S(1)} %collective-permute-done.refs_1_.refs_0_, bf16[1024,128]{1,0:T(8,128)(2,1)S(1)} %collective-permute-done.1.refs_1_, ...), custom_call_target="tpu_custom_call" | custom-call | tf_op jit(solution)/shard_map/attended_kernel/pallas_call | solution.py:45
  27.7 2.5 %collective-permute-start.7 = (bf16[128,1536]{1,0:T(8,128)(2,1)S(1)}, bf16[128,1536]{1,0:T(8,128)(2,1)S(1)}, u32[]{:S(2)}, u32[]{:S(2)}) collective-permute-start(bf16[128,1536]{1,0:T(8,128)(2,1)S(1)} %get-tuple-element.103), channel_id=1, source_target_pairs={{0,16},{8,24},{16,0},{24,8},{1,17},{9,25},{17,1},{25,9},{2,18},{10... | collective-permute-start | bytes 1179656 | tf_op jit(solution)/shard_map/ppermute | solution.py:264
  30.2 1.1 %collective-permute-start.6 = (bf16[128,1536]{1,0:T(8,128)(2,1)S(1)}, bf16[128,1536]{1,0:T(8,128)(2,1)S(1)}, u32[]{:S(2)}, u32[]{:S(2)}) collective-permute-start(bf16[128,1536]{1,0:T(8,128)(2,1)S(1)} %get-tuple-element.103), channel_id=1, source_target_pairs={{0,8},{8,0},{16,24},{24,16},{1,9},{9,1},{17,25},{25,17},{2,10},{10... | collective-permute-start | bytes 1179656 | tf_op jit(solution)/shard_map/ppermute | solution.py:264
  31.4 0.1 join_kernel.1
  31.5 1.8 %weight_kernel.1 = (bf16[128,1536]{1,0:T(8,128)(2,1)S(1)}, bf16[128,1536]{1,0:T(8,128)(2,1)S(1)}, f32[128,1536]{1,0:T(8,128)S(1)}, f32[128,1536]{1,0:T(8,128)S(1...) custom-call(bf16[256,512]{1,0:T(8,128)(2,1)S(1)} %get-tuple-element., ...), custom_call_target="tpu_custom_call" | custom-call | tf_op jit(solution)/shard_map/weight_kernel/pallas_call | solution.py:45
  33.4 1.0 %mix_kernel.3 = (f32[256,768]{1,0:T(8,128)S(1)}, f32[256,768]{1,0:T(8,128)S(1)}, bf16[256,512]{1,0:T(8,128)(2,1)S(1)}, bf16[256,512]{1,0:T(8,128)(2,1)S(1)}, bf1...) custom-call(bf16[256,512]{1,0:T(8,128)(2,1)S(1)} %get-tuple-element.101.refs_0_, ...), custom_call_target="tpu_custom_call" | custom-call | tf_op jit(solution)/shard_map/mix_kernel/pallas_call | solution.py:45
  34.4 0.5 collective-permute-start.11
  34.9 0.1 collective-permute-start.12
  35.0 0.9 %collective-permute-done.10.refs_1_ = bf16[256,512]{1,0:T(8,128)(2,1)S(1)} collective-permute-done((bf16[256,512]{1,0:T(8,128)(2,1)S(1)}, bf16[256,512]{1,0:T(8,128)(2,1)S(1)}, u32[]{:S(2)}, u32[]{:S(2)}) %collective-permute-start.10) | collective-permute-done | bytes 262176 | tf_op jit(solution)/shard_map/ppermute | solution.py:260
  36.0 0.4 collective-permute-done.11.refs_2_
  36.3 0.4 collective-permute-done.12.refs_3_
  36.7 0.1 ring_kernel.4
  36.8 2.6 %collective-permute-start.18 = (bf16[256,768]{1,0:T(8,128)(2,1)S(1)}, bf16[256,768]{1,0:T(8,128)(2,1)S(1)}, u32[]{:S(2)}, u32[]{:S(2)}) collective-permute-start(bf16[256,768]{1,0:T(8,128)(2,1)S(1)} %get-tuple-element.131), channel_id=1, source_target_pairs={{0,4},{2,0},{6,2},{4,6},{1,5},{3,1},{7,3},{5,7},{8,12},{10,8},{14,... | collective-permute-start | bytes 1179656 | tf_op jit(solution)/shard_map/ppermute | solution.py:374
  39.5 0.5 collective-permute-done.7.refs_1_.refs_5_.refs_4_
  39.9 1.5 %collective-permute-done.6.refs_0_.refs_4_.refs_3_ = bf16[128,1536]{1,0:T(8,128)(2,1)S(1)} collective-permute-done((bf16[128,1536]{1,0:T(8,128)(2,1)S(1)}, bf16[128,1536]{1,0:T(8,128)(2,1)S(1)}, u32[]{:S(2)}, u32[]{:S(2)}) %collective-permute-start.6) | collective-permute-done | bytes 393248 | tf_op jit(solution)/shard_map/ppermute | solution.py:264
  41.5 0.3 collective-permute-start.13
  41.8 1.1 %collective-permute-start.14 = (bf16[64,1536]{1,0:T(8,128)(2,1)S(1)}, bf16[64,1536]{1,0:T(8,128)(2,1)S(1)}, u32[]{:S(2)}, u32[]{:S(2)}) collective-permute-start(bf16[64,1536]{1,0:T(8,128)(2,1)S(1)} %get-tuple-element.118), channel_id=1, source_target_pairs={{0,8},{8,0},{16,24},{24,16},{1,9},{9,1},{17,25},{25,17},{2,10},{10... | collective-permute-start | bytes 589832 | tf_op jit(solution)/shard_map/ppermute | solution.py:264
  42.9 0.9 %collective-permute-start.15 = (bf16[128,1536]{1,0:T(8,128)(2,1)S(1)}, bf16[128,1536]{1,0:T(8,128)(2,1)S(1)}, u32[]{:S(2)}, u32[]{:S(2)}) collective-permute-start(bf16[128,1536]{1,0:T(8,128)(2,1)S(1)} %get-tuple-element.121), channel_id=1, source_target_pairs={{0,8},{8,0},{16,24},{24,16},{1,9},{9,1},{17,25},{25,17},{2,10},{10... | collective-permute-start | bytes 1179656 | tf_op jit(solution)/shard_map/ppermute | solution.py:264
  43.8 1.7 %collective-permute-start.16 = (bf16[128,1536]{1,0:T(8,128)(2,1)S(1)}, bf16[128,1536]{1,0:T(8,128)(2,1)S(1)}, u32[]{:S(2)}, u32[]{:S(2)}) collective-permute-start(bf16[128,1536]{1,0:T(8,128)(2,1)S(1)} %get-tuple-element.122), channel_id=1, source_target_pairs={{0,16},{8,24},{16,0},{24,8},{1,17},{9,25},{17,1},{25,9},{2,18},{10... | collective-permute-start | bytes 1179656 | tf_op jit(solution)/shard_map/ppermute | solution.py:264
  45.6 1.8 %grad_kernel.2 = (bf16[256,384]{1,0:T(8,128)(2,1)S(1)}, bf16[256,384]{1,0:T(8,128)(2,1)S(1)}, f32[8,128]{1,0:T(8,128)S(1)}) custom-call(bf16[256,3072]{1,0:T(8,128)(2,1)S(1)} %get-tuple-element.108.refs_2_.refs_0_, bf16[256,3072]{1,0:T(8,128)(2,1)S(1)} %collective-permute-done.2.refs_1_.refs_3_, bf16[512,1536]{1,0:T(8,128)(2,1)S(1)} %get-tuple-element.107.refs_2_, ...), custom_call_target="tpu_custom_call" | custom-call | tf_op jit(solution)/shard_map/grad_kernel/pallas_call | solution.py:45
  47.4 2.0 %collective-permute-done.13.refs_3_.refs_5_ = bf16[64,1536]{1,0:T(8,128)(2,1)S(1)} collective-permute-done((bf16[64,1536]{1,0:T(8,128)(2,1)S(1)}, bf16[64,1536]{1,0:T(8,128)(2,1)S(1)}, u32[]{:S(2)}, u32[]{:S(2)}) %collective-permute-start.13) | collective-permute-done | bytes 196640 | tf_op jit(solution)/shard_map/ppermute | solution.py:264
  49.4 0.3 collective-permute-done.14.refs_4_.refs_6_
  49.6 1.0 %grad_kernel.3 = (bf16[256,512]{1,0:T(8,128)(2,1)S(1)}, bf16[256,512]{1,0:T(8,128)(2,1)S(1)}, f32[8,128]{1,0:T(8,128)S(1)}) custom-call(bf16[256,3072]{1,0:T(8,128)(2,1)S(1)} %get-tuple-element.108.refs_2_.refs_0_, bf16[256,3072]{1,0:T(8,128)(2,1)S(1)} %collective-permute-done.2.refs_1_.refs_3_, bf16[512,1536]{1,0:T(8,128)(2,1)S(1)} %get-tuple-element.107.refs_2_, ...), custom_call_target="tpu_custom_call" | custom-call | tf_op jit(solution)/shard_map/grad_kernel/pallas_call | solution.py:45
  50.7 0.1 ring_kernel.5
  50.9 1.4 %collective-permute-done.17.refs_1_ = bf16[256,512]{1,0:T(8,128)(2,1)S(1)} collective-permute-done((bf16[256,512]{1,0:T(8,128)(2,1)S(1)}, bf16[256,512]{1,0:T(8,128)(2,1)S(1)}, u32[]{:S(2)}, u32[]{:S(2)}) %collective-permute-start.17) | collective-permute-done | bytes 262176 | tf_op jit(solution)/shard_map/ppermute | solution.py:260
  52.2 1.0 %back_contrib_kernel.1 = (bf16[256,1024]{1,0:T(8,128)(2,1)S(1)}, bf16[1040,128]{1,0:T(8,128)(2,1)S(1)}, f32[8,128]{1,0:T(8,128)S(1)}) custom-call(bf16[256,512]{1,0:T(8,128)(2,1)S(1)} %get-tuple-element.127.refs_0_, bf16[256,512]{1,0:T(8,128)(2,1)S(1)} %collective-permute-done.17.refs_1_, bf16[1024,512]{1,0:T(8,128)(2,1)S(1)} %get-tuple-element.95.refs_5_.refs_2_, ...), custom_call_target="tpu_custom_call" | custom-call | tf_op jit(solution)/shard_map/back_contrib_kernel/pallas_call | solution.py:45
  53.3 1.2 %collective-permute-start.21 = (bf16[1040,128]{1,0:T(8,128)(2,1)S(1)}, bf16[1040,128]{1,0:T(8,128)(2,1)S(1)}, u32[]{:S(2)}, u32[]{:S(2)}) collective-permute-start(bf16[1040,128]{1,0:T(8,128)(2,1)S(1)} %get-tuple-element.141.refs_0_), channel_id=1, source_target_pairs={{0,8},{8,0},{16,24},{24,16},{1,9},{9,1},{17,25},{25,17},{2,10},{10... | collective-permute-start | bytes 798728 | tf_op jit(solution)/shard_map/ppermute | solution.py:264
  54.5 2.6 %collective-permute-start.20 = (bf16[256,768]{1,0:T(8,128)(2,1)S(1)}, bf16[256,768]{1,0:T(8,128)(2,1)S(1)}, u32[]{:S(2)}, u32[]{:S(2)}) collective-permute-start(bf16[256,768]{1,0:T(8,128)(2,1)S(1)} %get-tuple-element.138), channel_id=1, source_target_pairs={{0,4},{2,0},{6,2},{4,6},{1,5},{3,1},{7,3},{5,7},{8,12},{10,8},{14,... | collective-permute-start | bytes 1179656 | tf_op jit(solution)/shard_map/ppermute | solution.py:374
  57.1 0.2 onward_kernel.1
  57.3 0.6 mix_kernel.4
  58.0 1.8 %collective-permute-start.25 = (bf16[128,1536]{1,0:T(8,128)(2,1)S(1)}, bf16[128,1536]{1,0:T(8,128)(2,1)S(1)}, u32[]{:S(2)}, u32[]{:S(2)}) collective-permute-start(bf16[128,1536]{1,0:T(8,128)(2,1)S(1)} %get-tuple-element.155), channel_id=1, source_target_pairs={{0,16},{8,24},{16,0},{24,8},{1,17},{9,25},{17,1},{25,9},{2,18},{10... | collective-permute-start | bytes 1179656 | tf_op jit(solution)/shard_map/ppermute | solution.py:264
  59.8 0.9 %collective-permute-start.26 = (bf16[128,1536]{1,0:T(8,128)(2,1)S(1)}, bf16[128,1536]{1,0:T(8,128)(2,1)S(1)}, u32[]{:S(2)}, u32[]{:S(2)}) collective-permute-start(bf16[128,1536]{1,0:T(8,128)(2,1)S(1)} %get-tuple-element.156), channel_id=1, source_target_pairs={{0,8},{8,0},{16,24},{24,16},{1,9},{9,1},{17,25},{25,17},{2,10},{10... | collective-permute-start | bytes 1179656 | tf_op jit(solution)/shard_map/ppermute | solution.py:264
  60.6 1.5 %collective-permute-done.21.refs_1_.refs_0_ = bf16[1040,128]{1,0:T(8,128)(2,1)S(1)} collective-permute-done((bf16[1040,128]{1,0:T(8,128)(2,1)S(1)}, bf16[1040,128]{1,0:T(8,128)(2,1)S(1)}, u32[]{:S(2)}, u32[]{:S(2)}) %collective-permute-start.21) | collective-permute-done | bytes 266272 | tf_op jit(solution)/shard_map/ppermute | solution.py:264
  62.1 0.2 back_pair_kernel.1
  62.3 1.5 %collective-permute-start.24 = (bf16[1024,128]{1,0:T(8,128)(2,1)S(1)}, bf16[1024,128]{1,0:T(8,128)(2,1)S(1)}, u32[]{:S(2)}, u32[]{:S(2)}) collective-permute-start(bf16[1024,128]{1,0:T(8,128)(2,1)S(1)} %get-tuple-element.151), channel_id=1, source_target_pairs={{16,0},{24,8},{17,1},{25,9},{18,2},{26,10},{19,3},{27,11},{20,4},{... | collective-permute-start | bytes 786440 | tf_op jit(solution)/shard_map/ppermute | solution.py:559
  63.8 4.4 %back_intra_kernel.1 = (bf16[256,1024]{1,0:T(8,128)(2,1)}, f32[256,1024]{1,0:T(8,128)S(1)}, f32[256,1024]{1,0:T(8,128)S(1)}, f32[8,128]{1,0:T(8,128)S(1)}) custom-call(bf16[256,1024]{1,0:T(8,128)(2,1)S(1)} %get-tuple-element.139.refs_0_, bf16[256,1024]{1,0:T(8,128)(2,1)S(1)} %bitcast.14, bf16[256,1024]{1,0:T(8,128)(2,1)S(1)} %bitcast.17, ...), custom_call_target="tpu_custom_call" | custom-call | tf_op jit(solution)/shard_map/back_intra_kernel/pallas_call | solution.py:45
  68.2 0.2 ring_kernel.6
  68.3 0.6 mix_kernel.5
  69.0 3.1 %collective-permute-start.23 = (bf16[256,768]{1,0:T(8,128)(2,1)S(1)}, bf16[256,768]{1,0:T(8,128)(2,1)S(1)}, u32[]{:S(2)}, u32[]{:S(2)}) collective-permute-start(bf16[256,768]{1,0:T(8,128)(2,1)S(1)} %get-tuple-element.150), channel_id=1, source_target_pairs={{0,4},{2,0},{6,2},{4,6},{1,5},{3,1},{7,3},{5,7},{8,12},{10,8},{14,... | collective-permute-start | bytes 1179656 | tf_op jit(solution)/shard_map/ppermute | solution.py:374
  72.1 1.1 %collective-permute-start.27 = (bf16[128,1536]{1,0:T(8,128)(2,1)S(1)}, bf16[128,1536]{1,0:T(8,128)(2,1)S(1)}, u32[]{:S(2)}, u32[]{:S(2)}) collective-permute-start(bf16[128,1536]{1,0:T(8,128)(2,1)S(1)} %get-tuple-element.165), channel_id=1, source_target_pairs={{0,8},{8,0},{16,24},{24,16},{1,9},{9,1},{17,25},{25,17},{2,10},{10... | collective-permute-start | bytes 1179656 | tf_op jit(solution)/shard_map/ppermute | solution.py:264
  73.3 2.6 %collective-permute-start.28 = (bf16[128,1536]{1,0:T(8,128)(2,1)S(1)}, bf16[128,1536]{1,0:T(8,128)(2,1)S(1)}, u32[]{:S(2)}, u32[]{:S(2)}) collective-permute-start(bf16[128,1536]{1,0:T(8,128)(2,1)S(1)} %get-tuple-element.166), channel_id=1, source_target_pairs={{0,16},{8,24},{16,0},{24,8},{1,17},{9,25},{17,1},{25,9},{2,18},{10... | collective-permute-start | bytes 1179656 | tf_op jit(solution)/shard_map/ppermute | solution.py:264
  75.9 0.2 total_kernel.2
  76.1 1.6 %back_inter_kernel.1 = (bf16[256,1024]{1,0:T(8,128)(2,1)}, bf16[256,1024]{1,0:T(8,128)(2,1)}, f32[8,128]{1,0:T(8,128)S(1)}) custom-call(bf16[1040,128]{1,0:T(8,128)(2,1)S(1)} %collective-permute-done.21.refs_1_.refs_0_, bf16[1024,128]{1,0:T(8,128)(2,1)S(1)} %collective-permute-done.24.refs_1_, bf16[256,1024]{1,0:T(8,128)(2,1)S(1)} %bitcast.18, ...), custom_call_target="tpu_custom_call" | custom-call | flops 2140000000 | tf_op jit(solution)/shard_map/back_inter_kernel/pallas_call | solution.py:45
  77.7 3.4 %collective-permute-done.23.refs_2_ = bf16[256,768]{1,0:T(8,128)(2,1)S(1)} collective-permute-done((bf16[256,768]{1,0:T(8,128)(2,1)S(1)}, bf16[256,768]{1,0:T(8,128)(2,1)S(1)}, u32[]{:S(2)}, u32[]{:S(2)}) %collective-permute-start.23) | collective-permute-done | bytes 393248 | tf_op jit(solution)/shard_map/ppermute | solution.py:374
  81.1 0.9 %ring_kernel.7 = (bf16[256,768]{1,0:T(8,128)(2,1)}, f32[8,128]{1,0:T(8,128)S(1)}) custom-call(f32[256,768]{1,0:T(8,128)S(1)} %get-tuple-element.148.refs_0_, bf16[256,768]{1,0:T(8,128)(2,1)S(1)} %collective-permute-done.22.refs_1_, bf16[256,768]{1,0:T(8,128)(2,1)S(1)} %collective-permute-done.23.refs_2_, f32[8,128]{1,0:T(8,128)S(1)} %get-tuple-element.159.refs_3_), custom_call_target="tpu_custom_call" | custom-call | flops 642000000 | tf_op jit(solution)/shard_map/ring_kernel/pallas_call | solution.py:45
  82.0 1.3 %collective-permute-done.27.refs_1_ = bf16[128,1536]{1,0:T(8,128)(2,1)S(1)} collective-permute-done((bf16[128,1536]{1,0:T(8,128)(2,1)S(1)}, bf16[128,1536]{1,0:T(8,128)(2,1)S(1)}, u32[]{:S(2)}, u32[]{:S(2)}) %collective-permute-start.27) | collective-permute-done | bytes 393248 | tf_op jit(solution)/shard_map/ppermute | solution.py:264
  83.3 1.8 %collective-permute-done.28.refs_2_ = bf16[128,1536]{1,0:T(8,128)(2,1)S(1)} collective-permute-done((bf16[128,1536]{1,0:T(8,128)(2,1)S(1)}, bf16[128,1536]{1,0:T(8,128)(2,1)S(1)}, u32[]{:S(2)}, u32[]{:S(2)}) %collective-permute-start.28) | collective-permute-done | bytes 393248 | tf_op jit(solution)/shard_map/ppermute | solution.py:264
  85.1 1.3 %total_kernel.3 = (f32[128,3072]{1,0:T(8,128)}, f32[8,128]{1,0:T(8,128)}) custom-call(f32[128,3072]{1,0:T(8,128)S(1)} %get-tuple-element.164.refs_0_, bf16[128,1536]{1,0:T(8,128)(2,1)S(1)} %collective-permute-done.27.refs_1_, bf16[128,1536]{1,0:T(8,128)(2,1)S(1)} %collective-permute-done.28.refs_2_, f32[8,128]{1,0:T(8,128)S(1)} %get-tuple-element.167.refs_3_), custom_call_target="tpu_custom_call" | custom-call | tf_op jit(solution)/shard_map/total_kernel/pallas_call | solution.py:45
  (38 shorter events, 0.6 us)
Async XLA Ops:
  0.6 19.8 %collective-permute-start.2 = (bf16[256,3072]{1,0:T(8,128)(2,1)}, bf16[256,3072]{1,0:T(8,128)(2,1)S(1)}, u32[]{:S(2)}, u32[]{:S(2)}) collective-permute-start(bf16[256,3072]{1,0:T(8,128)(2,1)} %bitcast.23), channel_id=1, source_target_pairs={{0,1},{1,0},{2,3},{3,2},{4,5},{5,4},{6,7},{7,6},{8,9},{9,8},{10,11... | collective-permute-start | bytes 4718600 | tf_op jit(solution)/shard_map/ppermute | solution.py:260
  1.1 19.7 %copy-start.6 = (f32[1,8,256]{2,1,0:T(8,128)S(1)}, f32[1,8,256]{2,1,0:T(8,128)}, u32[]{:S(2)}) copy-start(f32[1,8,256]{2,1,0:T(8,128)} %param.9) | copy-start | bytes 24580
  4.7 16.2 %copy-start = (bf16[1,256,1024]{2,1,0:T(8,128)(2,1)S(1)}, bf16[1,256,1024]{2,1,0:T(8,128)(2,1)}, u32[]{:S(2)}) copy-start(bf16[1,256,1024]{2,1,0:T(8,128)(2,1)} %param.6) | copy-start | bytes 1572868
  4.7 16.2 %copy-start.2 = (bf16[1,256,1024]{2,1,0:T(8,128)(2,1)S(1)}, bf16[1,256,1024]{2,1,0:T(8,128)(2,1)}, u32[]{:S(2)}) copy-start(bf16[1,256,1024]{2,1,0:T(8,128)(2,1)} %param.7) | copy-start | bytes 1572868
  4.7 16.2 %copy-start.3 = (bf16[1,256,1024]{2,1,0:T(8,128)(2,1)S(1)}, bf16[1,256,1024]{2,1,0:T(8,128)(2,1)}, u32[]{:S(2)}) copy-start(bf16[1,256,1024]{2,1,0:T(8,128)(2,1)} %param.8) | copy-start | bytes 1572868
  4.7 10.0 %collective-permute-start = (bf16[1040,128]{1,0:T(8,128)(2,1)}, bf16[1040,128]{1,0:T(8,128)(2,1)S(1)}, u32[]{:S(2)}, u32[]{:S(2)}) collective-permute-start(bf16[1040,128]{1,0:T(8,128)(2,1)} %get-tuple-element.87.refs_0_), channel_id=1, source_target_pairs={{0,8},{8,0},{16,24},{24,16},{1,9},{9,1},{17,25},{25,17},{2,10},{10... | collective-permute-start | bytes 798728 | tf_op jit(solution)/shard_map/ppermute | solution.py:264
  9.4 12.7 %collective-permute-start.4 = (bf16[128,1536]{1,0:T(8,128)(2,1)}, bf16[128,1536]{1,0:T(8,128)(2,1)S(1)}, u32[]{:S(2)}, u32[]{:S(2)}) collective-permute-start(bf16[128,1536]{1,0:T(8,128)(2,1)} %get-tuple-element.97.refs_0_), channel_id=1, source_target_pairs={{0,16},{8,24},{16,0},{24,8},{1,17},{9,25},{17,1},{25,9},{2,18},{10... | collective-permute-start | bytes 1179656 | tf_op jit(solution)/shard_map/ppermute | solution.py:264
  11.0 12.0 %collective-permute-start.3 = (bf16[128,1536]{1,0:T(8,128)(2,1)}, bf16[128,1536]{1,0:T(8,128)(2,1)S(1)}, u32[]{:S(2)}, u32[]{:S(2)}) collective-permute-start(bf16[128,1536]{1,0:T(8,128)(2,1)} %get-tuple-element.97.refs_0_), channel_id=1, source_target_pairs={{0,8},{8,0},{16,24},{24,16},{1,9},{9,1},{17,25},{25,17},{2,10},{10... | collective-permute-start | bytes 1179656 | tf_op jit(solution)/shard_map/ppermute | solution.py:264
  14.7 1.0 %copy-start.5 = (bf16[1040,128]{1,0:T(8,128)(2,1)S(1)}, bf16[1040,128]{1,0:T(8,128)(2,1)}, u32[]{:S(2)}) copy-start(bf16[1040,128]{1,0:T(8,128)(2,1)} %get-tuple-element.87.refs_0_) | copy-start | bytes 798724
  15.7 0.7 copy-start.7
  16.5 9.9 %collective-permute-start.1 = (bf16[1024,128]{1,0:T(8,128)(2,1)S(1)}, bf16[1024,128]{1,0:T(8,128)(2,1)S(1)}, u32[]{:S(2)}, u32[]{:S(2)}) collective-permute-start(bf16[1024,128]{1,0:T(8,128)(2,1)S(1)} %get-tuple-element.90), channel_id=1, source_target_pairs={{0,16},{8,24},{1,17},{9,25},{2,18},{10,26},{3,19},{11,27},{4,20},{... | collective-permute-start | bytes 786440 | tf_op jit(solution)/shard_map/ppermute | solution.py:430
  20.4 2.6 %copy-start.1 = (bf16[128,1536]{1,0:T(8,128)(2,1)S(1)}, bf16[128,1536]{1,0:T(8,128)(2,1)}, u32[]{:S(2)}) copy-start(bf16[128,1536]{1,0:T(8,128)(2,1)} %get-tuple-element.98.refs_2_.refs_3_) | copy-start | bytes 1179652
  20.8 5.6 %copy-start.4 = (bf16[1,256,3072]{2,1,0:T(8,128)(2,1)S(1)}, bf16[1,256,3072]{2,1,0:T(8,128)(2,1)}, u32[]{:S(2)}) copy-start(bf16[1,256,3072]{2,1,0:T(8,128)(2,1)} %param.11) | copy-start | bytes 4718596
  23.1 8.3 %collective-permute-start.8 = (bf16[64,1536]{1,0:T(8,128)(2,1)S(1)}, bf16[64,1536]{1,0:T(8,128)(2,1)S(1)}, u32[]{:S(2)}, u32[]{:S(2)}) collective-permute-start(bf16[64,1536]{1,0:T(8,128)(2,1)S(1)} %get-tuple-element.104), channel_id=1, source_target_pairs={{0,16},{8,24},{16,0},{24,8},{1,17},{9,25},{17,1},{25,9},{2,18},{10... | collective-permute-start | bytes 589832 | tf_op jit(solution)/shard_map/ppermute | solution.py:264
  24.9 6.5 %collective-permute-start.9 = (bf16[64,1536]{1,0:T(8,128)(2,1)S(1)}, bf16[64,1536]{1,0:T(8,128)(2,1)S(1)}, u32[]{:S(2)}, u32[]{:S(2)}) collective-permute-start(bf16[64,1536]{1,0:T(8,128)(2,1)S(1)} %get-tuple-element.105), channel_id=1, source_target_pairs={{0,8},{8,0},{16,24},{24,16},{1,9},{9,1},{17,25},{25,17},{2,10},{10... | collective-permute-start | bytes 589832 | tf_op jit(solution)/shard_map/ppermute | solution.py:264
  26.4 4.9 %copy-start.8 = (bf16[128,1536]{1,0:T(8,128)(2,1)S(1)}, bf16[128,1536]{1,0:T(8,128)(2,1)}, u32[]{:S(2)}) copy-start(bf16[128,1536]{1,0:T(8,128)(2,1)} %get-tuple-element.97.refs_0_) | copy-start | bytes 1179652
  27.6 3.9 %collective-permute-start.5 = (bf16[256,512]{1,0:T(8,128)(2,1)S(1)}, bf16[256,512]{1,0:T(8,128)(2,1)S(1)}, u32[]{:S(2)}, u32[]{:S(2)}) collective-permute-start(bf16[256,512]{1,0:T(8,128)(2,1)S(1)} %get-tuple-element.102), channel_id=1, source_target_pairs={{0,1},{1,0},{2,3},{3,2},{4,5},{5,4},{6,7},{7,6},{8,9},{9,8},{10,11... | collective-permute-start | bytes 786440 | tf_op jit(solution)/shard_map/ppermute | solution.py:260
  27.7 12.3 %collective-permute-start.7 = (bf16[128,1536]{1,0:T(8,128)(2,1)S(1)}, bf16[128,1536]{1,0:T(8,128)(2,1)S(1)}, u32[]{:S(2)}, u32[]{:S(2)}) collective-permute-start(bf16[128,1536]{1,0:T(8,128)(2,1)S(1)} %get-tuple-element.103), channel_id=1, source_target_pairs={{0,16},{8,24},{16,0},{24,8},{1,17},{9,25},{17,1},{25,9},{2,18},{10... | collective-permute-start | bytes 1179656 | tf_op jit(solution)/shard_map/ppermute | solution.py:264
  30.2 11.2 %collective-permute-start.6 = (bf16[128,1536]{1,0:T(8,128)(2,1)S(1)}, bf16[128,1536]{1,0:T(8,128)(2,1)S(1)}, u32[]{:S(2)}, u32[]{:S(2)}) collective-permute-start(bf16[128,1536]{1,0:T(8,128)(2,1)S(1)} %get-tuple-element.103), channel_id=1, source_target_pairs={{0,8},{8,0},{16,24},{24,16},{1,9},{9,1},{17,25},{25,17},{2,10},{10... | collective-permute-start | bytes 1179656 | tf_op jit(solution)/shard_map/ppermute | solution.py:264
  34.4 1.6 %collective-permute-start.10 = (bf16[256,512]{1,0:T(8,128)(2,1)S(1)}, bf16[256,512]{1,0:T(8,128)(2,1)S(1)}, u32[]{:S(2)}, u32[]{:S(2)}) collective-permute-start(bf16[256,512]{1,0:T(8,128)(2,1)S(1)} %get-tuple-element.112), channel_id=1, source_target_pairs={{0,1},{1,0},{2,3},{3,2},{4,5},{5,4},{6,7},{7,6},{8,9},{9,8},{10,11... | collective-permute-start | bytes 786440 | tf_op jit(solution)/shard_map/ppermute | solution.py:260
  34.4 1.9 %collective-permute-start.11 = (bf16[256,512]{1,0:T(8,128)(2,1)S(1)}, bf16[256,512]{1,0:T(8,128)(2,1)S(1)}, u32[]{:S(2)}, u32[]{:S(2)}) collective-permute-start(bf16[256,512]{1,0:T(8,128)(2,1)S(1)} %get-tuple-element.113), channel_id=1, source_target_pairs={{0,1},{1,0},{2,3},{3,2},{4,5},{5,4},{6,7},{7,6},{8,9},{9,8},{10,11... | collective-permute-start | bytes 786440 | tf_op jit(solution)/shard_map/ppermute | solution.py:260
  34.9 1.8 %collective-permute-start.12 = (bf16[256,512]{1,0:T(8,128)(2,1)S(1)}, bf16[256,512]{1,0:T(8,128)(2,1)S(1)}, u32[]{:S(2)}, u32[]{:S(2)}) collective-permute-start(bf16[256,512]{1,0:T(8,128)(2,1)S(1)} %get-tuple-element.114), channel_id=1, source_target_pairs={{0,1},{1,0},{2,3},{3,2},{4,5},{5,4},{6,7},{7,6},{8,9},{9,8},{10,11... | collective-permute-start | bytes 786440 | tf_op jit(solution)/shard_map/ppermute | solution.py:260
  36.8 13.9 %collective-permute-start.18 = (bf16[256,768]{1,0:T(8,128)(2,1)S(1)}, bf16[256,768]{1,0:T(8,128)(2,1)S(1)}, u32[]{:S(2)}, u32[]{:S(2)}) collective-permute-start(bf16[256,768]{1,0:T(8,128)(2,1)S(1)} %get-tuple-element.131), channel_id=1, source_target_pairs={{0,4},{2,0},{6,2},{4,6},{1,5},{3,1},{7,3},{5,7},{8,12},{10,8},{14,... | collective-permute-start | bytes 1179656 | tf_op jit(solution)/shard_map/ppermute | solution.py:374
  41.5 7.9 %collective-permute-start.13 = (bf16[64,1536]{1,0:T(8,128)(2,1)S(1)}, bf16[64,1536]{1,0:T(8,128)(2,1)S(1)}, u32[]{:S(2)}, u32[]{:S(2)}) collective-permute-start(bf16[64,1536]{1,0:T(8,128)(2,1)S(1)} %get-tuple-element.117), channel_id=1, source_target_pairs={{0,16},{8,24},{16,0},{24,8},{1,17},{9,25},{17,1},{25,9},{2,18},{10... | collective-permute-start | bytes 589832 | tf_op jit(solution)/shard_map/ppermute | solution.py:264
  41.8 7.8 %collective-permute-start.14 = (bf16[64,1536]{1,0:T(8,128)(2,1)S(1)}, bf16[64,1536]{1,0:T(8,128)(2,1)S(1)}, u32[]{:S(2)}, u32[]{:S(2)}) collective-permute-start(bf16[64,1536]{1,0:T(8,128)(2,1)S(1)} %get-tuple-element.118), channel_id=1, source_target_pairs={{0,8},{8,0},{16,24},{24,16},{1,9},{9,1},{17,25},{25,17},{2,10},{10... | collective-permute-start | bytes 589832 | tf_op jit(solution)/shard_map/ppermute | solution.py:264
  42.9 14.1 %collective-permute-start.15 = (bf16[128,1536]{1,0:T(8,128)(2,1)S(1)}, bf16[128,1536]{1,0:T(8,128)(2,1)S(1)}, u32[]{:S(2)}, u32[]{:S(2)}) collective-permute-start(bf16[128,1536]{1,0:T(8,128)(2,1)S(1)} %get-tuple-element.121), channel_id=1, source_target_pairs={{0,8},{8,0},{16,24},{24,16},{1,9},{9,1},{17,25},{25,17},{2,10},{10... | collective-permute-start | bytes 1179656 | tf_op jit(solution)/shard_map/ppermute | solution.py:264
  43.8 13.2 %collective-permute-start.16 = (bf16[128,1536]{1,0:T(8,128)(2,1)S(1)}, bf16[128,1536]{1,0:T(8,128)(2,1)S(1)}, u32[]{:S(2)}, u32[]{:S(2)}) collective-permute-start(bf16[128,1536]{1,0:T(8,128)(2,1)S(1)} %get-tuple-element.122), channel_id=1, source_target_pairs={{0,16},{8,24},{16,0},{24,8},{1,17},{9,25},{17,1},{25,9},{2,18},{10... | collective-permute-start | bytes 1179656 | tf_op jit(solution)/shard_map/ppermute | solution.py:264
  50.6 1.6 %collective-permute-start.17 = (bf16[256,512]{1,0:T(8,128)(2,1)S(1)}, bf16[256,512]{1,0:T(8,128)(2,1)S(1)}, u32[]{:S(2)}, u32[]{:S(2)}) collective-permute-start(bf16[256,512]{1,0:T(8,128)(2,1)S(1)} %get-tuple-element.128), channel_id=1, source_target_pairs={{0,1},{1,0},{2,3},{3,2},{4,5},{5,4},{6,7},{7,6},{8,9},{9,8},{10,11... | collective-permute-start | bytes 786440 | tf_op jit(solution)/shard_map/ppermute | solution.py:260
  53.3 8.9 %collective-permute-start.21 = (bf16[1040,128]{1,0:T(8,128)(2,1)S(1)}, bf16[1040,128]{1,0:T(8,128)(2,1)S(1)}, u32[]{:S(2)}, u32[]{:S(2)}) collective-permute-start(bf16[1040,128]{1,0:T(8,128)(2,1)S(1)} %get-tuple-element.141.refs_0_), channel_id=1, source_target_pairs={{0,8},{8,0},{16,24},{24,16},{1,9},{9,1},{17,25},{25,17},{2,10},{10... | collective-permute-start | bytes 798728 | tf_op jit(solution)/shard_map/ppermute | solution.py:264
  54.5 13.7 %collective-permute-start.20 = (bf16[256,768]{1,0:T(8,128)(2,1)S(1)}, bf16[256,768]{1,0:T(8,128)(2,1)S(1)}, u32[]{:S(2)}, u32[]{:S(2)}) collective-permute-start(bf16[256,768]{1,0:T(8,128)(2,1)S(1)} %get-tuple-element.138), channel_id=1, source_target_pairs={{0,4},{2,0},{6,2},{4,6},{1,5},{3,1},{7,3},{5,7},{8,12},{10,8},{14,... | collective-permute-start | bytes 1179656 | tf_op jit(solution)/shard_map/ppermute | solution.py:374
  57.9 10.3 %collective-permute-start.19 = (bf16[256,768]{1,0:T(8,128)(2,1)S(1)}, bf16[256,768]{1,0:T(8,128)(2,1)S(1)}, u32[]{:S(2)}, u32[]{:S(2)}) collective-permute-start(bf16[256,768]{1,0:T(8,128)(2,1)S(1)} %get-tuple-element.137), channel_id=1, source_target_pairs={{0,1},{1,0},{2,3},{3,2},{4,5},{5,4},{6,7},{7,6},{8,9},{9,8},{10,11... | collective-permute-start | bytes 1179656 | tf_op jit(solution)/shard_map/ppermute | solution.py:260
  58.0 14.2 %collective-permute-start.25 = (bf16[128,1536]{1,0:T(8,128)(2,1)S(1)}, bf16[128,1536]{1,0:T(8,128)(2,1)S(1)}, u32[]{:S(2)}, u32[]{:S(2)}) collective-permute-start(bf16[128,1536]{1,0:T(8,128)(2,1)S(1)} %get-tuple-element.155), channel_id=1, source_target_pairs={{0,16},{8,24},{16,0},{24,8},{1,17},{9,25},{17,1},{25,9},{2,18},{10... | collective-permute-start | bytes 1179656 | tf_op jit(solution)/shard_map/ppermute | solution.py:264
  59.8 13.5 %collective-permute-start.26 = (bf16[128,1536]{1,0:T(8,128)(2,1)S(1)}, bf16[128,1536]{1,0:T(8,128)(2,1)S(1)}, u32[]{:S(2)}, u32[]{:S(2)}) collective-permute-start(bf16[128,1536]{1,0:T(8,128)(2,1)S(1)} %get-tuple-element.156), channel_id=1, source_target_pairs={{0,8},{8,0},{16,24},{24,16},{1,9},{9,1},{17,25},{25,17},{2,10},{10... | collective-permute-start | bytes 1179656 | tf_op jit(solution)/shard_map/ppermute | solution.py:264
  62.3 13.8 %collective-permute-start.24 = (bf16[1024,128]{1,0:T(8,128)(2,1)S(1)}, bf16[1024,128]{1,0:T(8,128)(2,1)S(1)}, u32[]{:S(2)}, u32[]{:S(2)}) collective-permute-start(bf16[1024,128]{1,0:T(8,128)(2,1)S(1)} %get-tuple-element.151), channel_id=1, source_target_pairs={{16,0},{24,8},{17,1},{25,9},{18,2},{26,10},{19,3},{27,11},{20,4},{... | collective-permute-start | bytes 786440 | tf_op jit(solution)/shard_map/ppermute | solution.py:559
  68.9 8.8 %collective-permute-start.22 = (bf16[256,768]{1,0:T(8,128)(2,1)S(1)}, bf16[256,768]{1,0:T(8,128)(2,1)S(1)}, u32[]{:S(2)}, u32[]{:S(2)}) collective-permute-start(bf16[256,768]{1,0:T(8,128)(2,1)S(1)} %get-tuple-element.149), channel_id=1, source_target_pairs={{0,1},{1,0},{2,3},{3,2},{4,5},{5,4},{6,7},{7,6},{8,9},{9,8},{10,11... | collective-permute-start | bytes 1179656 | tf_op jit(solution)/shard_map/ppermute | solution.py:260
  69.0 12.1 %collective-permute-start.23 = (bf16[256,768]{1,0:T(8,128)(2,1)S(1)}, bf16[256,768]{1,0:T(8,128)(2,1)S(1)}, u32[]{:S(2)}, u32[]{:S(2)}) collective-permute-start(bf16[256,768]{1,0:T(8,128)(2,1)S(1)} %get-tuple-element.150), channel_id=1, source_target_pairs={{0,4},{2,0},{6,2},{4,6},{1,5},{3,1},{7,3},{5,7},{8,12},{10,8},{14,... | collective-permute-start | bytes 1179656 | tf_op jit(solution)/shard_map/ppermute | solution.py:374
  72.1 11.2 %collective-permute-start.27 = (bf16[128,1536]{1,0:T(8,128)(2,1)S(1)}, bf16[128,1536]{1,0:T(8,128)(2,1)S(1)}, u32[]{:S(2)}, u32[]{:S(2)}) collective-permute-start(bf16[128,1536]{1,0:T(8,128)(2,1)S(1)} %get-tuple-element.165), channel_id=1, source_target_pairs={{0,8},{8,0},{16,24},{24,16},{1,9},{9,1},{17,25},{25,17},{2,10},{10... | collective-permute-start | bytes 1179656 | tf_op jit(solution)/shard_map/ppermute | solution.py:264
  73.3 11.8 %collective-permute-start.28 = (bf16[128,1536]{1,0:T(8,128)(2,1)S(1)}, bf16[128,1536]{1,0:T(8,128)(2,1)S(1)}, u32[]{:S(2)}, u32[]{:S(2)}) collective-permute-start(bf16[128,1536]{1,0:T(8,128)(2,1)S(1)} %get-tuple-element.166), channel_id=1, source_target_pairs={{0,16},{8,24},{16,0},{24,8},{1,17},{9,25},{17,1},{25,9},{2,18},{10... | collective-permute-start | bytes 1179656 | tf_op jit(solution)/shard_map/ppermute | solution.py:264

commit v5 on v4

--- a/solution.py
+++ b/solution.py
@@ -12,7 +12,7 @@
 F32 = jnp.float32
 BF16 = jnp.bfloat16
 EXTRA = 16
-C_JOIN, C26, C17, C20, C24 = 1070000000, 642000000, 1284000000, 1070000000, 2140000000
+C_JOIN, C26, C17, C20, C24 = 1070000000, 642000000, 1284000000, 642000000, 2140000000
 
 
 def contract(a, b, dim_a, dim_b):
@@ -209,21 +209,26 @@
     store_decay(state_ref, row_ref[...], groups)
 
 
-def back_intra_kernel(
-    groups, grad_ref, q_ref, k_ref, v_ref, row_ref, col_ref, low_ref, qgrad_ref, kpart_ref, vpart_ref
-):
+def back_key_kernel(groups, grad_ref, q_ref, v_ref, row_ref, col_ref, dprobs_ref, kpart_ref):
+    lower = lower_mask(q_ref.shape[0])
+    for h in range(groups):
+        weights = spread_weights(row_ref, col_ref, lower, h)
+        dprobs = (contract(head(grad_ref, h), head(v_ref, h), 1, 1) * SCALE * weights).astype(BF16)
+        dprobs_ref[h] = dprobs
+        kpart_ref[:, h * DH : (h + 1) * DH] = contract(dprobs, head(q_ref, h), 0, 0)
+
+
+def back_query_kernel(groups, grad_ref, q_ref, k_ref, row_ref, col_ref, low_ref, dprobs_ref, qgrad_ref, vpart_ref):
     lower = lower_mask(q_ref.shape[0])
     factor = jnp.exp(col_ref[...]) * SCALE
     for h in range(groups):
         here = slice(h * DH, (h + 1) * DH)
         grad = head(grad_ref, h)
-        weights = spread_weights(row_ref, col_ref, lower, h)
-        dprobs = (contract(grad, head(v_ref, h), 1, 1) * SCALE * weights).astype(BF16)
         qgrad_ref[:, here] = (
-            contract(dprobs, head(k_ref, h), 1, 0) + contract(grad, low_ref[h], 1, 1) * factor[:, h : h + 1]
+            contract(dprobs_ref[h], head(k_ref, h), 1, 0)
+            + contract(grad, low_ref[h], 1, 1) * factor[:, h : h + 1]
         ).astype(BF16)
-        kpart_ref[:, here] = contract(dprobs, head(q_ref, h), 0, 0)
-        probs = probs_of(q_ref, k_ref, weights, h)
+        probs = probs_of(q_ref, k_ref, spread_weights(row_ref, col_ref, lower, h), h)
         vpart_ref[:, here] = contract(probs, grad, 0, 0)
 
 
@@ -330,32 +335,23 @@
 
 def weight_kernel(blocks, a_own, a_other, g_own, g_other, *outs):
     rows = a_own.shape[1] // 4
-    for (k, left, right), out in zip(blocks, outs):
-        here = slice(k * rows, (k + 1) * rows)
-        out[...] = (
-            contract(a_own[:, here], g_own[:, left:right], 0, 0)
-            + contract(a_other[:, here], g_other[:, left:right], 0, 0)
-        ).astype(out.dtype)
-
-
-def onward_kernel(mid_left, mid_right, far_left, far_right, left_ref, right_ref):
-    left_ref[...] = (mid_left[...] + far_left[...].astype(F32)).astype(BF16)
-    right_ref[...] = (mid_right[...] + far_right[...].astype(F32)).astype(BF16)
-
-
-def total_kernel(parts, own_ref, *refs):
-    half = own_ref.shape[1] // 2
-    out_ref = refs[-1]
-    sides = [own_ref[:, :half], own_ref[:, half:]]
-    for left, ref in zip(parts, refs[:-1]):
-        sides[left] = sides[left] + ref[...].astype(F32)
-    out_ref[:, :half], out_ref[:, half:] = sides
-
-
-def back_pair_kernel(groups, own_ref, near_ref, left_ref, right_ref, out_ref, left_again, right_again):
-    left_again[...] = left_ref[...]
-    right_again[...] = right_ref[...]
-    pair_kernel(groups, False, own_ref, near_ref, out_ref)
+    for stack, out in zip(blocks, outs):
+        for i, (k, left, right) in enumerate(stack):
+            here = slice(k * rows, (k + 1) * rows)
+            out[i * rows : (i + 1) * rows] = (
+                contract(a_own[:, here], g_own[:, left:right], 0, 0)
+                + contract(a_other[:, here], g_other[:, left:right], 0, 0)
+            ).astype(out.dtype)
+
+
+def onward_kernel(mid_ref, far_ref, out_ref):
+    out_ref[...] = (mid_ref[...] + far_ref[: mid_ref.shape[0]].astype(F32)).astype(BF16)
+
+
+def total_kernel(own_ref, left_ref, right_ref, out_ref):
+    rows, half = own_ref.shape[0], own_ref.shape[1] // 2
+    for here, ref in ((slice(0, half), left_ref), (slice(half, 2 * half), right_ref)):
+        out_ref[:, here] = own_ref[:, here] + ref[ref.shape[0] - rows :].astype(F32)
 
 
 def ring_kernel(j, count, own_ref, *refs):
@@ -507,11 +503,13 @@
 
     if four:
         small = lambda dtype: struct((rows, middle), dtype)
+        left, right = (0, middle), (middle, width)
         blocks = [
-            (3, 0, middle), (3, middle, width), (2, 0, middle), (1, middle, width), (1, 0, middle), (2, middle, width), (0, 0, width),
+            [(3, *left)], [(3, *right), (2, *right)], [(1, *left)], [(2, *left)], [(1, *right)], [(0, 0, width)],
         ]
-        *far, mid_left, mid_right, near_left, near_right, own_sum = weights(
-            blocks, [small(BF16)] * 2 + [small(F32)] * 2 + [small(BF16)] * 2 + [struct((rows, width), F32)]
+        far_left, both_right, near_left, mid_left, mid_right, own_sum = weights(
+            blocks,
+            [small(BF16), struct((2 * rows, middle), BF16), small(BF16), small(F32), small(F32), struct((rows, width), F32)],
         )
     terms = mix([first], 0, near_heads, 3 if four else 1)
     arrived = passed(ring(terms[0]))
@@ -519,7 +517,7 @@
         rest_one, rest_two = flipped(w_again, 1), flipped(w_again, 2)
         on_one, on_two = step(rows_kernel, [lower(w_rest)] * 2, rest_one, rest_two)
         rest = [w_rest, rest_one, rest_two, flipped(on_one, 2), flipped(on_two, 1)]
-        far_left, far_right = flipped(far[0], 1), flipped(far[1], 2)
+        far_left, both_right, near_left = flipped(far_left, 1), flipped(both_right, 2), flipped(near_left, 1)
         grad_own, grad_away = grad_of(rest[3:], 3 * rows, *grad_of(rest[:3], 0))
     else:
         grad_own, grad_away = grad_of(rest, 0)
@@ -542,38 +540,41 @@
     else:
         after = hops_of(back, False)
     if four:
-        to_left, to_right = step(onward_kernel, [small(BF16)] * 2, mid_left, mid_right, far_left, far_right)
-        on_right = flipped(to_right, 1)
-        near_right = flipped(near_right, 2)
+        on_left = flipped(step(onward_kernel, small(BF16), mid_left, far_left), 2)
     terms = mix(rest, 0, 1)
     if four:
-        pair, near_left, to_left = step(
-            functools.partial(back_pair_kernel, groups),
-            [struct((features, DH), BF16), small(BF16), small(BF16)],
-            back,
-            near,
-            near_left,
-            to_left,
-            work=C20,
+        pair = step(
+            functools.partial(pair_kernel, groups, False), struct((features, DH), BF16), back, near, work=C20
         )
         after = [near, lax.ppermute(pair, "ctx", [(2, 0), (3, 1)])]
-        near_left, on_left = flipped(near_left, 1), flipped(to_left, 2)
-    query_grad, key_part, value_part = step(
-        functools.partial(back_intra_kernel, groups),
-        (flat(BF16), flat(F32), flat(F32)),
+    dprobs, key_part = step(
+        functools.partial(back_key_kernel, groups),
+        (struct((groups, size, size), BF16), flat(F32)),
         grad,
         q,
-        k,
         v,
         row,
         col,
-        low,
     )
     for j in range(1, heads - near_heads):
         arrived = passed(ring(terms[0], arrived))
-        terms = mix(rest, j, 1)
-    if four:
-        own_sum = step(functools.partial(total_kernel, (1, 1)), struct((rows, width), F32), own_sum, near_right, on_right)
+        if four and j == 1:
+            on_right = flipped(step(onward_kernel, small(BF16), mid_right, both_right), 1)
+        if j == 1:
+            query_grad, value_part = step(
+                functools.partial(back_query_kernel, groups),
+                (flat(BF16), flat(F32)),
+                grad,
+                q,
+                k,
+                row,
+                col,
+                low,
+                dprobs,
+            )
+        terms = mix(rest, j, 1, 2 if four else 1)
+    if four:
+        own_sum = step(total_kernel, struct((rows, width), F32), own_sum, near_left, both_right)
     key_grad, value_grad = step(
         functools.partial(back_inter_kernel, groups, len(after)),
         (flat(BF16), flat(BF16)),
@@ -587,7 +588,7 @@
     )
     mixed = ring(terms[0], arrived, work=C26)
     if four:
-        w_grad = step(functools.partial(total_kernel, (0, 0)), struct((rows, width), F32), own_sum, near_left, on_left)
+        w_grad = step(total_kernel, struct((rows, width), F32), own_sum, on_left, on_right)
     else:
         w_grad = contract(a_own, g, 0, 0) + contract(a_other, g_other, 0, 0)
         w_grad = lax.psum_scatter(w_grad.astype(BF16), "ctx", scatter_dimension=0, tiled=True).astype(F32)

time: 86.8 us -> 82.2 us (0.947)
  waiting for transfers between devices: 19.3 us -> 16.4 us
  starting transfers between devices: 38.6 us -> 37 us
    ppermute x3, waiting for transfers between devices: 3.37 us -> 0.08 us  [passed(): return lax.ppermute(array, 'head', pairs)]
    ppermute x16 -> x15, starting transfers between devices: 23.5 us -> 21 us  [flipped(): return lax.ppermute(array, 'ctx', [(i, i ^ bit) for i in range(4)])]
    ppermute x8 -> x9, starting transfers between devices: 1.45 us -> 2.01 us  [swapped(): return lax.ppermute(array, 'dp', [(0, 1), (1, 0)])]
    ppermute x16 -> x15, waiting for transfers between devices: 12.8 us -> 13.2 us  [flipped(): return lax.ppermute(array, 'ctx', [(i, i ^ bit) for i in range(4)])]
    pallas_call x26 -> x28, Pallas kernels: 25.7 us -> 25.6 us  [call(): pl.pallas_call(body, name=getattr(kernel, 'func', kernel).__name__, out_s...]
    ppermute x8 -> x9, waiting for transfers between devices: 3.06 us -> 3.06 us  [swapped(): return lax.ppermute(array, 'dp', [(0, 1), (1, 0)])]
  transfers between devices with their start and end apart: 29 -> 29, of which waited for: 14 -> 13; matrix products, arithmetic and copies ran while one was open for 0% -> 0% of each run, Pallas kernels for 28% -> 30%
where the time goes in v5:
time: 82.2 us; the launch traced here: 81.9 us
  starting transfers between devices  37 us (45%)
  Pallas kernels  25.6 us (31%)
  waiting for transfers between devices  16.4 us (20%)
  local copies, waits for them, and re-layouts  1.68 us (2%)
  between operations  1.23 us (1%)
    pallas_call x28, Pallas kernels, call(): pl.pallas_call(body, name=getattr(kernel, 'func', kernel).__name__, out_s...  25.6 us
    ppermute x15, starting transfers between devices, flipped(): return lax.ppermute(array, 'ctx', [(i, i ^ bit) for i in range(4)])  21 us
    ppermute x15, waiting for transfers between devices, flipped(): return lax.ppermute(array, 'ctx', [(i, i ^ bit) for i in range(4)])  13.2 us
    ppermute x3, starting transfers between devices, passed(): return lax.ppermute(array, 'head', pairs)  8.67 us
    ppermute x1, starting transfers between devices, shards(): before = [near, lax.ppermute(pair, 'ctx', [(0, 2), (1, 3)])]  3.89 us
    ppermute x9, waiting for transfers between devices, swapped(): return lax.ppermute(array, 'dp', [(0, 1), (1, 0)])  3.06 us
    ppermute x9, starting transfers between devices, swapped(): return lax.ppermute(array, 'dp', [(0, 1), (1, 0)])  2.01 us
    unnamed x18, local copies, waits for them, and re-layouts  1.68 us
  transfers between devices with their start and end apart: 29, of which 13 were waited for; matrix products, arithmetic and copies ran while one was open for 0% of the time, Pallas kernels for 30%

profile of v5, /device:TPU:0, one launch (start us, length us, event | category | flops | bytes accessed | tf_op | source)
XLA Modules:
  0.0 81.9 jit_solution(2020015650877909177)
XLA Ops:
  0.6 0.5 collective-permute-start.2
  1.2 3.5 %contrib_kernel.1 = (bf16[1040,128]{1,0:T(8,128)(2,1)}, f32[8,128]{1,0:T(8,128)}) custom-call(bf16[256,1024]{1,0:T(8,128)(2,1)} %bitcast.20, bf16[256,1024]{1,0:T(8,128)(2,1)} %bitcast.16, f32[8,256]{1,0:T(8,128)} %bitcast.26), custom_call_target="tpu_custom_call" | custom-call | tf_op jit(solution)/shard_map/contrib_kernel/pallas_call | solution.py:45
  4.7 2.6 %collective-permute-start = (bf16[1040,128]{1,0:T(8,128)(2,1)}, bf16[1040,128]{1,0:T(8,128)(2,1)S(1)}, u32[]{:S(2)}, u32[]{:S(2)}) collective-permute-start(bf16[1040,128]{1,0:T(8,128)(2,1)} %get-tuple-element.88.refs_0_), channel_id=1, source_target_pairs={{0,8},{8,0},{16,24},{24,16},{1,9},{9,1},{17,25},{25,17},{2,10},{10... | collective-permute-start | bytes 798728 | tf_op jit(solution)/shard_map/ppermute | solution.py:269
  7.3 2.1 %columns_kernel.1 = (bf16[128,1536]{1,0:T(8,128)(2,1)}, bf16[128,1536]{1,0:T(8,128)(2,1)}, f32[8,128]{1,0:T(8,128)}) custom-call(bf16[128,3072]{1,0:T(8,128)(2,1)} %bitcast.28, f32[8,128]{1,0:T(8,128)} %get-tuple-element.89.refs_1_), custom_call_target="tpu_custom_call" | custom-call | tf_op jit(solution)/shard_map/columns_kernel/pallas_call | solution.py:45
  9.4 1.6 %collective-permute-start.4 = (bf16[128,1536]{1,0:T(8,128)(2,1)}, bf16[128,1536]{1,0:T(8,128)(2,1)S(1)}, u32[]{:S(2)}, u32[]{:S(2)}) collective-permute-start(bf16[128,1536]{1,0:T(8,128)(2,1)} %get-tuple-element.98.refs_0_), channel_id=1, source_target_pairs={{0,16},{8,24},{16,0},{24,8},{1,17},{9,25},{17,1},{25,9},{2,18},{10... | collective-permute-start | bytes 1179656 | tf_op jit(solution)/shard_map/ppermute | solution.py:269
  11.0 0.5 collective-permute-start.3
  11.6 3.2 %collective-permute-done.refs_1_.refs_0_ = bf16[1040,128]{1,0:T(8,128)(2,1)S(1)} collective-permute-done((bf16[1040,128]{1,0:T(8,128)(2,1)}, bf16[1040,128]{1,0:T(8,128)(2,1)S(1)}, u32[]{:S(2)}, u32[]{:S(2)}) %collective-permute-start) | collective-permute-done | bytes 266272 | tf_op jit(solution)/shard_map/ppermute | solution.py:269
  14.8 0.9 %copy-done.5 = bf16[1040,128]{1,0:T(8,128)(2,1)S(1)} copy-done((bf16[1040,128]{1,0:T(8,128)(2,1)S(1)}, bf16[1040,128]{1,0:T(8,128)(2,1)}, u32[]{:S(2)}) %copy-start.5) | copy-done | bytes 266264
  15.7 0.7 copy-done.7
  16.4 0.1 pair_kernel.2
  16.5 3.9 %collective-permute-start.1 = (bf16[1024,128]{1,0:T(8,128)(2,1)S(1)}, bf16[1024,128]{1,0:T(8,128)(2,1)S(1)}, u32[]{:S(2)}, u32[]{:S(2)}) collective-permute-start(bf16[1024,128]{1,0:T(8,128)(2,1)S(1)} %get-tuple-element.91), channel_id=1, source_target_pairs={{0,16},{8,24},{1,17},{9,25},{2,18},{10,26},{3,19},{11,27},{4,20},{... | collective-permute-start | bytes 786440 | tf_op jit(solution)/shard_map/ppermute | solution.py:426
  20.4 0.4 picks_kernel.1
  20.9 1.3 %intra_kernel.1 = (f32[8,256]{1,0:T(8,128)S(1)}, f32[256,8]{1,0:T(8,128)S(1)}, f32[256,1024]{1,0:T(8,128)S(1)}, f32[8,128]{1,0:T(8,128)S(1)}) custom-call(bf16[256,1024]{1,0:T(8,128)(2,1)S(1)} %bitcast.11, bf16[256,1024]{1,0:T(8,128)(2,1)S(1)} %bitcast.21, bf16[256,1024]{1,0:T(8,128)(2,1)S(1)} %bitcast.17, f32[8,256]{1,0:T(8,128)S(1)} %bitcast.27, ...), custom_call_target="tpu_custom_call" | custom-call | tf_op jit(solution)/shard_map/intra_kernel/pallas_call | solution.py:45
  22.2 0.8 collective-permute-done.3.refs_0_.refs_1_
  23.1 1.8 %collective-permute-start.8 = (bf16[64,1536]{1,0:T(8,128)(2,1)S(1)}, bf16[64,1536]{1,0:T(8,128)(2,1)S(1)}, u32[]{:S(2)}, u32[]{:S(2)}) collective-permute-start(bf16[64,1536]{1,0:T(8,128)(2,1)S(1)} %get-tuple-element.105), channel_id=1, source_target_pairs={{0,16},{8,24},{16,0},{24,8},{1,17},{9,25},{17,1},{25,9},{2,18},{10... | collective-permute-start | bytes 589832 | tf_op jit(solution)/shard_map/ppermute | solution.py:269
  24.9 1.5 %collective-permute-start.9 = (bf16[64,1536]{1,0:T(8,128)(2,1)S(1)}, bf16[64,1536]{1,0:T(8,128)(2,1)S(1)}, u32[]{:S(2)}, u32[]{:S(2)}) collective-permute-start(bf16[64,1536]{1,0:T(8,128)(2,1)S(1)} %get-tuple-element.106), channel_id=1, source_target_pairs={{0,8},{8,0},{16,24},{24,16},{1,9},{9,1},{17,25},{25,17},{2,10},{10... | collective-permute-start | bytes 589832 | tf_op jit(solution)/shard_map/ppermute | solution.py:269
  26.4 1.2 %attended_kernel.1 = (bf16[256,512]{1,0:T(8,128)(2,1)S(1)}, bf16[256,512]{1,0:T(8,128)(2,1)S(1)}, bf16[8,128,128]{2,1,0:T(8,128)(2,1)S(1)}, bf16[256,3072]{1,0:T(8,128)(2,1)S(1)}, f32[8,128]{1,0:T(8,128)S(1)}) custom-call(bf16[1040,128]{1,0:T(8,128)(2,1)S(1)} %collective-permute-done.refs_1_.refs_0_, bf16[1024,128]{1,0:T(8,128)(2,1)S(1)} %collective-permute-done.1.refs_1_, ...), custom_call_target="tpu_custom_call" | custom-call | tf_op jit(solution)/shard_map/attended_kernel/pallas_call | solution.py:45
  27.7 2.5 %collective-permute-start.7 = (bf16[128,1536]{1,0:T(8,128)(2,1)S(1)}, bf16[128,1536]{1,0:T(8,128)(2,1)S(1)}, u32[]{:S(2)}, u32[]{:S(2)}) collective-permute-start(bf16[128,1536]{1,0:T(8,128)(2,1)S(1)} %get-tuple-element.104), channel_id=1, source_target_pairs={{0,16},{8,24},{16,0},{24,8},{1,17},{9,25},{17,1},{25,9},{2,18},{10... | collective-permute-start | bytes 1179656 | tf_op jit(solution)/shard_map/ppermute | solution.py:269
  30.2 1.1 %collective-permute-start.6 = (bf16[128,1536]{1,0:T(8,128)(2,1)S(1)}, bf16[128,1536]{1,0:T(8,128)(2,1)S(1)}, u32[]{:S(2)}, u32[]{:S(2)}) collective-permute-start(bf16[128,1536]{1,0:T(8,128)(2,1)S(1)} %get-tuple-element.104), channel_id=1, source_target_pairs={{0,8},{8,0},{16,24},{24,16},{1,9},{9,1},{17,25},{25,17},{2,10},{10... | collective-permute-start | bytes 1179656 | tf_op jit(solution)/shard_map/ppermute | solution.py:269
  31.4 0.1 join_kernel.1
  31.5 1.8 %weight_kernel.1 = (bf16[128,1536]{1,0:T(8,128)(2,1)S(1)}, bf16[256,1536]{1,0:T(8,128)(2,1)S(1)}, bf16[128,1536]{1,0:T(8,128)(2,1)S(1)}, f32[128,1536]{1,0:T(8,1...) custom-call(bf16[256,512]{1,0:T(8,128)(2,1)S(1)} %get-tuple-element.102.refs_0_, ...), custom_call_target="tpu_custom_call" | custom-call | tf_op jit(solution)/shard_map/weight_kernel/pallas_call | solution.py:45
  33.4 1.0 %mix_kernel.3 = (f32[256,768]{1,0:T(8,128)S(1)}, f32[256,768]{1,0:T(8,128)S(1)}, bf16[256,512]{1,0:T(8,128)(2,1)S(1)}, bf16[256,512]{1,0:T(8,128)(2,1)S(1)}, bf1...) custom-call(bf16[256,512]{1,0:T(8,128)(2,1)S(1)} %get-tuple-element.102.refs_0_, ...), custom_call_target="tpu_custom_call" | custom-call | tf_op jit(solution)/shard_map/mix_kernel/pallas_call | solution.py:45
  34.4 0.5 collective-permute-start.11
  34.9 0.1 collective-permute-start.12
  35.0 0.9 %collective-permute-done.10.refs_1_ = bf16[256,512]{1,0:T(8,128)(2,1)S(1)} collective-permute-done((bf16[256,512]{1,0:T(8,128)(2,1)S(1)}, bf16[256,512]{1,0:T(8,128)(2,1)S(1)}, u32[]{:S(2)}, u32[]{:S(2)}) %collective-permute-start.10) | collective-permute-done | bytes 262176 | tf_op jit(solution)/shard_map/ppermute | solution.py:265
  36.0 0.4 collective-permute-done.11.refs_2_
  36.3 0.4 collective-permute-done.12.refs_3_
  36.7 0.1 ring_kernel.4
  36.8 2.6 %collective-permute-start.16 = (bf16[256,768]{1,0:T(8,128)(2,1)S(1)}, bf16[256,768]{1,0:T(8,128)(2,1)S(1)}, u32[]{:S(2)}, u32[]{:S(2)}) collective-permute-start(bf16[256,768]{1,0:T(8,128)(2,1)S(1)} %get-tuple-element.128), channel_id=1, source_target_pairs={{0,4},{2,0},{6,2},{4,6},{1,5},{3,1},{7,3},{5,7},{8,12},{10,8},{14,... | collective-permute-start | bytes 1179656 | tf_op jit(solution)/shard_map/ppermute | solution.py:370
  39.4 0.5 collective-permute-done.7.refs_1_.refs_5_.refs_4_
  39.9 1.5 %collective-permute-done.6.refs_0_.refs_4_.refs_3_ = bf16[128,1536]{1,0:T(8,128)(2,1)S(1)} collective-permute-done((bf16[128,1536]{1,0:T(8,128)(2,1)S(1)}, bf16[128,1536]{1,0:T(8,128)(2,1)S(1)}, u32[]{:S(2)}, u32[]{:S(2)}) %collective-permute-start.6) | collective-permute-done | bytes 393248 | tf_op jit(solution)/shard_map/ppermute | solution.py:269
  41.5 0.3 collective-permute-start.13
  41.8 1.1 %collective-permute-start.14 = (bf16[64,1536]{1,0:T(8,128)(2,1)S(1)}, bf16[64,1536]{1,0:T(8,128)(2,1)S(1)}, u32[]{:S(2)}, u32[]{:S(2)}) collective-permute-start(bf16[64,1536]{1,0:T(8,128)(2,1)S(1)} %get-tuple-element.119), channel_id=1, source_target_pairs={{0,8},{8,0},{16,24},{24,16},{1,9},{9,1},{17,25},{25,17},{2,10},{10... | collective-permute-start | bytes 589832 | tf_op jit(solution)/shard_map/ppermute | solution.py:269
  42.9 0.9 %collective-permute-start.18 = (bf16[128,1536]{1,0:T(8,128)(2,1)S(1)}, bf16[128,1536]{1,0:T(8,128)(2,1)S(1)}, u32[]{:S(2)}, u32[]{:S(2)}) collective-permute-start(bf16[128,1536]{1,0:T(8,128)(2,1)S(1)} %get-tuple-element.135), channel_id=1, source_target_pairs={{0,8},{8,0},{16,24},{24,16},{1,9},{9,1},{17,25},{25,17},{2,10},{10... | collective-permute-start | bytes 1179656 | tf_op jit(solution)/shard_map/ppermute | solution.py:269
  43.8 1.7 %collective-permute-start.19 = (bf16[256,1536]{1,0:T(8,128)(2,1)S(1)}, bf16[256,1536]{1,0:T(8,128)(2,1)S(1)}, u32[]{:S(2)}, u32[]{:S(2)}) collective-permute-start(bf16[256,1536]{1,0:T(8,128)(2,1)S(1)} %get-tuple-element.142), channel_id=1, source_target_pairs={{0,16},{8,24},{16,0},{24,8},{1,17},{9,25},{17,1},{25,9},{2,18},{10... | collective-permute-start | bytes 2359304 | tf_op jit(solution)/shard_map/ppermute | solution.py:269
  45.6 1.8 %grad_kernel.2 = (bf16[256,384]{1,0:T(8,128)(2,1)S(1)}, bf16[256,384]{1,0:T(8,128)(2,1)S(1)}, f32[8,128]{1,0:T(8,128)S(1)}) custom-call(bf16[256,3072]{1,0:T(8,128)(2,1)S(1)} %get-tuple-element.109.refs_2_.refs_0_, bf16[256,3072]{1,0:T(8,128)(2,1)S(1)} %collective-permute-done.2.refs_1_.refs_3_, bf16[512,1536]{1,0:T(8,128)(2,1)S(1)} %get-tuple-element.108.refs_2_, ...), custom_call_target="tpu_custom_call" | custom-call | tf_op jit(solution)/shard_map/grad_kernel/pallas_call | solution.py:45
  47.4 2.0 %collective-permute-done.13.refs_3_.refs_5_ = bf16[64,1536]{1,0:T(8,128)(2,1)S(1)} collective-permute-done((bf16[64,1536]{1,0:T(8,128)(2,1)S(1)}, bf16[64,1536]{1,0:T(8,128)(2,1)S(1)}, u32[]{:S(2)}, u32[]{:S(2)}) %collective-permute-start.13) | collective-permute-done | bytes 196640 | tf_op jit(solution)/shard_map/ppermute | solution.py:269
  49.4 0.3 collective-permute-done.14.refs_4_.refs_6_
  49.6 1.0 %grad_kernel.3 = (bf16[256,512]{1,0:T(8,128)(2,1)S(1)}, bf16[256,512]{1,0:T(8,128)(2,1)S(1)}, f32[8,128]{1,0:T(8,128)S(1)}) custom-call(bf16[256,3072]{1,0:T(8,128)(2,1)S(1)} %get-tuple-element.109.refs_2_.refs_0_, bf16[256,3072]{1,0:T(8,128)(2,1)S(1)} %collective-permute-done.2.refs_1_.refs_3_, bf16[512,1536]{1,0:T(8,128)(2,1)S(1)} %get-tuple-element.108.refs_2_, ...), custom_call_target="tpu_custom_call" | custom-call | tf_op jit(solution)/shard_map/grad_kernel/pallas_call | solution.py:45
  50.7 0.1 ring_kernel.5
  50.9 1.4 %collective-permute-done.15.refs_1_ = bf16[256,512]{1,0:T(8,128)(2,1)S(1)} collective-permute-done((bf16[256,512]{1,0:T(8,128)(2,1)S(1)}, bf16[256,512]{1,0:T(8,128)(2,1)S(1)}, u32[]{:S(2)}, u32[]{:S(2)}) %collective-permute-start.15) | collective-permute-done | bytes 262176 | tf_op jit(solution)/shard_map/ppermute | solution.py:265
  52.2 1.0 %back_contrib_kernel.1 = (bf16[256,1024]{1,0:T(8,128)(2,1)S(1)}, bf16[1040,128]{1,0:T(8,128)(2,1)S(1)}, f32[8,128]{1,0:T(8,128)S(1)}) custom-call(bf16[256,512]{1,0:T(8,128)(2,1)S(1)} %get-tuple-element.124.refs_0_, bf16[256,512]{1,0:T(8,128)(2,1)S(1)} %collective-permute-done.15.refs_1_, bf16[1024,512]{1,0:T(8,128)(2,1)S(1)} %get-tuple-element.96.refs_5_.refs_2_, ...), custom_call_target="tpu_custom_call" | custom-call | tf_op jit(solution)/shard_map/back_contrib_kernel/pallas_call | solution.py:45
  53.3 1.2 %collective-permute-start.17 = (bf16[1040,128]{1,0:T(8,128)(2,1)S(1)}, bf16[1040,128]{1,0:T(8,128)(2,1)S(1)}, u32[]{:S(2)}, u32[]{:S(2)}) collective-permute-start(bf16[1040,128]{1,0:T(8,128)(2,1)S(1)} %get-tuple-element.133.refs_0_), channel_id=1, source_target_pairs={{0,8},{8,0},{16,24},{24,16},{1,9},{9,1},{17,25},{25,17},{2,10},{10... | collective-permute-start | bytes 798728 | tf_op jit(solution)/shard_map/ppermute | solution.py:269
  54.5 2.6 %collective-permute-start.21 = (bf16[256,768]{1,0:T(8,128)(2,1)S(1)}, bf16[256,768]{1,0:T(8,128)(2,1)S(1)}, u32[]{:S(2)}, u32[]{:S(2)}) collective-permute-start(bf16[256,768]{1,0:T(8,128)(2,1)S(1)} %get-tuple-element.145), channel_id=1, source_target_pairs={{0,4},{2,0},{6,2},{4,6},{1,5},{3,1},{7,3},{5,7},{8,12},{10,8},{14,... | collective-permute-start | bytes 1179656 | tf_op jit(solution)/shard_map/ppermute | solution.py:370
  57.1 0.1 onward_kernel.2
  57.2 0.6 mix_kernel.4
  57.9 0.9 %collective-permute-start.26 = (bf16[128,1536]{1,0:T(8,128)(2,1)S(1)}, bf16[128,1536]{1,0:T(8,128)(2,1)S(1)}, u32[]{:S(2)}, u32[]{:S(2)}) collective-permute-start(bf16[128,1536]{1,0:T(8,128)(2,1)S(1)} %get-tuple-element.158), channel_id=1, source_target_pairs={{0,8},{8,0},{16,24},{24,16},{1,9},{9,1},{17,25},{25,17},{2,10},{10... | collective-permute-start | bytes 1179656 | tf_op jit(solution)/shard_map/ppermute | solution.py:269
  58.8 3.8 %collective-permute-done.17.refs_1_.refs_0_ = bf16[1040,128]{1,0:T(8,128)(2,1)S(1)} collective-permute-done((bf16[1040,128]{1,0:T(8,128)(2,1)S(1)}, bf16[1040,128]{1,0:T(8,128)(2,1)S(1)}, u32[]{:S(2)}, u32[]{:S(2)}) %collective-permute-start.17) | collective-permute-done | bytes 266272 | tf_op jit(solution)/shard_map/ppermute | solution.py:269
  62.6 0.1 pair_kernel.3
  62.7 1.5 %collective-permute-start.25 = (bf16[1024,128]{1,0:T(8,128)(2,1)S(1)}, bf16[1024,128]{1,0:T(8,128)(2,1)S(1)}, u32[]{:S(2)}, u32[]{:S(2)}) collective-permute-start(bf16[1024,128]{1,0:T(8,128)(2,1)S(1)} %get-tuple-element.154), channel_id=1, source_target_pairs={{16,0},{24,8},{17,1},{25,9},{18,2},{26,10},{19,3},{27,11},{20,4},{... | collective-permute-start | bytes 786440 | tf_op jit(solution)/shard_map/ppermute | solution.py:549
  64.2 1.2 %back_key_kernel.1 = (bf16[8,256,256]{2,1,0:T(8,128)(2,1)S(1)}, f32[256,1024]{1,0:T(8,128)S(1)}, f32[8,128]{1,0:T(8,128)S(1)}) custom-call(bf16[256,1024]{1,0:T(8,128)(2,1)S(1)} %get-tuple-element.131.refs_0_, bf16[256,1024]{1,0:T(8,128)(2,1)S(1)} %bitcast.14, bf16[256,1024]{1,0:T(8,128)(2,1)S(1)} %bitcast.18, ...), custom_call_target="tpu_custom_call" | custom-call | tf_op jit(solution)/shard_map/back_key_kernel/pallas_call | solution.py:45
  65.5 0.1 ring_kernel.6
  65.6 3.4 %collective-permute-start.24 = (bf16[256,768]{1,0:T(8,128)(2,1)S(1)}, bf16[256,768]{1,0:T(8,128)(2,1)S(1)}, u32[]{:S(2)}, u32[]{:S(2)}) collective-permute-start(bf16[256,768]{1,0:T(8,128)(2,1)S(1)} %get-tuple-element.153), channel_id=1, source_target_pairs={{0,4},{2,0},{6,2},{4,6},{1,5},{3,1},{7,3},{5,7},{8,12},{10,8},{14,... | collective-permute-start | bytes 1179656 | tf_op jit(solution)/shard_map/ppermute | solution.py:370
  69.0 1.8 %collective-permute-start.27 = (bf16[128,1536]{1,0:T(8,128)(2,1)S(1)}, bf16[128,1536]{1,0:T(8,128)(2,1)S(1)}, u32[]{:S(2)}, u32[]{:S(2)}) collective-permute-start(bf16[128,1536]{1,0:T(8,128)(2,1)S(1)} %get-tuple-element.167), channel_id=1, source_target_pairs={{0,16},{8,24},{16,0},{24,8},{1,17},{9,25},{17,1},{25,9},{2,18},{10... | collective-permute-start | bytes 1179656 | tf_op jit(solution)/shard_map/ppermute | solution.py:269
  70.8 0.1 onward_kernel.3
  70.9 1.2 %collective-permute-start.28 = (bf16[128,1536]{1,0:T(8,128)(2,1)S(1)}, bf16[128,1536]{1,0:T(8,128)(2,1)S(1)}, u32[]{:S(2)}, u32[]{:S(2)}) collective-permute-start(bf16[128,1536]{1,0:T(8,128)(2,1)S(1)} %get-tuple-element.168), channel_id=1, source_target_pairs={{0,8},{8,0},{16,24},{24,16},{1,9},{9,1},{17,25},{25,17},{2,10},{10... | collective-permute-start | bytes 1179656 | tf_op jit(solution)/shard_map/ppermute | solution.py:269
  72.1 3.2 %back_query_kernel.1 = (bf16[256,1024]{1,0:T(8,128)(2,1)}, f32[256,1024]{1,0:T(8,128)S(1)}, f32[8,128]{1,0:T(8,128)S(1)}) custom-call(bf16[256,1024]{1,0:T(8,128)(2,1)S(1)} %get-tuple-element.131.refs_0_, bf16[256,1024]{1,0:T(8,128)(2,1)S(1)} %bitcast.15, bf16[256,1024]{1,0:T(8,128)(2,1)S(1)} %bitcast.22, f32[8,256]{1,0:T(8,128)S(1)} %get-tuple-element.126.refs_5_.refs_3_, ...), custom_call_target="tpu_custom_call" | custom-call | tf_op jit(solution)/shard_map/back_query_kernel/pallas_call | solution.py:45
  75.3 0.6 mix_kernel.5
  76.0 0.1 total_kernel.2
  76.2 0.6 collective-permute-start.23
  76.7 1.6 %back_inter_kernel.1 = (bf16[256,1024]{1,0:T(8,128)(2,1)}, bf16[256,1024]{1,0:T(8,128)(2,1)}, f32[8,128]{1,0:T(8,128)S(1)}) custom-call(bf16[1040,128]{1,0:T(8,128)(2,1)S(1)} %collective-permute-done.17.refs_1_.refs_0_, bf16[1024,128]{1,0:T(8,128)(2,1)S(1)} %collective-permute-done.25.refs_1_, bf16[256,1024]{1,0:T(8,128)(2,1)S(1)} %bitcast.23, ...), custom_call_target="tpu_custom_call" | custom-call | flops 2140000000 | tf_op jit(solution)/shard_map/back_inter_kernel/pallas_call | solution.py:45
  78.4 0.9 %ring_kernel.7 = (bf16[256,768]{1,0:T(8,128)(2,1)}, f32[8,128]{1,0:T(8,128)S(1)}) custom-call(f32[256,768]{1,0:T(8,128)S(1)} %get-tuple-element.150.refs_0_, bf16[256,384]{1,0:T(8,128)(2,1)S(1)} %collective-permute-done.22.refs_1_, bf16[256,384]{1,0:T(8,128)(2,1)S(1)} %collective-permute-done.23.refs_2_, ...), custom_call_target="tpu_custom_call" | custom-call | flops 642000000 | tf_op jit(solution)/shard_map/ring_kernel/pallas_call | solution.py:45
  79.2 1.2 %collective-permute-done.27.refs_1_ = bf16[128,1536]{1,0:T(8,128)(2,1)S(1)} collective-permute-done((bf16[128,1536]{1,0:T(8,128)(2,1)S(1)}, bf16[128,1536]{1,0:T(8,128)(2,1)S(1)}, u32[]{:S(2)}, u32[]{:S(2)}) %collective-permute-start.27) | collective-permute-done | bytes 393248 | tf_op jit(solution)/shard_map/ppermute | solution.py:269
  80.5 1.3 %total_kernel.3 = (f32[128,3072]{1,0:T(8,128)}, f32[8,128]{1,0:T(8,128)}) custom-call(f32[128,3072]{1,0:T(8,128)S(1)} %get-tuple-element.166.refs_0_, bf16[128,1536]{1,0:T(8,128)(2,1)S(1)} %collective-permute-done.27.refs_1_, bf16[128,1536]{1,0:T(8,128)(2,1)S(1)} %collective-permute-done.28.refs_2_, f32[8,128]{1,0:T(8,128)S(1)} %get-tuple-element.169.refs_3_), custom_call_target="tpu_custom_call" | custom-call | tf_op jit(solution)/shard_map/total_kernel/pallas_call | solution.py:45
  (40 shorter events, 0.7 us)
Async XLA Ops:
  0.6 19.8 %collective-permute-start.2 = (bf16[256,3072]{1,0:T(8,128)(2,1)}, bf16[256,3072]{1,0:T(8,128)(2,1)S(1)}, u32[]{:S(2)}, u32[]{:S(2)}) collective-permute-start(bf16[256,3072]{1,0:T(8,128)(2,1)} %bitcast.24), channel_id=1, source_target_pairs={{0,1},{1,0},{2,3},{3,2},{4,5},{5,4},{6,7},{7,6},{8,9},{9,8},{10,11... | collective-permute-start | bytes 4718600 | tf_op jit(solution)/shard_map/ppermute | solution.py:265
  1.1 19.7 %copy-start.6 = (f32[1,8,256]{2,1,0:T(8,128)S(1)}, f32[1,8,256]{2,1,0:T(8,128)}, u32[]{:S(2)}) copy-start(f32[1,8,256]{2,1,0:T(8,128)} %param.9) | copy-start | bytes 24580
  4.7 16.2 %copy-start = (bf16[1,256,1024]{2,1,0:T(8,128)(2,1)S(1)}, bf16[1,256,1024]{2,1,0:T(8,128)(2,1)}, u32[]{:S(2)}) copy-start(bf16[1,256,1024]{2,1,0:T(8,128)(2,1)} %param.6) | copy-start | bytes 1572868
  4.7 16.2 %copy-start.2 = (bf16[1,256,1024]{2,1,0:T(8,128)(2,1)S(1)}, bf16[1,256,1024]{2,1,0:T(8,128)(2,1)}, u32[]{:S(2)}) copy-start(bf16[1,256,1024]{2,1,0:T(8,128)(2,1)} %param.8) | copy-start | bytes 1572868
  4.7 16.2 %copy-start.3 = (bf16[1,256,1024]{2,1,0:T(8,128)(2,1)S(1)}, bf16[1,256,1024]{2,1,0:T(8,128)(2,1)}, u32[]{:S(2)}) copy-start(bf16[1,256,1024]{2,1,0:T(8,128)(2,1)} %param.7) | copy-start | bytes 1572868
  4.7 10.0 %collective-permute-start = (bf16[1040,128]{1,0:T(8,128)(2,1)}, bf16[1040,128]{1,0:T(8,128)(2,1)S(1)}, u32[]{:S(2)}, u32[]{:S(2)}) collective-permute-start(bf16[1040,128]{1,0:T(8,128)(2,1)} %get-tuple-element.88.refs_0_), channel_id=1, source_target_pairs={{0,8},{8,0},{16,24},{24,16},{1,9},{9,1},{17,25},{25,17},{2,10},{10... | collective-permute-start | bytes 798728 | tf_op jit(solution)/shard_map/ppermute | solution.py:269
  9.4 12.7 %collective-permute-start.4 = (bf16[128,1536]{1,0:T(8,128)(2,1)}, bf16[128,1536]{1,0:T(8,128)(2,1)S(1)}, u32[]{:S(2)}, u32[]{:S(2)}) collective-permute-start(bf16[128,1536]{1,0:T(8,128)(2,1)} %get-tuple-element.98.refs_0_), channel_id=1, source_target_pairs={{0,16},{8,24},{16,0},{24,8},{1,17},{9,25},{17,1},{25,9},{2,18},{10... | collective-permute-start | bytes 1179656 | tf_op jit(solution)/shard_map/ppermute | solution.py:269
  11.0 12.0 %collective-permute-start.3 = (bf16[128,1536]{1,0:T(8,128)(2,1)}, bf16[128,1536]{1,0:T(8,128)(2,1)S(1)}, u32[]{:S(2)}, u32[]{:S(2)}) collective-permute-start(bf16[128,1536]{1,0:T(8,128)(2,1)} %get-tuple-element.98.refs_0_), channel_id=1, source_target_pairs={{0,8},{8,0},{16,24},{24,16},{1,9},{9,1},{17,25},{25,17},{2,10},{10... | collective-permute-start | bytes 1179656 | tf_op jit(solution)/shard_map/ppermute | solution.py:269
  14.7 1.0 %copy-start.5 = (bf16[1040,128]{1,0:T(8,128)(2,1)S(1)}, bf16[1040,128]{1,0:T(8,128)(2,1)}, u32[]{:S(2)}) copy-start(bf16[1040,128]{1,0:T(8,128)(2,1)} %get-tuple-element.88.refs_0_) | copy-start | bytes 798724
  15.7 0.7 copy-start.7
  16.5 9.9 %collective-permute-start.1 = (bf16[1024,128]{1,0:T(8,128)(2,1)S(1)}, bf16[1024,128]{1,0:T(8,128)(2,1)S(1)}, u32[]{:S(2)}, u32[]{:S(2)}) collective-permute-start(bf16[1024,128]{1,0:T(8,128)(2,1)S(1)} %get-tuple-element.91), channel_id=1, source_target_pairs={{0,16},{8,24},{1,17},{9,25},{2,18},{10,26},{3,19},{11,27},{4,20},{... | collective-permute-start | bytes 786440 | tf_op jit(solution)/shard_map/ppermute | solution.py:426
  20.4 2.6 %copy-start.1 = (bf16[128,1536]{1,0:T(8,128)(2,1)S(1)}, bf16[128,1536]{1,0:T(8,128)(2,1)}, u32[]{:S(2)}) copy-start(bf16[128,1536]{1,0:T(8,128)(2,1)} %get-tuple-element.99.refs_2_.refs_3_) | copy-start | bytes 1179652
  20.8 5.6 %copy-start.4 = (bf16[1,256,3072]{2,1,0:T(8,128)(2,1)S(1)}, bf16[1,256,3072]{2,1,0:T(8,128)(2,1)}, u32[]{:S(2)}) copy-start(bf16[1,256,3072]{2,1,0:T(8,128)(2,1)} %param.11) | copy-start | bytes 4718596
  23.1 8.3 %collective-permute-start.8 = (bf16[64,1536]{1,0:T(8,128)(2,1)S(1)}, bf16[64,1536]{1,0:T(8,128)(2,1)S(1)}, u32[]{:S(2)}, u32[]{:S(2)}) collective-permute-start(bf16[64,1536]{1,0:T(8,128)(2,1)S(1)} %get-tuple-element.105), channel_id=1, source_target_pairs={{0,16},{8,24},{16,0},{24,8},{1,17},{9,25},{17,1},{25,9},{2,18},{10... | collective-permute-start | bytes 589832 | tf_op jit(solution)/shard_map/ppermute | solution.py:269
  24.9 6.5 %collective-permute-start.9 = (bf16[64,1536]{1,0:T(8,128)(2,1)S(1)}, bf16[64,1536]{1,0:T(8,128)(2,1)S(1)}, u32[]{:S(2)}, u32[]{:S(2)}) collective-permute-start(bf16[64,1536]{1,0:T(8,128)(2,1)S(1)} %get-tuple-element.106), channel_id=1, source_target_pairs={{0,8},{8,0},{16,24},{24,16},{1,9},{9,1},{17,25},{25,17},{2,10},{10... | collective-permute-start | bytes 589832 | tf_op jit(solution)/shard_map/ppermute | solution.py:269
  26.4 4.9 %copy-start.8 = (bf16[128,1536]{1,0:T(8,128)(2,1)S(1)}, bf16[128,1536]{1,0:T(8,128)(2,1)}, u32[]{:S(2)}) copy-start(bf16[128,1536]{1,0:T(8,128)(2,1)} %get-tuple-element.98.refs_0_) | copy-start | bytes 1179652
  27.6 3.9 %collective-permute-start.5 = (bf16[256,512]{1,0:T(8,128)(2,1)S(1)}, bf16[256,512]{1,0:T(8,128)(2,1)S(1)}, u32[]{:S(2)}, u32[]{:S(2)}) collective-permute-start(bf16[256,512]{1,0:T(8,128)(2,1)S(1)} %get-tuple-element.103), channel_id=1, source_target_pairs={{0,1},{1,0},{2,3},{3,2},{4,5},{5,4},{6,7},{7,6},{8,9},{9,8},{10,11... | collective-permute-start | bytes 786440 | tf_op jit(solution)/shard_map/ppermute | solution.py:265
  27.7 12.3 %collective-permute-start.7 = (bf16[128,1536]{1,0:T(8,128)(2,1)S(1)}, bf16[128,1536]{1,0:T(8,128)(2,1)S(1)}, u32[]{:S(2)}, u32[]{:S(2)}) collective-permute-start(bf16[128,1536]{1,0:T(8,128)(2,1)S(1)} %get-tuple-element.104), channel_id=1, source_target_pairs={{0,16},{8,24},{16,0},{24,8},{1,17},{9,25},{17,1},{25,9},{2,18},{10... | collective-permute-start | bytes 1179656 | tf_op jit(solution)/shard_map/ppermute | solution.py:269
  30.2 11.2 %collective-permute-start.6 = (bf16[128,1536]{1,0:T(8,128)(2,1)S(1)}, bf16[128,1536]{1,0:T(8,128)(2,1)S(1)}, u32[]{:S(2)}, u32[]{:S(2)}) collective-permute-start(bf16[128,1536]{1,0:T(8,128)(2,1)S(1)} %get-tuple-element.104), channel_id=1, source_target_pairs={{0,8},{8,0},{16,24},{24,16},{1,9},{9,1},{17,25},{25,17},{2,10},{10... | collective-permute-start | bytes 1179656 | tf_op jit(solution)/shard_map/ppermute | solution.py:269
  34.4 1.6 %collective-permute-start.10 = (bf16[256,512]{1,0:T(8,128)(2,1)S(1)}, bf16[256,512]{1,0:T(8,128)(2,1)S(1)}, u32[]{:S(2)}, u32[]{:S(2)}) collective-permute-start(bf16[256,512]{1,0:T(8,128)(2,1)S(1)} %get-tuple-element.113), channel_id=1, source_target_pairs={{0,1},{1,0},{2,3},{3,2},{4,5},{5,4},{6,7},{7,6},{8,9},{9,8},{10,11... | collective-permute-start | bytes 786440 | tf_op jit(solution)/shard_map/ppermute | solution.py:265
  34.4 1.9 %collective-permute-start.11 = (bf16[256,512]{1,0:T(8,128)(2,1)S(1)}, bf16[256,512]{1,0:T(8,128)(2,1)S(1)}, u32[]{:S(2)}, u32[]{:S(2)}) collective-permute-start(bf16[256,512]{1,0:T(8,128)(2,1)S(1)} %get-tuple-element.114), channel_id=1, source_target_pairs={{0,1},{1,0},{2,3},{3,2},{4,5},{5,4},{6,7},{7,6},{8,9},{9,8},{10,11... | collective-permute-start | bytes 786440 | tf_op jit(solution)/shard_map/ppermute | solution.py:265
  34.9 1.8 %collective-permute-start.12 = (bf16[256,512]{1,0:T(8,128)(2,1)S(1)}, bf16[256,512]{1,0:T(8,128)(2,1)S(1)}, u32[]{:S(2)}, u32[]{:S(2)}) collective-permute-start(bf16[256,512]{1,0:T(8,128)(2,1)S(1)} %get-tuple-element.115), channel_id=1, source_target_pairs={{0,1},{1,0},{2,3},{3,2},{4,5},{5,4},{6,7},{7,6},{8,9},{9,8},{10,11... | collective-permute-start | bytes 786440 | tf_op jit(solution)/shard_map/ppermute | solution.py:265
  36.8 13.9 %collective-permute-start.16 = (bf16[256,768]{1,0:T(8,128)(2,1)S(1)}, bf16[256,768]{1,0:T(8,128)(2,1)S(1)}, u32[]{:S(2)}, u32[]{:S(2)}) collective-permute-start(bf16[256,768]{1,0:T(8,128)(2,1)S(1)} %get-tuple-element.128), channel_id=1, source_target_pairs={{0,4},{2,0},{6,2},{4,6},{1,5},{3,1},{7,3},{5,7},{8,12},{10,8},{14,... | collective-permute-start | bytes 1179656 | tf_op jit(solution)/shard_map/ppermute | solution.py:370
  41.5 7.9 %collective-permute-start.13 = (bf16[64,1536]{1,0:T(8,128)(2,1)S(1)}, bf16[64,1536]{1,0:T(8,128)(2,1)S(1)}, u32[]{:S(2)}, u32[]{:S(2)}) collective-permute-start(bf16[64,1536]{1,0:T(8,128)(2,1)S(1)} %get-tuple-element.118), channel_id=1, source_target_pairs={{0,16},{8,24},{16,0},{24,8},{1,17},{9,25},{17,1},{25,9},{2,18},{10... | collective-permute-start | bytes 589832 | tf_op jit(solution)/shard_map/ppermute | solution.py:269
  41.8 7.8 %collective-permute-start.14 = (bf16[64,1536]{1,0:T(8,128)(2,1)S(1)}, bf16[64,1536]{1,0:T(8,128)(2,1)S(1)}, u32[]{:S(2)}, u32[]{:S(2)}) collective-permute-start(bf16[64,1536]{1,0:T(8,128)(2,1)S(1)} %get-tuple-element.119), channel_id=1, source_target_pairs={{0,8},{8,0},{16,24},{24,16},{1,9},{9,1},{17,25},{25,17},{2,10},{10... | collective-permute-start | bytes 589832 | tf_op jit(solution)/shard_map/ppermute | solution.py:269
  42.9 14.1 %collective-permute-start.18 = (bf16[128,1536]{1,0:T(8,128)(2,1)S(1)}, bf16[128,1536]{1,0:T(8,128)(2,1)S(1)}, u32[]{:S(2)}, u32[]{:S(2)}) collective-permute-start(bf16[128,1536]{1,0:T(8,128)(2,1)S(1)} %get-tuple-element.135), channel_id=1, source_target_pairs={{0,8},{8,0},{16,24},{24,16},{1,9},{9,1},{17,25},{25,17},{2,10},{10... | collective-permute-start | bytes 1179656 | tf_op jit(solution)/shard_map/ppermute | solution.py:269
  43.8 27.0 %collective-permute-start.19 = (bf16[256,1536]{1,0:T(8,128)(2,1)S(1)}, bf16[256,1536]{1,0:T(8,128)(2,1)S(1)}, u32[]{:S(2)}, u32[]{:S(2)}) collective-permute-start(bf16[256,1536]{1,0:T(8,128)(2,1)S(1)} %get-tuple-element.142), channel_id=1, source_target_pairs={{0,16},{8,24},{16,0},{24,8},{1,17},{9,25},{17,1},{25,9},{2,18},{10... | collective-permute-start | bytes 2359304 | tf_op jit(solution)/shard_map/ppermute | solution.py:269
  50.6 1.6 %collective-permute-start.15 = (bf16[256,512]{1,0:T(8,128)(2,1)S(1)}, bf16[256,512]{1,0:T(8,128)(2,1)S(1)}, u32[]{:S(2)}, u32[]{:S(2)}) collective-permute-start(bf16[256,512]{1,0:T(8,128)(2,1)S(1)} %get-tuple-element.125), channel_id=1, source_target_pairs={{0,1},{1,0},{2,3},{3,2},{4,5},{5,4},{6,7},{7,6},{8,9},{9,8},{10,11... | collective-permute-start | bytes 786440 | tf_op jit(solution)/shard_map/ppermute | solution.py:265
  53.3 9.3 %collective-permute-start.17 = (bf16[1040,128]{1,0:T(8,128)(2,1)S(1)}, bf16[1040,128]{1,0:T(8,128)(2,1)S(1)}, u32[]{:S(2)}, u32[]{:S(2)}) collective-permute-start(bf16[1040,128]{1,0:T(8,128)(2,1)S(1)} %get-tuple-element.133.refs_0_), channel_id=1, source_target_pairs={{0,8},{8,0},{16,24},{24,16},{1,9},{9,1},{17,25},{25,17},{2,10},{10... | collective-permute-start | bytes 798728 | tf_op jit(solution)/shard_map/ppermute | solution.py:269
  54.5 11.0 %collective-permute-start.21 = (bf16[256,768]{1,0:T(8,128)(2,1)S(1)}, bf16[256,768]{1,0:T(8,128)(2,1)S(1)}, u32[]{:S(2)}, u32[]{:S(2)}) collective-permute-start(bf16[256,768]{1,0:T(8,128)(2,1)S(1)} %get-tuple-element.145), channel_id=1, source_target_pairs={{0,4},{2,0},{6,2},{4,6},{1,5},{3,1},{7,3},{5,7},{8,12},{10,8},{14,... | collective-permute-start | bytes 1179656 | tf_op jit(solution)/shard_map/ppermute | solution.py:370
  57.8 7.7 %collective-permute-start.20 = (bf16[256,768]{1,0:T(8,128)(2,1)S(1)}, bf16[256,768]{1,0:T(8,128)(2,1)S(1)}, u32[]{:S(2)}, u32[]{:S(2)}) collective-permute-start(bf16[256,768]{1,0:T(8,128)(2,1)S(1)} %get-tuple-element.144), channel_id=1, source_target_pairs={{0,1},{1,0},{2,3},{3,2},{4,5},{5,4},{6,7},{7,6},{8,9},{9,8},{10,11... | collective-permute-start | bytes 1179656 | tf_op jit(solution)/shard_map/ppermute | solution.py:265
  57.9 18.1 %collective-permute-start.26 = (bf16[128,1536]{1,0:T(8,128)(2,1)S(1)}, bf16[128,1536]{1,0:T(8,128)(2,1)S(1)}, u32[]{:S(2)}, u32[]{:S(2)}) collective-permute-start(bf16[128,1536]{1,0:T(8,128)(2,1)S(1)} %get-tuple-element.158), channel_id=1, source_target_pairs={{0,8},{8,0},{16,24},{24,16},{1,9},{9,1},{17,25},{25,17},{2,10},{10... | collective-permute-start | bytes 1179656 | tf_op jit(solution)/shard_map/ppermute | solution.py:269
  62.7 13.5 %collective-permute-start.25 = (bf16[1024,128]{1,0:T(8,128)(2,1)S(1)}, bf16[1024,128]{1,0:T(8,128)(2,1)S(1)}, u32[]{:S(2)}, u32[]{:S(2)}) collective-permute-start(bf16[1024,128]{1,0:T(8,128)(2,1)S(1)} %get-tuple-element.154), channel_id=1, source_target_pairs={{16,0},{24,8},{17,1},{25,9},{18,2},{26,10},{19,3},{27,11},{20,4},{... | collective-permute-start | bytes 786440 | tf_op jit(solution)/shard_map/ppermute | solution.py:549
  65.6 12.8 %collective-permute-start.24 = (bf16[256,768]{1,0:T(8,128)(2,1)S(1)}, bf16[256,768]{1,0:T(8,128)(2,1)S(1)}, u32[]{:S(2)}, u32[]{:S(2)}) collective-permute-start(bf16[256,768]{1,0:T(8,128)(2,1)S(1)} %get-tuple-element.153), channel_id=1, source_target_pairs={{0,4},{2,0},{6,2},{4,6},{1,5},{3,1},{7,3},{5,7},{8,12},{10,8},{14,... | collective-permute-start | bytes 1179656 | tf_op jit(solution)/shard_map/ppermute | solution.py:370
  69.0 11.4 %collective-permute-start.27 = (bf16[128,1536]{1,0:T(8,128)(2,1)S(1)}, bf16[128,1536]{1,0:T(8,128)(2,1)S(1)}, u32[]{:S(2)}, u32[]{:S(2)}) collective-permute-start(bf16[128,1536]{1,0:T(8,128)(2,1)S(1)} %get-tuple-element.167), channel_id=1, source_target_pairs={{0,16},{8,24},{16,0},{24,8},{1,17},{9,25},{17,1},{25,9},{2,18},{10... | collective-permute-start | bytes 1179656 | tf_op jit(solution)/shard_map/ppermute | solution.py:269
  70.9 9.5 %collective-permute-start.28 = (bf16[128,1536]{1,0:T(8,128)(2,1)S(1)}, bf16[128,1536]{1,0:T(8,128)(2,1)S(1)}, u32[]{:S(2)}, u32[]{:S(2)}) collective-permute-start(bf16[128,1536]{1,0:T(8,128)(2,1)S(1)} %get-tuple-element.168), channel_id=1, source_target_pairs={{0,8},{8,0},{16,24},{24,16},{1,9},{9,1},{17,25},{25,17},{2,10},{10... | collective-permute-start | bytes 1179656 | tf_op jit(solution)/shard_map/ppermute | solution.py:269
  75.9 2.4 %collective-permute-start.22 = (bf16[256,384]{1,0:T(8,128)(2,1)S(1)}, bf16[256,384]{1,0:T(8,128)(2,1)S(1)}, u32[]{:S(2)}, u32[]{:S(2)}) collective-permute-start(bf16[256,384]{1,0:T(8,128)(2,1)S(1)} %get-tuple-element.151), channel_id=1, source_target_pairs={{0,1},{1,0},{2,3},{3,2},{4,5},{5,4},{6,7},{7,6},{8,9},{9,8},{10,11... | collective-permute-start | bytes 589832 | tf_op jit(solution)/shard_map/ppermute | solution.py:265
  76.2 2.2 %collective-permute-start.23 = (bf16[256,384]{1,0:T(8,128)(2,1)S(1)}, bf16[256,384]{1,0:T(8,128)(2,1)S(1)}, u32[]{:S(2)}, u32[]{:S(2)}) collective-permute-start(bf16[256,384]{1,0:T(8,128)(2,1)S(1)} %get-tuple-element.152), channel_id=1, source_target_pairs={{0,1},{1,0},{2,3},{3,2},{4,5},{5,4},{6,7},{7,6},{8,9},{9,8},{10,11... | collective-permute-start | bytes 589832 | tf_op jit(solution)/shard_map/ppermute | solution.py:265

commit v6 on v5

--- a/solution.py
+++ b/solution.py
@@ -12,7 +12,7 @@
 F32 = jnp.float32
 BF16 = jnp.bfloat16
 EXTRA = 16
-C_JOIN, C26, C17, C20, C24 = 1070000000, 642000000, 1284000000, 642000000, 2140000000
+C_HOLD, C_JOIN, C26, C17, C20, C24 = 1070000000, 1070000000, 642000000, 1284000000, 642000000, 2140000000
 
 
 def contract(a, b, dim_a, dim_b):
@@ -131,14 +131,6 @@
     return copies
 
 
-def columns_kernel(w_ref, first_ref, rest_ref, sem):
-    count = first_ref.shape[1] * lax.axis_size("head") // w_ref.shape[1]
-    copies = ring_columns(w_ref, first_ref, 1, sem)
-    copies += ring_columns(w_ref, rest_ref, 1 + count, sem.at[pl.ds(count, sem.shape[0] - count)])
-    for copy in copies:
-        copy.wait()
-
-
 def sums(ld_ref, mask, rows):
     lower = mask.astype(F32)
     a, b = (lower, ld_ref[...]) if rows else (ld_ref[...], lower)
@@ -147,15 +139,33 @@
     )
 
 
-def contrib_kernel(groups, k_ref, v_ref, ld_ref, state_ref):
+def contrib_kernel(groups, k_hbm, v_hbm, ld_hbm, w_ref, state_ref, first_ref, rest_ref, k_ref, v_ref, ld_ref, sem, w_sem):
+    moves = [
+        pltpu.make_async_copy(source, held, sem.at[i])
+        for i, (source, held) in enumerate(((ld_hbm, ld_ref), (k_hbm, k_ref), (v_hbm, v_ref)))
+    ]
+    for move in moves:
+        move.start()
+    count = first_ref.shape[1] * lax.axis_size("head") // w_ref.shape[1]
+    copies = ring_columns(w_ref, first_ref, 1, w_sem)
+    copies += ring_columns(w_ref, rest_ref, 1 + count, w_sem.at[pl.ds(count, w_sem.shape[0] - count)])
+    moves[0].wait()
     size = k_ref.shape[0]
     mask = lower_mask(size)
     col = sums(ld_ref, mask, True)
     tail = jnp.exp(col[size - 1 :, :] - col)
+    store_decay(state_ref, sums(ld_ref, mask, False), groups)
+    moves[1].wait()
+    moves[2].wait()
     for h in range(groups):
         weighted = (head(k_ref, h).astype(F32) * tail[:, h : h + 1]).astype(BF16)
         state_ref[h * DH : (h + 1) * DH, :] = contract(weighted, head(v_ref, h), 0, 0).astype(BF16)
-    store_decay(state_ref, sums(ld_ref, mask, False), groups)
+    for copy in copies:
+        copy.wait()
+
+
+def again_kernel(ref, again_ref):
+    again_ref[...] = ref[...]
 
 
 def intra_kernel(groups, q_ref, k_ref, v_ref, ld_ref, row_ref, col_ref, intra_ref):
@@ -269,15 +279,9 @@
     return lax.ppermute(array, "ctx", [(i, i ^ bit) for i in range(4)])
 
 
-def pass_kernel(one, two, whole, on_one, on_two, again):
-    again[...] = whole[...]
-    rows_kernel(one, two, on_one, on_two)
-
-
-def rows_kernel(one, two, on_one, on_two):
-    half = on_one.shape[0]
-    on_one[...] = one[:half]
-    on_two[...] = two[half:]
+def rows_kernel(upper, ref, out_ref):
+    half = out_ref.shape[0]
+    out_ref[...] = ref[:half] if upper else ref[half:]
 
 
 def join_kernel(*refs):
@@ -407,21 +411,26 @@
 
     near_heads = heads // 2
     first_shape, rest_shape = (struct((rows, count * part), BF16) for count in (near_heads, heads - near_heads))
-    state = step(
-        functools.partial(contrib_kernel, groups), state_shape, k, v, ld, staged=(0, 1, 2), room=60
-    )
-    w_first, w_rest = step(
-        columns_kernel,
-        [first_shape, rest_shape],
+    state, w_first, w_rest = step(
+        functools.partial(contrib_kernel, groups),
+        [state_shape, first_shape, rest_shape],
+        k,
+        v,
+        ld,
         w,
-        free_in=(0,),
-        scratch=[pltpu.SemaphoreType.DMA((heads,))],
+        free_in=(0, 1, 2, 3),
+        scratch=[
+            *[pltpu.VMEM(array.shape, array.dtype) for array in (k, v, ld)],
+            pltpu.SemaphoreType.DMA((3,)),
+            pltpu.SemaphoreType.DMA((heads,)),
+        ],
         room=60,
     )
     g_other = swapped(g)
     if four:
         near = flipped(state, 1)
         first_two, first_one = flipped(w_first, 2), flipped(w_first, 1)
+        state = step(again_kernel, state_shape, state)
         pair = step(functools.partial(pair_kernel, groups, True), struct((features, DH), BF16), state, near)
         before = [near, lax.ppermute(pair, "ctx", [(0, 2), (1, 3)])]
         lower = lambda array: struct((rows // 2, array.shape[1]), BF16)
@@ -439,10 +448,10 @@
         ld,
     )
     if four:
-        on_one, on_two, w_again = step(
-            pass_kernel, [lower(w_first)] * 2 + [rest_shape], first_one, first_two, w_rest
-        )
-        first = [w_first, first_one, first_two, flipped(on_one, 2), flipped(on_two, 1)]
+        on_two = step(functools.partial(rows_kernel, True), lower(w_first), first_two)
+        on_one = step(functools.partial(rows_kernel, False), lower(w_first), first_one)
+        w_again = step(again_kernel, rest_shape, w_rest)
+        first = [w_first, first_one, first_two, flipped(on_two, 1), flipped(on_one, 2)]
     else:
         before = hops_of(state, True)
         first = lax.all_gather(w_first, "ctx", axis=0, tiled=True)
@@ -462,6 +471,7 @@
     )
     a_other = swapped(a_away)
     if four:
+        first[3] = step(again_kernel, lower(w_first), first[3], work=C_HOLD)
         first = step(join_kernel, struct((devices * rows, first_shape.shape[1]), BF16), *first, work=C_JOIN)
     held = pltpu.VMEM((features // 2, part), BF16)
 
@@ -501,6 +511,7 @@
             scratch=[pltpu.VMEM((here, width), BF16)],
         )
 
+    terms = mix([first], 0, near_heads, 3 if four else 1)
     if four:
         small = lambda dtype: struct((rows, middle), dtype)
         left, right = (0, middle), (middle, width)
@@ -511,12 +522,12 @@
             blocks,
             [small(BF16), struct((2 * rows, middle), BF16), small(BF16), small(F32), small(F32), struct((rows, width), F32)],
         )
-    terms = mix([first], 0, near_heads, 3 if four else 1)
     arrived = passed(ring(terms[0]))
     if four:
         rest_one, rest_two = flipped(w_again, 1), flipped(w_again, 2)
-        on_one, on_two = step(rows_kernel, [lower(w_rest)] * 2, rest_one, rest_two)
-        rest = [w_rest, rest_one, rest_two, flipped(on_one, 2), flipped(on_two, 1)]
+        on_two = step(functools.partial(rows_kernel, True), lower(w_rest), rest_two)
+        on_one = step(functools.partial(rows_kernel, False), lower(w_rest), rest_one)
+        rest = [w_rest, rest_one, rest_two, flipped(on_two, 1), flipped(on_one, 2)]
         far_left, both_right, near_left = flipped(far_left, 1), flipped(both_right, 2), flipped(near_left, 1)
         grad_own, grad_away = grad_of(rest[3:], 3 * rows, *grad_of(rest[:3], 0))
     else:

time: 82.2 us -> 79.6 us (0.968)
  Pallas kernels: 25.6 us -> 23.4 us
  starting transfers between devices: 37 us -> 36.1 us
    pallas_call x28 -> x32, Pallas kernels: 25.6 us -> 23.4 us  [call(): pl.pallas_call(body, name=getattr(kernel, 'func', kernel).__name__, out_s...]
    ppermute x9, waiting for transfers between devices: 3.06 us -> 1.4 us  [swapped(): return lax.ppermute(array, 'dp', [(0, 1), (1, 0)])]
    ppermute x15, waiting for transfers between devices: 13.2 us -> 14.6 us  [flipped(): return lax.ppermute(array, 'ctx', [(i, i ^ bit) for i in range(4)])]
    ppermute x15, starting transfers between devices: 21 us -> 20 us  [flipped(): return lax.ppermute(array, 'ctx', [(i, i ^ bit) for i in range(4)])]
  transfers between devices with their start and end apart: 29 -> 29, of which waited for: 13 -> 11; matrix products, arithmetic and copies ran while one was open for 0% -> 0% of each run, Pallas kernels for 30% -> 28%
where the time goes in v6:
time: 79.6 us; the launch traced here: 79.4 us
  starting transfers between devices  36.1 us (45%)
  Pallas kernels  23.4 us (29%)
  waiting for transfers between devices  16.6 us (21%)
  local copies, waits for them, and re-layouts  1.96 us (2%)
  between operations  1.3 us (2%)
    pallas_call x32, Pallas kernels, call(): pl.pallas_call(body, name=getattr(kernel, 'func', kernel).__name__, out_s...  23.4 us
    ppermute x15, starting transfers between devices, flipped(): return lax.ppermute(array, 'ctx', [(i, i ^ bit) for i in range(4)])  20 us
    ppermute x15, waiting for transfers between devices, flipped(): return lax.ppermute(array, 'ctx', [(i, i ^ bit) for i in range(4)])  14.6 us
    ppermute x3, starting transfers between devices, passed(): return lax.ppermute(array, 'head', pairs)  8.68 us
    ppermute x1, starting transfers between devices, shards(): before = [near, lax.ppermute(pair, 'ctx', [(0, 2), (1, 3)])]  3.89 us
    ppermute x9, starting transfers between devices, swapped(): return lax.ppermute(array, 'dp', [(0, 1), (1, 0)])  2.01 us
    unnamed x18, local copies, waits for them, and re-layouts  1.96 us
  transfers between devices with their start and end apart: 29, of which 11 were waited for; matrix products, arithmetic and copies ran while one was open for 0% of the time, Pallas kernels for 28%

profile of v6, /device:TPU:0, one launch (start us, length us, event | category | flops | bytes accessed | tf_op | source)
XLA Modules:
  0.0 79.4 jit_solution(14990460270414464616)
XLA Ops:
  0.6 0.5 collective-permute-start.2
  1.2 3.3 %contrib_kernel.1 = (bf16[1040,128]{1,0:T(8,128)(2,1)}, bf16[128,1536]{1,0:T(8,128)(2,1)}, bf16[128,1536]{1,0:T(8,128)(2,1)}, f32[8,128]{1,0:T(8,128)}) custom-call(bf16[256,1024]{1,0:T(8,128)(2,1)} %bitcast.20, bf16[256,1024]{1,0:T(8,128)(2,1)} %bitcast.16, f32[8,256]{1,0:T(8,128)} %bitcast.26, bf16[128,3072]{1,0:T(8,128)(2,1)} %bitcast.28), custom_call_target="tpu_custom_call" | custom-call | tf_op jit(solution)/shard_map/contrib_kernel/pallas_call | solution.py:45
  4.5 2.6 %collective-permute-start = (bf16[1040,128]{1,0:T(8,128)(2,1)}, bf16[1040,128]{1,0:T(8,128)(2,1)S(1)}, u32[]{:S(2)}, u32[]{:S(2)}) collective-permute-start(bf16[1040,128]{1,0:T(8,128)(2,1)} %get-tuple-element.94.refs_0_), channel_id=1, source_target_pairs={{0,8},{8,0},{16,24},{24,16},{1,9},{9,1},{17,25},{25,17},{2,10},{10... | collective-permute-start | bytes 798728 | tf_op jit(solution)/shard_map/ppermute | solution.py:279
  7.1 1.5 %collective-permute-start.4 = (bf16[128,1536]{1,0:T(8,128)(2,1)}, bf16[128,1536]{1,0:T(8,128)(2,1)S(1)}, u32[]{:S(2)}, u32[]{:S(2)}) collective-permute-start(bf16[128,1536]{1,0:T(8,128)(2,1)} %get-tuple-element.106.refs_0_), channel_id=1, source_target_pairs={{0,16},{8,24},{16,0},{24,8},{1,17},{9,25},{17,1},{25,9},{2,18},{10... | collective-permute-start | bytes 1179656 | tf_op jit(solution)/shard_map/ppermute | solution.py:279
  8.6 0.5 collective-permute-start.3
  9.1 0.9 %copy-done.5 = bf16[1040,128]{1,0:T(8,128)(2,1)S(1)} copy-done((bf16[1040,128]{1,0:T(8,128)(2,1)S(1)}, bf16[1040,128]{1,0:T(8,128)(2,1)}, u32[]{:S(2)}) %copy-start.5) | copy-done | bytes 266264
  10.1 0.7 copy-done.7
  10.8 3.7 %collective-permute-done.refs_1_.refs_0_ = bf16[1040,128]{1,0:T(8,128)(2,1)S(1)} collective-permute-done((bf16[1040,128]{1,0:T(8,128)(2,1)}, bf16[1040,128]{1,0:T(8,128)(2,1)S(1)}, u32[]{:S(2)}, u32[]{:S(2)}) %collective-permute-start) | collective-permute-done | bytes 266272 | tf_op jit(solution)/shard_map/ppermute | solution.py:279
  14.5 0.1 pair_kernel.2
  14.7 3.9 %collective-permute-start.1 = (bf16[1024,128]{1,0:T(8,128)(2,1)S(1)}, bf16[1024,128]{1,0:T(8,128)(2,1)S(1)}, u32[]{:S(2)}, u32[]{:S(2)}) collective-permute-start(bf16[1024,128]{1,0:T(8,128)(2,1)S(1)} %get-tuple-element.98), channel_id=1, source_target_pairs={{0,16},{8,24},{1,17},{9,25},{2,18},{10,26},{3,19},{11,27},{4,20},{... | collective-permute-start | bytes 786440 | tf_op jit(solution)/shard_map/ppermute | solution.py:435
  18.6 0.4 picks_kernel.1
  19.0 1.3 %intra_kernel.1 = (f32[8,256]{1,0:T(8,128)S(1)}, f32[256,8]{1,0:T(8,128)S(1)}, f32[256,1024]{1,0:T(8,128)S(1)}, f32[8,128]{1,0:T(8,128)S(1)}) custom-call(bf16[256,1024]{1,0:T(8,128)(2,1)S(1)} %bitcast.11, bf16[256,1024]{1,0:T(8,128)(2,1)S(1)} %bitcast.21, bf16[256,1024]{1,0:T(8,128)(2,1)S(1)} %bitcast.17, f32[8,256]{1,0:T(8,128)S(1)} %bitcast.27, ...), custom_call_target="tpu_custom_call" | custom-call | tf_op jit(solution)/shard_map/intra_kernel/pallas_call | solution.py:45
  20.4 1.6 %collective-permute-start.8 = (bf16[64,1536]{1,0:T(8,128)(2,1)S(1)}, bf16[64,1536]{1,0:T(8,128)(2,1)S(1)}, u32[]{:S(2)}, u32[]{:S(2)}) collective-permute-start(bf16[64,1536]{1,0:T(8,128)(2,1)S(1)} %get-tuple-element.114), channel_id=1, source_target_pairs={{0,8},{8,0},{16,24},{24,16},{1,9},{9,1},{17,25},{25,17},{2,10},{10... | collective-permute-start | bytes 589832 | tf_op jit(solution)/shard_map/ppermute | solution.py:279
  21.9 1.0 %collective-permute-done.3.refs_0_.refs_1_ = bf16[128,1536]{1,0:T(8,128)(2,1)S(1)} collective-permute-done((bf16[128,1536]{1,0:T(8,128)(2,1)}, bf16[128,1536]{1,0:T(8,128)(2,1)S(1)}, u32[]{:S(2)}, u32[]{:S(2)}) %collective-permute-start.3) | collective-permute-done | bytes 393248 | tf_op jit(solution)/shard_map/ppermute | solution.py:279
  23.0 2.0 %collective-permute-start.9 = (bf16[64,1536]{1,0:T(8,128)(2,1)S(1)}, bf16[64,1536]{1,0:T(8,128)(2,1)S(1)}, u32[]{:S(2)}, u32[]{:S(2)}) collective-permute-start(bf16[64,1536]{1,0:T(8,128)(2,1)S(1)} %get-tuple-element.117), channel_id=1, source_target_pairs={{0,16},{8,24},{16,0},{24,8},{1,17},{9,25},{17,1},{25,9},{2,18},{10... | collective-permute-start | bytes 589832 | tf_op jit(solution)/shard_map/ppermute | solution.py:279
  25.1 1.2 %attended_kernel.1 = (bf16[256,512]{1,0:T(8,128)(2,1)S(1)}, bf16[256,512]{1,0:T(8,128)(2,1)S(1)}, bf16[8,128,128]{2,1,0:T(8,128)(2,1)S(1)}, bf16[256,3072]{1,0:T(8,128)(2,1)S(1)}, f32[8,128]{1,0:T(8,128)S(1)}) custom-call(bf16[1040,128]{1,0:T(8,128)(2,1)S(1)} %collective-permute-done.refs_1_.refs_0_, bf16[1024,128]{1,0:T(8,128)(2,1)S(1)} %collective-permute-done.1.refs_1_, ...), custom_call_target="tpu_custom_call" | custom-call | tf_op jit(solution)/shard_map/attended_kernel/pallas_call | solution.py:45
  26.3 0.1 collective-permute-start.5
  26.4 1.0 %collective-permute-start.7 = (bf16[128,1536]{1,0:T(8,128)(2,1)S(1)}, bf16[128,1536]{1,0:T(8,128)(2,1)S(1)}, u32[]{:S(2)}, u32[]{:S(2)}) collective-permute-start(bf16[128,1536]{1,0:T(8,128)(2,1)S(1)} %get-tuple-element.113), channel_id=1, source_target_pairs={{0,16},{8,24},{16,0},{24,8},{1,17},{9,25},{17,1},{25,9},{2,18},{10... | collective-permute-start | bytes 1179656 | tf_op jit(solution)/shard_map/ppermute | solution.py:279
  27.4 1.5 %collective-permute-start.6 = (bf16[128,1536]{1,0:T(8,128)(2,1)S(1)}, bf16[128,1536]{1,0:T(8,128)(2,1)S(1)}, u32[]{:S(2)}, u32[]{:S(2)}) collective-permute-start(bf16[128,1536]{1,0:T(8,128)(2,1)S(1)} %get-tuple-element.113), channel_id=1, source_target_pairs={{0,8},{8,0},{16,24},{24,16},{1,9},{9,1},{17,25},{25,17},{2,10},{10... | collective-permute-start | bytes 1179656 | tf_op jit(solution)/shard_map/ppermute | solution.py:279
  28.9 0.7 collective-permute-done.9.refs_4_
  29.6 0.3 copy-done.8
  29.9 0.1 join_kernel.1
  30.0 1.0 %mix_kernel.3 = (f32[256,768]{1,0:T(8,128)S(1)}, f32[256,768]{1,0:T(8,128)S(1)}, bf16[256,512]{1,0:T(8,128)(2,1)S(1)}, bf16[256,512]{1,0:T(8,128)(2,1)S(1)}, bf1...) custom-call(bf16[256,512]{1,0:T(8,128)(2,1)S(1)} %get-tuple-element.111.refs_0_, ...), custom_call_target="tpu_custom_call" | custom-call | tf_op jit(solution)/shard_map/mix_kernel/pallas_call | solution.py:45
  31.1 0.5 collective-permute-start.11
  31.6 0.1 collective-permute-start.12
  31.7 1.8 %weight_kernel.1 = (bf16[128,1536]{1,0:T(8,128)(2,1)S(1)}, bf16[256,1536]{1,0:T(8,128)(2,1)S(1)}, bf16[128,1536]{1,0:T(8,128)(2,1)S(1)}, f32[128,1536]{1,0:T(8,1...) custom-call(bf16[256,512]{1,0:T(8,128)(2,1)S(1)} %get-tuple-element.111.refs_0_, ...), custom_call_target="tpu_custom_call" | custom-call | tf_op jit(solution)/shard_map/weight_kernel/pallas_call | solution.py:45
  33.6 0.1 ring_kernel.4
  33.6 2.6 %collective-permute-start.16 = (bf16[256,768]{1,0:T(8,128)(2,1)S(1)}, bf16[256,768]{1,0:T(8,128)(2,1)S(1)}, u32[]{:S(2)}, u32[]{:S(2)}) collective-permute-start(bf16[256,768]{1,0:T(8,128)(2,1)S(1)} %get-tuple-element.140), channel_id=1, source_target_pairs={{0,4},{2,0},{6,2},{4,6},{1,5},{3,1},{7,3},{5,7},{8,12},{10,8},{14,... | collective-permute-start | bytes 1179656 | tf_op jit(solution)/shard_map/ppermute | solution.py:374
  36.3 1.7 %collective-permute-done.7.refs_0_.refs_5_.refs_4_ = bf16[128,1536]{1,0:T(8,128)(2,1)S(1)} collective-permute-done((bf16[128,1536]{1,0:T(8,128)(2,1)S(1)}, bf16[128,1536]{1,0:T(8,128)(2,1)S(1)}, u32[]{:S(2)}, u32[]{:S(2)}) %collective-permute-start.7) | collective-permute-done | bytes 393248 | tf_op jit(solution)/shard_map/ppermute | solution.py:279
  38.0 0.6 collective-permute-done.6.refs_0_.refs_4_.refs_3_
  38.6 1.1 %collective-permute-start.14 = (bf16[64,1536]{1,0:T(8,128)(2,1)S(1)}, bf16[64,1536]{1,0:T(8,128)(2,1)S(1)}, u32[]{:S(2)}, u32[]{:S(2)}) collective-permute-start(bf16[64,1536]{1,0:T(8,128)(2,1)S(1)} %get-tuple-element.131), channel_id=1, source_target_pairs={{0,16},{8,24},{16,0},{24,8},{1,17},{9,25},{17,1},{25,9},{2,18},{10... | collective-permute-start | bytes 589832 | tf_op jit(solution)/shard_map/ppermute | solution.py:279
  39.8 1.5 %collective-permute-start.13 = (bf16[64,1536]{1,0:T(8,128)(2,1)S(1)}, bf16[64,1536]{1,0:T(8,128)(2,1)S(1)}, u32[]{:S(2)}, u32[]{:S(2)}) collective-permute-start(bf16[64,1536]{1,0:T(8,128)(2,1)S(1)} %get-tuple-element.129), channel_id=1, source_target_pairs={{0,8},{8,0},{16,24},{24,16},{1,9},{9,1},{17,25},{25,17},{2,10},{10... | collective-permute-start | bytes 589832 | tf_op jit(solution)/shard_map/ppermute | solution.py:279
  41.2 0.6 collective-permute-start.18
  41.8 0.9 %collective-permute-start.19 = (bf16[256,1536]{1,0:T(8,128)(2,1)S(1)}, bf16[256,1536]{1,0:T(8,128)(2,1)S(1)}, u32[]{:S(2)}, u32[]{:S(2)}) collective-permute-start(bf16[256,1536]{1,0:T(8,128)(2,1)S(1)} %get-tuple-element.154), channel_id=1, source_target_pairs={{0,16},{8,24},{16,0},{24,8},{1,17},{9,25},{17,1},{25,9},{2,18},{10... | collective-permute-start | bytes 2359304 | tf_op jit(solution)/shard_map/ppermute | solution.py:279
  42.7 1.8 %grad_kernel.2 = (bf16[256,384]{1,0:T(8,128)(2,1)S(1)}, bf16[256,384]{1,0:T(8,128)(2,1)S(1)}, f32[8,128]{1,0:T(8,128)S(1)}) custom-call(bf16[256,3072]{1,0:T(8,128)(2,1)S(1)} %get-tuple-element.125.refs_2_.refs_0_, bf16[256,3072]{1,0:T(8,128)(2,1)S(1)} %collective-permute-done.2.refs_1_.refs_3_, bf16[512,1536]{1,0:T(8,128)(2,1)S(1)} %get-tuple-element.119.refs_2_, ...), custom_call_target="tpu_custom_call" | custom-call | tf_op jit(solution)/shard_map/grad_kernel/pallas_call | solution.py:45
  44.6 2.0 %collective-permute-done.14.refs_4_.refs_6_ = bf16[64,1536]{1,0:T(8,128)(2,1)S(1)} collective-permute-done((bf16[64,1536]{1,0:T(8,128)(2,1)S(1)}, bf16[64,1536]{1,0:T(8,128)(2,1)S(1)}, u32[]{:S(2)}, u32[]{:S(2)}) %collective-permute-start.14) | collective-permute-done | bytes 196640 | tf_op jit(solution)/shard_map/ppermute | solution.py:279
  46.5 1.1 %collective-permute-done.13.refs_3_.refs_5_ = bf16[64,1536]{1,0:T(8,128)(2,1)S(1)} collective-permute-done((bf16[64,1536]{1,0:T(8,128)(2,1)S(1)}, bf16[64,1536]{1,0:T(8,128)(2,1)S(1)}, u32[]{:S(2)}, u32[]{:S(2)}) %collective-permute-start.13) | collective-permute-done | bytes 196640 | tf_op jit(solution)/shard_map/ppermute | solution.py:279
  47.6 1.0 %grad_kernel.3 = (bf16[256,512]{1,0:T(8,128)(2,1)S(1)}, bf16[256,512]{1,0:T(8,128)(2,1)S(1)}, f32[8,128]{1,0:T(8,128)S(1)}) custom-call(bf16[256,3072]{1,0:T(8,128)(2,1)S(1)} %get-tuple-element.125.refs_2_.refs_0_, bf16[256,3072]{1,0:T(8,128)(2,1)S(1)} %collective-permute-done.2.refs_1_.refs_3_, bf16[512,1536]{1,0:T(8,128)(2,1)S(1)} %get-tuple-element.119.refs_2_, ...), custom_call_target="tpu_custom_call" | custom-call | tf_op jit(solution)/shard_map/grad_kernel/pallas_call | solution.py:45
  48.7 0.1 ring_kernel.5
  48.8 1.4 %collective-permute-done.15.refs_1_ = bf16[256,512]{1,0:T(8,128)(2,1)S(1)} collective-permute-done((bf16[256,512]{1,0:T(8,128)(2,1)S(1)}, bf16[256,512]{1,0:T(8,128)(2,1)S(1)}, u32[]{:S(2)}, u32[]{:S(2)}) %collective-permute-start.15) | collective-permute-done | bytes 262176 | tf_op jit(solution)/shard_map/ppermute | solution.py:275
  50.2 1.0 %back_contrib_kernel.1 = (bf16[256,1024]{1,0:T(8,128)(2,1)S(1)}, bf16[1040,128]{1,0:T(8,128)(2,1)S(1)}, f32[8,128]{1,0:T(8,128)S(1)}) custom-call(bf16[256,512]{1,0:T(8,128)(2,1)S(1)} %get-tuple-element.136.refs_0_, bf16[256,512]{1,0:T(8,128)(2,1)S(1)} %collective-permute-done.15.refs_1_, bf16[1024,512]{1,0:T(8,128)(2,1)S(1)} %get-tuple-element.103.refs_5_.refs_2_, ...), custom_call_target="tpu_custom_call" | custom-call | tf_op jit(solution)/shard_map/back_contrib_kernel/pallas_call | solution.py:45
  51.3 1.5 %collective-permute-start.17 = (bf16[1040,128]{1,0:T(8,128)(2,1)S(1)}, bf16[1040,128]{1,0:T(8,128)(2,1)S(1)}, u32[]{:S(2)}, u32[]{:S(2)}) collective-permute-start(bf16[1040,128]{1,0:T(8,128)(2,1)S(1)} %get-tuple-element.145.refs_0_), channel_id=1, source_target_pairs={{0,8},{8,0},{16,24},{24,16},{1,9},{9,1},{17,25},{25,17},{2,10},{10... | collective-permute-start | bytes 798728 | tf_op jit(solution)/shard_map/ppermute | solution.py:279
  52.8 2.6 %collective-permute-start.21 = (bf16[256,768]{1,0:T(8,128)(2,1)S(1)}, bf16[256,768]{1,0:T(8,128)(2,1)S(1)}, u32[]{:S(2)}, u32[]{:S(2)}) collective-permute-start(bf16[256,768]{1,0:T(8,128)(2,1)S(1)} %get-tuple-element.157), channel_id=1, source_target_pairs={{0,4},{2,0},{6,2},{4,6},{1,5},{3,1},{7,3},{5,7},{8,12},{10,8},{14,... | collective-permute-start | bytes 1179656 | tf_op jit(solution)/shard_map/ppermute | solution.py:374
  55.4 0.1 onward_kernel.2
  55.5 0.6 mix_kernel.4
  56.2 0.6 collective-permute-start.26
  56.8 3.5 %collective-permute-done.17.refs_1_.refs_0_ = bf16[1040,128]{1,0:T(8,128)(2,1)S(1)} collective-permute-done((bf16[1040,128]{1,0:T(8,128)(2,1)S(1)}, bf16[1040,128]{1,0:T(8,128)(2,1)S(1)}, u32[]{:S(2)}, u32[]{:S(2)}) %collective-permute-start.17) | collective-permute-done | bytes 266272 | tf_op jit(solution)/shard_map/ppermute | solution.py:279
  60.3 0.1 pair_kernel.3
  60.5 1.5 %collective-permute-start.25 = (bf16[1024,128]{1,0:T(8,128)(2,1)S(1)}, bf16[1024,128]{1,0:T(8,128)(2,1)S(1)}, u32[]{:S(2)}, u32[]{:S(2)}) collective-permute-start(bf16[1024,128]{1,0:T(8,128)(2,1)S(1)} %get-tuple-element.166), channel_id=1, source_target_pairs={{16,0},{24,8},{17,1},{25,9},{18,2},{26,10},{19,3},{27,11},{20,4},{... | collective-permute-start | bytes 786440 | tf_op jit(solution)/shard_map/ppermute | solution.py:560
  61.9 1.2 %back_key_kernel.1 = (bf16[8,256,256]{2,1,0:T(8,128)(2,1)S(1)}, f32[256,1024]{1,0:T(8,128)S(1)}, f32[8,128]{1,0:T(8,128)S(1)}) custom-call(bf16[256,1024]{1,0:T(8,128)(2,1)S(1)} %get-tuple-element.143.refs_0_, bf16[256,1024]{1,0:T(8,128)(2,1)S(1)} %bitcast.14, bf16[256,1024]{1,0:T(8,128)(2,1)S(1)} %bitcast.18, ...), custom_call_target="tpu_custom_call" | custom-call | tf_op jit(solution)/shard_map/back_key_kernel/pallas_call | solution.py:45
  63.2 0.6 collective-permute-done.21.refs_2_
  63.8 0.1 ring_kernel.6
  63.9 3.4 %collective-permute-start.24 = (bf16[256,768]{1,0:T(8,128)(2,1)S(1)}, bf16[256,768]{1,0:T(8,128)(2,1)S(1)}, u32[]{:S(2)}, u32[]{:S(2)}) collective-permute-start(bf16[256,768]{1,0:T(8,128)(2,1)S(1)} %get-tuple-element.165), channel_id=1, source_target_pairs={{0,4},{2,0},{6,2},{4,6},{1,5},{3,1},{7,3},{5,7},{8,12},{10,8},{14,... | collective-permute-start | bytes 1179656 | tf_op jit(solution)/shard_map/ppermute | solution.py:374
  67.4 1.5 %collective-permute-start.27 = (bf16[128,1536]{1,0:T(8,128)(2,1)S(1)}, bf16[128,1536]{1,0:T(8,128)(2,1)S(1)}, u32[]{:S(2)}, u32[]{:S(2)}) collective-permute-start(bf16[128,1536]{1,0:T(8,128)(2,1)S(1)} %get-tuple-element.179), channel_id=1, source_target_pairs={{0,16},{8,24},{16,0},{24,8},{1,17},{9,25},{17,1},{25,9},{2,18},{10... | collective-permute-start | bytes 1179656 | tf_op jit(solution)/shard_map/ppermute | solution.py:279
  68.8 0.1 onward_kernel.3
  68.9 1.6 %collective-permute-start.28 = (bf16[128,1536]{1,0:T(8,128)(2,1)S(1)}, bf16[128,1536]{1,0:T(8,128)(2,1)S(1)}, u32[]{:S(2)}, u32[]{:S(2)}) collective-permute-start(bf16[128,1536]{1,0:T(8,128)(2,1)S(1)} %get-tuple-element.180), channel_id=1, source_target_pairs={{0,8},{8,0},{16,24},{24,16},{1,9},{9,1},{17,25},{25,17},{2,10},{10... | collective-permute-start | bytes 1179656 | tf_op jit(solution)/shard_map/ppermute | solution.py:279
  70.5 3.2 %back_query_kernel.1 = (bf16[256,1024]{1,0:T(8,128)(2,1)}, f32[256,1024]{1,0:T(8,128)S(1)}, f32[8,128]{1,0:T(8,128)S(1)}) custom-call(bf16[256,1024]{1,0:T(8,128)(2,1)S(1)} %get-tuple-element.143.refs_0_, bf16[256,1024]{1,0:T(8,128)(2,1)S(1)} %bitcast.15, bf16[256,1024]{1,0:T(8,128)(2,1)S(1)} %bitcast.22, f32[8,256]{1,0:T(8,128)S(1)} %get-tuple-element.138.refs_5_.refs_3_, ...), custom_call_target="tpu_custom_call" | custom-call | tf_op jit(solution)/shard_map/back_query_kernel/pallas_call | solution.py:45
  73.7 0.6 mix_kernel.5
  74.4 0.1 total_kernel.2
  74.5 0.6 collective-permute-start.23
  75.1 1.6 %back_inter_kernel.1 = (bf16[256,1024]{1,0:T(8,128)(2,1)}, bf16[256,1024]{1,0:T(8,128)(2,1)}, f32[8,128]{1,0:T(8,128)S(1)}) custom-call(bf16[1040,128]{1,0:T(8,128)(2,1)S(1)} %collective-permute-done.17.refs_1_.refs_0_, bf16[1024,128]{1,0:T(8,128)(2,1)S(1)} %collective-permute-done.25.refs_1_, bf16[256,1024]{1,0:T(8,128)(2,1)S(1)} %bitcast.23, ...), custom_call_target="tpu_custom_call" | custom-call | flops 2140000000 | tf_op jit(solution)/shard_map/back_inter_kernel/pallas_call | solution.py:45
  76.7 0.9 %ring_kernel.7 = (bf16[256,768]{1,0:T(8,128)(2,1)}, f32[8,128]{1,0:T(8,128)S(1)}) custom-call(f32[256,768]{1,0:T(8,128)S(1)} %get-tuple-element.162.refs_0_, bf16[256,384]{1,0:T(8,128)(2,1)S(1)} %collective-permute-done.22.refs_1_, bf16[256,384]{1,0:T(8,128)(2,1)S(1)} %collective-permute-done.23.refs_2_, ...), custom_call_target="tpu_custom_call" | custom-call | flops 642000000 | tf_op jit(solution)/shard_map/ring_kernel/pallas_call | solution.py:45
  77.6 0.3 collective-permute-done.27.refs_1_
  77.9 1.3 %total_kernel.3 = (f32[128,3072]{1,0:T(8,128)}, f32[8,128]{1,0:T(8,128)}) custom-call(f32[128,3072]{1,0:T(8,128)S(1)} %get-tuple-element.178.refs_0_, bf16[128,1536]{1,0:T(8,128)(2,1)S(1)} %collective-permute-done.27.refs_1_, bf16[128,1536]{1,0:T(8,128)(2,1)S(1)} %collective-permute-done.28.refs_2_, f32[8,128]{1,0:T(8,128)S(1)} %get-tuple-element.181.refs_3_), custom_call_target="tpu_custom_call" | custom-call | tf_op jit(solution)/shard_map/total_kernel/pallas_call | solution.py:45
  (44 shorter events, 0.6 us)
Async XLA Ops:
  0.6 17.9 %collective-permute-start.2 = (bf16[256,3072]{1,0:T(8,128)(2,1)}, bf16[256,3072]{1,0:T(8,128)(2,1)S(1)}, u32[]{:S(2)}, u32[]{:S(2)}) collective-permute-start(bf16[256,3072]{1,0:T(8,128)(2,1)} %bitcast.24), channel_id=1, source_target_pairs={{0,1},{1,0},{2,3},{3,2},{4,5},{5,4},{6,7},{7,6},{8,9},{9,8},{10,11... | collective-permute-start | bytes 4718600 | tf_op jit(solution)/shard_map/ppermute | solution.py:275
  1.1 17.9 %copy-start.6 = (f32[1,8,256]{2,1,0:T(8,128)S(1)}, f32[1,8,256]{2,1,0:T(8,128)}, u32[]{:S(2)}) copy-start(f32[1,8,256]{2,1,0:T(8,128)} %param.9) | copy-start | bytes 24580
  4.5 14.5 %copy-start = (bf16[1,256,1024]{2,1,0:T(8,128)(2,1)S(1)}, bf16[1,256,1024]{2,1,0:T(8,128)(2,1)}, u32[]{:S(2)}) copy-start(bf16[1,256,1024]{2,1,0:T(8,128)(2,1)} %param.6) | copy-start | bytes 1572868
  4.5 14.5 %copy-start.2 = (bf16[1,256,1024]{2,1,0:T(8,128)(2,1)S(1)}, bf16[1,256,1024]{2,1,0:T(8,128)(2,1)}, u32[]{:S(2)}) copy-start(bf16[1,256,1024]{2,1,0:T(8,128)(2,1)} %param.8) | copy-start | bytes 1572868
  4.5 14.5 %copy-start.3 = (bf16[1,256,1024]{2,1,0:T(8,128)(2,1)S(1)}, bf16[1,256,1024]{2,1,0:T(8,128)(2,1)}, u32[]{:S(2)}) copy-start(bf16[1,256,1024]{2,1,0:T(8,128)(2,1)} %param.7) | copy-start | bytes 1572868
  4.5 10.0 %collective-permute-start = (bf16[1040,128]{1,0:T(8,128)(2,1)}, bf16[1040,128]{1,0:T(8,128)(2,1)S(1)}, u32[]{:S(2)}, u32[]{:S(2)}) collective-permute-start(bf16[1040,128]{1,0:T(8,128)(2,1)} %get-tuple-element.94.refs_0_), channel_id=1, source_target_pairs={{0,8},{8,0},{16,24},{24,16},{1,9},{9,1},{17,25},{25,17},{2,10},{10... | collective-permute-start | bytes 798728 | tf_op jit(solution)/shard_map/ppermute | solution.py:279
  7.1 13.3 %collective-permute-start.4 = (bf16[128,1536]{1,0:T(8,128)(2,1)}, bf16[128,1536]{1,0:T(8,128)(2,1)S(1)}, u32[]{:S(2)}, u32[]{:S(2)}) collective-permute-start(bf16[128,1536]{1,0:T(8,128)(2,1)} %get-tuple-element.106.refs_0_), channel_id=1, source_target_pairs={{0,16},{8,24},{16,0},{24,8},{1,17},{9,25},{17,1},{25,9},{2,18},{10... | collective-permute-start | bytes 1179656 | tf_op jit(solution)/shard_map/ppermute | solution.py:279
  8.6 14.4 %collective-permute-start.3 = (bf16[128,1536]{1,0:T(8,128)(2,1)}, bf16[128,1536]{1,0:T(8,128)(2,1)S(1)}, u32[]{:S(2)}, u32[]{:S(2)}) collective-permute-start(bf16[128,1536]{1,0:T(8,128)(2,1)} %get-tuple-element.106.refs_0_), channel_id=1, source_target_pairs={{0,8},{8,0},{16,24},{24,16},{1,9},{9,1},{17,25},{25,17},{2,10},{10... | collective-permute-start | bytes 1179656 | tf_op jit(solution)/shard_map/ppermute | solution.py:279
  9.1 1.0 %copy-start.5 = (bf16[1040,128]{1,0:T(8,128)(2,1)S(1)}, bf16[1040,128]{1,0:T(8,128)(2,1)}, u32[]{:S(2)}) copy-start(bf16[1040,128]{1,0:T(8,128)(2,1)} %get-tuple-element.94.refs_0_) | copy-start | bytes 798724
  10.1 0.7 copy-start.7
  14.7 10.4 %collective-permute-start.1 = (bf16[1024,128]{1,0:T(8,128)(2,1)S(1)}, bf16[1024,128]{1,0:T(8,128)(2,1)S(1)}, u32[]{:S(2)}, u32[]{:S(2)}) collective-permute-start(bf16[1024,128]{1,0:T(8,128)(2,1)S(1)} %get-tuple-element.98), channel_id=1, source_target_pairs={{0,16},{8,24},{1,17},{9,25},{2,18},{10,26},{3,19},{11,27},{4,20},{... | collective-permute-start | bytes 786440 | tf_op jit(solution)/shard_map/ppermute | solution.py:435
  19.0 6.0 %copy-start.1 = (bf16[128,1536]{1,0:T(8,128)(2,1)S(1)}, bf16[128,1536]{1,0:T(8,128)(2,1)}, u32[]{:S(2)}) copy-start(bf16[128,1536]{1,0:T(8,128)(2,1)} %get-tuple-element.105.refs_0_.refs_3_.refs_2_) | copy-start | bytes 1179652
  19.0 6.1 %copy-start.4 = (bf16[1,256,3072]{2,1,0:T(8,128)(2,1)S(1)}, bf16[1,256,3072]{2,1,0:T(8,128)(2,1)}, u32[]{:S(2)}) copy-start(bf16[1,256,3072]{2,1,0:T(8,128)(2,1)} %param.11) | copy-start | bytes 4718596
  20.4 8.5 %collective-permute-start.8 = (bf16[64,1536]{1,0:T(8,128)(2,1)S(1)}, bf16[64,1536]{1,0:T(8,128)(2,1)S(1)}, u32[]{:S(2)}, u32[]{:S(2)}) collective-permute-start(bf16[64,1536]{1,0:T(8,128)(2,1)S(1)} %get-tuple-element.114), channel_id=1, source_target_pairs={{0,8},{8,0},{16,24},{24,16},{1,9},{9,1},{17,25},{25,17},{2,10},{10... | collective-permute-start | bytes 589832 | tf_op jit(solution)/shard_map/ppermute | solution.py:279
  23.0 6.6 %collective-permute-start.9 = (bf16[64,1536]{1,0:T(8,128)(2,1)S(1)}, bf16[64,1536]{1,0:T(8,128)(2,1)S(1)}, u32[]{:S(2)}, u32[]{:S(2)}) collective-permute-start(bf16[64,1536]{1,0:T(8,128)(2,1)S(1)} %get-tuple-element.117), channel_id=1, source_target_pairs={{0,16},{8,24},{16,0},{24,8},{1,17},{9,25},{17,1},{25,9},{2,18},{10... | collective-permute-start | bytes 589832 | tf_op jit(solution)/shard_map/ppermute | solution.py:279
  26.3 3.7 %collective-permute-start.5 = (bf16[256,512]{1,0:T(8,128)(2,1)S(1)}, bf16[256,512]{1,0:T(8,128)(2,1)S(1)}, u32[]{:S(2)}, u32[]{:S(2)}) collective-permute-start(bf16[256,512]{1,0:T(8,128)(2,1)S(1)} %get-tuple-element.112), channel_id=1, source_target_pairs={{0,1},{1,0},{2,3},{3,2},{4,5},{5,4},{6,7},{7,6},{8,9},{9,8},{10,11... | collective-permute-start | bytes 786440 | tf_op jit(solution)/shard_map/ppermute | solution.py:275
  26.4 11.6 %collective-permute-start.7 = (bf16[128,1536]{1,0:T(8,128)(2,1)S(1)}, bf16[128,1536]{1,0:T(8,128)(2,1)S(1)}, u32[]{:S(2)}, u32[]{:S(2)}) collective-permute-start(bf16[128,1536]{1,0:T(8,128)(2,1)S(1)} %get-tuple-element.113), channel_id=1, source_target_pairs={{0,16},{8,24},{16,0},{24,8},{1,17},{9,25},{17,1},{25,9},{2,18},{10... | collective-permute-start | bytes 1179656 | tf_op jit(solution)/shard_map/ppermute | solution.py:279
  27.4 11.2 %collective-permute-start.6 = (bf16[128,1536]{1,0:T(8,128)(2,1)S(1)}, bf16[128,1536]{1,0:T(8,128)(2,1)S(1)}, u32[]{:S(2)}, u32[]{:S(2)}) collective-permute-start(bf16[128,1536]{1,0:T(8,128)(2,1)S(1)} %get-tuple-element.113), channel_id=1, source_target_pairs={{0,8},{8,0},{16,24},{24,16},{1,9},{9,1},{17,25},{25,17},{2,10},{10... | collective-permute-start | bytes 1179656 | tf_op jit(solution)/shard_map/ppermute | solution.py:279
  28.9 1.0 %copy-start.8 = (bf16[128,1536]{1,0:T(8,128)(2,1)S(1)}, bf16[128,1536]{1,0:T(8,128)(2,1)}, u32[]{:S(2)}) copy-start(bf16[128,1536]{1,0:T(8,128)(2,1)} %get-tuple-element.106.refs_0_) | copy-start | bytes 1179652
  31.0 2.5 %collective-permute-start.10 = (bf16[256,512]{1,0:T(8,128)(2,1)S(1)}, bf16[256,512]{1,0:T(8,128)(2,1)S(1)}, u32[]{:S(2)}, u32[]{:S(2)}) collective-permute-start(bf16[256,512]{1,0:T(8,128)(2,1)S(1)} %get-tuple-element.122), channel_id=1, source_target_pairs={{0,1},{1,0},{2,3},{3,2},{4,5},{5,4},{6,7},{7,6},{8,9},{9,8},{10,11... | collective-permute-start | bytes 786440 | tf_op jit(solution)/shard_map/ppermute | solution.py:275
  31.1 2.4 %collective-permute-start.11 = (bf16[256,512]{1,0:T(8,128)(2,1)S(1)}, bf16[256,512]{1,0:T(8,128)(2,1)S(1)}, u32[]{:S(2)}, u32[]{:S(2)}) collective-permute-start(bf16[256,512]{1,0:T(8,128)(2,1)S(1)} %get-tuple-element.123), channel_id=1, source_target_pairs={{0,1},{1,0},{2,3},{3,2},{4,5},{5,4},{6,7},{7,6},{8,9},{9,8},{10,11... | collective-permute-start | bytes 786440 | tf_op jit(solution)/shard_map/ppermute | solution.py:275
  31.6 1.9 %collective-permute-start.12 = (bf16[256,512]{1,0:T(8,128)(2,1)S(1)}, bf16[256,512]{1,0:T(8,128)(2,1)S(1)}, u32[]{:S(2)}, u32[]{:S(2)}) collective-permute-start(bf16[256,512]{1,0:T(8,128)(2,1)S(1)} %get-tuple-element.124), channel_id=1, source_target_pairs={{0,1},{1,0},{2,3},{3,2},{4,5},{5,4},{6,7},{7,6},{8,9},{9,8},{10,11... | collective-permute-start | bytes 786440 | tf_op jit(solution)/shard_map/ppermute | solution.py:275
  33.6 15.1 %collective-permute-start.16 = (bf16[256,768]{1,0:T(8,128)(2,1)S(1)}, bf16[256,768]{1,0:T(8,128)(2,1)S(1)}, u32[]{:S(2)}, u32[]{:S(2)}) collective-permute-start(bf16[256,768]{1,0:T(8,128)(2,1)S(1)} %get-tuple-element.140), channel_id=1, source_target_pairs={{0,4},{2,0},{6,2},{4,6},{1,5},{3,1},{7,3},{5,7},{8,12},{10,8},{14,... | collective-permute-start | bytes 1179656 | tf_op jit(solution)/shard_map/ppermute | solution.py:374
  38.6 7.9 %collective-permute-start.14 = (bf16[64,1536]{1,0:T(8,128)(2,1)S(1)}, bf16[64,1536]{1,0:T(8,128)(2,1)S(1)}, u32[]{:S(2)}, u32[]{:S(2)}) collective-permute-start(bf16[64,1536]{1,0:T(8,128)(2,1)S(1)} %get-tuple-element.131), channel_id=1, source_target_pairs={{0,16},{8,24},{16,0},{24,8},{1,17},{9,25},{17,1},{25,9},{2,18},{10... | collective-permute-start | bytes 589832 | tf_op jit(solution)/shard_map/ppermute | solution.py:279
  39.8 7.9 %collective-permute-start.13 = (bf16[64,1536]{1,0:T(8,128)(2,1)S(1)}, bf16[64,1536]{1,0:T(8,128)(2,1)S(1)}, u32[]{:S(2)}, u32[]{:S(2)}) collective-permute-start(bf16[64,1536]{1,0:T(8,128)(2,1)S(1)} %get-tuple-element.129), channel_id=1, source_target_pairs={{0,8},{8,0},{16,24},{24,16},{1,9},{9,1},{17,25},{25,17},{2,10},{10... | collective-permute-start | bytes 589832 | tf_op jit(solution)/shard_map/ppermute | solution.py:279
  41.2 14.2 %collective-permute-start.18 = (bf16[128,1536]{1,0:T(8,128)(2,1)S(1)}, bf16[128,1536]{1,0:T(8,128)(2,1)S(1)}, u32[]{:S(2)}, u32[]{:S(2)}) collective-permute-start(bf16[128,1536]{1,0:T(8,128)(2,1)S(1)} %get-tuple-element.147), channel_id=1, source_target_pairs={{0,8},{8,0},{16,24},{24,16},{1,9},{9,1},{17,25},{25,17},{2,10},{10... | collective-permute-start | bytes 1179656 | tf_op jit(solution)/shard_map/ppermute | solution.py:279
  41.8 27.0 %collective-permute-start.19 = (bf16[256,1536]{1,0:T(8,128)(2,1)S(1)}, bf16[256,1536]{1,0:T(8,128)(2,1)S(1)}, u32[]{:S(2)}, u32[]{:S(2)}) collective-permute-start(bf16[256,1536]{1,0:T(8,128)(2,1)S(1)} %get-tuple-element.154), channel_id=1, source_target_pairs={{0,16},{8,24},{16,0},{24,8},{1,17},{9,25},{17,1},{25,9},{2,18},{10... | collective-permute-start | bytes 2359304 | tf_op jit(solution)/shard_map/ppermute | solution.py:279
  48.6 1.6 %collective-permute-start.15 = (bf16[256,512]{1,0:T(8,128)(2,1)S(1)}, bf16[256,512]{1,0:T(8,128)(2,1)S(1)}, u32[]{:S(2)}, u32[]{:S(2)}) collective-permute-start(bf16[256,512]{1,0:T(8,128)(2,1)S(1)} %get-tuple-element.137), channel_id=1, source_target_pairs={{0,1},{1,0},{2,3},{3,2},{4,5},{5,4},{6,7},{7,6},{8,9},{9,8},{10,11... | collective-permute-start | bytes 786440 | tf_op jit(solution)/shard_map/ppermute | solution.py:275
  51.3 9.1 %collective-permute-start.17 = (bf16[1040,128]{1,0:T(8,128)(2,1)S(1)}, bf16[1040,128]{1,0:T(8,128)(2,1)S(1)}, u32[]{:S(2)}, u32[]{:S(2)}) collective-permute-start(bf16[1040,128]{1,0:T(8,128)(2,1)S(1)} %get-tuple-element.145.refs_0_), channel_id=1, source_target_pairs={{0,8},{8,0},{16,24},{24,16},{1,9},{9,1},{17,25},{25,17},{2,10},{10... | collective-permute-start | bytes 798728 | tf_op jit(solution)/shard_map/ppermute | solution.py:279
  52.8 11.0 %collective-permute-start.21 = (bf16[256,768]{1,0:T(8,128)(2,1)S(1)}, bf16[256,768]{1,0:T(8,128)(2,1)S(1)}, u32[]{:S(2)}, u32[]{:S(2)}) collective-permute-start(bf16[256,768]{1,0:T(8,128)(2,1)S(1)} %get-tuple-element.157), channel_id=1, source_target_pairs={{0,4},{2,0},{6,2},{4,6},{1,5},{3,1},{7,3},{5,7},{8,12},{10,8},{14,... | collective-permute-start | bytes 1179656 | tf_op jit(solution)/shard_map/ppermute | solution.py:374
  56.1 7.7 %collective-permute-start.20 = (bf16[256,768]{1,0:T(8,128)(2,1)S(1)}, bf16[256,768]{1,0:T(8,128)(2,1)S(1)}, u32[]{:S(2)}, u32[]{:S(2)}) collective-permute-start(bf16[256,768]{1,0:T(8,128)(2,1)S(1)} %get-tuple-element.156), channel_id=1, source_target_pairs={{0,1},{1,0},{2,3},{3,2},{4,5},{5,4},{6,7},{7,6},{8,9},{9,8},{10,11... | collective-permute-start | bytes 1179656 | tf_op jit(solution)/shard_map/ppermute | solution.py:275
  56.2 18.1 %collective-permute-start.26 = (bf16[128,1536]{1,0:T(8,128)(2,1)S(1)}, bf16[128,1536]{1,0:T(8,128)(2,1)S(1)}, u32[]{:S(2)}, u32[]{:S(2)}) collective-permute-start(bf16[128,1536]{1,0:T(8,128)(2,1)S(1)} %get-tuple-element.170), channel_id=1, source_target_pairs={{0,8},{8,0},{16,24},{24,16},{1,9},{9,1},{17,25},{25,17},{2,10},{10... | collective-permute-start | bytes 1179656 | tf_op jit(solution)/shard_map/ppermute | solution.py:279
  60.5 14.1 %collective-permute-start.25 = (bf16[1024,128]{1,0:T(8,128)(2,1)S(1)}, bf16[1024,128]{1,0:T(8,128)(2,1)S(1)}, u32[]{:S(2)}, u32[]{:S(2)}) collective-permute-start(bf16[1024,128]{1,0:T(8,128)(2,1)S(1)} %get-tuple-element.166), channel_id=1, source_target_pairs={{16,0},{24,8},{17,1},{25,9},{18,2},{26,10},{19,3},{27,11},{20,4},{... | collective-permute-start | bytes 786440 | tf_op jit(solution)/shard_map/ppermute | solution.py:560
  63.9 12.8 %collective-permute-start.24 = (bf16[256,768]{1,0:T(8,128)(2,1)S(1)}, bf16[256,768]{1,0:T(8,128)(2,1)S(1)}, u32[]{:S(2)}, u32[]{:S(2)}) collective-permute-start(bf16[256,768]{1,0:T(8,128)(2,1)S(1)} %get-tuple-element.165), channel_id=1, source_target_pairs={{0,4},{2,0},{6,2},{4,6},{1,5},{3,1},{7,3},{5,7},{8,12},{10,8},{14,... | collective-permute-start | bytes 1179656 | tf_op jit(solution)/shard_map/ppermute | solution.py:374
  67.4 10.5 %collective-permute-start.27 = (bf16[128,1536]{1,0:T(8,128)(2,1)S(1)}, bf16[128,1536]{1,0:T(8,128)(2,1)S(1)}, u32[]{:S(2)}, u32[]{:S(2)}) collective-permute-start(bf16[128,1536]{1,0:T(8,128)(2,1)S(1)} %get-tuple-element.179), channel_id=1, source_target_pairs={{0,16},{8,24},{16,0},{24,8},{1,17},{9,25},{17,1},{25,9},{2,18},{10... | collective-permute-start | bytes 1179656 | tf_op jit(solution)/shard_map/ppermute | solution.py:279
  68.9 9.0 %collective-permute-start.28 = (bf16[128,1536]{1,0:T(8,128)(2,1)S(1)}, bf16[128,1536]{1,0:T(8,128)(2,1)S(1)}, u32[]{:S(2)}, u32[]{:S(2)}) collective-permute-start(bf16[128,1536]{1,0:T(8,128)(2,1)S(1)} %get-tuple-element.180), channel_id=1, source_target_pairs={{0,8},{8,0},{16,24},{24,16},{1,9},{9,1},{17,25},{25,17},{2,10},{10... | collective-permute-start | bytes 1179656 | tf_op jit(solution)/shard_map/ppermute | solution.py:279
  74.3 2.4 %collective-permute-start.22 = (bf16[256,384]{1,0:T(8,128)(2,1)S(1)}, bf16[256,384]{1,0:T(8,128)(2,1)S(1)}, u32[]{:S(2)}, u32[]{:S(2)}) collective-permute-start(bf16[256,384]{1,0:T(8,128)(2,1)S(1)} %get-tuple-element.163), channel_id=1, source_target_pairs={{0,1},{1,0},{2,3},{3,2},{4,5},{5,4},{6,7},{7,6},{8,9},{9,8},{10,11... | collective-permute-start | bytes 589832 | tf_op jit(solution)/shard_map/ppermute | solution.py:275
  74.5 2.2 %collective-permute-start.23 = (bf16[256,384]{1,0:T(8,128)(2,1)S(1)}, bf16[256,384]{1,0:T(8,128)(2,1)S(1)}, u32[]{:S(2)}, u32[]{:S(2)}) collective-permute-start(bf16[256,384]{1,0:T(8,128)(2,1)S(1)} %get-tuple-element.164), channel_id=1, source_target_pairs={{0,1},{1,0},{2,3},{3,2},{4,5},{5,4},{6,7},{7,6},{8,9},{9,8},{10,11... | collective-permute-start | bytes 589832 | tf_op jit(solution)/shard_map/ppermute | solution.py:275

commit v7 on v6

--- a/solution.py
+++ b/solution.py
@@ -63,8 +63,8 @@
     return jax.ShapeDtypeStruct(shape, dtype)
 
 
-def store_decay(out_ref, row, groups):
-    decay = jnp.broadcast_to(jnp.exp(row[:, -1:]), (groups, DH))
+def store_decay(out_ref, total, groups):
+    decay = jnp.broadcast_to(jnp.exp(total), (groups, DH))
     high = decay.astype(BF16).astype(F32)
     both = jnp.concatenate([high, decay - high], axis=0)
     out_ref[groups * DH : groups * DH + EXTRA, :] = both.astype(BF16)
@@ -80,6 +80,8 @@
         near, far = refs
         bit = side(forward)
         decay = load_decay(near, groups) * bit + (1.0 - bit)
+        row = (lax.axis_index("ctx") // 2).astype(F32)
+        decay = decay * (row if forward else 1.0 - row)
         return lambda h: rows_of(near, h) * bit + decay[h : h + 1, :] * rows_of(far, h)
     decays = [load_decay(ref, groups) for ref in refs[:-1]]
 
@@ -132,11 +134,17 @@
 
 
 def sums(ld_ref, mask, rows):
-    lower = mask.astype(F32)
-    a, b = (lower, ld_ref[...]) if rows else (ld_ref[...], lower)
-    return lax.dot_general(
-        a, b, (((1,), (1,)), ((), ())), precision=lax.Precision.HIGHEST, preferred_element_type=F32
-    )
+    groups, left, terms = ld_ref.shape[0], ld_ref[...], []
+    for _ in range(3):
+        terms.append(left.astype(BF16))
+        left = left - terms[-1].astype(F32)
+    terms = jnp.concatenate([term.astype(F32) for term in terms], axis=0).astype(BF16)
+    lower = mask.astype(F32).astype(BF16)
+    if rows:
+        total = contract(lower, terms, 1, 1)
+        return total[:, :groups] + total[:, groups : 2 * groups] + total[:, 2 * groups :]
+    total = contract(terms, lower, 1, 1)
+    return total[:groups] + total[groups : 2 * groups] + total[2 * groups :]
 
 
 def contrib_kernel(groups, k_hbm, v_hbm, ld_hbm, w_ref, state_ref, first_ref, rest_ref, k_ref, v_ref, ld_ref, sem, w_sem):
@@ -154,7 +162,7 @@
     mask = lower_mask(size)
     col = sums(ld_ref, mask, True)
     tail = jnp.exp(col[size - 1 :, :] - col)
-    store_decay(state_ref, sums(ld_ref, mask, False), groups)
+    store_decay(state_ref, jnp.sum(ld_ref[...], axis=1, keepdims=True), groups)
     moves[1].wait()
     moves[2].wait()
     for h in range(groups):
@@ -216,7 +224,7 @@
     for h in range(groups):
         weighted = (head(q_ref, h).astype(F32) * factor[:, h : h + 1]).astype(BF16)
         state_ref[h * DH : (h + 1) * DH, :] = contract(weighted, head(grad_ref, h), 0, 0).astype(BF16)
-    store_decay(state_ref, row_ref[...], groups)
+    store_decay(state_ref, row_ref[:, -1:], groups)
 
 
 def back_key_kernel(groups, grad_ref, q_ref, v_ref, row_ref, col_ref, dprobs_ref, kpart_ref):
@@ -432,7 +440,7 @@
         first_two, first_one = flipped(w_first, 2), flipped(w_first, 1)
         state = step(again_kernel, state_shape, state)
         pair = step(functools.partial(pair_kernel, groups, True), struct((features, DH), BF16), state, near)
-        before = [near, lax.ppermute(pair, "ctx", [(0, 2), (1, 3)])]
+        before = [near, flipped(pair, 2)]
         lower = lambda array: struct((rows // 2, array.shape[1]), BF16)
     pick_own, pick_other = step(
         functools.partial(picks_kernel, groups, rows_each),

time: 79.6 us -> 79.4 us (level)
  waiting for transfers between devices: 16.6 us -> 20.1 us
  starting transfers between devices: 36.1 us -> 32.9 us
    ppermute x1 -> x0, starting transfers between devices: 3.89 us -> none  [shards(): before = [near, lax.ppermute(pair, 'ctx', [(0, 2), (1, 3)])]]
    ppermute x15 -> x16, waiting for transfers between devices: 14.6 us -> 17.8 us  [flipped(): return lax.ppermute(array, 'ctx', [(i, i ^ bit) for i in range(4)])]
    ppermute x15 -> x16, starting transfers between devices: 20 us -> 20.7 us  [flipped(): return lax.ppermute(array, 'ctx', [(i, i ^ bit) for i in range(4)])]
  transfers between devices with their start and end apart: 29 -> 29, of which waited for: 11 -> 12; matrix products, arithmetic and copies ran while one was open for 0% -> 0% of each run, Pallas kernels for 28% -> 28%
where the time goes in v7:
time: 79.4 us; the launch traced here: 79.1 us
  starting transfers between devices  32.9 us (41%)
  Pallas kernels  23.2 us (29%)
  waiting for transfers between devices  20.1 us (25%)
  local copies, waits for them, and re-layouts  1.68 us (2%)
  between operations  1.28 us (2%)
    pallas_call x32, Pallas kernels, call(): pl.pallas_call(body, name=getattr(kernel, 'func', kernel).__name__, out_s...  23.2 us
    ppermute x16, starting transfers between devices, flipped(): return lax.ppermute(array, 'ctx', [(i, i ^ bit) for i in range(4)])  20.7 us
    ppermute x16, waiting for transfers between devices, flipped(): return lax.ppermute(array, 'ctx', [(i, i ^ bit) for i in range(4)])  17.8 us
    ppermute x3, starting transfers between devices, passed(): return lax.ppermute(array, 'head', pairs)  8.68 us
    ppermute x9, starting transfers between devices, swapped(): return lax.ppermute(array, 'dp', [(0, 1), (1, 0)])  2.01 us
    unnamed x18, local copies, waits for them, and re-layouts  1.68 us
  transfers between devices with their start and end apart: 29, of which 12 were waited for; matrix products, arithmetic and copies ran while one was open for 0% of the time, Pallas kernels for 28%

profile of v7, /device:TPU:0, one launch (start us, length us, event | category | flops | bytes accessed | tf_op | source)
XLA Modules:
  0.0 79.1 jit_solution(11385182586539452190)
XLA Ops:
  0.6 0.5 collective-permute-start.2
  1.2 3.3 %contrib_kernel.1 = (bf16[1040,128]{1,0:T(8,128)(2,1)}, bf16[128,1536]{1,0:T(8,128)(2,1)}, bf16[128,1536]{1,0:T(8,128)(2,1)}, f32[8,128]{1,0:T(8,128)}) custom-call(bf16[256,1024]{1,0:T(8,128)(2,1)} %bitcast.20, bf16[256,1024]{1,0:T(8,128)(2,1)} %bitcast.16, f32[8,256]{1,0:T(8,128)} %bitcast.26, bf16[128,3072]{1,0:T(8,128)(2,1)} %bitcast.28), custom_call_target="tpu_custom_call" | custom-call | tf_op jit(solution)/shard_map/contrib_kernel/pallas_call | solution.py:45
  4.5 2.6 %collective-permute-start = (bf16[1040,128]{1,0:T(8,128)(2,1)}, bf16[1040,128]{1,0:T(8,128)(2,1)S(1)}, u32[]{:S(2)}, u32[]{:S(2)}) collective-permute-start(bf16[1040,128]{1,0:T(8,128)(2,1)} %get-tuple-element.94.refs_0_), channel_id=1, source_target_pairs={{0,8},{8,0},{16,24},{24,16},{1,9},{9,1},{17,25},{25,17},{2,10},{10... | collective-permute-start | bytes 798728 | tf_op jit(solution)/shard_map/ppermute | solution.py:287
  7.0 1.5 %collective-permute-start.4 = (bf16[128,1536]{1,0:T(8,128)(2,1)}, bf16[128,1536]{1,0:T(8,128)(2,1)S(1)}, u32[]{:S(2)}, u32[]{:S(2)}) collective-permute-start(bf16[128,1536]{1,0:T(8,128)(2,1)} %get-tuple-element.106.refs_0_), channel_id=1, source_target_pairs={{0,16},{8,24},{16,0},{24,8},{1,17},{9,25},{17,1},{25,9},{2,18},{10... | collective-permute-start | bytes 1179656 | tf_op jit(solution)/shard_map/ppermute | solution.py:287
  8.6 0.5 collective-permute-start.3
  9.1 0.9 %copy-done.5 = bf16[1040,128]{1,0:T(8,128)(2,1)S(1)} copy-done((bf16[1040,128]{1,0:T(8,128)(2,1)S(1)}, bf16[1040,128]{1,0:T(8,128)(2,1)}, u32[]{:S(2)}) %copy-start.5) | copy-done | bytes 266264
  10.1 0.7 copy-done.7
  10.8 3.7 %collective-permute-done.refs_1_.refs_0_ = bf16[1040,128]{1,0:T(8,128)(2,1)S(1)} collective-permute-done((bf16[1040,128]{1,0:T(8,128)(2,1)}, bf16[1040,128]{1,0:T(8,128)(2,1)S(1)}, u32[]{:S(2)}, u32[]{:S(2)}) %collective-permute-start) | collective-permute-done | bytes 266272 | tf_op jit(solution)/shard_map/ppermute | solution.py:287
  14.5 0.1 pair_kernel.2
  14.6 2.0 %collective-permute-start.1 = (bf16[1024,128]{1,0:T(8,128)(2,1)S(1)}, bf16[1024,128]{1,0:T(8,128)(2,1)S(1)}, u32[]{:S(2)}, u32[]{:S(2)}) collective-permute-start(bf16[1024,128]{1,0:T(8,128)(2,1)S(1)} %get-tuple-element.98), channel_id=1, source_target_pairs={{0,16},{8,24},{16,0},{24,8},{1,17},{9,25},{17,1},{25,9},{2,18},{10... | collective-permute-start | bytes 786440 | tf_op jit(solution)/shard_map/ppermute | solution.py:287
  16.7 0.4 picks_kernel.1
  17.1 1.2 %intra_kernel.1 = (f32[8,256]{1,0:T(8,128)S(1)}, f32[256,8]{1,0:T(8,128)S(1)}, f32[256,1024]{1,0:T(8,128)S(1)}, f32[8,128]{1,0:T(8,128)S(1)}) custom-call(bf16[256,1024]{1,0:T(8,128)(2,1)S(1)} %bitcast.11, bf16[256,1024]{1,0:T(8,128)(2,1)S(1)} %bitcast.21, bf16[256,1024]{1,0:T(8,128)(2,1)S(1)} %bitcast.17, f32[8,256]{1,0:T(8,128)S(1)} %bitcast.27, ...), custom_call_target="tpu_custom_call" | custom-call | tf_op jit(solution)/shard_map/intra_kernel/pallas_call | solution.py:45
  18.3 0.9 %collective-permute-done.4.refs_0_.refs_2_ = bf16[128,1536]{1,0:T(8,128)(2,1)S(1)} collective-permute-done((bf16[128,1536]{1,0:T(8,128)(2,1)}, bf16[128,1536]{1,0:T(8,128)(2,1)S(1)}, u32[]{:S(2)}, u32[]{:S(2)}) %collective-permute-start.4) | collective-permute-done | bytes 393248 | tf_op jit(solution)/shard_map/ppermute | solution.py:287
  19.2 0.7 collective-permute-start.8
  19.9 3.0 %collective-permute-done.3.refs_0_.refs_1_ = bf16[128,1536]{1,0:T(8,128)(2,1)S(1)} collective-permute-done((bf16[128,1536]{1,0:T(8,128)(2,1)}, bf16[128,1536]{1,0:T(8,128)(2,1)S(1)}, u32[]{:S(2)}, u32[]{:S(2)}) %collective-permute-start.3) | collective-permute-done | bytes 393248 | tf_op jit(solution)/shard_map/ppermute | solution.py:287
  23.0 2.0 %collective-permute-start.9 = (bf16[64,1536]{1,0:T(8,128)(2,1)S(1)}, bf16[64,1536]{1,0:T(8,128)(2,1)S(1)}, u32[]{:S(2)}, u32[]{:S(2)}) collective-permute-start(bf16[64,1536]{1,0:T(8,128)(2,1)S(1)} %get-tuple-element.117), channel_id=1, source_target_pairs={{0,16},{8,24},{16,0},{24,8},{1,17},{9,25},{17,1},{25,9},{2,18},{10... | collective-permute-start | bytes 589832 | tf_op jit(solution)/shard_map/ppermute | solution.py:287
  25.1 1.2 %attended_kernel.1 = (bf16[256,512]{1,0:T(8,128)(2,1)S(1)}, bf16[256,512]{1,0:T(8,128)(2,1)S(1)}, bf16[8,128,128]{2,1,0:T(8,128)(2,1)S(1)}, bf16[256,3072]{1,0:T(8,128)(2,1)S(1)}, f32[8,128]{1,0:T(8,128)S(1)}) custom-call(bf16[1040,128]{1,0:T(8,128)(2,1)S(1)} %collective-permute-done.refs_1_.refs_0_, bf16[1024,128]{1,0:T(8,128)(2,1)S(1)} %collective-permute-done.1.refs_1_, ...), custom_call_target="tpu_custom_call" | custom-call | tf_op jit(solution)/shard_map/attended_kernel/pallas_call | solution.py:45
  26.3 0.6 collective-permute-start.7
  27.0 1.4 %collective-permute-start.6 = (bf16[128,1536]{1,0:T(8,128)(2,1)S(1)}, bf16[128,1536]{1,0:T(8,128)(2,1)S(1)}, u32[]{:S(2)}, u32[]{:S(2)}) collective-permute-start(bf16[128,1536]{1,0:T(8,128)(2,1)S(1)} %get-tuple-element.113), channel_id=1, source_target_pairs={{0,8},{8,0},{16,24},{24,16},{1,9},{9,1},{17,25},{25,17},{2,10},{10... | collective-permute-start | bytes 1179656 | tf_op jit(solution)/shard_map/ppermute | solution.py:287
  28.5 1.2 %collective-permute-done.9.refs_4_ = bf16[64,1536]{1,0:T(8,128)(2,1)S(1)} collective-permute-done((bf16[64,1536]{1,0:T(8,128)(2,1)S(1)}, bf16[64,1536]{1,0:T(8,128)(2,1)S(1)}, u32[]{:S(2)}, u32[]{:S(2)}) %collective-permute-start.9) | collective-permute-done | bytes 196640 | tf_op jit(solution)/shard_map/ppermute | solution.py:287
  29.7 0.1 join_kernel.1
  29.8 1.0 %mix_kernel.3 = (f32[256,768]{1,0:T(8,128)S(1)}, f32[256,768]{1,0:T(8,128)S(1)}, bf16[256,512]{1,0:T(8,128)(2,1)S(1)}, bf16[256,512]{1,0:T(8,128)(2,1)S(1)}, bf1...) custom-call(bf16[256,512]{1,0:T(8,128)(2,1)S(1)} %get-tuple-element.111.refs_0_, ...), custom_call_target="tpu_custom_call" | custom-call | tf_op jit(solution)/shard_map/mix_kernel/pallas_call | solution.py:45
  30.8 0.1 collective-permute-start.10
  30.9 0.5 collective-permute-start.11
  31.4 0.1 collective-permute-start.12
  31.4 1.8 %weight_kernel.1 = (bf16[128,1536]{1,0:T(8,128)(2,1)S(1)}, bf16[256,1536]{1,0:T(8,128)(2,1)S(1)}, bf16[128,1536]{1,0:T(8,128)(2,1)S(1)}, f32[128,1536]{1,0:T(8,1...) custom-call(bf16[256,512]{1,0:T(8,128)(2,1)S(1)} %get-tuple-element.111.refs_0_, ...), custom_call_target="tpu_custom_call" | custom-call | tf_op jit(solution)/shard_map/weight_kernel/pallas_call | solution.py:45
  33.3 0.1 ring_kernel.4
  33.4 2.7 %collective-permute-start.16 = (bf16[256,768]{1,0:T(8,128)(2,1)S(1)}, bf16[256,768]{1,0:T(8,128)(2,1)S(1)}, u32[]{:S(2)}, u32[]{:S(2)}) collective-permute-start(bf16[256,768]{1,0:T(8,128)(2,1)S(1)} %get-tuple-element.140), channel_id=1, source_target_pairs={{0,4},{2,0},{6,2},{4,6},{1,5},{3,1},{7,3},{5,7},{8,12},{10,8},{14,... | collective-permute-start | bytes 1179656 | tf_op jit(solution)/shard_map/ppermute | solution.py:382
  36.1 1.9 %collective-permute-done.7.refs_0_.refs_5_.refs_4_ = bf16[128,1536]{1,0:T(8,128)(2,1)S(1)} collective-permute-done((bf16[128,1536]{1,0:T(8,128)(2,1)S(1)}, bf16[128,1536]{1,0:T(8,128)(2,1)S(1)}, u32[]{:S(2)}, u32[]{:S(2)}) %collective-permute-start.7) | collective-permute-done | bytes 393248 | tf_op jit(solution)/shard_map/ppermute | solution.py:287
  38.0 0.2 collective-permute-done.6.refs_0_.refs_4_.refs_3_
  38.2 1.5 %collective-permute-start.14 = (bf16[64,1536]{1,0:T(8,128)(2,1)S(1)}, bf16[64,1536]{1,0:T(8,128)(2,1)S(1)}, u32[]{:S(2)}, u32[]{:S(2)}) collective-permute-start(bf16[64,1536]{1,0:T(8,128)(2,1)S(1)} %get-tuple-element.131), channel_id=1, source_target_pairs={{0,16},{8,24},{16,0},{24,8},{1,17},{9,25},{17,1},{25,9},{2,18},{10... | collective-permute-start | bytes 589832 | tf_op jit(solution)/shard_map/ppermute | solution.py:287
  39.7 1.5 %collective-permute-start.13 = (bf16[64,1536]{1,0:T(8,128)(2,1)S(1)}, bf16[64,1536]{1,0:T(8,128)(2,1)S(1)}, u32[]{:S(2)}, u32[]{:S(2)}) collective-permute-start(bf16[64,1536]{1,0:T(8,128)(2,1)S(1)} %get-tuple-element.129), channel_id=1, source_target_pairs={{0,8},{8,0},{16,24},{24,16},{1,9},{9,1},{17,25},{25,17},{2,10},{10... | collective-permute-start | bytes 589832 | tf_op jit(solution)/shard_map/ppermute | solution.py:287
  41.2 0.5 collective-permute-start.18
  41.7 0.6 collective-permute-start.19
  42.3 1.8 %grad_kernel.2 = (bf16[256,384]{1,0:T(8,128)(2,1)S(1)}, bf16[256,384]{1,0:T(8,128)(2,1)S(1)}, f32[8,128]{1,0:T(8,128)S(1)}) custom-call(bf16[256,3072]{1,0:T(8,128)(2,1)S(1)} %get-tuple-element.125.refs_2_.refs_0_, bf16[256,3072]{1,0:T(8,128)(2,1)S(1)} %collective-permute-done.2.refs_1_.refs_3_, bf16[512,1536]{1,0:T(8,128)(2,1)S(1)} %get-tuple-element.119.refs_2_, ...), custom_call_target="tpu_custom_call" | custom-call | tf_op jit(solution)/shard_map/grad_kernel/pallas_call | solution.py:45
  44.1 2.0 %collective-permute-done.14.refs_4_.refs_6_ = bf16[64,1536]{1,0:T(8,128)(2,1)S(1)} collective-permute-done((bf16[64,1536]{1,0:T(8,128)(2,1)S(1)}, bf16[64,1536]{1,0:T(8,128)(2,1)S(1)}, u32[]{:S(2)}, u32[]{:S(2)}) %collective-permute-start.14) | collective-permute-done | bytes 196640 | tf_op jit(solution)/shard_map/ppermute | solution.py:287
  46.1 1.5 %collective-permute-done.13.refs_3_.refs_5_ = bf16[64,1536]{1,0:T(8,128)(2,1)S(1)} collective-permute-done((bf16[64,1536]{1,0:T(8,128)(2,1)S(1)}, bf16[64,1536]{1,0:T(8,128)(2,1)S(1)}, u32[]{:S(2)}, u32[]{:S(2)}) %collective-permute-start.13) | collective-permute-done | bytes 196640 | tf_op jit(solution)/shard_map/ppermute | solution.py:287
  47.6 1.0 %grad_kernel.3 = (bf16[256,512]{1,0:T(8,128)(2,1)S(1)}, bf16[256,512]{1,0:T(8,128)(2,1)S(1)}, f32[8,128]{1,0:T(8,128)S(1)}) custom-call(bf16[256,3072]{1,0:T(8,128)(2,1)S(1)} %get-tuple-element.125.refs_2_.refs_0_, bf16[256,3072]{1,0:T(8,128)(2,1)S(1)} %collective-permute-done.2.refs_1_.refs_3_, bf16[512,1536]{1,0:T(8,128)(2,1)S(1)} %get-tuple-element.119.refs_2_, ...), custom_call_target="tpu_custom_call" | custom-call | tf_op jit(solution)/shard_map/grad_kernel/pallas_call | solution.py:45
  48.6 0.1 ring_kernel.5
  48.8 1.4 %collective-permute-done.15.refs_1_ = bf16[256,512]{1,0:T(8,128)(2,1)S(1)} collective-permute-done((bf16[256,512]{1,0:T(8,128)(2,1)S(1)}, bf16[256,512]{1,0:T(8,128)(2,1)S(1)}, u32[]{:S(2)}, u32[]{:S(2)}) %collective-permute-start.15) | collective-permute-done | bytes 262176 | tf_op jit(solution)/shard_map/ppermute | solution.py:283
  50.2 1.0 %back_contrib_kernel.1 = (bf16[256,1024]{1,0:T(8,128)(2,1)S(1)}, bf16[1040,128]{1,0:T(8,128)(2,1)S(1)}, f32[8,128]{1,0:T(8,128)S(1)}) custom-call(bf16[256,512]{1,0:T(8,128)(2,1)S(1)} %get-tuple-element.136.refs_0_, bf16[256,512]{1,0:T(8,128)(2,1)S(1)} %collective-permute-done.15.refs_1_, bf16[1024,512]{1,0:T(8,128)(2,1)S(1)} %get-tuple-element.103.refs_5_.refs_2_, ...), custom_call_target="tpu_custom_call" | custom-call | tf_op jit(solution)/shard_map/back_contrib_kernel/pallas_call | solution.py:45
  51.2 1.6 %collective-permute-start.17 = (bf16[1040,128]{1,0:T(8,128)(2,1)S(1)}, bf16[1040,128]{1,0:T(8,128)(2,1)S(1)}, u32[]{:S(2)}, u32[]{:S(2)}) collective-permute-start(bf16[1040,128]{1,0:T(8,128)(2,1)S(1)} %get-tuple-element.145.refs_0_), channel_id=1, source_target_pairs={{0,8},{8,0},{16,24},{24,16},{1,9},{9,1},{17,25},{25,17},{2,10},{10... | collective-permute-start | bytes 798728 | tf_op jit(solution)/shard_map/ppermute | solution.py:287
  52.8 2.6 %collective-permute-start.21 = (bf16[256,768]{1,0:T(8,128)(2,1)S(1)}, bf16[256,768]{1,0:T(8,128)(2,1)S(1)}, u32[]{:S(2)}, u32[]{:S(2)}) collective-permute-start(bf16[256,768]{1,0:T(8,128)(2,1)S(1)} %get-tuple-element.157), channel_id=1, source_target_pairs={{0,4},{2,0},{6,2},{4,6},{1,5},{3,1},{7,3},{5,7},{8,12},{10,8},{14,... | collective-permute-start | bytes 1179656 | tf_op jit(solution)/shard_map/ppermute | solution.py:382
  55.4 0.1 onward_kernel.2
  55.5 0.6 mix_kernel.4
  56.2 0.6 collective-permute-start.26
  56.7 3.3 %collective-permute-done.17.refs_1_.refs_0_ = bf16[1040,128]{1,0:T(8,128)(2,1)S(1)} collective-permute-done((bf16[1040,128]{1,0:T(8,128)(2,1)S(1)}, bf16[1040,128]{1,0:T(8,128)(2,1)S(1)}, u32[]{:S(2)}, u32[]{:S(2)}) %collective-permute-start.17) | collective-permute-done | bytes 266272 | tf_op jit(solution)/shard_map/ppermute | solution.py:287
  60.1 0.1 pair_kernel.3
  60.2 1.5 %collective-permute-start.25 = (bf16[1024,128]{1,0:T(8,128)(2,1)S(1)}, bf16[1024,128]{1,0:T(8,128)(2,1)S(1)}, u32[]{:S(2)}, u32[]{:S(2)}) collective-permute-start(bf16[1024,128]{1,0:T(8,128)(2,1)S(1)} %get-tuple-element.166), channel_id=1, source_target_pairs={{16,0},{24,8},{17,1},{25,9},{18,2},{26,10},{19,3},{27,11},{20,4},{... | collective-permute-start | bytes 786440 | tf_op jit(solution)/shard_map/ppermute | solution.py:568
  61.7 1.2 %back_key_kernel.1 = (bf16[8,256,256]{2,1,0:T(8,128)(2,1)S(1)}, f32[256,1024]{1,0:T(8,128)S(1)}, f32[8,128]{1,0:T(8,128)S(1)}) custom-call(bf16[256,1024]{1,0:T(8,128)(2,1)S(1)} %get-tuple-element.143.refs_0_, bf16[256,1024]{1,0:T(8,128)(2,1)S(1)} %bitcast.14, bf16[256,1024]{1,0:T(8,128)(2,1)S(1)} %bitcast.18, ...), custom_call_target="tpu_custom_call" | custom-call | tf_op jit(solution)/shard_map/back_key_kernel/pallas_call | solution.py:45
  62.9 0.8 %collective-permute-done.21.refs_2_ = bf16[256,768]{1,0:T(8,128)(2,1)S(1)} collective-permute-done((bf16[256,768]{1,0:T(8,128)(2,1)S(1)}, bf16[256,768]{1,0:T(8,128)(2,1)S(1)}, u32[]{:S(2)}, u32[]{:S(2)}) %collective-permute-start.21) | collective-permute-done | bytes 393248 | tf_op jit(solution)/shard_map/ppermute | solution.py:382
  63.7 0.1 ring_kernel.6
  63.9 3.4 %collective-permute-start.24 = (bf16[256,768]{1,0:T(8,128)(2,1)S(1)}, bf16[256,768]{1,0:T(8,128)(2,1)S(1)}, u32[]{:S(2)}, u32[]{:S(2)}) collective-permute-start(bf16[256,768]{1,0:T(8,128)(2,1)S(1)} %get-tuple-element.165), channel_id=1, source_target_pairs={{0,4},{2,0},{6,2},{4,6},{1,5},{3,1},{7,3},{5,7},{8,12},{10,8},{14,... | collective-permute-start | bytes 1179656 | tf_op jit(solution)/shard_map/ppermute | solution.py:382
  67.3 1.5 %collective-permute-start.27 = (bf16[128,1536]{1,0:T(8,128)(2,1)S(1)}, bf16[128,1536]{1,0:T(8,128)(2,1)S(1)}, u32[]{:S(2)}, u32[]{:S(2)}) collective-permute-start(bf16[128,1536]{1,0:T(8,128)(2,1)S(1)} %get-tuple-element.179), channel_id=1, source_target_pairs={{0,16},{8,24},{16,0},{24,8},{1,17},{9,25},{17,1},{25,9},{2,18},{10... | collective-permute-start | bytes 1179656 | tf_op jit(solution)/shard_map/ppermute | solution.py:287
  68.8 0.1 onward_kernel.3
  68.9 1.6 %collective-permute-start.28 = (bf16[128,1536]{1,0:T(8,128)(2,1)S(1)}, bf16[128,1536]{1,0:T(8,128)(2,1)S(1)}, u32[]{:S(2)}, u32[]{:S(2)}) collective-permute-start(bf16[128,1536]{1,0:T(8,128)(2,1)S(1)} %get-tuple-element.180), channel_id=1, source_target_pairs={{0,8},{8,0},{16,24},{24,16},{1,9},{9,1},{17,25},{25,17},{2,10},{10... | collective-permute-start | bytes 1179656 | tf_op jit(solution)/shard_map/ppermute | solution.py:287
  70.4 3.2 %back_query_kernel.1 = (bf16[256,1024]{1,0:T(8,128)(2,1)}, f32[256,1024]{1,0:T(8,128)S(1)}, f32[8,128]{1,0:T(8,128)S(1)}) custom-call(bf16[256,1024]{1,0:T(8,128)(2,1)S(1)} %get-tuple-element.143.refs_0_, bf16[256,1024]{1,0:T(8,128)(2,1)S(1)} %bitcast.15, bf16[256,1024]{1,0:T(8,128)(2,1)S(1)} %bitcast.22, f32[8,256]{1,0:T(8,128)S(1)} %get-tuple-element.138.refs_5_.refs_3_, ...), custom_call_target="tpu_custom_call" | custom-call | tf_op jit(solution)/shard_map/back_query_kernel/pallas_call | solution.py:45
  73.6 0.6 mix_kernel.5
  74.3 0.1 total_kernel.2
  74.5 0.6 collective-permute-start.23
  75.0 1.6 %back_inter_kernel.1 = (bf16[256,1024]{1,0:T(8,128)(2,1)}, bf16[256,1024]{1,0:T(8,128)(2,1)}, f32[8,128]{1,0:T(8,128)S(1)}) custom-call(bf16[1040,128]{1,0:T(8,128)(2,1)S(1)} %collective-permute-done.17.refs_1_.refs_0_, bf16[1024,128]{1,0:T(8,128)(2,1)S(1)} %collective-permute-done.25.refs_1_, bf16[256,1024]{1,0:T(8,128)(2,1)S(1)} %bitcast.23, ...), custom_call_target="tpu_custom_call" | custom-call | flops 2140000000 | tf_op jit(solution)/shard_map/back_inter_kernel/pallas_call | solution.py:45
  76.7 0.9 %ring_kernel.7 = (bf16[256,768]{1,0:T(8,128)(2,1)}, f32[8,128]{1,0:T(8,128)S(1)}) custom-call(f32[256,768]{1,0:T(8,128)S(1)} %get-tuple-element.162.refs_0_, bf16[256,384]{1,0:T(8,128)(2,1)S(1)} %collective-permute-done.22.refs_1_, bf16[256,384]{1,0:T(8,128)(2,1)S(1)} %collective-permute-done.23.refs_2_, ...), custom_call_target="tpu_custom_call" | custom-call | flops 642000000 | tf_op jit(solution)/shard_map/ring_kernel/pallas_call | solution.py:45
  77.6 0.1 collective-permute-done.27.refs_1_
  77.7 1.3 %total_kernel.3 = (f32[128,3072]{1,0:T(8,128)}, f32[8,128]{1,0:T(8,128)}) custom-call(f32[128,3072]{1,0:T(8,128)S(1)} %get-tuple-element.178.refs_0_, bf16[128,1536]{1,0:T(8,128)(2,1)S(1)} %collective-permute-done.27.refs_1_, bf16[128,1536]{1,0:T(8,128)(2,1)S(1)} %collective-permute-done.28.refs_2_, f32[8,128]{1,0:T(8,128)S(1)} %get-tuple-element.181.refs_3_), custom_call_target="tpu_custom_call" | custom-call | tf_op jit(solution)/shard_map/total_kernel/pallas_call | solution.py:45
  (44 shorter events, 0.6 us)
Async XLA Ops:
  0.6 16.0 %collective-permute-start.2 = (bf16[256,3072]{1,0:T(8,128)(2,1)}, bf16[256,3072]{1,0:T(8,128)(2,1)S(1)}, u32[]{:S(2)}, u32[]{:S(2)}) collective-permute-start(bf16[256,3072]{1,0:T(8,128)(2,1)} %bitcast.24), channel_id=1, source_target_pairs={{0,1},{1,0},{2,3},{3,2},{4,5},{5,4},{6,7},{7,6},{8,9},{9,8},{10,11... | collective-permute-start | bytes 4718600 | tf_op jit(solution)/shard_map/ppermute | solution.py:283
  1.1 16.0 %copy-start.6 = (f32[1,8,256]{2,1,0:T(8,128)S(1)}, f32[1,8,256]{2,1,0:T(8,128)}, u32[]{:S(2)}) copy-start(f32[1,8,256]{2,1,0:T(8,128)} %param.9) | copy-start | bytes 24580
  4.4 12.7 %copy-start = (bf16[1,256,1024]{2,1,0:T(8,128)(2,1)S(1)}, bf16[1,256,1024]{2,1,0:T(8,128)(2,1)}, u32[]{:S(2)}) copy-start(bf16[1,256,1024]{2,1,0:T(8,128)(2,1)} %param.6) | copy-start | bytes 1572868
  4.4 12.7 %copy-start.2 = (bf16[1,256,1024]{2,1,0:T(8,128)(2,1)S(1)}, bf16[1,256,1024]{2,1,0:T(8,128)(2,1)}, u32[]{:S(2)}) copy-start(bf16[1,256,1024]{2,1,0:T(8,128)(2,1)} %param.8) | copy-start | bytes 1572868
  4.5 12.7 %copy-start.3 = (bf16[1,256,1024]{2,1,0:T(8,128)(2,1)S(1)}, bf16[1,256,1024]{2,1,0:T(8,128)(2,1)}, u32[]{:S(2)}) copy-start(bf16[1,256,1024]{2,1,0:T(8,128)(2,1)} %param.7) | copy-start | bytes 1572868
  4.5 10.0 %collective-permute-start = (bf16[1040,128]{1,0:T(8,128)(2,1)}, bf16[1040,128]{1,0:T(8,128)(2,1)S(1)}, u32[]{:S(2)}, u32[]{:S(2)}) collective-permute-start(bf16[1040,128]{1,0:T(8,128)(2,1)} %get-tuple-element.94.refs_0_), channel_id=1, source_target_pairs={{0,8},{8,0},{16,24},{24,16},{1,9},{9,1},{17,25},{25,17},{2,10},{10... | collective-permute-start | bytes 798728 | tf_op jit(solution)/shard_map/ppermute | solution.py:287
  7.0 12.2 %collective-permute-start.4 = (bf16[128,1536]{1,0:T(8,128)(2,1)}, bf16[128,1536]{1,0:T(8,128)(2,1)S(1)}, u32[]{:S(2)}, u32[]{:S(2)}) collective-permute-start(bf16[128,1536]{1,0:T(8,128)(2,1)} %get-tuple-element.106.refs_0_), channel_id=1, source_target_pairs={{0,16},{8,24},{16,0},{24,8},{1,17},{9,25},{17,1},{25,9},{2,18},{10... | collective-permute-start | bytes 1179656 | tf_op jit(solution)/shard_map/ppermute | solution.py:287
  8.6 14.4 %collective-permute-start.3 = (bf16[128,1536]{1,0:T(8,128)(2,1)}, bf16[128,1536]{1,0:T(8,128)(2,1)S(1)}, u32[]{:S(2)}, u32[]{:S(2)}) collective-permute-start(bf16[128,1536]{1,0:T(8,128)(2,1)} %get-tuple-element.106.refs_0_), channel_id=1, source_target_pairs={{0,8},{8,0},{16,24},{24,16},{1,9},{9,1},{17,25},{25,17},{2,10},{10... | collective-permute-start | bytes 1179656 | tf_op jit(solution)/shard_map/ppermute | solution.py:287
  9.1 1.0 %copy-start.5 = (bf16[1040,128]{1,0:T(8,128)(2,1)S(1)}, bf16[1040,128]{1,0:T(8,128)(2,1)}, u32[]{:S(2)}) copy-start(bf16[1040,128]{1,0:T(8,128)(2,1)} %get-tuple-element.94.refs_0_) | copy-start | bytes 798724
  10.0 0.7 copy-start.7
  14.6 10.4 %collective-permute-start.1 = (bf16[1024,128]{1,0:T(8,128)(2,1)S(1)}, bf16[1024,128]{1,0:T(8,128)(2,1)S(1)}, u32[]{:S(2)}, u32[]{:S(2)}) collective-permute-start(bf16[1024,128]{1,0:T(8,128)(2,1)S(1)} %get-tuple-element.98), channel_id=1, source_target_pairs={{0,16},{8,24},{16,0},{24,8},{1,17},{9,25},{17,1},{25,9},{2,18},{10... | collective-permute-start | bytes 786440 | tf_op jit(solution)/shard_map/ppermute | solution.py:287
  17.1 7.9 %copy-start.1 = (bf16[128,1536]{1,0:T(8,128)(2,1)S(1)}, bf16[128,1536]{1,0:T(8,128)(2,1)}, u32[]{:S(2)}) copy-start(bf16[128,1536]{1,0:T(8,128)(2,1)} %get-tuple-element.105.refs_0_.refs_3_.refs_2_) | copy-start | bytes 1179652
  17.1 8.0 %copy-start.4 = (bf16[1,256,3072]{2,1,0:T(8,128)(2,1)S(1)}, bf16[1,256,3072]{2,1,0:T(8,128)(2,1)}, u32[]{:S(2)}) copy-start(bf16[1,256,3072]{2,1,0:T(8,128)(2,1)} %param.11) | copy-start | bytes 4718596
  19.2 9.2 %collective-permute-start.8 = (bf16[64,1536]{1,0:T(8,128)(2,1)S(1)}, bf16[64,1536]{1,0:T(8,128)(2,1)S(1)}, u32[]{:S(2)}, u32[]{:S(2)}) collective-permute-start(bf16[64,1536]{1,0:T(8,128)(2,1)S(1)} %get-tuple-element.114), channel_id=1, source_target_pairs={{0,8},{8,0},{16,24},{24,16},{1,9},{9,1},{17,25},{25,17},{2,10},{10... | collective-permute-start | bytes 589832 | tf_op jit(solution)/shard_map/ppermute | solution.py:287
  23.0 6.7 %collective-permute-start.9 = (bf16[64,1536]{1,0:T(8,128)(2,1)S(1)}, bf16[64,1536]{1,0:T(8,128)(2,1)S(1)}, u32[]{:S(2)}, u32[]{:S(2)}) collective-permute-start(bf16[64,1536]{1,0:T(8,128)(2,1)S(1)} %get-tuple-element.117), channel_id=1, source_target_pairs={{0,16},{8,24},{16,0},{24,8},{1,17},{9,25},{17,1},{25,9},{2,18},{10... | collective-permute-start | bytes 589832 | tf_op jit(solution)/shard_map/ppermute | solution.py:287
  26.3 3.5 %collective-permute-start.5 = (bf16[256,512]{1,0:T(8,128)(2,1)S(1)}, bf16[256,512]{1,0:T(8,128)(2,1)S(1)}, u32[]{:S(2)}, u32[]{:S(2)}) collective-permute-start(bf16[256,512]{1,0:T(8,128)(2,1)S(1)} %get-tuple-element.112), channel_id=1, source_target_pairs={{0,1},{1,0},{2,3},{3,2},{4,5},{5,4},{6,7},{7,6},{8,9},{9,8},{10,11... | collective-permute-start | bytes 786440 | tf_op jit(solution)/shard_map/ppermute | solution.py:283
  26.3 11.6 %collective-permute-start.7 = (bf16[128,1536]{1,0:T(8,128)(2,1)S(1)}, bf16[128,1536]{1,0:T(8,128)(2,1)S(1)}, u32[]{:S(2)}, u32[]{:S(2)}) collective-permute-start(bf16[128,1536]{1,0:T(8,128)(2,1)S(1)} %get-tuple-element.113), channel_id=1, source_target_pairs={{0,16},{8,24},{16,0},{24,8},{1,17},{9,25},{17,1},{25,9},{2,18},{10... | collective-permute-start | bytes 1179656 | tf_op jit(solution)/shard_map/ppermute | solution.py:287
  27.0 11.2 %collective-permute-start.6 = (bf16[128,1536]{1,0:T(8,128)(2,1)S(1)}, bf16[128,1536]{1,0:T(8,128)(2,1)S(1)}, u32[]{:S(2)}, u32[]{:S(2)}) collective-permute-start(bf16[128,1536]{1,0:T(8,128)(2,1)S(1)} %get-tuple-element.113), channel_id=1, source_target_pairs={{0,8},{8,0},{16,24},{24,16},{1,9},{9,1},{17,25},{25,17},{2,10},{10... | collective-permute-start | bytes 1179656 | tf_op jit(solution)/shard_map/ppermute | solution.py:287
  28.4 1.2 %copy-start.8 = (bf16[128,1536]{1,0:T(8,128)(2,1)S(1)}, bf16[128,1536]{1,0:T(8,128)(2,1)}, u32[]{:S(2)}) copy-start(bf16[128,1536]{1,0:T(8,128)(2,1)} %get-tuple-element.106.refs_0_) | copy-start | bytes 1179652
  30.8 2.5 %collective-permute-start.10 = (bf16[256,512]{1,0:T(8,128)(2,1)S(1)}, bf16[256,512]{1,0:T(8,128)(2,1)S(1)}, u32[]{:S(2)}, u32[]{:S(2)}) collective-permute-start(bf16[256,512]{1,0:T(8,128)(2,1)S(1)} %get-tuple-element.122), channel_id=1, source_target_pairs={{0,1},{1,0},{2,3},{3,2},{4,5},{5,4},{6,7},{7,6},{8,9},{9,8},{10,11... | collective-permute-start | bytes 786440 | tf_op jit(solution)/shard_map/ppermute | solution.py:283
  30.9 2.4 %collective-permute-start.11 = (bf16[256,512]{1,0:T(8,128)(2,1)S(1)}, bf16[256,512]{1,0:T(8,128)(2,1)S(1)}, u32[]{:S(2)}, u32[]{:S(2)}) collective-permute-start(bf16[256,512]{1,0:T(8,128)(2,1)S(1)} %get-tuple-element.123), channel_id=1, source_target_pairs={{0,1},{1,0},{2,3},{3,2},{4,5},{5,4},{6,7},{7,6},{8,9},{9,8},{10,11... | collective-permute-start | bytes 786440 | tf_op jit(solution)/shard_map/ppermute | solution.py:283
  31.4 1.9 %collective-permute-start.12 = (bf16[256,512]{1,0:T(8,128)(2,1)S(1)}, bf16[256,512]{1,0:T(8,128)(2,1)S(1)}, u32[]{:S(2)}, u32[]{:S(2)}) collective-permute-start(bf16[256,512]{1,0:T(8,128)(2,1)S(1)} %get-tuple-element.124), channel_id=1, source_target_pairs={{0,1},{1,0},{2,3},{3,2},{4,5},{5,4},{6,7},{7,6},{8,9},{9,8},{10,11... | collective-permute-start | bytes 786440 | tf_op jit(solution)/shard_map/ppermute | solution.py:283
  33.4 15.2 %collective-permute-start.16 = (bf16[256,768]{1,0:T(8,128)(2,1)S(1)}, bf16[256,768]{1,0:T(8,128)(2,1)S(1)}, u32[]{:S(2)}, u32[]{:S(2)}) collective-permute-start(bf16[256,768]{1,0:T(8,128)(2,1)S(1)} %get-tuple-element.140), channel_id=1, source_target_pairs={{0,4},{2,0},{6,2},{4,6},{1,5},{3,1},{7,3},{5,7},{8,12},{10,8},{14,... | collective-permute-start | bytes 1179656 | tf_op jit(solution)/shard_map/ppermute | solution.py:382
  38.2 7.9 %collective-permute-start.14 = (bf16[64,1536]{1,0:T(8,128)(2,1)S(1)}, bf16[64,1536]{1,0:T(8,128)(2,1)S(1)}, u32[]{:S(2)}, u32[]{:S(2)}) collective-permute-start(bf16[64,1536]{1,0:T(8,128)(2,1)S(1)} %get-tuple-element.131), channel_id=1, source_target_pairs={{0,16},{8,24},{16,0},{24,8},{1,17},{9,25},{17,1},{25,9},{2,18},{10... | collective-permute-start | bytes 589832 | tf_op jit(solution)/shard_map/ppermute | solution.py:287
  39.7 7.8 %collective-permute-start.13 = (bf16[64,1536]{1,0:T(8,128)(2,1)S(1)}, bf16[64,1536]{1,0:T(8,128)(2,1)S(1)}, u32[]{:S(2)}, u32[]{:S(2)}) collective-permute-start(bf16[64,1536]{1,0:T(8,128)(2,1)S(1)} %get-tuple-element.129), channel_id=1, source_target_pairs={{0,8},{8,0},{16,24},{24,16},{1,9},{9,1},{17,25},{25,17},{2,10},{10... | collective-permute-start | bytes 589832 | tf_op jit(solution)/shard_map/ppermute | solution.py:287
  41.2 14.1 %collective-permute-start.18 = (bf16[128,1536]{1,0:T(8,128)(2,1)S(1)}, bf16[128,1536]{1,0:T(8,128)(2,1)S(1)}, u32[]{:S(2)}, u32[]{:S(2)}) collective-permute-start(bf16[128,1536]{1,0:T(8,128)(2,1)S(1)} %get-tuple-element.147), channel_id=1, source_target_pairs={{0,8},{8,0},{16,24},{24,16},{1,9},{9,1},{17,25},{25,17},{2,10},{10... | collective-permute-start | bytes 1179656 | tf_op jit(solution)/shard_map/ppermute | solution.py:287
  41.7 27.0 %collective-permute-start.19 = (bf16[256,1536]{1,0:T(8,128)(2,1)S(1)}, bf16[256,1536]{1,0:T(8,128)(2,1)S(1)}, u32[]{:S(2)}, u32[]{:S(2)}) collective-permute-start(bf16[256,1536]{1,0:T(8,128)(2,1)S(1)} %get-tuple-element.154), channel_id=1, source_target_pairs={{0,16},{8,24},{16,0},{24,8},{1,17},{9,25},{17,1},{25,9},{2,18},{10... | collective-permute-start | bytes 2359304 | tf_op jit(solution)/shard_map/ppermute | solution.py:287
  48.6 1.6 %collective-permute-start.15 = (bf16[256,512]{1,0:T(8,128)(2,1)S(1)}, bf16[256,512]{1,0:T(8,128)(2,1)S(1)}, u32[]{:S(2)}, u32[]{:S(2)}) collective-permute-start(bf16[256,512]{1,0:T(8,128)(2,1)S(1)} %get-tuple-element.137), channel_id=1, source_target_pairs={{0,1},{1,0},{2,3},{3,2},{4,5},{5,4},{6,7},{7,6},{8,9},{9,8},{10,11... | collective-permute-start | bytes 786440 | tf_op jit(solution)/shard_map/ppermute | solution.py:283
  51.2 8.9 %collective-permute-start.17 = (bf16[1040,128]{1,0:T(8,128)(2,1)S(1)}, bf16[1040,128]{1,0:T(8,128)(2,1)S(1)}, u32[]{:S(2)}, u32[]{:S(2)}) collective-permute-start(bf16[1040,128]{1,0:T(8,128)(2,1)S(1)} %get-tuple-element.145.refs_0_), channel_id=1, source_target_pairs={{0,8},{8,0},{16,24},{24,16},{1,9},{9,1},{17,25},{25,17},{2,10},{10... | collective-permute-start | bytes 798728 | tf_op jit(solution)/shard_map/ppermute | solution.py:287
  52.8 11.0 %collective-permute-start.21 = (bf16[256,768]{1,0:T(8,128)(2,1)S(1)}, bf16[256,768]{1,0:T(8,128)(2,1)S(1)}, u32[]{:S(2)}, u32[]{:S(2)}) collective-permute-start(bf16[256,768]{1,0:T(8,128)(2,1)S(1)} %get-tuple-element.157), channel_id=1, source_target_pairs={{0,4},{2,0},{6,2},{4,6},{1,5},{3,1},{7,3},{5,7},{8,12},{10,8},{14,... | collective-permute-start | bytes 1179656 | tf_op jit(solution)/shard_map/ppermute | solution.py:382
  56.1 7.7 %collective-permute-start.20 = (bf16[256,768]{1,0:T(8,128)(2,1)S(1)}, bf16[256,768]{1,0:T(8,128)(2,1)S(1)}, u32[]{:S(2)}, u32[]{:S(2)}) collective-permute-start(bf16[256,768]{1,0:T(8,128)(2,1)S(1)} %get-tuple-element.156), channel_id=1, source_target_pairs={{0,1},{1,0},{2,3},{3,2},{4,5},{5,4},{6,7},{7,6},{8,9},{9,8},{10,11... | collective-permute-start | bytes 1179656 | tf_op jit(solution)/shard_map/ppermute | solution.py:283
  56.2 18.1 %collective-permute-start.26 = (bf16[128,1536]{1,0:T(8,128)(2,1)S(1)}, bf16[128,1536]{1,0:T(8,128)(2,1)S(1)}, u32[]{:S(2)}, u32[]{:S(2)}) collective-permute-start(bf16[128,1536]{1,0:T(8,128)(2,1)S(1)} %get-tuple-element.170), channel_id=1, source_target_pairs={{0,8},{8,0},{16,24},{24,16},{1,9},{9,1},{17,25},{25,17},{2,10},{10... | collective-permute-start | bytes 1179656 | tf_op jit(solution)/shard_map/ppermute | solution.py:287
  60.2 14.2 %collective-permute-start.25 = (bf16[1024,128]{1,0:T(8,128)(2,1)S(1)}, bf16[1024,128]{1,0:T(8,128)(2,1)S(1)}, u32[]{:S(2)}, u32[]{:S(2)}) collective-permute-start(bf16[1024,128]{1,0:T(8,128)(2,1)S(1)} %get-tuple-element.166), channel_id=1, source_target_pairs={{16,0},{24,8},{17,1},{25,9},{18,2},{26,10},{19,3},{27,11},{20,4},{... | collective-permute-start | bytes 786440 | tf_op jit(solution)/shard_map/ppermute | solution.py:568
  63.9 12.8 %collective-permute-start.24 = (bf16[256,768]{1,0:T(8,128)(2,1)S(1)}, bf16[256,768]{1,0:T(8,128)(2,1)S(1)}, u32[]{:S(2)}, u32[]{:S(2)}) collective-permute-start(bf16[256,768]{1,0:T(8,128)(2,1)S(1)} %get-tuple-element.165), channel_id=1, source_target_pairs={{0,4},{2,0},{6,2},{4,6},{1,5},{3,1},{7,3},{5,7},{8,12},{10,8},{14,... | collective-permute-start | bytes 1179656 | tf_op jit(solution)/shard_map/ppermute | solution.py:382
  67.3 10.4 %collective-permute-start.27 = (bf16[128,1536]{1,0:T(8,128)(2,1)S(1)}, bf16[128,1536]{1,0:T(8,128)(2,1)S(1)}, u32[]{:S(2)}, u32[]{:S(2)}) collective-permute-start(bf16[128,1536]{1,0:T(8,128)(2,1)S(1)} %get-tuple-element.179), channel_id=1, source_target_pairs={{0,16},{8,24},{16,0},{24,8},{1,17},{9,25},{17,1},{25,9},{2,18},{10... | collective-permute-start | bytes 1179656 | tf_op jit(solution)/shard_map/ppermute | solution.py:287
  68.9 8.8 %collective-permute-start.28 = (bf16[128,1536]{1,0:T(8,128)(2,1)S(1)}, bf16[128,1536]{1,0:T(8,128)(2,1)S(1)}, u32[]{:S(2)}, u32[]{:S(2)}) collective-permute-start(bf16[128,1536]{1,0:T(8,128)(2,1)S(1)} %get-tuple-element.180), channel_id=1, source_target_pairs={{0,8},{8,0},{16,24},{24,16},{1,9},{9,1},{17,25},{25,17},{2,10},{10... | collective-permute-start | bytes 1179656 | tf_op jit(solution)/shard_map/ppermute | solution.py:287
  74.2 2.4 %collective-permute-start.22 = (bf16[256,384]{1,0:T(8,128)(2,1)S(1)}, bf16[256,384]{1,0:T(8,128)(2,1)S(1)}, u32[]{:S(2)}, u32[]{:S(2)}) collective-permute-start(bf16[256,384]{1,0:T(8,128)(2,1)S(1)} %get-tuple-element.163), channel_id=1, source_target_pairs={{0,1},{1,0},{2,3},{3,2},{4,5},{5,4},{6,7},{7,6},{8,9},{9,8},{10,11... | collective-permute-start | bytes 589832 | tf_op jit(solution)/shard_map/ppermute | solution.py:283
  74.5 2.2 %collective-permute-start.23 = (bf16[256,384]{1,0:T(8,128)(2,1)S(1)}, bf16[256,384]{1,0:T(8,128)(2,1)S(1)}, u32[]{:S(2)}, u32[]{:S(2)}) collective-permute-start(bf16[256,384]{1,0:T(8,128)(2,1)S(1)} %get-tuple-element.164), channel_id=1, source_target_pairs={{0,1},{1,0},{2,3},{3,2},{4,5},{5,4},{6,7},{7,6},{8,9},{9,8},{10,11... | collective-permute-start | bytes 589832 | tf_op jit(solution)/shard_map/ppermute | solution.py:283
